TPU v7x, 32 devices: a whole 2x2x4 slice. The times are simulated.
32 devices in a mesh: dp: 2 (over y), seq: 4 (over z), tensor: 4 (over x, core).
Axes of the slice: x: 2, y: 2, z: 4, core: 2. Of those that a mesh axis runs over, the one named last changes fastest.
Arguments:
- tokens: bfloat16 [8192, 2048], P(('dp', 'seq')), may hold values from -6 to 6
- sequence_lengths: int32 [2, 3], P('dp'), may hold values from 1 to 4094, as said below
- output_cotangent: bfloat16 [8192, 2048], P(('dp', 'seq')), may hold values from -6 to 6
- query_weight: bfloat16 [2048, 2048], P(('dp', 'seq'), 'tensor'), may hold values from -0.125 to 0.125
- key_weight: bfloat16 [2048, 512], P(('dp', 'seq'), 'tensor'), may hold values from -0.125 to 0.125
- value_weight: bfloat16 [2048, 512], P(('dp', 'seq'), 'tensor'), may hold values from -0.125 to 0.125
- output_weight: bfloat16 [2048, 2048], P('tensor', ('dp', 'seq')), may hold values from -2 to 2
- gate_weight: bfloat16 [2048, 8192], P(('dp', 'seq'), 'tensor'), may hold values from -0.125 to 0.125
- up_weight: bfloat16 [2048, 8192], P(('dp', 'seq'), 'tensor'), may hold values from -0.125 to 0.125
- down_weight: bfloat16 [8192, 2048], P('tensor', ('dp', 'seq')), may hold values from -0.0625 to 0.0625
- attention_norm_gain: bfloat16 [2048], replicated, may hold values from 0.5 to 1.5
- feedforward_norm_gain: bfloat16 [2048], replicated, may hold values from 0.5 to 1.5
- query_adapter_down: bfloat16 [2048, 8], replicated, may hold values from -0.125 to 0.125
- key_adapter_down: bfloat16 [2048, 8], replicated, may hold values from -0.125 to 0.125
- value_adapter_down: bfloat16 [2048, 8], replicated, may hold values from -0.125 to 0.125
- output_adapter_up: bfloat16 [2048, 8], replicated, may hold values from -0.75 to 0.75
- query_adapter_up: bfloat16 [32, 64, 8], P('tensor'), may hold values from -0.75 to 0.75
- key_adapter_up: bfloat16 [8, 64, 8], P('tensor'), may hold values from -0.75 to 0.75
- value_adapter_up: bfloat16 [8, 64, 8], P('tensor'), may hold values from -0.75 to 0.75
- output_adapter_down: bfloat16 [32, 64, 8], P('tensor'), may hold values from -2 to 2
- feature_map_query: bfloat16 [32, 64, 64], P('tensor'), may hold values from -1 to 1
- feature_map_key: bfloat16 [8, 64, 64], P('tensor'), may hold values from -1 to 1
Outputs:
- block_out: bfloat16 [8192, 2048], P(('dp', 'seq'))
- grad_tokens: float32 [8192, 2048], P(('dp', 'seq'))
- grad_q_down: float32 [2048, 8], P(('dp', 'seq', 'tensor'))
- grad_k_down: float32 [2048, 8], P(('dp', 'seq', 'tensor'))
- grad_v_down: float32 [2048, 8], P(('dp', 'seq', 'tensor'))
- grad_o_up: float32 [2048, 8], P(('dp', 'seq', 'tensor'))
- query_up_gradient: float32 [32, 64, 8], P('tensor', ('dp', 'seq'))
- grad_k_up: float32 [8, 64, 8], P('tensor', ('dp', 'seq'))
- value_up_gradient: float32 [8, 64, 8], P('tensor', ('dp', 'seq'))
- grad_o_down: float32 [32, 64, 8], P('tensor', ('dp', 'seq'))
- grad_fmap_q: float32 [32, 64, 64], P('tensor', ('dp', 'seq'))
- grad_fmap_k: float32 [8, 64, 64], P('tensor', ('dp', 'seq'))
Inputs may be any that keep to these rules, and one draw needn't show every extreme that they name: `sequence_lengths`: in each group the 3 lengths add up to 4096; one of them, in a place drawn from the seed, is longer than 3072. The first group holds one sequence of 4094 tokens and two of 1 token.
All inputs are finite; a program needn't handle non-finite values.
Results may differ from a plain program's by a relative error of at most 0.014.
Values may be sent and summed in bfloat16 or wider, within the bound.
No kernel may reach another device: no remote copies, remote signals or barrier semaphores. Data moves between devices by JAX's collectives and lax.ppermute only.
A program may use at most 256 MiB of HBM per device.

v0:
```python
import math

import jax
import jax.numpy as jnp
from jax import lax
from jax.sharding import PartitionSpec as P

WIN = 64


epsilon = 1e-05
rope_base = 500000.0
highest = lax.Precision.HIGHEST


def shifted(array, axis, by):
    count = lax.axis_size(axis)
    pairs = [(i, i + by) for i in range(count) if 0 <= i + by < count]
    return lax.ppermute(array, axis, pairs)


def carried_in(array, axis, combine, identity, reverse):
    count, here = (lax.axis_size(axis), lax.axis_index(axis))
    everything = jax.tree.map(lambda part: lax.all_gather(part, axis), array)
    start = jax.tree.map(
        lambda part, zero: jnp.broadcast_to(jnp.asarray(zero, part.dtype), part.shape),
        array,
        identity,
    )

    def turn(k, before):
        at = count - 1 - k if reverse else k
        reached = at > here if reverse else at < here
        new = combine(before, jax.tree.map(lambda part: part[at], everything))
        return jax.tree.map(lambda a, b: jnp.where(reached, a, b), new, before)

    return lax.fori_loop(0, count, turn, start)


def product_lowered(left, right):
    return jnp.dot(left, right, preferred_element_type=jnp.float32)


def dot_trans(left, right):
    return lax.dot_general(
        left, right, (((1,), (1,)), ((), ())), preferred_element_type=jnp.float32
    )


def product_highest(left, right):
    return jnp.dot(left, right, precision=highest)


def rms_scale(value_rows_all, gain):
    return (
        value_rows_all
        * lax.rsqrt(jnp.mean(value_rows_all * value_rows_all, axis=-1, keepdims=True) + epsilon)
        * gain
    )


def rms_back(value_rows_all, gain, grads):
    factor = lax.rsqrt(jnp.mean(value_rows_all * value_rows_all, axis=-1, keepdims=True) + epsilon)
    normed = value_rows_all * factor
    scaled = grads * gain
    return factor * (scaled - normed * jnp.mean(normed * scaled, axis=-1, keepdims=True))


def rope_tables(relative, head_columns):
    half_width = head_columns // 2
    ladder = jnp.arange(half_width).astype(jnp.float32)
    inverse = jnp.exp(ladder * (-2.0 * math.log(rope_base) / head_columns))
    angles = relative.astype(jnp.float32)[:, None] * inverse[None, :]
    return (jnp.cos(angles), jnp.sin(angles))


def apply_rotation(value_rows_all, cosine_table, sine_table):
    half_width = value_rows_all.shape[-1] // 2
    first_half = value_rows_all[..., :half_width]
    second_half = value_rows_all[..., half_width:]
    cos_rows = cosine_table[:, None, :]
    sin_rows = sine_table[:, None, :]
    return jnp.concatenate(
        [
            first_half * cos_rows - second_half * sin_rows,
            second_half * cos_rows + first_half * sin_rows,
        ],
        axis=-1,
    )


def doc_layout(lengths, positions):
    ends_at = jnp.cumsum(lengths)
    starts_at = ends_at - lengths
    doc_index = jnp.sum((positions[:, None] >= ends_at[None, :]).astype(jnp.int32), axis=1)
    marks = jnp.arange(lengths.shape[0])
    start_of = jnp.sum(
        jnp.where(doc_index[:, None] == marks[None, :], starts_at[None, :], 0), axis=1
    )
    return (doc_index, positions - start_of)


def features(value_rows_all, maps):
    logits = jnp.einsum("thd,hde->the", value_rows_all, maps, preferred_element_type=jnp.float32)
    return (
        jnp.concatenate(
            [jax.nn.softmax(logits, axis=-1), jax.nn.softmax(-logits, axis=-1)], axis=-1
        ),
        logits,
    )


def features_back(logits, grads, value_rows_all, maps):
    half_width = logits.shape[-1]
    upper = jax.nn.softmax(logits, axis=-1)
    lower = jax.nn.softmax(-logits, axis=-1)
    grad_upper = grads[..., :half_width]
    grad_lower = grads[..., half_width:]
    grad_logits = upper * (
        grad_upper - jnp.sum(upper * grad_upper, axis=-1, keepdims=True)
    ) - lower * (grad_lower - jnp.sum(lower * grad_lower, axis=-1, keepdims=True))
    rounded = grad_logits.astype(jnp.bfloat16)
    grad_values = jnp.einsum("the,hde->thd", rounded, maps, preferred_element_type=jnp.float32)
    grad_maps = jnp.einsum(
        "thd,the->hde", value_rows_all, rounded, preferred_element_type=jnp.float32
    )
    return (grad_values, grad_maps)


def carry_join(earlier, later):
    return (
        later[0] + later[2] * earlier[0],
        later[1] + later[2] * earlier[1],
        earlier[2] * later[2],
    )


def per_device(
    tokens,
    sequence_lengths,
    output_cotangent,
    query_weight,
    key_weight,
    value_weight,
    output_weight,
    gate_weight,
    up_weight,
    down_weight,
    attention_norm_gain,
    feedforward_norm_gain,
    query_adapter_down,
    key_adapter_down,
    value_adapter_down,
    output_adapter_up,
    query_adapter_up,
    key_adapter_up,
    value_adapter_up,
    output_adapter_down,
    feature_map_query,
    feature_map_key,
):
    num_tokens = tokens.shape[0]
    local_heads, head_columns, adapter_rank = query_adapter_up.shape
    local_key_value = key_adapter_up.shape[0]
    grouping = local_heads // local_key_value
    score_scale = head_columns ** (-0.5)
    key_rows = num_tokens + WIN
    block_rows = min(num_tokens, 512)
    num_blocks = num_tokens // block_rows
    query_width = local_heads * head_columns
    key_value_width = local_key_value * head_columns
    first_row = lax.axis_index("seq") * num_tokens
    lengths = sequence_lengths[0]
    w_query_all, w_key_all, w_value_all, w_gate_all, w_up_all = (
        lax.all_gather(query_weight, ("dp", "seq"), axis=0, tiled=True),
        lax.all_gather(key_weight, ("dp", "seq"), axis=0, tiled=True),
        lax.all_gather(value_weight, ("dp", "seq"), axis=0, tiled=True),
        lax.all_gather(gate_weight, ("dp", "seq"), axis=0, tiled=True),
        lax.all_gather(up_weight, ("dp", "seq"), axis=0, tiled=True),
    )
    output_weight_stacked, w_down_all = (
        lax.all_gather(output_weight, ("dp", "seq"), axis=1, tiled=True),
        lax.all_gather(down_weight, ("dp", "seq"), axis=1, tiled=True),
    )
    query_pos = first_row + jnp.arange(num_tokens)
    key_pos = first_row - WIN + jnp.arange(key_rows)
    query_doc, query_rel = doc_layout(lengths, query_pos)
    key_doc, key_rel = doc_layout(lengths, key_pos)
    key_valid = key_pos >= 0
    cosine_table, sine_table = rope_tables(query_rel, head_columns)
    inputs_f = tokens.astype(jnp.float32)
    gain_attn = attention_norm_gain.astype(jnp.float32)
    gain_mlp = feedforward_norm_gain.astype(jnp.float32)
    normed = rms_scale(inputs_f, gain_attn).astype(jnp.bfloat16)
    down_stacked = jnp.concatenate(
        [query_adapter_down, key_adapter_down, value_adapter_down], axis=1
    )
    rank_product = product_lowered(normed, down_stacked)
    query_up_product = query_adapter_up.reshape(query_width, adapter_rank)
    key_up_product = key_adapter_up.reshape(key_value_width, adapter_rank)
    value_up_product = value_adapter_up.reshape(key_value_width, adapter_rank)
    q_raw = product_lowered(normed, w_query_all) + product_highest(
        rank_product[:, :adapter_rank], query_up_product.astype(jnp.float32).T
    )
    k_raw = product_lowered(normed, w_key_all) + product_highest(
        rank_product[:, adapter_rank : 2 * adapter_rank], key_up_product.astype(jnp.float32).T
    )
    v_raw = product_lowered(normed, w_value_all) + product_highest(
        rank_product[:, 2 * adapter_rank :], value_up_product.astype(jnp.float32).T
    )
    q_rot = apply_rotation(
        q_raw.reshape(num_tokens, local_heads, head_columns), cosine_table, sine_table
    ).astype(jnp.bfloat16)
    k_rot = apply_rotation(
        k_raw.reshape(num_tokens, local_key_value, head_columns), cosine_table, sine_table
    ).astype(jnp.bfloat16)
    v_vals = v_raw.reshape(num_tokens, local_key_value, head_columns).astype(jnp.bfloat16)
    rim_keys, rim_values = shifted(
        (k_rot[num_tokens - WIN :], v_vals[num_tokens - WIN :]), "seq", 1
    )
    keys_ext = jnp.concatenate([rim_keys, k_rot], axis=0)
    values_ext = jnp.concatenate([rim_values, v_vals], axis=0)
    phi_q_f, logits_q = features(q_rot, feature_map_query)
    phi_q = phi_q_f.astype(jnp.bfloat16)
    phi_k_f, logits_k = features(keys_ext, feature_map_key)
    phi_k = phi_k_f.astype(jnp.bfloat16)
    include = (key_valid[:num_tokens] & (key_doc[:num_tokens] == key_doc[num_tokens - 1])).astype(
        jnp.bfloat16
    )
    opens = jnp.any(key_valid[:num_tokens] & (key_rel[:num_tokens] == 0))
    passing = 1.0 - opens.astype(jnp.float32)
    masked_phi = phi_k[:num_tokens] * include[:, None, None]
    contrib = jnp.einsum(
        "ekf,ekd->kfd", masked_phi, values_ext[:num_tokens], preferred_element_type=jnp.float32
    )
    contrib_norm = jnp.sum(masked_phi.astype(jnp.float32), axis=0)
    identity = (jnp.zeros_like(contrib), jnp.zeros_like(contrib_norm), jnp.ones((), jnp.float32))
    state_in, norm_in, passed_all = carried_in(
        (contrib, contrib_norm, passing), "seq", carry_join, identity, False
    )
    prior = first_row - WIN - 1
    prior_doc, prior_rel = doc_layout(lengths, jnp.reshape(prior, (1,)))
    use_state = ((query_doc == prior_doc[0]) & (prior >= 0)).astype(jnp.float32)

    def block_scores(block_index):
        block_start = block_index * block_rows
        q_block = lax.dynamic_slice_in_dim(q_rot, block_start, block_rows, 0).reshape(
            block_rows, local_key_value, grouping, head_columns
        )
        phi_block = lax.dynamic_slice_in_dim(phi_q, block_start, block_rows, 0).reshape(
            block_rows, local_key_value, grouping, 2 * head_columns
        )
        q_pos_block = lax.dynamic_slice_in_dim(query_pos, block_start, block_rows, 0)
        q_doc_block = lax.dynamic_slice_in_dim(query_doc, block_start, block_rows, 0)
        same_doc = (q_doc_block[:, None] == key_doc[None, :]) & key_valid[None, :]
        gaps = q_pos_block[:, None] - key_pos[None, :]
        mask_win = same_doc & (gaps >= 0) & (gaps < WIN)
        mask_lin = (same_doc & (gaps >= WIN)).astype(jnp.float32)
        raw_scores = (
            jnp.einsum("tkgd,ekd->kgte", q_block, keys_ext, preferred_element_type=jnp.float32)
            * score_scale
        )
        weights_win = jnp.where(mask_win, jnp.exp(raw_scores), 0.0)
        weights_lin = (
            jnp.einsum("tkgf,ekf->kgte", phi_block, phi_k, preferred_element_type=jnp.float32)
            * mask_lin
        )
        use_block = lax.dynamic_slice_in_dim(use_state, block_start, block_rows, 0)
        return (q_block, phi_block, weights_win, weights_lin, mask_lin, use_block)

    def forward_block(block_index):
        q_block, phi_block, weights_win, weights_lin, mask_lin, use_block = block_scores(
            block_index
        )
        weights = weights_win + weights_lin
        phi_float = phi_block.astype(jnp.float32)
        totals = (
            jnp.sum(weights, axis=-1)
            + jnp.einsum("tkgf,kf->kgt", phi_float, norm_in, precision=highest) * use_block
        )
        numer = jnp.einsum(
            "kgte,ekd->kgtd",
            weights.astype(jnp.bfloat16),
            values_ext,
            preferred_element_type=jnp.float32,
        )
        numer = (
            numer
            + jnp.einsum("tkgf,kfd->kgtd", phi_float, state_in, precision=highest)
            * use_block[:, None]
        )
        attended = numer / totals[..., None]
        return (jnp.transpose(attended, (2, 0, 1, 3)).reshape(block_rows, query_width), totals)

    block_ids = jnp.arange(num_blocks)
    attended_all, totals_all = lax.map(forward_block, block_ids)
    attended_f = attended_all.reshape(num_tokens, query_width)
    attended_bfloat = attended_f.astype(jnp.bfloat16)
    output_down_flattened = output_adapter_down.reshape(query_width, adapter_rank)
    output_lowered = product_lowered(attended_bfloat, output_down_flattened)
    output_portion = product_lowered(attended_bfloat, output_weight_stacked) + product_highest(
        output_lowered, output_adapter_up.astype(jnp.float32).T
    )
    o_total = lax.psum(output_portion, "tensor")
    hidden = inputs_f + o_total
    normed_mlp = rms_scale(hidden, gain_mlp).astype(jnp.bfloat16)
    gate_value = product_lowered(normed_mlp, w_gate_all)
    up_value = product_lowered(normed_mlp, w_up_all)
    sigmoid_gate = jax.nn.sigmoid(gate_value)
    silu_gate = gate_value * sigmoid_gate
    activated = (silu_gate * up_value).astype(jnp.bfloat16)
    mlp_total = lax.psum(product_lowered(activated, w_down_all), "tensor")
    block_out = (hidden + mlp_total).astype(jnp.bfloat16)
    w_query_back, w_key_back, w_value_back, w_gate_back, w_up_back = (
        lax.all_gather(query_weight, ("dp", "seq"), axis=0, tiled=True),
        lax.all_gather(key_weight, ("dp", "seq"), axis=0, tiled=True),
        lax.all_gather(value_weight, ("dp", "seq"), axis=0, tiled=True),
        lax.all_gather(gate_weight, ("dp", "seq"), axis=0, tiled=True),
        lax.all_gather(up_weight, ("dp", "seq"), axis=0, tiled=True),
    )
    w_output_back, w_down_back = (
        lax.all_gather(output_weight, ("dp", "seq"), axis=1, tiled=True),
        lax.all_gather(down_weight, ("dp", "seq"), axis=1, tiled=True),
    )
    grad_act = dot_trans(output_cotangent, w_down_back)
    grad_gate = (
        grad_act * up_value * sigmoid_gate * (1.0 + gate_value * (1.0 - sigmoid_gate))
    ).astype(jnp.bfloat16)
    grad_up = (grad_act * silu_gate).astype(jnp.bfloat16)
    grad_normed_mlp = dot_trans(grad_gate, w_gate_back) + dot_trans(grad_up, w_up_back)
    grad_normed_mlp = lax.psum(grad_normed_mlp, "tensor")
    grad_hidden = output_cotangent.astype(jnp.float32) + rms_back(hidden, gain_mlp, grad_normed_mlp)
    branch_gradient = grad_hidden.astype(jnp.bfloat16)
    output_up_product = product_lowered(branch_gradient, output_adapter_up)
    grad_attended = dot_trans(branch_gradient, w_output_back) + product_highest(
        output_up_product, output_down_flattened.astype(jnp.float32).T
    )
    grad_o_down = product_highest(attended_bfloat.astype(jnp.float32).T, output_up_product).reshape(
        local_heads, head_columns, adapter_rank
    )
    grad_o_up = product_highest(branch_gradient.astype(jnp.float32).T, output_lowered)
    shaped = (block_rows, local_key_value, grouping, head_columns)

    def backward_block(carried, block_index):
        grad_keys, grad_phik, grad_values, grad_state, grad_norm = carried
        q_block, phi_block, weights_win, weights_lin, mask_lin, use_block = block_scores(
            block_index
        )
        weights = weights_win + weights_lin
        block_start = block_index * block_rows
        totals = totals_all[block_index]
        out_block = jnp.transpose(
            lax.dynamic_slice_in_dim(attended_f, block_start, block_rows, 0).reshape(shaped),
            (1, 2, 0, 3),
        )
        grad_block = jnp.transpose(
            lax.dynamic_slice_in_dim(grad_attended, block_start, block_rows, 0).reshape(shaped),
            (1, 2, 0, 3),
        )
        grad_totals = -jnp.sum(grad_block * out_block, axis=-1) / totals
        grad_numer = (grad_block / totals[..., None]).astype(jnp.bfloat16)
        grad_weights = (
            jnp.einsum("kgtd,ekd->kgte", grad_numer, values_ext, preferred_element_type=jnp.float32)
            + grad_totals[..., None]
        )
        grad_scores = (grad_weights * weights_win).astype(jnp.bfloat16)
        grad_lin = (grad_weights * mask_lin).astype(jnp.bfloat16)
        grad_q_block = (
            jnp.einsum("kgte,ekd->tkgd", grad_scores, keys_ext, preferred_element_type=jnp.float32)
            * score_scale
        )
        grad_keys = (
            grad_keys
            + jnp.einsum("kgte,tkgd->ekd", grad_scores, q_block, preferred_element_type=jnp.float32)
            * score_scale
        )
        numer_float = grad_numer.astype(jnp.float32)
        use_rows = use_block[:, None, None, None]
        from_state = jnp.einsum(
            "kgtd,kfd->tkgf", numer_float, state_in, precision=highest
        ) + jnp.einsum("kgt,kf->tkgf", grad_totals, norm_in, precision=highest)
        grad_phiq_block = (
            jnp.einsum("kgte,ekf->tkgf", grad_lin, phi_k, preferred_element_type=jnp.float32)
            + from_state * use_rows
        )
        grad_phik = grad_phik + jnp.einsum(
            "kgte,tkgf->ekf", grad_lin, phi_block, preferred_element_type=jnp.float32
        )
        grad_values = grad_values + jnp.einsum(
            "kgte,kgtd->ekd",
            weights.astype(jnp.bfloat16),
            grad_numer,
            preferred_element_type=jnp.float32,
        )
        phi_used = phi_block.astype(jnp.float32) * use_rows
        grad_state = grad_state + jnp.einsum(
            "tkgf,kgtd->kfd", phi_used, numer_float, precision=highest
        )
        grad_norm = grad_norm + jnp.einsum("tkgf,kgt->kf", phi_used, grad_totals, precision=highest)
        pieces = (
            grad_q_block.reshape(block_rows, local_heads, head_columns),
            grad_phiq_block.reshape(block_rows, local_heads, 2 * head_columns),
        )
        return ((grad_keys, grad_phik, grad_values, grad_state, grad_norm), pieces)

    start_grads = (
        jnp.zeros((key_rows, local_key_value, head_columns), jnp.float32),
        jnp.zeros((key_rows, local_key_value, 2 * head_columns), jnp.float32),
        jnp.zeros((key_rows, local_key_value, head_columns), jnp.float32),
        jnp.zeros_like(contrib),
        jnp.zeros_like(contrib_norm),
    )
    summed_grads, block_pieces = lax.scan(backward_block, start_grads, block_ids)
    grad_keys, grad_phik, grad_values, grad_state, grad_norm = summed_grads
    grad_q_rot = block_pieces[0].reshape(num_tokens, local_heads, head_columns)
    grad_phiq = block_pieces[1].reshape(num_tokens, local_heads, 2 * head_columns)
    later_state, later_norm, passed_later = carried_in(
        (grad_state, grad_norm, passing), "seq", carry_join, identity, True
    )
    include_f = include.astype(jnp.float32)[:, None, None]
    head_values = values_ext[:num_tokens].astype(jnp.float32)
    extra_phik = (
        jnp.einsum("ekd,kfd->ekf", head_values, later_state, precision=highest) + later_norm[None]
    ) * include_f
    extra_values = jnp.einsum(
        "ekf,kfd->ekd", masked_phi.astype(jnp.float32), later_state, precision=highest
    )
    tail_pad = ((0, WIN), (0, 0), (0, 0))
    grad_phik = grad_phik + jnp.pad(extra_phik, tail_pad)
    grad_values = grad_values + jnp.pad(extra_values, tail_pad)
    from_features_k, grad_fmap_k = features_back(logits_k, grad_phik, keys_ext, feature_map_key)
    grad_keys = grad_keys + from_features_k
    from_features_q, grad_fmap_q = features_back(logits_q, grad_phiq, q_rot, feature_map_query)
    grad_q_rot = grad_q_rot + from_features_q
    back_keys, back_values = shifted((grad_keys[:WIN], grad_values[:WIN]), "seq", -1)
    lead_pad = ((num_tokens - WIN, 0), (0, 0), (0, 0))
    grad_k_own = grad_keys[WIN:] + jnp.pad(back_keys, lead_pad)
    grad_v_own = grad_values[WIN:] + jnp.pad(back_values, lead_pad)
    query_unrotated_gradient = (
        apply_rotation(grad_q_rot, cosine_table, -sine_table)
        .astype(jnp.bfloat16)
        .reshape(num_tokens, query_width)
    )
    key_unrotated_gradient = (
        apply_rotation(grad_k_own, cosine_table, -sine_table)
        .astype(jnp.bfloat16)
        .reshape(num_tokens, key_value_width)
    )
    value_unrotated_gradient = grad_v_own.astype(jnp.bfloat16).reshape(num_tokens, key_value_width)
    grad_normed = (
        dot_trans(query_unrotated_gradient, w_query_back)
        + dot_trans(key_unrotated_gradient, w_key_back)
        + dot_trans(value_unrotated_gradient, w_value_back)
    )
    ups_all = jnp.concatenate(
        [
            product_lowered(query_unrotated_gradient, query_up_product),
            product_lowered(key_unrotated_gradient, key_up_product),
            product_lowered(value_unrotated_gradient, value_up_product),
        ],
        axis=1,
    )
    grad_normed = grad_normed + product_highest(ups_all, down_stacked.astype(jnp.float32).T)
    grad_normed = lax.psum(grad_normed, "tensor")
    grad_tokens = grad_hidden + rms_back(inputs_f, gain_attn, grad_normed)
    down_stacked_gradient = product_highest(normed.astype(jnp.float32).T, ups_all)
    query_up_gradient = product_highest(
        query_unrotated_gradient.astype(jnp.float32).T, rank_product[:, :adapter_rank]
    ).reshape(local_heads, head_columns, adapter_rank)
    grad_k_up = product_highest(
        key_unrotated_gradient.astype(jnp.float32).T,
        rank_product[:, adapter_rank : 2 * adapter_rank],
    ).reshape(local_key_value, head_columns, adapter_rank)
    value_up_gradient = product_highest(
        value_unrotated_gradient.astype(jnp.float32).T, rank_product[:, 2 * adapter_rank :]
    ).reshape(local_key_value, head_columns, adapter_rank)
    shared = (
        lax.psum_scatter(
            down_stacked_gradient[:, :adapter_rank],
            ("dp", "seq", "tensor"),
            scatter_dimension=0,
            tiled=True,
        ),
        lax.psum_scatter(
            down_stacked_gradient[:, adapter_rank : 2 * adapter_rank],
            ("dp", "seq", "tensor"),
            scatter_dimension=0,
            tiled=True,
        ),
        lax.psum_scatter(
            down_stacked_gradient[:, 2 * adapter_rank :],
            ("dp", "seq", "tensor"),
            scatter_dimension=0,
            tiled=True,
        ),
        lax.psum_scatter(grad_o_up, ("dp", "seq", "tensor"), scatter_dimension=0, tiled=True),
    )
    per_head = (
        lax.psum_scatter(query_up_gradient, ("dp", "seq"), scatter_dimension=1, tiled=True),
        lax.psum_scatter(grad_k_up, ("dp", "seq"), scatter_dimension=1, tiled=True),
        lax.psum_scatter(value_up_gradient, ("dp", "seq"), scatter_dimension=1, tiled=True),
        lax.psum_scatter(grad_o_down, ("dp", "seq"), scatter_dimension=1, tiled=True),
        lax.psum_scatter(grad_fmap_q, ("dp", "seq"), scatter_dimension=1, tiled=True),
        lax.psum_scatter(grad_fmap_k, ("dp", "seq"), scatter_dimension=1, tiled=True),
    )
    return (
        block_out,
        grad_tokens,
        shared[0],
        shared[1],
        shared[2],
        shared[3],
        per_head[0],
        per_head[1],
        per_head[2],
        per_head[3],
        per_head[4],
        per_head[5],
    )


def solution(mesh):
    return jax.shard_map(
        per_device,
        mesh=mesh,
        in_specs=(
            P(("dp", "seq"), None),
            P("dp", None),
            P(("dp", "seq"), None),
            P(("dp", "seq"), "tensor"),
            P(("dp", "seq"), "tensor"),
            P(("dp", "seq"), "tensor"),
            P("tensor", ("dp", "seq")),
            P(("dp", "seq"), "tensor"),
            P(("dp", "seq"), "tensor"),
            P("tensor", ("dp", "seq")),
            P(),
            P(),
            P(),
            P(),
            P(),
            P(),
            P("tensor", None, None),
            P("tensor", None, None),
            P("tensor", None, None),
            P("tensor", None, None),
            P("tensor", None, None),
            P("tensor", None, None),
        ),
        out_specs=(
            P(("dp", "seq"), None),
            P(("dp", "seq"), None),
            P(("dp", "seq", "tensor"), None),
            P(("dp", "seq", "tensor"), None),
            P(("dp", "seq", "tensor"), None),
            P(("dp", "seq", "tensor"), None),
            P("tensor", ("dp", "seq"), None),
            P("tensor", ("dp", "seq"), None),
            P("tensor", ("dp", "seq"), None),
            P("tensor", ("dp", "seq"), None),
            P("tensor", ("dp", "seq"), None),
            P("tensor", ("dp", "seq"), None),
        ),
        check_vma=False,
    )
```

profile of v0, /device:TPU:0, one launch (start us, length us, event | category | flops | bytes accessed | tf_op | source)
XLA Modules:
  0.0 2556.8 jit_solution(2176471557722244012)
XLA Ops:
  12.1 35.9 %all_gather.62 = bf16[2048,128]{1,0:T(8,128)(2,1)S(1)} all-gather(bf16[256,128]{1,0:T(8,128)(2,1)S(1)} %copy-done.77), channel_id=1, replica_groups=mesh['dp'=2,'seq'=4,'tensor'=4] {'dp','seq'}, dimensions={0}, use_global_device_ids=true | all-gather | bytes 589824 | tf_op jit(solution)/shard_map/all_gather | solution.py:177
  56.7 33.9 %all_gather.61 = bf16[2048,128]{1,0:T(8,128)(2,1)S(1)} all-gather(bf16[256,128]{1,0:T(8,128)(2,1)S(1)} %copy-done.78), channel_id=1, replica_groups=mesh['dp'=2,'seq'=4,'tensor'=4] {'dp','seq'}, dimensions={0}, use_global_device_ids=true | all-gather | bytes 589824 | tf_op jit(solution)/shard_map/all_gather | solution.py:176
  126.1 15.0 all-gather
  167.2 66.6 %while.75 = (s32[]{:T(128)}, f32[2,512,512]{1,2,0:T(8,128)}, f32[2,2,4,512]{3,2,1,0:T(4,128)S(1)}, s32[2]{0:T(128)S(1)}, s32[1024]{0:T(1024)S(1)}, /*index=5*/s3...) while((s32[]{:T(128)}, f32[2,512,512]{1,2,0:T(8,128)}, ...), condition=%wide.region_21.22_spmd.clone.clone, body=%wide.region_19.21_spmd.clone.clone.sunk | while | flops 2723757312 | bytes 92625160 | solution.py:296
  250.4 150.3 %all-reduce.10.cloned.1.call-done = f32[1024,2048]{1,0:T(8,128)} async-done(((f32[1024,2048]{1,0:T(8,128)}), f32[1024,2048]{1,0:T(8,128)}) %all-reduce.10.cloned.1.call-update) | async-done | bytes 8388624 | tf_op jit(solution)/shard_map/psum | solution.py:304
  409.6 118.2 %all-gather.16.cloned.1.call-done = bf16[2048,2048]{1,0:T(8,128)(2,1)} async-done(((bf16[256,2048]{1,0:T(8,128)(2,1)}), bf16[2048,2048]{1,0:T(8,128)(2,1)}) %all-gather.16.cloned.1.call-update) | async-done | bytes 8388624 | tf_op jit(solution)/shard_map/all_gather | solution.py:178
  527.7 15.7 fusion.177
  543.5 109.4 %all-gather.18.cloned.1.call-done = bf16[2048,2048]{1,0:T(8,128)(2,1)} async-done(((bf16[256,2048]{1,0:T(8,128)(2,1)}), bf16[2048,2048]{1,0:T(8,128)(2,1)}) %all-gather.18.cloned.1.call-update) | async-done | bytes 8388624 | tf_op jit(solution)/shard_map/all_gather | solution.py:179
  652.9 15.7 fusion.176
  668.6 109.7 %all-gather.20.cloned.1.call-done = bf16[2048,2048]{1,0:T(8,128)(2,1)} async-done(((bf16[2048,256]{1,0:T(8,128)(2,1)}), bf16[2048,2048]{1,0:T(8,128)(2,1)}) %all-gather.20.cloned.1.call-update) | async-done | bytes 8388624 | tf_op jit(solution)/shard_map/all_gather | solution.py:183
  792.9 17.1 fusion.74
  810.0 26.4 %fusion.76 = f32[1024,2048]{1,0:T(8,128)} fusion(f32[1024,2048]{1,0:T(8,128)} %fusion.74, bf16[2048,2048]{1,0:T(8,128)(2,1)} %all-gather.16.cloned.1.call-done, f32[1024,2048]{1,0:T(8,128)} %fusion.177, f32[1024,2048]{1,0:T(8,128)} %fusion.196, f32[1024,2048]{1,0:T(8,128)} %fusion.176), kind=kOutput, calls=%fused_computation.132 | convolution fusion | flops 8613003264 | bytes 50331648 | tf_op jit(solution)/shard_map/dot_general | solution.py:45
  836.6 18.2 fusion.73
  854.7 132.9 %all-reduce.12.cloned.1.call-done = f32[1024,2048]{1,0:T(8,128)} async-done(((f32[1024,2048]{1,0:T(8,128)}), f32[1024,2048]{1,0:T(8,128)}) %all-reduce.12.cloned.1.call-update) | async-done | bytes 8388624 | tf_op jit(solution)/shard_map/psum | solution.py:331
  1018.9 300.6 %while.76 = (s32[]{:T(128)}, f32[1088,2,64]{0,2,1:T(8,128)}, f32[1088,2,128]{2,0,1:T(8,128)}, f32[1088,2,64]{0,2,1:T(8,128)}, f32[2,128,64]{1,2,0:T(8,128)}, /*i...) while((s32[]{:T(128)}, f32[1088,2,64]{0,2,1:T(8,128)}, ...), condition=%wide.region_29.30_spmd.clone.clone.clone, body=%wide.region_27.29_spmd.clone.clone.clone.sunk | while | flops 7161036288 | bytes 230894000 | solution.py:413
  1070.6 38.0 %dynamic_update_slice.35 = f32[2,512,8,128]{1,0,3,2:T(2,128)} dynamic-update-slice(f32[2,512,8,128]{1,0,3,2:T(2,128)} %get-tuple-element.1707, f32[1,512,8,128]{1,0,3,2:T(1,128)} %copy.204, s32[]{:T(128)S(6)} %copy.240, s32[]{:T(128)} %constant.151.clone.1..sunk.3, s32[]{:T(128)} %constant.151.clone.1..sunk.3, s32[]{:T(128)} %constant.151.clone.1..sunk.3) | dynamic-update-slice | bytes 4194308 | tf_op jit(solution)/shard_map/while/body/jit(dynamic_update_index_in_dim)/dynamic_update_slice | solution.py:413
  1108.6 17.8 fusion.348
  1149.0 19.5 dynamic_update_slice.34
  1221.1 38.0 %dynamic_update_slice.35 = f32[2,512,8,128]{1,0,3,2:T(2,128)} dynamic-update-slice(f32[2,512,8,128]{1,0,3,2:T(2,128)} %get-tuple-element.1707, f32[1,512,8,128]{1,0,3,2:T(1,128)} %copy.204, s32[]{:T(128)S(6)} %copy.240, s32[]{:T(128)} %constant.151.clone.1..sunk.3, s32[]{:T(128)} %constant.151.clone.1..sunk.3, s32[]{:T(128)} %constant.151.clone.1..sunk.3) | dynamic-update-slice | bytes 4194308 | tf_op jit(solution)/shard_map/while/body/jit(dynamic_update_index_in_dim)/dynamic_update_slice | solution.py:413
  1259.1 17.8 fusion.348
  1299.6 19.5 dynamic_update_slice.34
  1444.7 52.5 %reduce-scatter.37.cloned.1.call-done = f32[64,8]{1,0:T(8,128)} async-done(((f32[2048,8]{1,0:T(8,128)}), f32[64,8]{1,0:T(8,128)}) %reduce-scatter.37.cloned.1.call-update) | async-done | bytes 2064
  1498.6 132.0 %reduce-scatter.35.cloned.1.call-done = f32[64,8]{1,0:T(8,128)} async-done(((f32[2048,8]{1,0:T(8,128)}), f32[64,8]{1,0:T(8,128)}) %reduce-scatter.35.cloned.1.call-update) | async-done | bytes 2064
  1632.0 132.0 %reduce-scatter.33.cloned.1.call-done = f32[64,8]{1,0:T(8,128)} async-done(((f32[2048,8]{1,0:T(8,128)}), f32[64,8]{1,0:T(8,128)}) %reduce-scatter.33.cloned.1.call-update) | async-done | bytes 2064
  1765.5 133.0 %reduce-scatter.31.cloned.1.call-done = f32[64,8]{1,0:T(8,128)} async-done(((f32[2048,8]{1,0:T(8,128)}), f32[64,8]{1,0:T(8,128)}) %reduce-scatter.31.cloned.1.call-update) | async-done | bytes 2064
  1899.9 286.4 %all-reduce.14.cloned.1.call-done = (f32[1024,2048]{1,0:T(8,128)}, f32[1024,2048]{1,0:T(8,128)}) async-done(((f32[1024,2048]{1,0:T(8,128)}, f32[1024,2048]{1,0:T(8,128)}), (f32[1024,2048]{1,0:T(8,128)}, f32[1024,2048]{1,0:T(8,128)})) %all-reduce.14.cloned.1.call-update) | async-done | bytes 16777232 | tf_op jit(solution)/shard_map/psum | solution.py:312
  2210.5 41.4 %reduce-scatter.25.cloned.1.call-done = f32[8,8,8]{2,1,0:T(8,128)} async-done(((f32[8,64,8]{2,1,0:T(8,128)}), f32[8,8,8]{2,1,0:T(8,128)}) %reduce-scatter.25.cloned.1.call-update) | async-done | bytes 2064 | tf_op jit(solution)/shard_map/reduce_scatter | solution.py:502
  2251.9 64.5 %reduce-scatter.19.cloned.1.call-done = f32[8,8,8]{2,1,0:T(8,128)} async-done(((f32[8,64,8]{2,1,0:T(8,128)}), f32[8,8,8]{2,1,0:T(8,128)}) %reduce-scatter.19.cloned.1.call-update) | async-done | bytes 2064 | tf_op jit(solution)/shard_map/reduce_scatter | solution.py:499
  2316.5 56.2 %reduce-scatter.23.cloned.1.call-done = f32[2,8,8]{2,1,0:T(8,128)} async-done(((f32[2,64,8]{2,1,0:T(8,128)}), f32[2,8,8]{2,1,0:T(8,128)}) %reduce-scatter.23.cloned.1.call-update) | async-done | bytes 528 | tf_op jit(solution)/shard_map/reduce_scatter | solution.py:501
  2372.7 56.3 %reduce-scatter.21.cloned.1.call-done = f32[2,8,8]{2,1,0:T(8,128)} async-done(((f32[2,64,8]{2,1,0:T(8,128)}), f32[2,8,8]{2,1,0:T(8,128)}) %reduce-scatter.21.cloned.1.call-update) | async-done | bytes 528 | tf_op jit(solution)/shard_map/reduce_scatter | solution.py:500
  2429.0 56.3 %reduce-scatter.29.cloned.1.call-done = f32[2,8,64]{2,1,0:T(8,128)} async-done(((f32[2,64,64]{2,1,0:T(8,128)}), f32[2,8,64]{2,1,0:T(8,128)}) %reduce-scatter.29.cloned.1.call-update) | async-done | bytes 4112 | tf_op jit(solution)/shard_map/reduce_scatter | solution.py:504
  2485.2 64.5 %reduce-scatter.27.cloned.1.call-done = f32[8,8,64]{2,1,0:T(8,128)} async-done(((f32[8,64,64]{2,1,0:T(8,128)}), f32[8,8,64]{2,1,0:T(8,128)}) %reduce-scatter.27.cloned.1.call-update) | async-done | bytes 16400 | tf_op jit(solution)/shard_map/reduce_scatter | solution.py:503
  (554 shorter events, 524.9 us)
Async XLA Ops:
  7.2 152.2 %copy-start = (bf16[8,64,64]{2,1,0:T(8,128)(2,1)S(1)}, bf16[8,64,64]{2,1,0:T(8,128)(2,1)}, u32[]{:S(2)}) copy-start(bf16[8,64,64]{2,1,0:T(8,128)(2,1)} %param.50) | copy-start | bytes 196612
  7.2 40.8 %copy-start.87 = (bf16[2048,8]{0,1:T(8,128)(2,1)S(1)}, bf16[2048,8]{0,1:T(8,128)(2,1)}, u32[]{:S(2)}) copy-start(bf16[2048,8]{0,1:T(8,128)(2,1)} %param.44) | copy-start | bytes 98308
  7.2 144.2 %all-gather.12.cloned.1.call-start = ((), (), s32[]{:S(2)}) async-start(), calls=%async_computation.10 | async-start | bytes 2359296 | tf_op jit(solution)/shard_map/all_gather | solution.py:175
  8.0 230.4 %all-gather.14.cloned.1.call-start = ((), (), s32[]{:S(2)}) async-start(), calls=%async_computation.11 | async-start | bytes 2359296 | tf_op jit(solution)/shard_map/all_gather | solution.py:182
  50.4 106.3 %copy-start.49 = (f32[1024,24]{0,1:T(8,128)}, f32[1024,24]{0,1:T(8,128)S(1)}, u32[]{:S(2)}) copy-start(f32[1024,24]{0,1:T(8,128)S(1)} %fusion.193) | copy-start | bytes 294916
  52.5 73.3 %collective-permute-start.1 = (bf16[64,2,64]{0,2,1:T(8,128)(2,1)S(1)}, bf16[64,2,64]{0,2,1:T(8,128)(2,1)S(1)}, u32[]{:S(2)}, u32[]{:S(2)}) collective-permute-start(bf16[64,2,64]{0,2,1:T(8,128)(2,1)S(1)} %bitcast.532), channel_id=1, source_target_pairs={{0,4},{4,8},{8,12},{1,5},{5,9},{9,13},{2,6},{6,10},{10,14},{3,7},{... | collective-permute-start | bytes 49160 | tf_op jit(solution)/shard_map/ppermute | solution.py:19
  91.8 66.0 %copy-start.30 = (f32[1024,32]{0,1:T(8,128)}, f32[1024,32]{0,1:T(8,128)S(1)}, u32[]{:S(2)}) copy-start(f32[1024,32]{0,1:T(8,128)S(1)} %get-tuple-element.1219) | copy-start | bytes 393220
  96.0 54.5 %copy-start.46 = (bf16[1024,2,32]{0,2,1:T(8,128)(2,1)}, bf16[1024,2,32]{0,2,1:T(8,128)(2,1)S(1)}, u32[]{:S(2)}) copy-start(bf16[1024,2,32]{0,2,1:T(8,128)(2,1)S(1)} %get-tuple-element.1212) | copy-start | bytes 393220
  96.0 54.5 %copy-start.47 = (bf16[1024,2,32]{0,2,1:T(8,128)(2,1)}, bf16[1024,2,32]{0,2,1:T(8,128)(2,1)S(1)}, u32[]{:S(2)}) copy-start(bf16[1024,2,32]{0,2,1:T(8,128)(2,1)S(1)} %get-tuple-element.1213) | copy-start | bytes 393220
  96.1 17.4 collective-permute-start
  97.5 303.1 %all-reduce.10.cloned.1.call-start = ((), (), s32[]{:S(2)}) async-start(), calls=%async_computation.12 | async-start | bytes 16777216 | tf_op jit(solution)/shard_map/psum | solution.py:304
  113.5 124.5 %copy-start.71 = (bf16[512,8]{0,1:T(8,128)(2,1)}, bf16[512,8]{0,1:T(8,128)(2,1)S(1)}, u32[]{:S(2)}) copy-start(bf16[512,8]{0,1:T(8,128)(2,1)S(1)} %reshape.419) | copy-start | bytes 24580
  115.6 41.1 %copy-start.39 = (bf16[1024,2,128]{0,2,1:T(8,128)(2,1)}, bf16[1024,2,128]{0,2,1:T(8,128)(2,1)S(1)}, u32[]{:S(2)}) copy-start(bf16[1024,2,128]{0,2,1:T(8,128)(2,1)S(1)} %get-tuple-element.1197) | copy-start | bytes 1572868
  248.6 279.2 %all-gather.16.cloned.1.call-start = ((), (), s32[]{:S(2)}) async-start(), calls=%async_computation.13 | async-start | bytes 9437184 | tf_op jit(solution)/shard_map/all_gather | solution.py:178
  249.1 403.7 %all-gather.18.cloned.1.call-start = ((), (), s32[]{:S(2)}) async-start(), calls=%async_computation.14 | async-start | bytes 9437184 | tf_op jit(solution)/shard_map/all_gather | solution.py:179
  249.7 528.6 %all-gather.20.cloned.1.call-start = ((), (), s32[]{:S(2)}) async-start(), calls=%async_computation.15 | async-start | bytes 9437184 | tf_op jit(solution)/shard_map/all_gather | solution.py:183
  250.3 737.4 %all-reduce.12.cloned.1.call-start = ((), (), s32[]{:S(2)}) async-start(), calls=%async_computation.16 | async-start | bytes 16777216 | tf_op jit(solution)/shard_map/psum | solution.py:331
  836.5 660.8 %reduce-scatter.37.cloned.1.call-start = ((), (), s32[]{:S(2)}) async-start(), calls=%async_computation.26 | async-start | bytes 1081344
  1361.2 33.9 %collective-permute-start.3 = (f32[64,2,64]{0,2,1:T(8,128)S(1)}, f32[64,2,64]{0,2,1:T(8,128)S(1)}, u32[]{:S(2)}, u32[]{:S(2)}) collective-permute-start(f32[64,2,64]{0,2,1:T(8,128)S(1)} %slice.157), channel_id=1, source_target_pairs={{4,0},{8,4},{12,8},{5,1},{9,5},{13,9},{6,2},{10,6},{14,10},{7,3},{... | collective-permute-start | bytes 98312 | tf_op jit(solution)/shard_map/ppermute | solution.py:19
  1362.6 268.0 %reduce-scatter.35.cloned.1.call-start = ((), (), s32[]{:S(2)}) async-start(), calls=%async_computation.25 | async-start | bytes 1081344
  1368.7 26.8 %collective-permute-start.2 = (f32[64,2,64]{0,2,1:T(8,128)S(1)}, f32[64,2,64]{0,2,1:T(8,128)S(1)}, u32[]{:S(2)}, u32[]{:S(2)}) collective-permute-start(f32[64,2,64]{0,2,1:T(8,128)S(1)} %slice.153), channel_id=1, source_target_pairs={{4,0},{8,4},{12,8},{5,1},{9,5},{13,9},{6,2},{10,6},{14,10},{7,3},{... | collective-permute-start | bytes 98312 | tf_op jit(solution)/shard_map/ppermute | solution.py:19
  1400.1 363.9 %reduce-scatter.33.cloned.1.call-start = ((), (), s32[]{:S(2)}) async-start(), calls=%async_computation.24 | async-start | bytes 1081344
  1406.3 492.1 %reduce-scatter.31.cloned.1.call-start = ((), (), s32[]{:S(2)}) async-start(), calls=%async_computation.23 | async-start | bytes 1081344
  1413.4 772.8 %all-reduce.14.cloned.1.call-start = ((), (), s32[]{:S(2)}) async-start(), calls=%async_computation.27 | async-start | bytes 33554432 | tf_op jit(solution)/shard_map/psum | solution.py:312
  1426.4 825.5 %reduce-scatter.25.cloned.1.call-start = ((), (), s32[]{:S(2)}) async-start(), calls=%async_computation.20 | async-start | bytes 294912 | tf_op jit(solution)/shard_map/reduce_scatter | solution.py:502
  1429.3 887.2 %reduce-scatter.19.cloned.1.call-start = ((), (), s32[]{:S(2)}) async-start(), calls=%async_computation.17 | async-start | bytes 294912 | tf_op jit(solution)/shard_map/reduce_scatter | solution.py:499
  1431.0 941.6 %reduce-scatter.23.cloned.1.call-start = ((), (), s32[]{:S(2)}) async-start(), calls=%async_computation.19 | async-start | bytes 73728 | tf_op jit(solution)/shard_map/reduce_scatter | solution.py:501
  1432.1 996.9 %reduce-scatter.21.cloned.1.call-start = ((), (), s32[]{:S(2)}) async-start(), calls=%async_computation.18 | async-start | bytes 73728 | tf_op jit(solution)/shard_map/reduce_scatter | solution.py:500
  1434.0 1051.2 %reduce-scatter.29.cloned.1.call-start = ((), (), s32[]{:S(2)}) async-start(), calls=%async_computation.22 | async-start | bytes 73728 | tf_op jit(solution)/shard_map/reduce_scatter | solution.py:504
  1437.1 749.2 %copy-start.68 = (f32[2048]{0:T(1024)S(1)}, f32[2048]{0:T(1024)}, u32[]{:S(2)}) copy-start(f32[2048]{0:T(1024)} %copy-done.67) | copy-start | bytes 24580
  1437.1 749.2 %copy-start.74 = (f32[1024]{0:T(1024)S(1)}, f32[1024]{0:T(1024)}, u32[]{:S(2)}) copy-start(f32[1024]{0:T(1024)} %copy-done.73) | copy-start | bytes 12292
  1437.1 1112.6 %reduce-scatter.27.cloned.1.call-start = ((), (), s32[]{:S(2)}) async-start(), calls=%async_computation.21 | async-start | bytes 294912 | tf_op jit(solution)/shard_map/reduce_scatter | solution.py:503
  (107 other events, 1045.4 us)
Sparse Core Ops, SparseCore 0:
  10.2 57.9 all-gather.11
  97.6 53.3 all-gather.13
  248.7 151.9 all-reduce.9
  402.6 125.0 all-gather.15
  529.7 123.1 all-gather.17
  654.7 123.5 all-gather.19
  836.6 151.0 all-reduce.11
  1362.8 134.3 reduce-scatter.36
  1499.5 131.0 reduce-scatter.34
  1632.7 131.3 reduce-scatter.32
  1767.0 131.4 reduce-scatter.30
  1900.9 285.3 all-reduce.13
  2190.2 61.7 reduce-scatter.24
  2255.7 60.7 reduce-scatter.18
  2320.0 52.6 reduce-scatter.22
  2376.2 52.6 reduce-scatter.20
  2432.5 52.6 reduce-scatter.28
  2489.0 60.6 reduce-scatter.26
where the time goes:
time: 2570 us; the launch traced here: 2560 us
  waiting for transfers between devices  1700 us (66%)
  matrix products  403 us (16%)
  local copies, waits for them, and re-layouts  202 us (8%)
  blocking collectives  129 us (5%)
  other arithmetic  91.6 us (4%)
    unnamed x22, waiting for transfers between devices  452 us
    psum x1, waiting for transfers between devices, per_device(): mlp_total = lax.psum(product_lowered(activated, w_down_all), 'tensor')  286 us
    psum x1, waiting for transfers between devices, per_device(): o_total = lax.psum(output_portion, 'tensor')  150 us
    psum x1, waiting for transfers between devices, per_device(): grad_normed_mlp = lax.psum(grad_normed_mlp, 'tensor')  133 us
    dynamic_update_slice x8, local copies, waits for them, and re-layouts, per_device(): lax.scan(backward_block, start_grads, block_ids)  129 us
    all_gather x1, waiting for transfers between devices, per_device(): lax.all_gather(gate_weight, ('dp', 'seq'), axis=0, tiled=True)  118 us
    all_gather x1, waiting for transfers between devices, per_device(): lax.all_gather(down_weight, ('dp', 'seq'), axis=1, tiled=True)  110 us
    all_gather x1, waiting for transfers between devices, per_device(): lax.all_gather(up_weight, ('dp', 'seq'), axis=0, tiled=True)  109 us
  transfers between devices with their start and end apart: 22, of which 16 were waited for; matrix products, arithmetic and copies ran while one was open for 11% of the time, Pallas kernels for 0%

commit v1 on v0

v1 whole, which is shorter than its diff:
```python
import math

import jax
import jax.numpy as jnp
from jax import lax
from jax.experimental import pallas as pl
from jax.experimental.pallas import tpu as pltpu
from jax.sharding import PartitionSpec as P

WIN = 64
CHUNK = 128
AUG = 80
RING = 8
FFN_PARTS = 4

epsilon = 1e-05
rope_base = 500000.0
bf16, f32, i32 = jnp.bfloat16, jnp.float32, jnp.int32
MIB = 1 << 20


def nn(a, b):
    return lax.dot_general(a, b, (((1,), (0,)), ((), ())), preferred_element_type=f32)


def nt(a, b):
    return lax.dot_general(a, b, (((1,), (1,)), ((), ())), preferred_element_type=f32)


def tn(a, b):
    return lax.dot_general(a, b, (((0,), (0,)), ((), ())), preferred_element_type=f32)


def halves(x, axis):
    high = x.astype(bf16)
    return jnp.concatenate([high, (x - high.astype(f32)).astype(bf16)], axis=axis)


def halves_outside(x, axis):
    high = lax.reduce_precision(x, 8, 7)
    return jnp.concatenate([high, x - high], axis=axis).astype(bf16)


def exchange(x, axis, bit):
    count = lax.axis_size(axis)
    return lax.ppermute(x, axis, [(i, i ^ bit) for i in range(count)])


def shifted(x, axis, by):
    count = lax.axis_size(axis)
    return lax.ppermute(x, axis, [(i, i + by) for i in range(count) if 0 <= i + by < count])


def place_of(index, seq):
    row, col = index // seq, index % seq
    return row * seq + (col if row % 2 == 0 else seq - 1 - col)


def place_of_traced(index, seq):
    row, col = index // seq, index % seq
    return row * seq + jnp.where(row % 2 == 0, col, seq - 1 - col)


def weight_ring(block, after):
    dp, seq = lax.axis_size("dp"), lax.axis_size("seq")
    count = dp * seq
    if count > RING:
        return [lax.all_gather(block, ("dp", "seq"), axis=0, tiled=True)]
    order = [place_of(i, seq) for i in range(count)]
    up = [(order[i], order[(i + 1) % count]) for i in range(count)]
    half = block.shape[0] // 2
    a, b = block[:half], block[half:]
    if after:
        a, b = lax.optimization_barrier((a, b, *after))[:2]
    first, second = [a], [b]
    for _ in range(count - 1):
        a = lax.ppermute(a, ("dp", "seq"), up)
        b = lax.ppermute(b, ("dp", "seq"), [(j, i) for i, j in up])
        first.append(a)
        second.append(b)
    return first + second


def ring_offsets(rows):
    dp, seq = lax.axis_size("dp"), lax.axis_size("seq")
    count = dp * seq
    if count > RING:
        return jnp.zeros((1,), i32)
    place = place_of_traced(lax.axis_index("dp") * seq + lax.axis_index("seq"), seq)
    steps = jnp.arange(count)
    first = place_of_traced((place - steps) % count, seq) * rows
    second = place_of_traced((place + steps) % count, seq) * rows + rows // 2
    return jnp.concatenate([first, second]).astype(i32)


def reduce_to_own(x, axis):
    size, index = lax.axis_size(axis), lax.axis_index(axis)
    while size > 1:
        half = size // 2
        bit = (index // half) % 2
        x = x.reshape((2, half) + x.shape[1:])
        send = lax.dynamic_index_in_dim(x, 1 - bit, 0, keepdims=False)
        keep = lax.dynamic_index_in_dim(x, bit, 0, keepdims=False)
        x = keep + exchange(send, axis, half)
        size = half
    return x[0]


def reduce_quarters(far, near):
    far_mine = far[1].astype(f32) + exchange(far[0], "tensor", 1).astype(f32)
    crossed = exchange(far_mine.astype(bf16), "tensor", 2)
    near_mine = near[1].astype(f32) + exchange(near[0], "tensor", 1).astype(f32)
    return near_mine + crossed.astype(f32)


def gather_quarters(own):
    across = exchange(own, "tensor", 2)
    beside = exchange(own, "tensor", 1)
    last = exchange(across, "tensor", 1)
    return jnp.stack([own, beside, across, last])


def load_pieces(pieces, offsets, held, sems):
    copies = [
        pltpu.make_async_copy(
            piece,
            held.at[pl.ds(pl.multiple_of(offsets[i], 16), piece.shape[0])],
            sems.at[i],
        )
        for i, piece in enumerate(pieces)
    ]
    for copy in copies:
        copy.start()
    for copy in copies:
        copy.wait()


def params(limit):
    return pltpu.CompilerParams(vmem_limit_bytes=limit * MIB)


def cost(flops, moved, exps=0):
    return pl.CostEstimate(flops=int(flops), bytes_accessed=int(moved), transcendentals=int(exps))


ANY = pl.BlockSpec(memory_space=pl.ANY)


def whole(shape):
    return pl.BlockSpec(shape, lambda *_: (0,) * len(shape))


def rope(x, cos, sin):
    width = 2 * cos.shape[0]
    half = width // 2
    out = []
    for at in range(0, x.shape[0], width):
        x1, x2 = x[at : at + half], x[at + half : at + width]
        out += [x1 * cos - x2 * sin, x2 * cos + x1 * sin]
    return jnp.concatenate(out, axis=0)


def hedgehog(a, width):
    out = []
    for at in range(0, a.shape[0], width):
        one = a[at : at + width]
        for e in (
            jnp.exp(one - jnp.max(one, axis=0, keepdims=True)),
            jnp.exp(jnp.min(one, axis=0, keepdims=True) - one),
        ):
            out.append(e * (1.0 / jnp.sum(e, axis=0, keepdims=True)))
    return jnp.concatenate(out, axis=0).astype(bf16)


def hedgehog_back(phi, grad, width):
    out = []
    for at in range(0, phi.shape[0], 2 * width):
        p1, p2 = phi[at : at + width].astype(f32), phi[at + width : at + 2 * width].astype(f32)
        d1, d2 = grad[at : at + width], grad[at + width : at + 2 * width]
        out.append(
            p1 * (d1 - jnp.sum(p1 * d1, axis=0, keepdims=True))
            - p2 * (d2 - jnp.sum(p2 * d2, axis=0, keepdims=True))
        )
    return jnp.concatenate(out, axis=0).astype(bf16)


def prep_body(dims, offsets, last_docs, nx, low_up, cos_q, sin_q, cos_k, sin_k, map_q, map_k, doc_row, *rest):
    tokens, ext, q_width, kv_width, head, n_pieces, chunks = dims
    pieces, rest = rest[:n_pieces], rest[n_pieces:]
    q_t, phi_q, k_n, k_t, v_n, v_a, phi_kn, phi_kt, contrib, held, sems = rest
    load_pieces(pieces, offsets, held, sems)
    kv_heads = kv_width // head
    step = ext // 3
    v_a[...] = jnp.zeros(v_a.shape, bf16)
    for at in range(0, ext, step):
        rows = pl.ds(at, step)
        raw = nn(nx[rows, :], held[:, q_width:]) + low_up[rows, q_width:]
        v = raw[:, kv_width:].astype(bf16)
        v_n[rows, :] = v
        v_tr = raw[:, kv_width:].T.astype(bf16)
        for k in range(kv_heads):
            v_a[k * AUG : k * AUG + head, rows] = v_tr[k * head : (k + 1) * head]
            v_a[k * AUG + head : (k + 1) * AUG, rows] = (
                lax.broadcasted_iota(i32, (AUG - head, step), 0) < 2
            ).astype(f32).astype(bf16)
        k_rot = rope(raw[:, :kv_width].T, cos_k[:, rows], sin_k[:, rows])
        k_bf = k_rot.astype(bf16)
        k_t[:, rows] = k_bf
        k_n[rows, :] = k_rot.T.astype(bf16)
        phi = hedgehog(nn(map_k[...], k_bf), head)
        phi_kt[:, rows] = phi
        phi_kn[rows, :] = phi.astype(f32).T.astype(bf16)
    incl = (doc_row[:, :tokens] == last_docs[chunks]).astype(f32).astype(bf16)
    for k in range(kv_heads):
        masked = v_a[k * AUG : (k + 1) * AUG, :tokens] * incl
        contrib[k] = nn(masked, phi_kn[:tokens, k * 2 * head : (k + 1) * 2 * head])
    step = tokens // 2
    group = q_width // kv_heads
    for at in range(0, tokens, step):
        rows = pl.ds(at, step)
        raw = nn(nx[pl.ds(WIN + at, step), :], held[:, :q_width])
        raw = raw + low_up[pl.ds(WIN + at, step), :q_width]
        q_bf = rope(raw.T, cos_q[:, rows], sin_q[:, rows]).astype(bf16)
        q_t[:, rows] = q_bf
        for k in range(kv_heads):
            logits = nn(map_q[k], q_bf[k * group : (k + 1) * group])
            phi_q[2 * k * group : 2 * (k + 1) * group, rows] = hedgehog(logits, head)


def masks(q_doc, k_doc, heads):
    keys = CHUNK + WIN
    j = lax.broadcasted_iota(i32, (keys, CHUNK), 0)
    t = lax.broadcasted_iota(i32, (keys, CHUNK), 1)
    same = k_doc == q_doc
    win = same & (j > t) & (j <= t + WIN)
    lin = (same & (j <= t))[:CHUNK]
    win_f = jnp.concatenate([win.astype(f32)] * heads, axis=1)
    lin_f = jnp.concatenate([lin.astype(f32)] * heads, axis=1)
    return win_f > 0.5, lin_f > 0.5


def side(ref, first, count, size):
    return jnp.concatenate([ref[first + g * size : first + (g + 1) * size, :] for g in range(count)], axis=1)


def window_weights(q, phi_q, k_win, phi_k, win, lin, scale):
    scores = nn(k_win, q)
    weights_win = jnp.where(win, jnp.exp(scores * scale), 0.0)
    linear = jnp.where(lin, nn(phi_k, phi_q), 0.0)
    return weights_win, jnp.concatenate([weights_win[:CHUNK] + linear, weights_win[CHUNK:]], axis=0)


def forward_body(dims, last_docs, q_t, phi_q, k_n, v_a, phi_kn, doc_col, doc_row, q_doc, state_in, att, att_t, totals, states, state):
    kv_heads, group, head = dims
    chunk = pl.program_id(0)
    start = pl.multiple_of(chunk * CHUNK, CHUNK)

    @pl.when(chunk == 0)
    def _():
        state[...] = state_in[...]

    keys = CHUNK + WIN
    win, lin = masks(q_doc[...], doc_col[pl.ds(start, keys), :], group)
    use = (q_doc[...] == last_docs[chunk]).astype(f32)
    use = jnp.concatenate([use] * group, axis=1)
    incl = (doc_row[:, pl.ds(start, CHUNK)] == last_docs[chunk + 1]).astype(f32).astype(bf16)
    passing = (last_docs[chunk] == last_docs[chunk + 1]).astype(f32)
    scale = head**-0.5
    out = []
    for k in range(kv_heads):
        q = side(q_t, k * group * head, group, head)
        phi = side(phi_q, 2 * k * group * head, group, 2 * head)
        k_win = k_n[pl.ds(start, keys), k * head : (k + 1) * head]
        phi_k = phi_kn[pl.ds(start, CHUNK), 2 * k * head : 2 * (k + 1) * head]
        v_win = v_a[k * AUG : (k + 1) * AUG, pl.ds(start, 2 * CHUNK)]
        _, weights = window_weights(q, phi, k_win, phi_k, win, lin, scale)
        before = state[k]
        from_state = nn(before.astype(bf16), phi) * use
        total = jnp.sum(weights, axis=0, keepdims=True) + from_state[head : head + 1]
        numer = nn(v_win[:, :keys], weights.astype(bf16))[:head] + from_state[:head]
        attended = numer * (1.0 / total)
        for g in range(group):
            out.append(attended[:, g * CHUNK : (g + 1) * CHUNK])
            totals[k * group + g : k * group + g + 1, :] = total[:, g * CHUNK : (g + 1) * CHUNK]
        states[0, k] = before.T.astype(bf16)
        state[k] = nn(v_win[:, :CHUNK] * incl, phi_k) + passing * before
    attended = jnp.concatenate(out, axis=0)
    att_t[...] = attended
    att[...] = attended.T.astype(bf16)


def o_body(n_pieces, offsets, nat, att, down, up, *rest):
    pieces = rest[:n_pieces]
    part, lowered, held, sems = rest[n_pieces:]

    @pl.when(pl.program_id(0) == 0)
    def _():
        load_pieces(pieces, offsets, held, sems)

    low = nn(att[...], down[...])
    lowered[0] = low
    part[0] = (nt(att[...], held[...]) + nn(halves(low, 1), up[...])).astype(bf16)


def ffn_body(n_pieces, units, first, offsets, order, nat, n2, cot, *rest):
    pieces, rest = rest[:n_pieces], rest[n_pieces:]
    if first:
        mlp, grad, held, sems = rest
    else:
        mlp_in, grad_in, mlp, grad, held, sems = rest

    @pl.when(pl.program_id(0) == 0)
    def _():
        load_pieces(pieces, offsets, held, sems)

    gate = nn(n2[0], held[:, :units])
    up = nn(n2[0], held[:, units : 2 * units])
    grad_act = nn(cot[...], held[:, 2 * units :])
    s = 1.0 / (1.0 + jnp.exp(-gate))
    silu = gate * s
    act = (silu * up).astype(bf16)
    grad_gate = (grad_act * up * s * (1.0 + gate * (1.0 - s))).astype(bf16)
    grad_up = (grad_act * silu).astype(bf16)
    down_sum = nt(act, held[:, 2 * units :])
    grad_sum = nt(grad_gate, held[:, :units]) + nt(grad_up, held[:, units : 2 * units])
    if not first:
        down_sum = down_sum + mlp_in[0]
        grad_sum = grad_sum + grad_in[0]
    mlp[0] = down_sum.astype(mlp.dtype)
    grad[0] = grad_sum.astype(grad.dtype)


def go_body(dims, offsets, nat, before_doc, branch, o_up, o_down, att_t, totals, phi_q, q_doc, *rest):
    n_pieces, kv_heads, group, head = dims
    pieces = rest[:n_pieces]
    numer, grad_totals, up_product, dstate, held, sems = rest[n_pieces:]

    @pl.when(pl.program_id(0) == 0)
    def _():
        load_pieces(pieces, offsets, held, sems)
        dstate[...] = jnp.zeros(dstate.shape, f32)

    up = nn(branch[0], o_up[...])
    up_product[...] = up
    grad = (nn(branch[0], held[...]) + nn(halves(up, 1), o_down[...])).T
    use = (q_doc[...] == before_doc[0]).astype(f32)
    columns = grad.shape[1]
    for k in range(kv_heads):
        total = jnp.zeros((2 * head, AUG), f32)
        for g in range(group):
            h = k * group + g
            rows = slice(h * head, (h + 1) * head)
            inverse = 1.0 / totals[h : h + 1, :]
            one = grad[rows]
            g_total = -jnp.sum(one * att_t[rows, :], axis=0, keepdims=True) * inverse
            g_numer = (one * inverse).astype(bf16)
            numer[rows, :] = g_numer
            grad_totals[h : h + 1, :] = g_total
            aug = augmented(g_numer, g_total * use, columns, head, use)
            total = total + nt(phi_q[2 * h * head : 2 * (h + 1) * head, :], aug)
        dstate[k] += total


def augmented(g_numer, g_total, columns, head, use=None):
    top = g_numer if use is None else g_numer * use.astype(bf16)
    high = g_total.astype(bf16).astype(f32)
    row = lax.broadcasted_iota(i32, (AUG - head, columns), 0)
    below = jnp.where(row == 0, high, jnp.where(row == 1, g_total - high, 0.0))
    return jnp.concatenate([top, below.astype(bf16)], axis=0)


def backward_body(
    dims, last_docs, q_t, phi_q, numer, grad_totals, k_n, k_t, v_n, v_a, phi_kn, phi_kt, doc_col, doc_row, q_doc,
    states, later_in, cos_q, sin_q, map_q, map_k,
    g_nat, g_kt, g_vt, g_map_q, g_map_k, later, acc_phi,
):
    kv_heads, group, head, chunks = dims
    step = pl.program_id(0)
    chunk = chunks - 1 - step
    start = pl.multiple_of(chunk * CHUNK, CHUNK)
    keys = CHUNK + WIN

    @pl.when(step == 0)
    def _():
        later[...] = later_in[...]
        g_kt[...] = jnp.zeros(g_kt.shape, f32)
        g_vt[...] = jnp.zeros(g_vt.shape, f32)
        acc_phi[...] = jnp.zeros(acc_phi.shape, f32)
        g_map_q[...] = jnp.zeros(g_map_q.shape, f32)

    win, lin = masks(q_doc[...], doc_col[pl.ds(start, keys), :], group)
    use1 = (q_doc[...] == last_docs[chunk]).astype(f32)
    use = jnp.concatenate([use1] * group, axis=1)
    incl = (doc_row[:, pl.ds(start, CHUNK)] == last_docs[chunk + 1]).astype(f32)
    passing = (last_docs[chunk] == last_docs[chunk + 1]).astype(f32)
    scale = head**-0.5
    two = pl.ds(start, 2 * CHUNK)
    one = pl.ds(start, CHUNK)
    pad = jnp.zeros((head, 2 * CHUNK - keys), f32)
    grads = []
    for k in range(kv_heads):
        lanes = slice(k * head, (k + 1) * head)
        wide = slice(2 * k * head, 2 * (k + 1) * head)
        q = side(q_t, k * group * head, group, head)
        phi = side(phi_q, 2 * k * group * head, group, 2 * head)
        gn = side(numer, k * group * head, group, head)
        gt = side(grad_totals, k * group, group, 1)
        weights_win, weights = window_weights(
            q, phi, k_n[pl.ds(start, keys), lanes], phi_kn[one, wide], win, lin, scale
        )
        grad_w = nn(v_n[pl.ds(start, keys), lanes], gn) + gt
        gs = (grad_w * weights_win).astype(bf16)
        gl = jnp.where(lin, grad_w[:CHUNK], 0.0).astype(bf16)
        gq = nn(k_t[lanes, two][:, :keys], gs) * scale
        gk = nt(q, gs) * scale
        gv = nt(gn, weights.astype(bf16))
        aug = augmented(gn, gt, group * CHUNK, head)
        gphi_q = nn(phi_kt[wide, one], gl) + use * nn(states[0, k], aug)
        gphi_k = nt(phi, gl)
        after = later[k]
        after_bf = after.astype(bf16)
        v_aug = v_a[k * AUG : (k + 1) * AUG, one]
        gphi_k = gphi_k + incl * nn(after_bf, v_aug)
        from_later = incl * nn(after.T.astype(bf16), phi_kt[wide, one])[:head]
        gv = gv + jnp.concatenate([from_later, jnp.zeros((head, keys - CHUNK), f32)], axis=1)
        later[k] = nt(phi, augmented(gn, gt * use, group * CHUNK, head, use)) + passing * after
        g_kt[lanes, two] += jnp.concatenate([gk, pad], axis=1)
        g_vt[lanes, two] += jnp.concatenate([gv, pad], axis=1)
        acc_phi[wide, one] += gphi_k
        heads = [slice(g * CHUNK, (g + 1) * CHUNK) for g in range(group)]
        rows = slice(k * group * head, (k + 1) * group * head)
        grad_phi = jnp.concatenate([gphi_q[:, at] for at in heads], axis=0)
        phi_rows = phi_q[2 * k * group * head : 2 * (k + 1) * group * head, :]
        ga = hedgehog_back(phi_rows, grad_phi, head)
        gq_rows = jnp.concatenate([gq[:, at] for at in heads], axis=0) + tn(map_q[k], ga)
        g_map_q[k] += nt(q_t[rows, :], ga)
        grads.append(rope(gq_rows, cos_q[...], -sin_q[...]))
    g_nat[...] = jnp.concatenate(grads, axis=0).T.astype(bf16)

    @pl.when(step == chunks - 1)
    def _():
        ga = hedgehog_back(phi_kt[...], acc_phi[...], head)
        g_kt[...] += tn(map_k[...], ga)
        g_map_k[...] = nt(k_t[...], ga)


def gn_body(n_pieces, offsets, nat, g_q, g_kv, ups_q, ups_kv, downs, *rest):
    pieces = rest[:n_pieces]
    part, ups, held, sems = rest[n_pieces:]

    @pl.when(pl.program_id(0) == 0)
    def _():
        load_pieces(pieces, offsets, held, sems)

    q_width = g_q.shape[1]
    up = nn(g_q[...], ups_q[...]) + nn(g_kv[...], ups_kv[...])
    ups[0] = up
    total = nt(g_q[...], held[:, :q_width]) + nt(g_kv[...], held[:, q_width:])
    part[0] = (total + nn(halves(up, 1), downs[...])).astype(bf16)


def place_body(nat, x, out):
    out[...] = x[0].astype(out.dtype)


def place(x, nat, dtype):
    count, rows, width = x.shape
    return pl.pallas_call(
        place_body,
        grid_spec=pltpu.PrefetchScalarGridSpec(
            num_scalar_prefetch=1,
            grid=(count,),
            in_specs=[pl.BlockSpec((1, rows, width), lambda i, nat: (i, 0, 0))],
            out_specs=pl.BlockSpec((rows, width), lambda i, nat: (nat[i], 0)),
        ),
        out_shape=jax.ShapeDtypeStruct((count * rows, width), dtype),
        compiler_params=params(32),
        cost_estimate=cost(0, x.size * 6),
        name="place",
    )(nat, x)


def rms_factor(x):
    return lax.rsqrt(jnp.mean(x * x, axis=-1, keepdims=True) + epsilon)


def rms_back(x, gain, grads):
    factor = rms_factor(x)
    unit = x * factor
    scaled = grads * gain
    return factor * (scaled - unit * jnp.mean(unit * scaled, axis=-1, keepdims=True))


def block_diagonal(blocks):
    count, rows, cols = blocks.shape
    eye = jnp.eye(count, dtype=blocks.dtype)
    return (blocks[:, :, None, :] * eye[:, None, :, None]).reshape(count * rows, count * cols)


def diagonal_blocks(x, count):
    size = x.shape[0] // count
    return jnp.stack([x[i * size : (i + 1) * size, i * size : (i + 1) * size] for i in range(count)])


def per_device(
    tokens,
    sequence_lengths,
    output_cotangent,
    query_weight,
    key_weight,
    value_weight,
    output_weight,
    gate_weight,
    up_weight,
    down_weight,
    attention_norm_gain,
    feedforward_norm_gain,
    query_adapter_down,
    key_adapter_down,
    value_adapter_down,
    output_adapter_up,
    query_adapter_up,
    key_adapter_up,
    value_adapter_up,
    output_adapter_down,
    feature_map_query,
    feature_map_key,
):
    rows, model = tokens.shape
    heads, head, rank = query_adapter_up.shape
    kv_heads = key_adapter_up.shape[0]
    group = heads // kv_heads
    q_width, kv_width = heads * head, kv_heads * head
    seq, ring = lax.axis_size("seq"), lax.axis_size("dp") * lax.axis_size("seq")
    here = lax.axis_index("seq")
    chunks = rows // CHUNK
    ext = -(-(rows + WIN) // CHUNK) * CHUNK
    quarter = rows // 4
    units = gate_weight.shape[1] // FFN_PARTS

    core, far = lax.axis_index("tensor") % 2, lax.axis_index("tensor") // 2
    nat = jnp.stack([core * 2 + far, (1 - core) * 2 + far, core * 2 + 1 - far, (1 - core) * 2 + 1 - far]).astype(i32)
    own_rows = lambda x: lax.dynamic_slice_in_dim(x, nat[0] * quarter, quarter, 0)

    offsets = ring_offsets(query_weight.shape[0])
    n_pieces = offsets.shape[0]
    qkv_pieces = weight_ring(jnp.concatenate([query_weight, key_weight, value_weight], axis=1), ())
    o_pieces = weight_ring(output_weight.T, qkv_pieces[n_pieces // 2 - 2 : n_pieces // 2 - 1] if n_pieces > 1 else ())
    ffn_pieces, chain = [], [qkv_pieces, o_pieces]
    for j in range(FFN_PARTS):
        cols = slice(j * units, (j + 1) * units)
        packed = jnp.concatenate([gate_weight[:, cols], up_weight[:, cols], down_weight[cols].T], axis=1)
        behind = chain[-2]
        after = (behind[n_pieces // 2 - 1], behind[-1]) if n_pieces > 1 else ()
        ffn_pieces.append(weight_ring(packed, after))
        chain.append(ffn_pieces[-1])

    lengths = sequence_lengths[0]
    ends = jnp.cumsum(lengths)
    first_row = here * rows

    def docs_of(at):
        return jnp.where(at >= 0, jnp.sum((at[:, None] >= ends[None, :]).astype(i32), axis=1), -1)

    def angles_of(at):
        doc = docs_of(at)
        starts = ends - lengths
        start = jnp.sum(jnp.where(doc[:, None] == jnp.arange(lengths.shape[0])[None, :], starts[None, :], 0), axis=1)
        ladder = jnp.arange(head // 2).astype(f32)
        inverse = jnp.exp(ladder * (-2.0 * math.log(rope_base) / head))
        angles = inverse[:, None] * (at - start).astype(f32)[None, :]
        return jnp.cos(angles), jnp.sin(angles)

    q_at = first_row + jnp.arange(rows)
    k_index = jnp.arange(ext)
    k_at = first_row - WIN + k_index
    q_doc = docs_of(q_at)[None, :]
    k_doc = jnp.where(k_index < rows + WIN, docs_of(k_at), -2)
    doc_col, doc_row = k_doc[:, None], k_doc[None, :]
    last_docs = docs_of(first_row - WIN - 1 + CHUNK * jnp.arange(chunks + 1))
    block_docs = docs_of(rows * jnp.arange(seq + 1) - WIN - 1)
    passes = (block_docs[:-1] == block_docs[1:]).astype(f32)
    cos_q, sin_q = angles_of(q_at)
    cos_k, sin_k = angles_of(k_at)

    halo = shifted(tokens[rows - WIN :], "seq", 1)
    spare = jnp.zeros((ext - rows - WIN, model), bf16)
    seen = jnp.concatenate([halo, tokens, spare], axis=0).astype(f32)
    gain_attn = attention_norm_gain.astype(f32)
    gain_mlp = feedforward_norm_gain.astype(f32)
    normed = (seen * rms_factor(seen) * gain_attn).astype(bf16)
    downs = jnp.concatenate([query_adapter_down, key_adapter_down, value_adapter_down], axis=1)
    low = nn(normed, downs)
    ups = jnp.zeros((q_width + 2 * kv_width, 3 * rank), bf16)
    ups = ups.at[:q_width, :rank].set(query_adapter_up.reshape(q_width, rank))
    ups = ups.at[q_width : q_width + kv_width, rank : 2 * rank].set(key_adapter_up.reshape(kv_width, rank))
    ups = ups.at[q_width + kv_width :, 2 * rank :].set(value_adapter_up.reshape(kv_width, rank))
    low_up = nt(halves_outside(low, 1), jnp.concatenate([ups, ups], axis=1))
    maps_q = jnp.stack(
        [block_diagonal(feature_map_query[k * group : (k + 1) * group].transpose(0, 2, 1)) for k in range(kv_heads)]
    )
    maps_k = block_diagonal(feature_map_key.transpose(0, 2, 1))

    sems = pltpu.SemaphoreType.DMA((n_pieces,))
    qkv_width = q_width + 2 * kv_width
    held_qkv = pltpu.VMEM((model, qkv_width), bf16)
    held_o = pltpu.VMEM((model, q_width), bf16)

    dims = (rows, ext, q_width, kv_width, head, n_pieces, chunks)
    shapes = [
        ((q_width, rows), bf16),
        ((2 * q_width, rows), bf16),
        ((ext, kv_width), bf16),
        ((kv_width, ext), bf16),
        ((ext, kv_width), bf16),
        ((kv_heads * AUG, ext), bf16),
        ((ext, 2 * kv_width), bf16),
        ((2 * kv_width, ext), bf16),
        ((kv_heads, AUG, 2 * head), f32),
    ]
    prep_in = (normed, low_up, cos_q, sin_q, cos_k, sin_k, maps_q, maps_k, doc_row)
    q_t, phi_q, k_n, k_t, v_n, v_a, phi_kn, phi_kt, contrib = pl.pallas_call(
        lambda *refs: prep_body(dims, *refs),
        grid_spec=pltpu.PrefetchScalarGridSpec(
            num_scalar_prefetch=2,
            grid=(1,),
            in_specs=[whole(x.shape) for x in prep_in] + [ANY] * n_pieces,
            out_specs=[whole(s) for s, _ in shapes],
            scratch_shapes=[held_qkv, sems],
        ),
        out_shape=[jax.ShapeDtypeStruct(s, d) for s, d in shapes],
        compiler_params=params(56),
        cost_estimate=cost(2 * rows * model * qkv_width, 20 * MIB, 3 * rows * q_width),
        name="prep",
    )(offsets, last_docs, *prep_in, *qkv_pieces)

    state_in = jnp.zeros_like(contrib)
    factor = jnp.ones((), f32)
    for by in range(1, seq):
        state_in = state_in + factor * shifted(contrib, "seq", by)
        factor = factor * passes[jnp.maximum(here - by, 0)]

    column = lambda r: pl.BlockSpec((r, CHUNK), lambda c, *_: (0, c))
    att, att_t, totals, states = pl.pallas_call(
        lambda *refs: forward_body((kv_heads, group, head), *refs),
        grid_spec=pltpu.PrefetchScalarGridSpec(
            num_scalar_prefetch=1,
            grid=(chunks,),
            in_specs=[
                column(q_width),
                column(2 * q_width),
                whole(k_n.shape),
                whole(v_a.shape),
                whole(phi_kn.shape),
                whole(doc_col.shape),
                whole(doc_row.shape),
                column(1),
                whole(state_in.shape),
            ],
            out_specs=[
                pl.BlockSpec((CHUNK, q_width), lambda c, *_: (c, 0)),
                column(q_width),
                column(heads),
                pl.BlockSpec((1, kv_heads, 2 * head, AUG), lambda c, *_: (c, 0, 0, 0)),
            ],
            scratch_shapes=[pltpu.VMEM(state_in.shape, f32)],
        ),
        out_shape=[
            jax.ShapeDtypeStruct((rows, q_width), bf16),
            jax.ShapeDtypeStruct((q_width, rows), f32),
            jax.ShapeDtypeStruct((heads, rows), f32),
            jax.ShapeDtypeStruct((chunks, kv_heads, 2 * head, AUG), bf16),
        ],
        compiler_params=params(48),
        cost_estimate=cost(2 * heads * rows * 256 * 256, 10 * MIB, rows * heads * 192),
        name="attend",
    )(last_docs, q_t, phi_q, k_n, v_a, phi_kn, doc_col, doc_row, q_doc, state_in)

    o_down = output_adapter_down.reshape(q_width, rank)
    o_up_t = jnp.concatenate([output_adapter_up.T, output_adapter_up.T], axis=0)
    order_far, order_near = jnp.array([3, 2], i32), jnp.array([1, 0], i32)

    def o_part(which):
        return pl.pallas_call(
            lambda *refs: o_body(n_pieces, *refs),
            grid_spec=pltpu.PrefetchScalarGridSpec(
                num_scalar_prefetch=2,
                grid=(2,),
                in_specs=[
                    pl.BlockSpec((quarter, q_width), lambda i, off, nat: (nat[i], 0)),
                    whole(o_down.shape),
                    whole(o_up_t.shape),
                ]
                + [ANY] * n_pieces,
                out_specs=[
                    pl.BlockSpec((1, quarter, model), lambda i, *_: (i, 0, 0)),
                    pl.BlockSpec((1, quarter, rank), lambda i, *_: (i, 0, 0)),
                ],
                scratch_shapes=[held_o, sems],
            ),
            out_shape=[
                jax.ShapeDtypeStruct((2, quarter, model), bf16),
                jax.ShapeDtypeStruct((2, quarter, rank), f32),
            ],
            compiler_params=params(32),
            cost_estimate=cost(2 * rows * model * q_width / 2, 5 * MIB),
            name="project",
        )(offsets, nat[which], att, o_down, o_up_t, *o_pieces)

    o_far, low_far = o_part(order_far)
    o_near, low_near = o_part(order_near)
    lowered = jnp.concatenate([low_near[1], low_near[0], low_far[1], low_far[0]], axis=0)
    hidden = own_rows(tokens).astype(f32) + reduce_quarters(o_far, o_near)
    normed_mlp = gather_quarters((hidden * rms_factor(hidden) * gain_mlp).astype(bf16))

    def ffn(pieces, which, sums, out_type):
        count = which.shape[0]
        block = lambda: pl.BlockSpec((1, quarter, model), lambda i, off, order, nat: (order[i], 0, 0))
        in_order = pl.BlockSpec((1, quarter, model), lambda i, *_: (i, 0, 0))
        out = jax.ShapeDtypeStruct((count, quarter, model), out_type)
        share = count / 4
        aliases = {5 + n_pieces: 0, 6 + n_pieces: 1} if sums and out_type == f32 else {}
        return pl.pallas_call(
            lambda *refs: ffn_body(n_pieces, units, not sums, *refs),
            grid_spec=pltpu.PrefetchScalarGridSpec(
                num_scalar_prefetch=3,
                grid=(count,),
                in_specs=[
                    block(),
                    pl.BlockSpec((quarter, model), lambda i, off, order, nat: (nat[i], 0)),
                ]
                + [ANY] * n_pieces
                + [block() for _ in sums],
                out_specs=[in_order, in_order],
                scratch_shapes=[pltpu.VMEM((model, 3 * units), bf16), sems],
            ),
            out_shape=[out, out],
            input_output_aliases=aliases,
            compiler_params=params(52),
            cost_estimate=cost(12 * rows * model * units * share, 46 * MIB * share, rows * units * share),
            name="feed_forward",
        )(offsets, which, nat[which], normed_mlp, output_cotangent, *pieces, *sums)

    every = jnp.arange(4).astype(i32)
    sums = ()
    for pieces in ffn_pieces[:-1]:
        sums = tuple(ffn(pieces, every, sums, f32))
    mlp_far, grad_far = ffn(ffn_pieces[-1], order_far, sums, bf16)
    mlp_near, grad_near = ffn(ffn_pieces[-1], order_near, sums, bf16)
    grad_normed_mlp = reduce_quarters(grad_far, grad_near)
    grad_hidden = own_rows(output_cotangent).astype(f32) + rms_back(hidden, gain_mlp, grad_normed_mlp)
    branch = gather_quarters(grad_hidden.astype(bf16))

    o_down_t = jnp.concatenate([o_down.T, o_down.T], axis=0)
    by_quarter = lambda r: pl.BlockSpec((r, quarter), lambda i, off, nat, before: (0, nat[i]))
    numer, grad_totals, up_product, dstate = pl.pallas_call(
        lambda *refs: go_body((n_pieces, kv_heads, group, head), *refs),
        grid_spec=pltpu.PrefetchScalarGridSpec(
            num_scalar_prefetch=3,
            grid=(4,),
            in_specs=[
                pl.BlockSpec((1, quarter, model), lambda i, *_: (i, 0, 0)),
                whole((model, rank)),
                whole(o_down_t.shape),
                by_quarter(q_width),
                by_quarter(heads),
                by_quarter(2 * q_width),
                by_quarter(1),
            ]
            + [ANY] * n_pieces,
            out_specs=[
                by_quarter(q_width),
                by_quarter(heads),
                pl.BlockSpec((quarter, rank), lambda i, off, nat, before: (nat[i], 0)),
                whole((kv_heads, 2 * head, AUG)),
            ],
            scratch_shapes=[held_o, sems],
        ),
        out_shape=[
            jax.ShapeDtypeStruct((q_width, rows), bf16),
            jax.ShapeDtypeStruct((heads, rows), f32),
            jax.ShapeDtypeStruct((rows, rank), f32),
            jax.ShapeDtypeStruct((kv_heads, 2 * head, AUG), f32),
        ],
        compiler_params=params(48),
        cost_estimate=cost(2 * rows * model * q_width, 14 * MIB),
        name="project_back",
    )(offsets, nat, last_docs[:1], branch, output_adapter_up, o_down_t, att_t, totals, phi_q, q_doc, *o_pieces)

    later_in = jnp.zeros_like(dstate)
    factor = jnp.ones((), f32)
    for by in range(1, seq):
        later_in = later_in + factor * shifted(dstate, "seq", -by)
        factor = factor * passes[jnp.minimum(here + by, seq - 1)]

    back_column = lambda r: pl.BlockSpec((r, CHUNK), lambda c, *_: (0, chunks - 1 - c))
    back_in = (
        (q_t, back_column(q_width)),
        (phi_q, back_column(2 * q_width)),
        (numer, back_column(q_width)),
        (grad_totals, back_column(heads)),
        (k_n, None),
        (k_t, None),
        (v_n, None),
        (v_a, None),
        (phi_kn, None),
        (phi_kt, None),
        (doc_col, None),
        (doc_row, None),
        (q_doc, back_column(1)),
        (states, pl.BlockSpec((1, kv_heads, 2 * head, AUG), lambda c, *_: (chunks - 1 - c, 0, 0, 0))),
        (later_in, None),
        (cos_q, back_column(head // 2)),
        (sin_q, back_column(head // 2)),
        (maps_q, None),
        (maps_k, None),
    )
    g_q, g_kt, g_vt, g_map_q, g_map_k = pl.pallas_call(
        lambda *refs: backward_body((kv_heads, group, head, chunks), *refs),
        grid_spec=pltpu.PrefetchScalarGridSpec(
            num_scalar_prefetch=1,
            grid=(chunks,),
            in_specs=[whole(x.shape) if spec is None else spec for x, spec in back_in],
            out_specs=[
                pl.BlockSpec((CHUNK, q_width), lambda c, *_: (chunks - 1 - c, 0)),
                whole((kv_width, ext)),
                whole((kv_width, ext)),
                whole((kv_heads, group * head, group * head)),
                whole((kv_width, kv_width)),
            ],
            scratch_shapes=[pltpu.VMEM(dstate.shape, f32), pltpu.VMEM((2 * kv_width, ext), f32)],
        ),
        out_shape=[
            jax.ShapeDtypeStruct((rows, q_width), bf16),
            jax.ShapeDtypeStruct((kv_width, ext), f32),
            jax.ShapeDtypeStruct((kv_width, ext), f32),
            jax.ShapeDtypeStruct((kv_heads, group * head, group * head), f32),
            jax.ShapeDtypeStruct((kv_width, kv_width), f32),
        ],
        compiler_params=params(52),
        cost_estimate=cost(6 * heads * rows * 256 * 256, 12 * MIB, rows * heads * 192),
        name="attend_back",
    )(last_docs, *[x for x, _ in back_in])

    returned = shifted(jnp.concatenate([g_kt[:, :WIN], g_vt[:, :WIN]], axis=0), "seq", -1)
    lead = ((0, 0), (rows - WIN, 0))
    g_k = g_kt[:, WIN : WIN + rows] + jnp.pad(returned[:kv_width], lead)
    g_v = g_vt[:, WIN : WIN + rows] + jnp.pad(returned[kv_width:], lead)
    g_k = rope(g_k, cos_q, -sin_q)
    g_kv = jnp.concatenate([g_k, g_v], axis=0).astype(bf16).T

    downs_t = jnp.concatenate([downs.T, downs.T], axis=0)

    def gn_part(which):
        by_rows = lambda w: pl.BlockSpec((quarter, w), lambda i, off, nat: (nat[i], 0))
        return pl.pallas_call(
            lambda *refs: gn_body(n_pieces, *refs),
            grid_spec=pltpu.PrefetchScalarGridSpec(
                num_scalar_prefetch=2,
                grid=(2,),
                in_specs=[
                    by_rows(q_width),
                    by_rows(2 * kv_width),
                    whole((q_width, 3 * rank)),
                    whole((2 * kv_width, 3 * rank)),
                    whole(downs_t.shape),
                ]
                + [ANY] * n_pieces,
                out_specs=[
                    pl.BlockSpec((1, quarter, model), lambda i, *_: (i, 0, 0)),
                    pl.BlockSpec((1, quarter, 3 * rank), lambda i, *_: (i, 0, 0)),
                ],
                scratch_shapes=[held_qkv, sems],
            ),
            out_shape=[
                jax.ShapeDtypeStruct((2, quarter, model), bf16),
                jax.ShapeDtypeStruct((2, quarter, 3 * rank), f32),
            ],
            compiler_params=params(32),
            cost_estimate=cost(rows * model * qkv_width, 7 * MIB),
            name="norm_back",
        )(offsets, nat[which], g_q, g_kv, ups[:q_width], ups[q_width:], downs_t, *qkv_pieces)

    gn_far, ups_far = gn_part(order_far)
    gn_near, ups_near = gn_part(order_near)
    grad_normed = reduce_quarters(gn_far, gn_near)
    grad_rows = grad_hidden + rms_back(own_rows(tokens).astype(f32), gain_attn, grad_normed)
    grad_tokens = place(gather_quarters(grad_rows.astype(bf16)), nat, f32)
    mlp = reduce_quarters(mlp_far, mlp_near)
    block_out = place(gather_quarters((hidden + mlp).astype(bf16)), nat, bf16)

    def joined(x):
        return x[:, : x.shape[1] // 2] + x[:, x.shape[1] // 2 :]

    low_own = halves_outside(low[WIN : WIN + rows], 1)
    g_q_up = joined(tn(g_q, low_own))[:, :rank]
    g_kv_up = joined(tn(g_kv, low_own))
    g_k_up = g_kv_up[:kv_width, rank : 2 * rank]
    g_v_up = g_kv_up[kv_width:, 2 * rank :]
    ups_rel = jnp.stack([ups_near[1], ups_near[0], ups_far[1], ups_far[0]])
    ups_nat = jnp.zeros_like(ups_rel).at[nat].set(ups_rel).reshape(rows, 3 * rank)
    g_downs = joined(tn(normed[WIN : WIN + rows], halves_outside(ups_nat, 1)))
    g_o_up = joined(tn(branch.reshape(rows, model), halves_outside(lowered, 1)))
    g_o_down = joined(tn(att, halves_outside(up_product, 1)))
    shared = jnp.concatenate([g_downs, g_o_up], axis=1).reshape(ring, 4, model // ring // 4, 4 * rank)
    shared = reduce_to_own(shared.transpose(1, 0, 2, 3), "tensor")

    def by_rows_of_head(x, count):
        return x.reshape(count, ring, head // ring, -1).transpose(1, 0, 2, 3)

    per_head = [
        by_rows_of_head(g_q_up, heads),
        by_rows_of_head(g_k_up, kv_heads),
        by_rows_of_head(g_v_up, kv_heads),
        by_rows_of_head(g_o_down, heads),
        by_rows_of_head(jnp.concatenate([diagonal_blocks(g_map_q[k], group) for k in range(kv_heads)]), heads),
        by_rows_of_head(diagonal_blocks(g_map_k, kv_heads), kv_heads),
    ]
    parts = [shared] + per_head
    flat = jnp.concatenate([x.reshape(ring, -1) for x in parts], axis=1)
    flat = reduce_to_own(flat.reshape(-1, seq, flat.shape[1]), "dp")
    flat = reduce_to_own(flat, "seq")
    out, at = [], 0
    for x in parts:
        size = x.size // ring
        out.append(flat[at : at + size].reshape(x.shape[1:]))
        at += size
    shared_out = out[0]
    return (
        block_out,
        grad_tokens,
        shared_out[:, :rank],
        shared_out[:, rank : 2 * rank],
        shared_out[:, 2 * rank : 3 * rank],
        shared_out[:, 3 * rank :],
        *out[1:],
    )


def solution(mesh):
    return jax.shard_map(
        per_device,
        mesh=mesh,
        in_specs=(
            P(("dp", "seq"), None),
            P("dp", None),
            P(("dp", "seq"), None),
            P(("dp", "seq"), "tensor"),
            P(("dp", "seq"), "tensor"),
            P(("dp", "seq"), "tensor"),
            P("tensor", ("dp", "seq")),
            P(("dp", "seq"), "tensor"),
            P(("dp", "seq"), "tensor"),
            P("tensor", ("dp", "seq")),
            P(),
            P(),
            P(),
            P(),
            P(),
            P(),
            P("tensor", None, None),
            P("tensor", None, None),
            P("tensor", None, None),
            P("tensor", None, None),
            P("tensor", None, None),
            P("tensor", None, None),
        ),
        out_specs=(
            P(("dp", "seq"), None),
            P(("dp", "seq"), None),
            P(("dp", "seq", "tensor"), None),
            P(("dp", "seq", "tensor"), None),
            P(("dp", "seq", "tensor"), None),
            P(("dp", "seq", "tensor"), None),
            P("tensor", ("dp", "seq"), None),
            P("tensor", ("dp", "seq"), None),
            P("tensor", ("dp", "seq"), None),
            P("tensor", ("dp", "seq"), None),
            P("tensor", ("dp", "seq"), None),
            P("tensor", ("dp", "seq"), None),
        ),
        check_vma=False,
    )
```

time: 2570 us -> 790 us (0.31)
  waiting for transfers between devices: 1700 us -> 272 us
  matrix products: 403 us -> 12.9 us
  Pallas kernels: 0 us -> 188 us
  blocking collectives: 129 us -> 0 us
  starting transfers between devices: 8.23 us -> 116 us
  local copies, waits for them, and re-layouts: 202 us -> 121 us
  other arithmetic: 91.6 us -> 62.3 us
    psum x3 -> x0, waiting for transfers between devices: 570 us -> none  [the longest x1 286 us: per_device(): mlp_total = lax.psum(product_lowered(activated, w_down_all), 'tensor')]
    unnamed x22 -> x0, waiting for transfers between devices: 452 us -> none
    dot_general x68 -> x7, matrix products: 394 us -> 12.9 us  [the longest x5 8.48 us: tn(): lax.dot_general(a, b, (((0,), (0,)), ((), ())), preferred_element_type=f32)]
    reduce_scatter x6 -> x0, waiting for transfers between devices: 339 us -> none  [the longest x1 64.5 us: per_device(): lax.psum_scatter(query_up_gradient, ('dp', 'seq'), scatter_dimension=1, t...]
    all_gather x5 -> x0, waiting for transfers between devices: 337 us -> none  [the longest x1 118 us: per_device(): lax.all_gather(gate_weight, ('dp', 'seq'), axis=0, tiled=True)]
    ppermute x4 -> x121, waiting for transfers between devices: 0.01 us -> 272 us  [the longest x29 135 us: exchange(): return lax.ppermute(x, axis, [(i, i ^ bit) for i in range(count)])]
    pallas_call x0 -> x15, Pallas kernels: none -> 188 us  [the longest x5 97.2 us: ffn(): pl.pallas_call(lambda *refs: ffn_body(n_pieces, units, not sums, *refs),...]
    dynamic_update_slice x10 -> x0, local copies, waits for them, and re-layouts: 129 us -> none  [the longest x8 129 us: per_device(): lax.scan(backward_block, start_grads, block_ids)]
  transfers between devices with their start and end apart: 22 -> 121, of which waited for: 16 -> 47; matrix products, arithmetic and copies ran while one was open for 11% -> 17% of each run, Pallas kernels for 0% -> 22%
where the time goes in v1:
time: 790 us; the launch traced here: 778 us
  waiting for transfers between devices  272 us (34%)
  Pallas kernels  188 us (24%)
  local copies, waits for them, and re-layouts  121 us (15%)
  starting transfers between devices  116 us (15%)
  other arithmetic  62.3 us (8%)
  matrix products  12.9 us (2%)
    ppermute x29, waiting for transfers between devices, exchange(): return lax.ppermute(x, axis, [(i, i ^ bit) for i in range(count)])  135 us
    pallas_call x5, Pallas kernels, ffn(): pl.pallas_call(lambda *refs: ffn_body(n_pieces, units, not sums, *refs),...  97.2 us
    ppermute x42, waiting for transfers between devices, weight_ring(): a = lax.ppermute(a, ('dp', 'seq'), up)  85.8 us
    unnamed x498, local copies, waits for them, and re-layouts  70.8 us
    ppermute x42, starting transfers between devices, weight_ring(): b = lax.ppermute(b, ('dp', 'seq'), [(j, i) for i, j in up])  59.6 us
    ppermute x42, waiting for transfers between devices, weight_ring(): b = lax.ppermute(b, ('dp', 'seq'), [(j, i) for i, j in up])  41.6 us
    ppermute x42, starting transfers between devices, weight_ring(): a = lax.ppermute(a, ('dp', 'seq'), up)  22.8 us
    ppermute x8, starting transfers between devices, shifted(): lax.ppermute(x, axis, [(i, i + by) for i in range(count) if 0 <= i + by <...  17.9 us
  transfers between devices with their start and end apart: 121, of which 47 were waited for; matrix products, arithmetic and copies ran while one was open for 17% of the time, Pallas kernels for 22%

profile of v1, /device:TPU:0, one launch (start us, length us, event | category | flops | bytes accessed | tf_op | source)
XLA Modules:
  0.0 777.9 jit_solution(15099315917595385615)
XLA Ops:
  42.7 5.2 collective-permute-done.3.refs_14_.refs_10_
  59.4 5.4 collective-permute-done.9.refs_21_.refs_17_
  103.9 15.5 %prep.1 = (bf16[512,1024]{1,0:T(8,128)(2,1)}, bf16[1024,1024]{1,0:T(8,128)(2,1)}, bf16[1152,128]{1,0:T(8,128)(2,1)}, bf16[128,1152]{1,0:T(8,128)(2,1)}, bf16[115...) custom-call(s32[16]{0:T(128)} %pad_add_fusion.1.refs_0_, ...), custom_call_target="tpu_custom_call" | custom-call | flops 3221225472 | bytes 20971520 | tf_op jit(solution)/shard_map/prep/pallas_call | solution.py:622
  143.7 9.2 %attend.1 = (bf16[1024,512]{1,0:T(8,128)(2,1)S(1)}, f32[512,1024]{1,0:T(8,128)}, f32[8,1024]{1,0:T(8,128)S(1)}, bf16[8,2,128,80]{3,2,1,0:T(8,128)(2,1)S(1)}) custom-call(s32[9]{0:T(128)S(1)} %copy-done.127, bf16[512,1024]{1,0:T(8,128)(2,1)S(1)} %copy-done.5, bf16[1024,1024]{1,0:T(8,128)(2,1)} %get-tuple-element.99.refs_2_.refs_8_, ...), custom_call_target="tpu_custom_call" | custom-call | flops 1073741824 | bytes 10485760 | tf_op jit(solution)/shard_map/attend/pallas_call | solution.py:644
  157.2 6.5 project.3
  183.8 6.5 project.2
  195.5 7.1 collective-permute-done.69.refs_9_
  204.8 6.3 collective-permute-done.40.refs_8_
  221.2 6.9 collective-permute-done.41.refs_9_
  231.5 4.9 collective-permute-done.71.refs_11_
  238.5 6.3 collective-permute-done.42.refs_10_
  248.1 5.1 collective-permute-done.72.refs_12_
  265.4 4.7 collective-permute-done.80.refs_6_
  272.2 6.3 collective-permute-done.44.refs_12_
  281.3 5.6 collective-permute-done.81.refs_7_
  350.9 20.5 %feed_forward.5 = (f32[4,256,2048]{2,1,0:T(8,128)}, f32[4,256,2048]{2,1,0:T(8,128)}) custom-call(s32[16]{0:T(128)S(1)} %copy-done.125, s32[4]{0:T(128)S(1)} %iota.127.refs_1_, s32[4]{0:T(128)S(1)} %gather_fusion.2, bf16[4,256,2048]{2,1,0:T(8,128)(2,1)} %pad_maximum_fusion.refs_3_, bf16[1024,2048]{1,0:T(8,128)(2,1)} %refs_4_.10, ...), custom_call_target="tpu_custom_call" | custom-call | flops 12884901888 | bytes 48234496 | tf_op jit(solution)/shard_map/feed_forward/pallas_call | solution.py:723
  375.8 23.2 %feed_forward.6 = (f32[4,256,2048]{2,1,0:T(8,128)}, f32[4,256,2048]{2,1,0:T(8,128)}) custom-call(s32[16]{0:T(128)S(1)} %copy-done.125, s32[4]{0:T(128)S(1)} %iota.126.refs_1_, s32[4]{0:T(128)S(1)} %gather_fusion.2, bf16[4,256,2048]{2,1,0:T(8,128)(2,1)} %pad_maximum_fusion.refs_3_, ...), custom_call_target="tpu_custom_call", output_to_operand_aliasing={{0}: (21, {}), {1}: (22, {})} | custom-call | flops 12884901888 | bytes 48234496 | tf_op jit(solution)/shard_map/feed_forward/pallas_call | solution.py:723
  402.0 23.0 %feed_forward.7 = (f32[4,256,2048]{2,1,0:T(8,128)}, f32[4,256,2048]{2,1,0:T(8,128)}) custom-call(s32[16]{0:T(128)S(1)} %copy-done.125, s32[4]{0:T(128)S(1)} %iota.124.refs_1_, s32[4]{0:T(128)S(1)} %gather_fusion.2, bf16[4,256,2048]{2,1,0:T(8,128)(2,1)} %pad_maximum_fusion.refs_3_, ...), custom_call_target="tpu_custom_call", output_to_operand_aliasing={{0}: (21, {}), {1}: (22, {})} | custom-call | flops 12884901888 | bytes 48234496 | tf_op jit(solution)/shard_map/feed_forward/pallas_call | solution.py:723
  425.9 15.2 %feed_forward.9 = (bf16[2,256,2048]{2,1,0:T(8,128)(2,1)}, bf16[2,256,2048]{2,1,0:T(8,128)(2,1)}) custom-call(s32[16]{0:T(128)S(1)} %copy-done.125, s32[2]{0:T(128)S(1)} %copy-done.132, s32[2]{0:T(128)S(1)} %copy-done.134, bf16[4,256,2048]{2,1,0:T(8,128)(2,1)} %pad_maximum_fusion.refs_3_, bf16[1024,2048]{1,0:T(8,128)(2,1)} %refs_4_.10, ...), custom_call_target="tpu_custom_call" | custom-call | flops 6442450944 | bytes 24117248 | tf_op jit(solution)/shard_map/feed_forward/pallas_call | solution.py:723
  443.4 15.4 %feed_forward.8 = (bf16[2,256,2048]{2,1,0:T(8,128)(2,1)}, bf16[2,256,2048]{2,1,0:T(8,128)(2,1)}) custom-call(s32[16]{0:T(128)S(1)} %copy-done.125, s32[2]{0:T(128)S(1)} %copy-done.130, s32[2]{0:T(128)S(1)} %copy-done.137, bf16[4,256,2048]{2,1,0:T(8,128)(2,1)} %pad_maximum_fusion.refs_3_, bf16[1024,2048]{1,0:T(8,128)(2,1)} %refs_4_.10, ...), custom_call_target="tpu_custom_call" | custom-call | flops 6442450944 | bytes 24117248 | tf_op jit(solution)/shard_map/feed_forward/pallas_call | solution.py:723
  464.3 22.7 %collective-permute-done.102 = bf16[256,2048]{1,0:T(8,128)(2,1)S(1)} collective-permute-done((bf16[256,2048]{1,0:T(8,128)(2,1)S(1)}, bf16[256,2048]{1,0:T(8,128)(2,1)S(1)}, u32[]{:S(2)}, u32[]{:S(2)}) %collective-permute-start.102) | collective-permute-done | bytes 1048608 | tf_op jit(solution)/shard_map/ppermute | solution.py:46
  487.8 20.9 %collective-permute-done.96 = bf16[256,2048]{1,0:T(8,128)(2,1)S(1)} collective-permute-done((bf16[256,2048]{1,0:T(8,128)(2,1)S(1)}, bf16[256,2048]{1,0:T(8,128)(2,1)S(1)}, u32[]{:S(2)}, u32[]{:S(2)}) %collective-permute-start.96) | collective-permute-done | bytes 1048608 | tf_op jit(solution)/shard_map/ppermute | solution.py:46
  516.0 23.6 %collective-permute-done.104 = bf16[256,2048]{1,0:T(8,128)(2,1)} collective-permute-done((bf16[256,2048]{1,0:T(8,128)(2,1)}, bf16[256,2048]{1,0:T(8,128)(2,1)}, u32[]{:S(2)}, u32[]{:S(2)}) %collective-permute-start.104) | collective-permute-done | bytes 1048608 | tf_op jit(solution)/shard_map/ppermute | solution.py:46
  544.6 15.8 %collective-permute-done.98 = bf16[256,2048]{1,0:T(8,128)(2,1)} collective-permute-done((bf16[256,2048]{1,0:T(8,128)(2,1)}, bf16[256,2048]{1,0:T(8,128)(2,1)}, u32[]{:S(2)}, u32[]{:S(2)}) %collective-permute-start.98) | collective-permute-done | bytes 1048608 | tf_op jit(solution)/shard_map/ppermute | solution.py:46
  564.7 12.2 %project_back.1 = (bf16[512,1024]{1,0:T(8,128)(2,1)S(1)}, f32[8,1024]{1,0:T(8,128)S(1)}, f32[1024,8]{1,0:T(8,128)S(1)}, f32[2,128,80]{2,1,0:T(8,128)S(1)}) custom-call(s32[16]{0:T(128)S(1)} %copy-done.125, s32[4]{0:T(128)S(1)} %pad_add_fusion.nat.refs_1_, s32[1]{0:T(128)S(1)} %bitcast.228, bf16[4,256,2048]{2,1,0:T(8,128)(2,1)} %pad_maximum_fusion.2.refs_3_, ...), custom_call_target="tpu_custom_call" | custom-call | flops 2147483648 | bytes 14680064 | tf_op jit(solution)/shard_map/project_back/pallas_call | solution.py:756
  587.0 7.2 collective-permute-done.107
  594.9 17.4 %attend_back.1 = (bf16[1024,512]{1,0:T(8,128)(2,1)}, f32[128,1152]{1,0:T(8,128)}, f32[128,1152]{1,0:T(8,128)}, f32[2,256,256]{2,1,0:T(8,128)}, f32[128,128]{1,0:T(8,128)S(1)}) custom-call(s32[9]{0:T(128)S(1)} %copy-done.128, bf16[512,1024]{1,0:T(8,128)(2,1)} %get-tuple-element.98.refs_1_, bf16[1024,1024]{1,0:T(8,128)(2,1)} %get-tuple-element.99.refs_2_.refs_8_, ...), custom_call_target="tpu_custom_call" | custom-call | flops 3221225472 | bytes 12582912 | tf_op jit(solution)/shard_map/attend_back/pallas_call | solution.py:818
  640.6 8.0 %norm_back.2 = (bf16[2,256,2048]{2,1,0:T(8,128)(2,1)S(1)}, f32[2,256,24]{2,1,0:T(8,128)S(1)}) custom-call(s32[16]{0:T(128)S(1)} %copy-done.126, s32[2]{0:T(128)S(1)} %copy-done.138, bf16[1024,512]{1,0:T(8,128)(2,1)S(1)} %copy-done.3, bf16[1024,256]{1,0:T(8,128)(2,1)S(1)} %bitcast.226, bf16[512,24]{1,0:T(8,128)(2,1)S(1)} %copy-done.113, ...), custom_call_target="tpu_custom_call" | custom-call | flops 1610612736 | bytes 7340032 | tf_op jit(solution)/shard_map/norm_back/pallas_call | solution.py:856
  666.7 8.0 %norm_back.3 = (bf16[2,256,2048]{2,1,0:T(8,128)(2,1)S(1)}, f32[2,256,24]{2,1,0:T(8,128)S(1)}) custom-call(s32[16]{0:T(128)S(1)} %copy-done.126, s32[2]{0:T(128)S(1)} %copy-done.135, bf16[1024,512]{1,0:T(8,128)(2,1)S(1)} %copy-done.4, bf16[1024,256]{1,0:T(8,128)(2,1)S(1)} %bitcast.227, bf16[512,24]{1,0:T(8,128)(2,1)S(1)} %copy-done.113, ...), custom_call_target="tpu_custom_call" | custom-call | flops 1610612736 | bytes 7340032 | tf_op jit(solution)/shard_map/norm_back/pallas_call | solution.py:856
  686.0 9.0 %collective-permute-done.116 = f32[2,8,64,32]{3,2,1,0:T(8,128)S(1)} collective-permute-done((f32[2,8,64,32]{3,2,1,0:T(8,128)}, f32[2,8,64,32]{3,2,1,0:T(8,128)S(1)}, u32[]{:S(2)}, u32[]{:S(2)}) %collective-permute-start.116) | collective-permute-done | bytes 131104 | tf_op jit(solution)/shard_map/ppermute | solution.py:46
  713.8 21.4 %collective-permute-done.112 = bf16[256,2048]{1,0:T(8,128)(2,1)S(1)} collective-permute-done((bf16[256,2048]{1,0:T(8,128)(2,1)S(1)}, bf16[256,2048]{1,0:T(8,128)(2,1)S(1)}, u32[]{:S(2)}, u32[]{:S(2)}) %collective-permute-start.112) | collective-permute-done | bytes 1048608 | tf_op jit(solution)/shard_map/ppermute | solution.py:46
  748.9 15.7 %collective-permute-done.114 = bf16[256,2048]{1,0:T(8,128)(2,1)S(1)} collective-permute-done((bf16[256,2048]{1,0:T(8,128)(2,1)}, bf16[256,2048]{1,0:T(8,128)(2,1)S(1)}, u32[]{:S(2)}, u32[]{:S(2)}) %collective-permute-start.114) | collective-permute-done | bytes 1048608 | tf_op jit(solution)/shard_map/ppermute | solution.py:46
  (930 shorter events, 390.6 us)
Async XLA Ops:
  3.5 32.4 %collective-permute-start.1 = (bf16[128,768]{1,0:T(8,128)(2,1)S(1)}, bf16[128,768]{1,0:T(8,128)(2,1)S(1)}, u32[]{:S(2)}, u32[]{:S(2)}) collective-permute-start(bf16[128,768]{1,0:T(8,128)(2,1)S(1)} %get-tuple-element.235.refs_11_.refs_7_), channel_id=1, source_target_pairs={{0,4},{4,8},{8,12},{12,28},{28,24},{24,20},{20,16},{16,0},{1,5},{5... | collective-permute-start | bytes 589832 | tf_op jit(solution)/shard_map/ppermute | solution.py:77
  6.5 50.7 %collective-permute-start.8 = (bf16[128,768]{1,0:T(8,128)(2,1)S(1)}, bf16[128,768]{1,0:T(8,128)(2,1)S(1)}, u32[]{:S(2)}, u32[]{:S(2)}) collective-permute-start(bf16[128,768]{1,0:T(8,128)(2,1)S(1)} %get-tuple-element.234.refs_19_.refs_15_), channel_id=1, source_target_pairs={{4,0},{8,4},{12,8},{28,12},{24,28},{20,24},{16,20},{0,16},{5,1},{9... | collective-permute-start | bytes 589832 | tf_op jit(solution)/shard_map/ppermute | solution.py:78
  8.2 58.6 %collective-permute-start = (bf16[64,2048]{1,0:T(8,128)(2,1)}, bf16[64,2048]{1,0:T(8,128)(2,1)}, u32[]{:S(2)}, u32[]{:S(2)}) collective-permute-start(bf16[64,2048]{1,0:T(8,128)(2,1)} %slice.387), channel_id=1, source_target_pairs={{0,4},{4,8},{8,12},{1,5},{5,9},{9,13},{2,6},{6,10},{10,14},{3,7},{... | collective-permute-start | bytes 786440 | tf_op jit(solution)/shard_map/ppermute | solution.py:51
  99.7 26.5 %collective-permute-start.22 = (bf16[128,512]{1,0:T(8,128)(2,1)S(1)}, bf16[128,512]{1,0:T(8,128)(2,1)S(1)}, u32[]{:S(2)}, u32[]{:S(2)}) collective-permute-start(bf16[128,512]{1,0:T(8,128)(2,1)S(1)} %collective-permute-done.21.refs_9_.refs_14_), channel_id=1, source_target_pairs={{0,4},{4,8},{8,12},{12,28},{28,24},{24,20},{20,16},{16,0},{1,5},{5... | collective-permute-start | bytes 393224 | tf_op jit(solution)/shard_map/ppermute | solution.py:77
  101.3 25.0 %collective-permute-start.29 = (bf16[128,512]{1,0:T(8,128)(2,1)S(1)}, bf16[128,512]{1,0:T(8,128)(2,1)S(1)}, u32[]{:S(2)}, u32[]{:S(2)}) collective-permute-start(bf16[128,512]{1,0:T(8,128)(2,1)S(1)} %collective-permute-done.28.refs_17_.refs_22_), channel_id=1, source_target_pairs={{4,0},{8,4},{12,8},{28,12},{24,28},{20,24},{16,20},{0,16},{5,1},{9... | collective-permute-start | bytes 393224 | tf_op jit(solution)/shard_map/ppermute | solution.py:78
  165.4 37.5 %collective-permute-start.33 = (bf16[256,2048]{1,0:T(8,128)(2,1)}, bf16[256,2048]{1,0:T(8,128)(2,1)}, u32[]{:S(2)}, u32[]{:S(2)}) collective-permute-start(bf16[256,2048]{1,0:T(8,128)(2,1)} %slice_bitcast_fusion.6), channel_id=1, source_target_pairs={{0,1},{1,0},{2,3},{3,2},{4,5},{5,4},{6,7},{7,6},{8,9},{9,8},{10,11... | collective-permute-start | bytes 3145736 | tf_op jit(solution)/shard_map/ppermute | solution.py:46
  165.5 24.8 %collective-permute-start.68 = (bf16[128,1536]{1,0:T(8,128)(2,1)}, bf16[128,1536]{1,0:T(8,128)(2,1)}, u32[]{:S(2)}, u32[]{:S(2)}) collective-permute-start(bf16[128,1536]{1,0:T(8,128)(2,1)} %collective-permute-done.67.refs_7_), channel_id=1, source_target_pairs={{0,4},{4,8},{8,12},{12,28},{28,24},{24,20},{20,16},{16,0},{1,5},{5... | collective-permute-start | bytes 1179656 | tf_op jit(solution)/shard_map/ppermute | solution.py:77
  165.7 24.8 %collective-permute-start.75 = (bf16[128,1536]{1,0:T(8,128)(2,1)}, bf16[128,1536]{1,0:T(8,128)(2,1)}, u32[]{:S(2)}, u32[]{:S(2)}) collective-permute-start(bf16[128,1536]{1,0:T(8,128)(2,1)} %collective-permute-done.74.refs_15_), channel_id=1, source_target_pairs={{4,0},{8,4},{12,8},{28,12},{24,28},{20,24},{16,20},{0,16},{5,1},{9... | collective-permute-start | bytes 1179656 | tf_op jit(solution)/shard_map/ppermute | solution.py:78
  167.6 24.8 %collective-permute-start.39 = (bf16[128,1536]{1,0:T(8,128)(2,1)}, bf16[128,1536]{1,0:T(8,128)(2,1)}, u32[]{:S(2)}, u32[]{:S(2)}) collective-permute-start(bf16[128,1536]{1,0:T(8,128)(2,1)} %collective-permute-done.38.refs_6_), channel_id=1, source_target_pairs={{0,4},{4,8},{8,12},{12,28},{28,24},{24,20},{20,16},{16,0},{1,5},{5... | collective-permute-start | bytes 1179656 | tf_op jit(solution)/shard_map/ppermute | solution.py:77
  167.7 24.8 %collective-permute-start.46 = (bf16[128,1536]{1,0:T(8,128)(2,1)}, bf16[128,1536]{1,0:T(8,128)(2,1)}, u32[]{:S(2)}, u32[]{:S(2)}) collective-permute-start(bf16[128,1536]{1,0:T(8,128)(2,1)} %collective-permute-done.45.refs_14_), channel_id=1, source_target_pairs={{4,0},{8,4},{12,8},{28,12},{24,28},{20,24},{16,20},{0,16},{5,1},{9... | collective-permute-start | bytes 1179656 | tf_op jit(solution)/shard_map/ppermute | solution.py:78
  202.7 52.6 %collective-permute-start.32 = (bf16[256,2048]{1,0:T(8,128)(2,1)}, bf16[256,2048]{1,0:T(8,128)(2,1)}, u32[]{:S(2)}, u32[]{:S(2)}) collective-permute-start(bf16[256,2048]{1,0:T(8,128)(2,1)} %slice_bitcast_fusion.7), channel_id=1, source_target_pairs={{0,1},{1,0},{2,3},{3,2},{4,5},{5,4},{6,7},{7,6},{8,9},{9,8},{10,11... | collective-permute-start | bytes 3145736 | tf_op jit(solution)/shard_map/ppermute | solution.py:46
  219.6 37.0 %collective-permute-start.34 = (bf16[256,2048]{1,0:T(8,128)(2,1)}, bf16[256,2048]{1,0:T(8,128)(2,1)S(1)}, u32[]{:S(2)}, u32[]{:S(2)}) collective-permute-start(bf16[256,2048]{1,0:T(8,128)(2,1)} %fusion.23), channel_id=1, source_target_pairs={{0,2},{1,3},{2,0},{3,1},{4,6},{5,7},{6,4},{7,5},{8,10},{9,11},{10,... | collective-permute-start | bytes 3145736 | tf_op jit(solution)/shard_map/ppermute | solution.py:46
  259.6 30.1 %collective-permute-start.36 = (bf16[256,2048]{1,0:T(8,128)(2,1)S(1)}, bf16[256,2048]{1,0:T(8,128)(2,1)}, u32[]{:S(2)}, u32[]{:S(2)}) collective-permute-start(bf16[256,2048]{1,0:T(8,128)(2,1)S(1)} %multiply_convert_fusion), channel_id=1, source_target_pairs={{0,2},{1,3},{2,0},{3,1},{4,6},{5,7},{6,4},{7,5},{8,10},{9,11},{10,... | collective-permute-start | bytes 3145736 | tf_op jit(solution)/shard_map/ppermute | solution.py:46
  261.7 38.7 %collective-permute-start.35 = (bf16[256,2048]{1,0:T(8,128)(2,1)S(1)}, bf16[256,2048]{1,0:T(8,128)(2,1)S(1)}, u32[]{:S(2)}, u32[]{:S(2)}) collective-permute-start(bf16[256,2048]{1,0:T(8,128)(2,1)S(1)} %multiply_convert_fusion), channel_id=1, source_target_pairs={{0,1},{1,0},{2,3},{3,2},{4,5},{5,4},{6,7},{7,6},{8,9},{9,8},{10,11... | collective-permute-start | bytes 3145736 | tf_op jit(solution)/shard_map/ppermute | solution.py:46
  300.4 42.1 %collective-permute-start.37 = (bf16[256,2048]{1,0:T(8,128)(2,1)}, bf16[256,2048]{1,0:T(8,128)(2,1)}, u32[]{:S(2)}, u32[]{:S(2)}) collective-permute-start(bf16[256,2048]{1,0:T(8,128)(2,1)} %collective-permute-done.36), channel_id=1, source_target_pairs={{0,1},{1,0},{2,3},{3,2},{4,5},{5,4},{6,7},{7,6},{8,9},{9,8},{10,11... | collective-permute-start | bytes 3145736 | tf_op jit(solution)/shard_map/ppermute | solution.py:46
  337.5 34.0 %collective-permute-start.85 = (bf16[128,1536]{1,0:T(8,128)(2,1)S(1)}, bf16[128,1536]{1,0:T(8,128)(2,1)S(1)}, u32[]{:S(2)}, u32[]{:S(2)}) collective-permute-start(bf16[128,1536]{1,0:T(8,128)(2,1)S(1)} %collective-permute-done.84.refs_10_), channel_id=1, source_target_pairs={{0,4},{4,8},{8,12},{12,28},{28,24},{24,20},{20,16},{16,0},{1,5},{5... | collective-permute-start | bytes 1179656 | tf_op jit(solution)/shard_map/ppermute | solution.py:77
  341.1 31.1 %collective-permute-start.92 = (bf16[128,1536]{1,0:T(8,128)(2,1)S(1)}, bf16[128,1536]{1,0:T(8,128)(2,1)S(1)}, u32[]{:S(2)}, u32[]{:S(2)}) collective-permute-start(bf16[128,1536]{1,0:T(8,128)(2,1)S(1)} %collective-permute-done.91.refs_18_), channel_id=1, source_target_pairs={{4,0},{8,4},{12,8},{28,12},{24,28},{20,24},{16,20},{0,16},{5,1},{9... | collective-permute-start | bytes 1179656 | tf_op jit(solution)/shard_map/ppermute | solution.py:78
  346.1 27.5 %collective-permute-start.56 = (bf16[128,1536]{1,0:T(8,128)(2,1)S(1)}, bf16[128,1536]{1,0:T(8,128)(2,1)S(1)}, u32[]{:S(2)}, u32[]{:S(2)}) collective-permute-start(bf16[128,1536]{1,0:T(8,128)(2,1)S(1)} %collective-permute-done.55.refs_9_), channel_id=1, source_target_pairs={{0,4},{4,8},{8,12},{12,28},{28,24},{24,20},{20,16},{16,0},{1,5},{5... | collective-permute-start | bytes 1179656 | tf_op jit(solution)/shard_map/ppermute | solution.py:77
  371.5 29.6 %collective-permute-start.86 = (bf16[128,1536]{1,0:T(8,128)(2,1)S(1)}, bf16[128,1536]{1,0:T(8,128)(2,1)S(1)}, u32[]{:S(2)}, u32[]{:S(2)}) collective-permute-start(bf16[128,1536]{1,0:T(8,128)(2,1)S(1)} %collective-permute-done.85.refs_11_), channel_id=1, source_target_pairs={{0,4},{4,8},{8,12},{12,28},{28,24},{24,20},{20,16},{16,0},{1,5},{5... | collective-permute-start | bytes 1179656 | tf_op jit(solution)/shard_map/ppermute | solution.py:77
  372.2 28.9 %collective-permute-start.93 = (bf16[128,1536]{1,0:T(8,128)(2,1)S(1)}, bf16[128,1536]{1,0:T(8,128)(2,1)S(1)}, u32[]{:S(2)}, u32[]{:S(2)}) collective-permute-start(bf16[128,1536]{1,0:T(8,128)(2,1)S(1)} %collective-permute-done.92.refs_19_), channel_id=1, source_target_pairs={{4,0},{8,4},{12,8},{28,12},{24,28},{20,24},{16,20},{0,16},{5,1},{9... | collective-permute-start | bytes 1179656 | tf_op jit(solution)/shard_map/ppermute | solution.py:78
  373.6 25.4 %collective-permute-start.57 = (bf16[128,1536]{1,0:T(8,128)(2,1)S(1)}, bf16[128,1536]{1,0:T(8,128)(2,1)S(1)}, u32[]{:S(2)}, u32[]{:S(2)}) collective-permute-start(bf16[128,1536]{1,0:T(8,128)(2,1)S(1)} %collective-permute-done.56.refs_10_), channel_id=1, source_target_pairs={{0,4},{4,8},{8,12},{12,28},{28,24},{24,20},{20,16},{16,0},{1,5},{5... | collective-permute-start | bytes 1179656 | tf_op jit(solution)/shard_map/ppermute | solution.py:77
  374.2 25.5 %collective-permute-start.64 = (bf16[128,1536]{1,0:T(8,128)(2,1)S(1)}, bf16[128,1536]{1,0:T(8,128)(2,1)S(1)}, u32[]{:S(2)}, u32[]{:S(2)}) collective-permute-start(bf16[128,1536]{1,0:T(8,128)(2,1)S(1)} %collective-permute-done.63.refs_18_), channel_id=1, source_target_pairs={{4,0},{8,4},{12,8},{28,12},{24,28},{20,24},{16,20},{0,16},{5,1},{9... | collective-permute-start | bytes 1179656 | tf_op jit(solution)/shard_map/ppermute | solution.py:78
  399.0 26.0 %collective-permute-start.58 = (bf16[128,1536]{1,0:T(8,128)(2,1)S(1)}, bf16[128,1536]{1,0:T(8,128)(2,1)S(1)}, u32[]{:S(2)}, u32[]{:S(2)}) collective-permute-start(bf16[128,1536]{1,0:T(8,128)(2,1)S(1)} %collective-permute-done.57.refs_11_), channel_id=1, source_target_pairs={{0,4},{4,8},{8,12},{12,28},{28,24},{24,20},{20,16},{16,0},{1,5},{5... | collective-permute-start | bytes 1179656 | tf_op jit(solution)/shard_map/ppermute | solution.py:77
  399.7 25.3 %collective-permute-start.65 = (bf16[128,1536]{1,0:T(8,128)(2,1)S(1)}, bf16[128,1536]{1,0:T(8,128)(2,1)S(1)}, u32[]{:S(2)}, u32[]{:S(2)}) collective-permute-start(bf16[128,1536]{1,0:T(8,128)(2,1)S(1)} %collective-permute-done.64.refs_19_), channel_id=1, source_target_pairs={{4,0},{8,4},{12,8},{28,12},{24,28},{20,24},{16,20},{0,16},{5,1},{9... | collective-permute-start | bytes 1179656 | tf_op jit(solution)/shard_map/ppermute | solution.py:78
  460.9 26.1 %collective-permute-start.102 = (bf16[256,2048]{1,0:T(8,128)(2,1)S(1)}, bf16[256,2048]{1,0:T(8,128)(2,1)S(1)}, u32[]{:S(2)}, u32[]{:S(2)}) collective-permute-start(bf16[256,2048]{1,0:T(8,128)(2,1)S(1)} %fusion.16), channel_id=1, source_target_pairs={{0,2},{1,3},{2,0},{3,1},{4,6},{5,7},{6,4},{7,5},{8,10},{9,11},{10,... | collective-permute-start | bytes 3145736 | tf_op jit(solution)/shard_map/ppermute | solution.py:46
  462.6 25.2 %collective-permute-start.94 = (bf16[256,2048]{1,0:T(8,128)(2,1)S(1)}, bf16[256,2048]{1,0:T(8,128)(2,1)S(1)}, u32[]{:S(2)}, u32[]{:S(2)}) collective-permute-start(bf16[256,2048]{1,0:T(8,128)(2,1)S(1)} %slice_bitcast_fusion.5), channel_id=1, source_target_pairs={{0,1},{1,0},{2,3},{3,2},{4,5},{5,4},{6,7},{7,6},{8,9},{9,8},{10,11... | collective-permute-start | bytes 3145736 | tf_op jit(solution)/shard_map/ppermute | solution.py:46
  463.1 45.6 %collective-permute-start.96 = (bf16[256,2048]{1,0:T(8,128)(2,1)S(1)}, bf16[256,2048]{1,0:T(8,128)(2,1)S(1)}, u32[]{:S(2)}, u32[]{:S(2)}) collective-permute-start(bf16[256,2048]{1,0:T(8,128)(2,1)S(1)} %fusion.19), channel_id=1, source_target_pairs={{0,2},{1,3},{2,0},{3,1},{4,6},{5,7},{6,4},{7,5},{8,10},{9,11},{10,... | collective-permute-start | bytes 3145736 | tf_op jit(solution)/shard_map/ppermute | solution.py:46
  513.3 26.4 %collective-permute-start.104 = (bf16[256,2048]{1,0:T(8,128)(2,1)}, bf16[256,2048]{1,0:T(8,128)(2,1)}, u32[]{:S(2)}, u32[]{:S(2)}) collective-permute-start(bf16[256,2048]{1,0:T(8,128)(2,1)} %get-tuple-element.200), channel_id=1, source_target_pairs={{0,2},{1,3},{2,0},{3,1},{4,6},{5,7},{6,4},{7,5},{8,10},{9,11},{10,... | collective-permute-start | bytes 3145736 | tf_op jit(solution)/shard_map/ppermute | solution.py:46
  515.5 45.0 %collective-permute-start.103 = (bf16[256,2048]{1,0:T(8,128)(2,1)}, bf16[256,2048]{1,0:T(8,128)(2,1)}, u32[]{:S(2)}, u32[]{:S(2)}) collective-permute-start(bf16[256,2048]{1,0:T(8,128)(2,1)} %get-tuple-element.200), channel_id=1, source_target_pairs={{0,1},{1,0},{2,3},{3,2},{4,5},{5,4},{6,7},{7,6},{8,9},{9,8},{10,11... | collective-permute-start | bytes 3145736 | tf_op jit(solution)/shard_map/ppermute | solution.py:46
  515.5 45.0 %collective-permute-start.98 = (bf16[256,2048]{1,0:T(8,128)(2,1)}, bf16[256,2048]{1,0:T(8,128)(2,1)}, u32[]{:S(2)}, u32[]{:S(2)}) collective-permute-start(bf16[256,2048]{1,0:T(8,128)(2,1)} %get-tuple-element.205), channel_id=1, source_target_pairs={{0,2},{1,3},{2,0},{3,1},{4,6},{5,7},{6,4},{7,5},{8,10},{9,11},{10,... | collective-permute-start | bytes 3145736 | tf_op jit(solution)/shard_map/ppermute | solution.py:46
  544.1 199.3 %collective-permute-start.97 = (bf16[256,2048]{1,0:T(8,128)(2,1)}, bf16[256,2048]{1,0:T(8,128)(2,1)}, u32[]{:S(2)}, u32[]{:S(2)}) collective-permute-start(bf16[256,2048]{1,0:T(8,128)(2,1)} %get-tuple-element.205), channel_id=1, source_target_pairs={{0,1},{1,0},{2,3},{3,2},{4,5},{5,4},{6,7},{7,6},{8,9},{9,8},{10,11... | collective-permute-start | bytes 3145736 | tf_op jit(solution)/shard_map/ppermute | solution.py:46
  560.5 183.0 %collective-permute-start.99 = (bf16[256,2048]{1,0:T(8,128)(2,1)}, bf16[256,2048]{1,0:T(8,128)(2,1)}, u32[]{:S(2)}, u32[]{:S(2)}) collective-permute-start(bf16[256,2048]{1,0:T(8,128)(2,1)} %collective-permute-done.98), channel_id=1, source_target_pairs={{0,1},{1,0},{2,3},{3,2},{4,5},{5,4},{6,7},{7,6},{8,9},{9,8},{10,11... | collective-permute-start | bytes 3145736 | tf_op jit(solution)/shard_map/ppermute | solution.py:46
  (321 other events, 4234.4 us)

commit v2 on v1

--- a/solution.py
+++ b/solution.py
@@ -11,7 +11,8 @@
 CHUNK = 128
 AUG = 80
 RING = 8
-FFN_PARTS = 4
+FFN_UNITS = ((384, 384), (640, 640))
+BIG = 60
 
 epsilon = 1e-05
 rope_base = 500000.0
@@ -61,63 +62,59 @@
     return row * seq + jnp.where(row % 2 == 0, col, seq - 1 - col)
 
 
-def weight_ring(block, after):
-    dp, seq = lax.axis_size("dp"), lax.axis_size("seq")
-    count = dp * seq
-    if count > RING:
-        return [lax.all_gather(block, ("dp", "seq"), axis=0, tiled=True)]
-    order = [place_of(i, seq) for i in range(count)]
-    up = [(order[i], order[(i + 1) % count]) for i in range(count)]
-    half = block.shape[0] // 2
-    a, b = block[:half], block[half:]
-    if after:
-        a, b = lax.optimization_barrier((a, b, *after))[:2]
-    first, second = [a], [b]
-    for _ in range(count - 1):
-        a = lax.ppermute(a, ("dp", "seq"), up)
-        b = lax.ppermute(b, ("dp", "seq"), [(j, i) for i, j in up])
-        first.append(a)
-        second.append(b)
-    return first + second
-
-
-def ring_offsets(rows):
-    dp, seq = lax.axis_size("dp"), lax.axis_size("seq")
-    count = dp * seq
-    if count > RING:
-        return jnp.zeros((1,), i32)
-    place = place_of_traced(lax.axis_index("dp") * seq + lax.axis_index("seq"), seq)
-    steps = jnp.arange(count)
-    first = place_of_traced((place - steps) % count, seq) * rows
-    second = place_of_traced((place + steps) % count, seq) * rows + rows // 2
-    return jnp.concatenate([first, second]).astype(i32)
-
-
-def reduce_to_own(x, axis):
-    size, index = lax.axis_size(axis), lax.axis_index(axis)
-    while size > 1:
-        half = size // 2
-        bit = (index // half) % 2
-        x = x.reshape((2, half) + x.shape[1:])
-        send = lax.dynamic_index_in_dim(x, 1 - bit, 0, keepdims=False)
-        keep = lax.dynamic_index_in_dim(x, bit, 0, keepdims=False)
-        x = keep + exchange(send, axis, half)
-        size = half
-    return x[0]
-
-
-def reduce_quarters(far, near):
-    far_mine = far[1].astype(f32) + exchange(far[0], "tensor", 1).astype(f32)
-    crossed = exchange(far_mine.astype(bf16), "tensor", 2)
-    near_mine = near[1].astype(f32) + exchange(near[0], "tensor", 1).astype(f32)
-    return near_mine + crossed.astype(f32)
-
-
-def gather_quarters(own):
-    across = exchange(own, "tensor", 2)
-    beside = exchange(own, "tensor", 1)
-    last = exchange(across, "tensor", 1)
-    return jnp.stack([own, beside, across, last])
+class Clock:
+    def __init__(self):
+        self.now = jnp.zeros((), i32)
+
+    def wait(self, *arrays):
+        *out, self.now = lax.optimization_barrier((*arrays, self.now))
+        return out
+
+    def tie(self, x):
+        return self.wait(x)[0]
+
+
+class Chain:
+    def __init__(self, clock, way, pack, *blocks):
+        block = pack(*clock.wait(*blocks))
+        dp, seq = lax.axis_size("dp"), lax.axis_size("seq")
+        self.clock, self.count = clock, dp * seq
+        self.ringed = self.count <= RING
+        rows = block.shape[0]
+        if not self.ringed:
+            self.lanes = [[lax.all_gather(block, ("dp", "seq"), axis=0, tiled=True)]]
+            self.offsets = jnp.zeros((1,), i32)
+            return
+        order = [place_of(i, seq) for i in range(self.count)]
+        up = [(order[i], order[(i + 1) % self.count]) for i in range(self.count)]
+        down = [(j, i) for i, j in up]
+        place = place_of_traced(lax.axis_index("dp") * seq + lax.axis_index("seq"), seq)
+        steps = jnp.arange(self.count)
+        came_up = place_of_traced((place - steps) % self.count, seq) * rows
+        came_down = place_of_traced((place + steps) % self.count, seq) * rows
+        if way:
+            self.lanes, self.ways = [[block]], [up if way > 0 else down]
+            self.offsets = (came_up if way > 0 else came_down).astype(i32)
+        else:
+            half = rows // 2
+            self.lanes, self.ways = [[block[:half]], [block[half:]]], [up, down]
+            self.offsets = jnp.concatenate([came_up, came_down + half]).astype(i32)
+
+    def settle(self):
+        if self.ringed:
+            came = self.clock.wait(*[lane[-1] for lane in self.lanes])
+            for lane, x in zip(self.lanes, came):
+                lane[-1] = x
+
+    def step(self):
+        if self.ringed:
+            self.settle()
+            for lane, way in zip(self.lanes, self.ways):
+                lane.append(lax.ppermute(lane[-1], ("dp", "seq"), way))
+
+    def pieces(self):
+        self.settle()
+        return [piece for lane in self.lanes for piece in lane]
 
 
 def load_pieces(pieces, offsets, held, sems):
@@ -139,8 +136,7 @@
     return pltpu.CompilerParams(vmem_limit_bytes=limit * MIB)
 
 
-def cost(flops, moved, exps=0):
-    return pl.CostEstimate(flops=int(flops), bytes_accessed=int(moved), transcendentals=int(exps))
+SMALL = pl.CostEstimate(flops=1, bytes_accessed=1, transcendentals=0)
 
 
 ANY = pl.BlockSpec(memory_space=pl.ANY)
@@ -289,60 +285,152 @@
     att[...] = attended.T.astype(bf16)
 
 
+def store_at(step, value, outs):
+    for i, out in enumerate(outs):
+
+        @pl.when(step == i)
+        def _(out=out):
+            out[...] = value.astype(out.dtype)
+
+
 def o_body(n_pieces, offsets, nat, att, down, up, *rest):
     pieces = rest[:n_pieces]
-    part, lowered, held, sems = rest[n_pieces:]
-
-    @pl.when(pl.program_id(0) == 0)
+    part0, part1, lowered, held, sems = rest[-5:]
+    step = pl.program_id(0)
+
+    @pl.when(step == 0)
     def _():
         load_pieces(pieces, offsets, held, sems)
 
     low = nn(att[...], down[...])
-    lowered[0] = low
-    part[0] = (nt(att[...], held[...]) + nn(halves(low, 1), up[...])).astype(bf16)
-
-
-def ffn_body(n_pieces, units, first, offsets, order, nat, n2, cot, *rest):
-    pieces, rest = rest[:n_pieces], rest[n_pieces:]
-    if first:
-        mlp, grad, held, sems = rest
-    else:
-        mlp_in, grad_in, mlp, grad, held, sems = rest
-
-    @pl.when(pl.program_id(0) == 0)
+    lowered[...] = low
+    store_at(step, nt(att[...], held[...]) + nn(halves(low, 1), up[...]), (part0, part1))
+
+
+def quarter_copies(quarters, held, sems, first=0):
+    return [pltpu.make_async_copy(x, held.at[first + i], sems.at[first + i]) for i, x in enumerate(quarters)]
+
+
+def quarter_of(step, quarters, held, sems):
+    for i, copy in enumerate(quarter_copies(quarters, held, sems)):
+
+        @pl.when(step == i)
+        def _(copy=copy):
+            copy.wait()
+
+    return held[step]
+
+
+def ffn_body(lots, units, summed, last, offsets, nat, cot, *rest):
+    count, n_out = sum(lots), 4 if last else 2
+    quarters, pieces, rest = rest[:2], rest[2 : 2 + count], rest[2 + count :]
+    sums, outs, rest = rest[: 2 * summed], rest[2 * summed : 2 * summed + n_out], rest[2 * summed + n_out :]
+    rows, rows_sems, held, sems, out_held, out_sems, *rest = rest
+    step = pl.program_id(0)
+
+    def at_first(act):
+        pl.when(step == 0)(act)
+
+    def copies(which):
+        made, at, i = [], 0, 0
+        for lot, size in zip(lots, units):
+            for _ in range(lot):
+                made.append(
+                    pltpu.make_async_copy(
+                        pieces[i].at[:, pl.ds(which * size, size)],
+                        held.at[which, pl.ds(pl.multiple_of(offsets[i], 16), pieces[i].shape[0]), pl.ds(at, size)],
+                        sems.at[which, i],
+                    )
+                )
+                i += 1
+            at += size
+        return made
+
+    def sum_copy(i, kind):
+        return pltpu.make_async_copy(sums[kind].at[i], rest[0].at[i, kind], rest[1].at[i, kind])
+
+    def out_copy(i, kind):
+        out = outs[2 * (1 - kind) + i] if last else outs[kind].at[i]
+        return pltpu.make_async_copy(out_held.at[i, kind], out, out_sems.at[i, kind])
+
+    @at_first
     def _():
-        load_pieces(pieces, offsets, held, sems)
-
-    gate = nn(n2[0], held[:, :units])
-    up = nn(n2[0], held[:, units : 2 * units])
-    grad_act = nn(cot[...], held[:, 2 * units :])
+        first = copies(0)
+        for copy in quarter_copies(quarters[:1], rows, rows_sems) + first:
+            copy.start()
+        for copy in quarter_copies(quarters[1:], rows, rows_sems, 1):
+            copy.start()
+        for copy in first:
+            copy.wait()
+        for copy in copies(1):
+            copy.start()
+
+    n2 = quarter_of(step, quarters, rows, rows_sems)
+    gate = nn(n2, held[0])
+
+    @at_first
+    def _():
+        for copy in copies(1):
+            copy.wait()
+        for copy in copies(2):
+            copy.start()
+
+    up = nn(n2, held[1])
+
+    @at_first
+    def _():
+        for copy in copies(2):
+            copy.wait()
+        for i in range(2 if summed else 0):
+            for kind in (1, 0):
+                sum_copy(i, kind).start()
+
+    grad_act = nn(cot[...], held[2])
     s = 1.0 / (1.0 + jnp.exp(-gate))
     silu = gate * s
     act = (silu * up).astype(bf16)
     grad_gate = (grad_act * up * s * (1.0 + gate * (1.0 - s))).astype(bf16)
     grad_up = (grad_act * silu).astype(bf16)
-    down_sum = nt(act, held[:, 2 * units :])
-    grad_sum = nt(grad_gate, held[:, :units]) + nt(grad_up, held[:, units : 2 * units])
-    if not first:
-        down_sum = down_sum + mlp_in[0]
-        grad_sum = grad_sum + grad_in[0]
-    mlp[0] = down_sum.astype(mlp.dtype)
-    grad[0] = grad_sum.astype(grad.dtype)
-
-
-def go_body(dims, offsets, nat, before_doc, branch, o_up, o_down, att_t, totals, phi_q, q_doc, *rest):
-    n_pieces, kv_heads, group, head = dims
-    pieces = rest[:n_pieces]
-    numer, grad_totals, up_product, dstate, held, sems = rest[n_pieces:]
-
-    @pl.when(pl.program_id(0) == 0)
+
+    def finish(kind, total):
+        if summed:
+            sum_copy(step, kind).wait()
+            total = total + rest[0][step, kind]
+        out_held[step, kind] = total.astype(out_held.dtype)
+        for i in range(2):
+
+            @pl.when(step == i)
+            def _(i=i):
+                out_copy(i, kind).start()
+
+    finish(1, nt(grad_gate, held[0]) + nt(grad_up, held[1]))
+    finish(0, nt(act, held[2]))
+
+    @pl.when(step == 1)
     def _():
+        for i in range(2):
+            for kind in range(2):
+                out_copy(i, kind).wait()
+
+
+def go_body(dims, offsets, nat, before_doc, o_up, o_down, att_t, totals, phi_q, q_doc, *rest):
+    n_pieces, kv_heads, group, head, later = dims
+    quarters, pieces, rest = rest[:2], rest[2 : 2 + n_pieces], rest[2 + n_pieces :]
+    earlier, rest = rest[: 4 * later], rest[4 * later :]
+    numer, grad_totals, up_product, dstate, rows_held, rows_sems, held, sems = rest
+    step = pl.program_id(0)
+
+    @pl.when(step == 0)
+    def _():
+        for copy in quarter_copies(quarters, rows_held, rows_sems):
+            copy.start()
         load_pieces(pieces, offsets, held, sems)
-        dstate[...] = jnp.zeros(dstate.shape, f32)
-
-    up = nn(branch[0], o_up[...])
+        dstate[...] = earlier[3][...] if later else jnp.zeros(dstate.shape, f32)
+
+    branch = quarter_of(step, quarters, rows_held, rows_sems)
+    up = nn(branch, o_up[...])
     up_product[...] = up
-    grad = (nn(branch[0], held[...]) + nn(halves(up, 1), o_down[...])).T
+    grad = (nn(branch, held[...]) + nn(halves(up, 1), o_down[...])).T
     use = (q_doc[...] == before_doc[0]).astype(f32)
     columns = grad.shape[1]
     for k in range(kv_heads):
@@ -371,8 +459,8 @@
 
 def backward_body(
     dims, last_docs, q_t, phi_q, numer, grad_totals, k_n, k_t, v_n, v_a, phi_kn, phi_kt, doc_col, doc_row, q_doc,
-    states, later_in, cos_q, sin_q, map_q, map_k,
-    g_nat, g_kt, g_vt, g_map_q, g_map_k, later, acc_phi,
+    states, cos_q, sin_q, map_q,
+    g_nat, g_kt, g_vt, acc_phi, g_map_q, later,
 ):
     kv_heads, group, head, chunks = dims
     step = pl.program_id(0)
@@ -382,7 +470,7 @@
 
     @pl.when(step == 0)
     def _():
-        later[...] = later_in[...]
+        later[...] = jnp.zeros(later.shape, f32)
         g_kt[...] = jnp.zeros(g_kt.shape, f32)
         g_vt[...] = jnp.zeros(g_vt.shape, f32)
         acc_phi[...] = jnp.zeros(acc_phi.shape, f32)
@@ -437,47 +525,118 @@
         grads.append(rope(gq_rows, cos_q[...], -sin_q[...]))
     g_nat[...] = jnp.concatenate(grads, axis=0).T.astype(bf16)
 
-    @pl.when(step == chunks - 1)
-    def _():
-        ga = hedgehog_back(phi_kt[...], acc_phi[...], head)
-        g_kt[...] += tn(map_k[...], ga)
-        g_map_k[...] = nt(k_t[...], ga)
-
-
-def gn_body(n_pieces, offsets, nat, g_q, g_kv, ups_q, ups_kv, downs, *rest):
+
+def keys_back_body(dims, last_docs, factors, g_kt, g_vt, g_phi, v_a, phi_kt, k_t, doc_row, map_k, *rest):
+    kv_heads, head, chunks, rows = dims
+    later, (g_own, g_halo, g_map_k) = rest[:-3], rest[-3:]
+    ext = g_kt.shape[1]
+    incl = (doc_row[...] == last_docs[chunks]) & (lax.broadcasted_iota(i32, (1, ext), 1) < rows)
+    incl = incl.astype(f32)
+    phi_grads, v_grads = [], []
+    for k in range(kv_heads):
+        wide = slice(2 * k * head, 2 * (k + 1) * head)
+        after = jnp.zeros(later[0].shape[1:], f32)
+        for i, x in enumerate(later):
+            after = after + factors[i] * x[k]
+        phi_grads.append(g_phi[wide, :] + incl * nn(after.astype(bf16), v_a[k * AUG : (k + 1) * AUG, :]))
+        from_later = nn(after.T.astype(bf16), phi_kt[wide, :])[:head]
+        v_grads.append(g_vt[k * head : (k + 1) * head, :] + incl * from_later)
+    ga = hedgehog_back(phi_kt[...], jnp.concatenate(phi_grads, axis=0), head)
+    g_map_k[...] = nt(k_t[...], ga)
+    g_k = g_kt[...] + tn(map_k[...], ga)
+    for i, grad in enumerate((g_k, jnp.concatenate(v_grads, axis=0))):
+        mine = slice(i * kv_heads * head, (i + 1) * kv_heads * head)
+        g_own[mine, :] = grad[:, WIN : WIN + rows]
+        g_halo[mine, :] = jnp.concatenate([jnp.zeros((kv_heads * head, CHUNK - WIN), f32), grad[:, :WIN]], axis=1)
+
+
+def adapters_body(
+    dims, nat, g_q, g_own, g_halo, cos, sin, ups, low, normed, lowered, att, up_product, g_map_q, g_map_k, *rest
+):
+    rows, window, head, rank = dims
+    branch, (g_kv, low_back, by_head, shared) = rest[:4], rest[4:]
+    half = g_own.shape[0] // 2
+    wide = rows - g_halo.shape[1]
+    k = jnp.concatenate([g_own[:half, :wide], g_own[:half, wide:] + g_halo[:half]], axis=1)
+    v = jnp.concatenate([g_own[half:, :wide], g_own[half:, wide:] + g_halo[half:]], axis=1)
+    kv = jnp.concatenate([rope(k, cos[...], -sin[...]), v], axis=0).T.astype(bf16)
+    g_kv[...] = kv
+    q_width = g_q.shape[1]
+    up = nn(g_q[...], ups[:q_width]) + nn(kv, ups[q_width:])
+    up_halves = halves(up, 1)
+    low_back[...] = up_halves
+
+    def joined(x, axis):
+        one, other = jnp.split(x, 2, axis=axis)
+        return one + other
+
+    low_halves = halves(low[...], 1)
+    g_q_up = joined(tn(g_q[...], low_halves), 1)[:, :rank]
+    g_kv_up = joined(tn(kv, low_halves), 1)
+    g_o_down = joined(tn(att[...], halves(up_product[...], 1)), 1)
+    by_head[...] = jnp.zeros(by_head.shape, f32)
+    q_heads, kv_heads = q_width // head, half // head
+    group = q_heads // kv_heads
+    for h in range(q_heads):
+        mine, at = slice(h * head, (h + 1) * head), (h % group) * head
+        by_head[h, :, :head] = g_map_q[h // group, at : at + head, at : at + head]
+        by_head[h, :, head : head + rank] = g_q_up[mine]
+        by_head[h, :, head + rank : head + 2 * rank] = g_o_down[mine]
+    for h in range(kv_heads):
+        mine = slice(h * head, (h + 1) * head)
+        by_head[q_heads + h, :, :head] = g_map_k[mine, mine]
+        by_head[q_heads + h, :, head : head + rank] = g_kv_up[mine, rank : 2 * rank]
+        by_head[q_heads + h, :, head + rank : head + 2 * rank] = g_kv_up[half + h * head : half + (h + 1) * head, 2 * rank :]
+    shared[: 3 * rank, :] = joined(tn(up_halves, normed[window : window + rows, :]), 0)
+    o_up = 0.0
+    for i, x in enumerate(branch):
+        part = lowered[pl.ds(pl.multiple_of(nat[i] * x.shape[0], x.shape[0]), x.shape[0]), :]
+        o_up = o_up + tn(halves(part, 1), x[...])
+    shared[3 * rank :, :] = joined(o_up, 0)
+
+
+def gn_body(n_pieces, offsets, nat, g_q, g_kv, low_back, downs, *rest):
     pieces = rest[:n_pieces]
-    part, ups, held, sems = rest[n_pieces:]
-
-    @pl.when(pl.program_id(0) == 0)
+    part0, part1, held, sems = rest[n_pieces:]
+    step = pl.program_id(0)
+
+    @pl.when(step == 0)
     def _():
         load_pieces(pieces, offsets, held, sems)
 
     q_width = g_q.shape[1]
-    up = nn(g_q[...], ups_q[...]) + nn(g_kv[...], ups_kv[...])
-    ups[0] = up
     total = nt(g_q[...], held[:, :q_width]) + nt(g_kv[...], held[:, q_width:])
-    part[0] = (total + nn(halves(up, 1), downs[...])).astype(bf16)
-
-
-def place_body(nat, x, out):
-    out[...] = x[0].astype(out.dtype)
-
-
-def place(x, nat, dtype):
-    count, rows, width = x.shape
+    store_at(step, total + nn(low_back[...], downs[...]), (part0, part1))
+
+
+def place_body(nat, *refs):
+    quarters, (out, held, sems) = refs[:4], refs[4:]
+    step = pl.program_id(0)
+
+    @pl.when(step == 0)
+    def _():
+        for copy in quarter_copies(quarters, held, sems):
+            copy.start()
+
+    out[...] = quarter_of(step, quarters, held, sems).astype(out.dtype)
+
+
+def place(quarters, nat, dtype):
+    rows, width = quarters[0].shape
     return pl.pallas_call(
         place_body,
         grid_spec=pltpu.PrefetchScalarGridSpec(
             num_scalar_prefetch=1,
-            grid=(count,),
-            in_specs=[pl.BlockSpec((1, rows, width), lambda i, nat: (i, 0, 0))],
+            grid=(4,),
+            in_specs=[ANY] * 4,
             out_specs=pl.BlockSpec((rows, width), lambda i, nat: (nat[i], 0)),
+            scratch_shapes=[pltpu.VMEM((4, rows, width), bf16), pltpu.SemaphoreType.DMA((4,))],
         ),
-        out_shape=jax.ShapeDtypeStruct((count * rows, width), dtype),
+        out_shape=jax.ShapeDtypeStruct((4 * rows, width), dtype),
         compiler_params=params(32),
-        cost_estimate=cost(0, x.size * 6),
+        cost_estimate=SMALL,
         name="place",
-    )(nat, x)
+    )(nat, *quarters)
 
 
 def rms_factor(x):
@@ -536,24 +695,40 @@
     chunks = rows // CHUNK
     ext = -(-(rows + WIN) // CHUNK) * CHUNK
     quarter = rows // 4
-    units = gate_weight.shape[1] // FFN_PARTS
 
     core, far = lax.axis_index("tensor") % 2, lax.axis_index("tensor") // 2
     nat = jnp.stack([core * 2 + far, (1 - core) * 2 + far, core * 2 + 1 - far, (1 - core) * 2 + 1 - far]).astype(i32)
     own_rows = lambda x: lax.dynamic_slice_in_dim(x, nat[0] * quarter, quarter, 0)
 
-    offsets = ring_offsets(query_weight.shape[0])
+    clock = Clock()
+    beside_each_other = lambda *blocks: jnp.concatenate(blocks, axis=1)
+    qkv_chain = Chain(clock, 0, beside_each_other, query_weight, key_weight, value_weight)
+    qkv_chain.step()
+    o_chain = Chain(clock, 0, jnp.transpose, output_weight)
+    o_chain.step()
+    offsets = qkv_chain.offsets
     n_pieces = offsets.shape[0]
-    qkv_pieces = weight_ring(jnp.concatenate([query_weight, key_weight, value_weight], axis=1), ())
-    o_pieces = weight_ring(output_weight.T, qkv_pieces[n_pieces // 2 - 2 : n_pieces // 2 - 1] if n_pieces > 1 else ())
-    ffn_pieces, chain = [], [qkv_pieces, o_pieces]
-    for j in range(FFN_PARTS):
-        cols = slice(j * units, (j + 1) * units)
-        packed = jnp.concatenate([gate_weight[:, cols], up_weight[:, cols], down_weight[cols].T], axis=1)
-        behind = chain[-2]
-        after = (behind[n_pieces // 2 - 1], behind[-1]) if n_pieces > 1 else ()
-        ffn_pieces.append(weight_ring(packed, after))
-        chain.append(ffn_pieces[-1])
+    assert sum(map(sum, FFN_UNITS)) == gate_weight.shape[1]
+
+    def ffn_chains(part):
+        made = []
+        at = sum(map(sum, FFN_UNITS[:part]))
+        for units, way in zip(FFN_UNITS[part], (1, -1)):
+            cols = slice(at, at + units)
+            pack = lambda gate, up, down, cols=cols: jnp.concatenate([gate[:, cols], up[:, cols], down[cols].T], axis=1)
+            made.append(Chain(clock, way, pack, gate_weight, up_weight, down_weight))
+            at += units
+        return made
+
+    def turn(part):
+        for chain in chains[part]:
+            chain.settle()
+        for chain in chains[part]:
+            chain.step()
+
+    def round_qkv_o():
+        qkv_chain.step()
+        o_chain.step()
 
     lengths = sequence_lengths[0]
     ends = jnp.cumsum(lengths)
@@ -582,24 +757,40 @@
     passes = (block_docs[:-1] == block_docs[1:]).astype(f32)
     cos_q, sin_q = angles_of(q_at)
     cos_k, sin_k = angles_of(k_at)
+    cos_q, sin_q, cos_k, sin_k = clock.wait(cos_q, sin_q, cos_k, sin_k)
 
     halo = shifted(tokens[rows - WIN :], "seq", 1)
+    round_qkv_o()
+    (halo,) = clock.wait(halo)
     spare = jnp.zeros((ext - rows - WIN, model), bf16)
     seen = jnp.concatenate([halo, tokens, spare], axis=0).astype(f32)
     gain_attn = attention_norm_gain.astype(f32)
     gain_mlp = feedforward_norm_gain.astype(f32)
-    normed = (seen * rms_factor(seen) * gain_attn).astype(bf16)
+    factor = clock.tie(rms_factor(seen))
+    round_qkv_o()
+    normed = clock.tie((seen * factor * gain_attn).astype(bf16))
     downs = jnp.concatenate([query_adapter_down, key_adapter_down, value_adapter_down], axis=1)
-    low = nn(normed, downs)
+    low = clock.tie(nn(normed, downs))
+    round_qkv_o()
     ups = jnp.zeros((q_width + 2 * kv_width, 3 * rank), bf16)
     ups = ups.at[:q_width, :rank].set(query_adapter_up.reshape(q_width, rank))
     ups = ups.at[q_width : q_width + kv_width, rank : 2 * rank].set(key_adapter_up.reshape(kv_width, rank))
     ups = ups.at[q_width + kv_width :, 2 * rank :].set(value_adapter_up.reshape(kv_width, rank))
-    low_up = nt(halves_outside(low, 1), jnp.concatenate([ups, ups], axis=1))
+    low_up = clock.tie(nt(halves_outside(low, 1), jnp.concatenate([ups, ups], axis=1)))
+    round_qkv_o()
     maps_q = jnp.stack(
         [block_diagonal(feature_map_query[k * group : (k + 1) * group].transpose(0, 2, 1)) for k in range(kv_heads)]
     )
     maps_k = block_diagonal(feature_map_key.transpose(0, 2, 1))
+    maps_q, maps_k = clock.wait(maps_q, maps_k)
+    round_qkv_o()
+    chains = [ffn_chains(0)]
+    for chain in chains[0]:
+        chain.settle()
+    for _ in range(ring - 7):
+        round_qkv_o()
+    qkv_pieces = qkv_chain.pieces()
+    turn(0)
 
     sems = pltpu.SemaphoreType.DMA((n_pieces,))
     qkv_width = q_width + 2 * kv_width
@@ -630,15 +821,20 @@
         ),
         out_shape=[jax.ShapeDtypeStruct(s, d) for s, d in shapes],
         compiler_params=params(56),
-        cost_estimate=cost(2 * rows * model * qkv_width, 20 * MIB, 3 * rows * q_width),
+        cost_estimate=SMALL,
         name="prep",
-    )(offsets, last_docs, *prep_in, *qkv_pieces)
-
+    )(clock.tie(offsets), last_docs, *prep_in, *qkv_pieces)
+    (contrib,) = clock.wait(contrib)
+    turn(0)
+
+    coming = clock.wait(*[shifted(contrib, "seq", by) for by in range(1, seq)])
     state_in = jnp.zeros_like(contrib)
     factor = jnp.ones((), f32)
     for by in range(1, seq):
-        state_in = state_in + factor * shifted(contrib, "seq", by)
+        state_in = state_in + factor * coming[by - 1]
         factor = factor * passes[jnp.maximum(here - by, 0)]
+    state_in = clock.tie(state_in)
+    turn(0)
 
     column = lambda r: pl.BlockSpec((r, CHUNK), lambda c, *_: (0, c))
     att, att_t, totals, states = pl.pallas_call(
@@ -672,126 +868,179 @@
             jax.ShapeDtypeStruct((chunks, kv_heads, 2 * head, AUG), bf16),
         ],
         compiler_params=params(48),
-        cost_estimate=cost(2 * heads * rows * 256 * 256, 10 * MIB, rows * heads * 192),
+        cost_estimate=SMALL,
         name="attend",
     )(last_docs, q_t, phi_q, k_n, v_a, phi_kn, doc_col, doc_row, q_doc, state_in)
-
+    att = clock.tie(att)
+
+    o_pieces = o_chain.pieces()
     o_down = output_adapter_down.reshape(q_width, rank)
     o_up_t = jnp.concatenate([output_adapter_up.T, output_adapter_up.T], axis=0)
-    order_far, order_near = jnp.array([3, 2], i32), jnp.array([1, 0], i32)
-
-    def o_part(which):
+    one_quarter = jax.ShapeDtypeStruct((quarter, model), bf16)
+
+    def o_part(first, earlier):
         return pl.pallas_call(
             lambda *refs: o_body(n_pieces, *refs),
             grid_spec=pltpu.PrefetchScalarGridSpec(
                 num_scalar_prefetch=2,
                 grid=(2,),
                 in_specs=[
-                    pl.BlockSpec((quarter, q_width), lambda i, off, nat: (nat[i], 0)),
+                    pl.BlockSpec((quarter, q_width), lambda i, off, nat: (nat[first - i], 0)),
                     whole(o_down.shape),
                     whole(o_up_t.shape),
                 ]
-                + [ANY] * n_pieces,
-                out_specs=[
-                    pl.BlockSpec((1, quarter, model), lambda i, *_: (i, 0, 0)),
-                    pl.BlockSpec((1, quarter, rank), lambda i, *_: (i, 0, 0)),
-                ],
+                + [ANY] * (n_pieces + len(earlier)),
+                out_specs=[whole((quarter, model))] * 2
+                + [pl.BlockSpec((quarter, rank), lambda i, off, nat: (nat[first - i], 0))],
                 scratch_shapes=[held_o, sems],
             ),
-            out_shape=[
-                jax.ShapeDtypeStruct((2, quarter, model), bf16),
-                jax.ShapeDtypeStruct((2, quarter, rank), f32),
-            ],
-            compiler_params=params(32),
-            cost_estimate=cost(2 * rows * model * q_width / 2, 5 * MIB),
+            out_shape=[one_quarter, one_quarter, jax.ShapeDtypeStruct((rows, rank), f32)],
+            input_output_aliases={5 + n_pieces: 2} if earlier else {},
+            compiler_params=params(BIG),
+            cost_estimate=SMALL,
             name="project",
-        )(offsets, nat[which], att, o_down, o_up_t, *o_pieces)
-
-    o_far, low_far = o_part(order_far)
-    o_near, low_near = o_part(order_near)
-    lowered = jnp.concatenate([low_near[1], low_near[0], low_far[1], low_far[0]], axis=0)
-    hidden = own_rows(tokens).astype(f32) + reduce_quarters(o_far, o_near)
-    normed_mlp = gather_quarters((hidden * rms_factor(hidden) * gain_mlp).astype(bf16))
-
-    def ffn(pieces, which, sums, out_type):
-        count = which.shape[0]
-        block = lambda: pl.BlockSpec((1, quarter, model), lambda i, off, order, nat: (order[i], 0, 0))
-        in_order = pl.BlockSpec((1, quarter, model), lambda i, *_: (i, 0, 0))
-        out = jax.ShapeDtypeStruct((count, quarter, model), out_type)
-        share = count / 4
-        aliases = {5 + n_pieces: 0, 6 + n_pieces: 1} if sums and out_type == f32 else {}
+        )(clock.tie(offsets), nat, att, o_down, o_up_t, *o_pieces, *earlier)
+
+    o_far0, o_far1, lowered = o_part(3, ())
+    (o_far0,) = clock.wait(o_far0)
+    turn(0)
+    beside = exchange(clock.tie(o_far0), "tensor", 1)
+    o_near0, o_near1, lowered = o_part(1, (lowered,))
+    (beside,) = clock.wait(beside)
+    o_far = clock.tie((o_far1.astype(f32) + beside.astype(f32)).astype(bf16))
+    across = exchange(o_far, "tensor", 2)
+    (o_near0,) = clock.wait(o_near0)
+    beside = exchange(o_near0, "tensor", 1)
+    (beside,) = clock.wait(beside)
+    chains.append(ffn_chains(1))
+    turn(0)
+    (across,) = clock.wait(across)
+    hidden = own_rows(tokens).astype(f32) + (o_near1.astype(f32) + beside.astype(f32) + across.astype(f32))
+    (hidden,) = clock.wait(hidden)
+    normed_mlp = clock.tie((hidden * rms_factor(hidden) * gain_mlp).astype(bf16))
+    across, beside = exchange(normed_mlp, "tensor", 2), exchange(normed_mlp, "tensor", 1)
+    (beside,) = clock.wait(beside)
+    turn(0)
+    turn(0)
+    (across,) = clock.wait(across)
+    last = clock.tie(exchange(across, "tensor", 1))
+    normed_mlp = [normed_mlp, beside, across, last]
+
+    def ffn(part, quarters, sums):
+        units, last = FFN_UNITS[part], part == len(FFN_UNITS) - 1
+        lots = [chain.pieces() for chain in chains[part]]
+        sizes = tuple(map(len, lots))
+        pieces = [piece for lot in lots for piece in lot]
+        ring_offsets = jnp.concatenate([chain.offsets for chain in chains[part]])
+        first = quarters[0]
+        summed = jax.ShapeDtypeStruct((2, quarter, model), f32)
         return pl.pallas_call(
-            lambda *refs: ffn_body(n_pieces, units, not sums, *refs),
+            lambda *refs: ffn_body(sizes, units, bool(sums), last, *refs),
+            grid_spec=pltpu.PrefetchScalarGridSpec(
+                num_scalar_prefetch=2,
+                grid=(2,),
+                in_specs=[pl.BlockSpec((quarter, model), lambda i, off, nat: (nat[first - i], 0))]
+                + [ANY] * (2 + len(pieces) + len(sums)),
+                out_specs=[ANY] * (4 if last else 2),
+                scratch_shapes=[
+                    pltpu.VMEM((2, quarter, model), bf16),
+                    pltpu.SemaphoreType.DMA((2,)),
+                    pltpu.VMEM((3, model, sum(units)), bf16),
+                    pltpu.SemaphoreType.DMA((3, len(pieces))),
+                    pltpu.VMEM((2, 2, quarter, model), bf16 if last else f32),
+                    pltpu.SemaphoreType.DMA((2, 2)),
+                ]
+                + [pltpu.VMEM((2, 2, quarter, model), f32), pltpu.SemaphoreType.DMA((2, 2))] * bool(sums),
+            ),
+            out_shape=[one_quarter] * 4 if last else [summed] * 2,
+            compiler_params=params(BIG),
+            cost_estimate=SMALL,
+            name="feed_forward",
+        )(clock.tie(ring_offsets), nat, output_cotangent, *[normed_mlp[q] for q in quarters], *pieces, *sums)
+
+    for chain in chains[0]:
+        chain.settle()
+    turn(1)
+    sums_far = clock.wait(*ffn(0, (3, 2), ()))
+    turn(1)
+    sums_near = clock.wait(*ffn(0, (1, 0), ()))
+    for _ in range(ring - 3):
+        turn(1)
+    gn_far0, gn_far1, mlp_far0, mlp_far1 = ffn(1, (3, 2), sums_far)
+    gn_far0, mlp_far0 = clock.wait(gn_far0, mlp_far0)
+    beside = exchange(gn_far0, "tensor", 1)
+    mlp_beside_far = exchange(mlp_far0, "tensor", 1)
+    (beside,) = clock.wait(beside)
+    across = exchange(clock.tie((gn_far1.astype(f32) + beside.astype(f32)).astype(bf16)), "tensor", 2)
+    gn_near0, gn_near1, mlp_near0, mlp_near1 = ffn(1, (1, 0), sums_near)
+    gn_near0, mlp_near0 = clock.wait(gn_near0, mlp_near0)
+    (mlp_beside_far,) = clock.wait(mlp_beside_far)
+    mlp_far = clock.tie((mlp_far1.astype(f32) + mlp_beside_far.astype(f32)).astype(bf16))
+    across, gn_near0 = clock.wait(across, gn_near0)
+    beside = exchange(gn_near0, "tensor", 1)
+    (beside,) = clock.wait(beside)
+    grad_normed_mlp = gn_near1.astype(f32) + beside.astype(f32) + across.astype(f32)
+    grad_hidden = own_rows(output_cotangent).astype(f32) + rms_back(hidden, gain_mlp, grad_normed_mlp)
+    grad_hidden = clock.tie(grad_hidden)
+    branch = clock.tie(grad_hidden.astype(bf16))
+    across, beside = exchange(branch, "tensor", 2), exchange(branch, "tensor", 1)
+    mlp_beside = exchange(clock.tie(mlp_near0), "tensor", 1)
+    (beside,) = clock.wait(beside)
+
+    o_down_t = jnp.concatenate([o_down.T, o_down.T], axis=0)
+    sizes = [((q_width, rows), bf16), ((heads, rows), f32), ((rows, rank), f32), ((kv_heads, 2 * head, AUG), f32)]
+
+    def go_part(first, quarters, earlier):
+        by_quarter = lambda r: pl.BlockSpec((r, quarter), lambda i, off, nat, before: (0, nat[first + i]))
+        late = bool(earlier)
+        return pl.pallas_call(
+            lambda *refs: go_body((n_pieces, kv_heads, group, head, late), *refs),
             grid_spec=pltpu.PrefetchScalarGridSpec(
                 num_scalar_prefetch=3,
-                grid=(count,),
+                grid=(2,),
                 in_specs=[
-                    block(),
-                    pl.BlockSpec((quarter, model), lambda i, off, order, nat: (nat[i], 0)),
+                    whole((model, rank)),
+                    whole(o_down_t.shape),
+                    by_quarter(q_width),
+                    by_quarter(heads),
+                    by_quarter(2 * q_width),
+                    by_quarter(1),
                 ]
-                + [ANY] * n_pieces
-                + [block() for _ in sums],
-                out_specs=[in_order, in_order],
-                scratch_shapes=[pltpu.VMEM((model, 3 * units), bf16), sems],
+                + [ANY] * (2 + n_pieces)
+                + ([ANY] * 3 + [whole(sizes[3][0])]) * late,
+                out_specs=[
+                    by_quarter(q_width),
+                    by_quarter(heads),
+                    pl.BlockSpec((quarter, rank), lambda i, off, nat, before: (nat[first + i], 0)),
+                    whole(sizes[3][0]),
+                ],
+                scratch_shapes=[
+                    pltpu.VMEM((2, quarter, model), bf16),
+                    pltpu.SemaphoreType.DMA((2,)),
+                    held_o,
+                    sems,
+                ],
             ),
-            out_shape=[out, out],
-            input_output_aliases=aliases,
-            compiler_params=params(52),
-            cost_estimate=cost(12 * rows * model * units * share, 46 * MIB * share, rows * units * share),
-            name="feed_forward",
-        )(offsets, which, nat[which], normed_mlp, output_cotangent, *pieces, *sums)
-
-    every = jnp.arange(4).astype(i32)
-    sums = ()
-    for pieces in ffn_pieces[:-1]:
-        sums = tuple(ffn(pieces, every, sums, f32))
-    mlp_far, grad_far = ffn(ffn_pieces[-1], order_far, sums, bf16)
-    mlp_near, grad_near = ffn(ffn_pieces[-1], order_near, sums, bf16)
-    grad_normed_mlp = reduce_quarters(grad_far, grad_near)
-    grad_hidden = own_rows(output_cotangent).astype(f32) + rms_back(hidden, gain_mlp, grad_normed_mlp)
-    branch = gather_quarters(grad_hidden.astype(bf16))
-
-    o_down_t = jnp.concatenate([o_down.T, o_down.T], axis=0)
-    by_quarter = lambda r: pl.BlockSpec((r, quarter), lambda i, off, nat, before: (0, nat[i]))
-    numer, grad_totals, up_product, dstate = pl.pallas_call(
-        lambda *refs: go_body((n_pieces, kv_heads, group, head), *refs),
-        grid_spec=pltpu.PrefetchScalarGridSpec(
-            num_scalar_prefetch=3,
-            grid=(4,),
-            in_specs=[
-                pl.BlockSpec((1, quarter, model), lambda i, *_: (i, 0, 0)),
-                whole((model, rank)),
-                whole(o_down_t.shape),
-                by_quarter(q_width),
-                by_quarter(heads),
-                by_quarter(2 * q_width),
-                by_quarter(1),
-            ]
-            + [ANY] * n_pieces,
-            out_specs=[
-                by_quarter(q_width),
-                by_quarter(heads),
-                pl.BlockSpec((quarter, rank), lambda i, off, nat, before: (nat[i], 0)),
-                whole((kv_heads, 2 * head, AUG)),
-            ],
-            scratch_shapes=[held_o, sems],
-        ),
-        out_shape=[
-            jax.ShapeDtypeStruct((q_width, rows), bf16),
-            jax.ShapeDtypeStruct((heads, rows), f32),
-            jax.ShapeDtypeStruct((rows, rank), f32),
-            jax.ShapeDtypeStruct((kv_heads, 2 * head, AUG), f32),
-        ],
-        compiler_params=params(48),
-        cost_estimate=cost(2 * rows * model * q_width, 14 * MIB),
-        name="project_back",
-    )(offsets, nat, last_docs[:1], branch, output_adapter_up, o_down_t, att_t, totals, phi_q, q_doc, *o_pieces)
-
-    later_in = jnp.zeros_like(dstate)
-    factor = jnp.ones((), f32)
-    for by in range(1, seq):
-        later_in = later_in + factor * shifted(dstate, "seq", -by)
-        factor = factor * passes[jnp.minimum(here + by, seq - 1)]
+            out_shape=[jax.ShapeDtypeStruct(s, d) for s, d in sizes],
+            input_output_aliases={11 + n_pieces + i: i for i in range(3)} if late else {},
+            compiler_params=params(BIG),
+            cost_estimate=SMALL,
+            name="project_back",
+        )(
+            clock.tie(offsets), nat, last_docs[:1], output_adapter_up, o_down_t, att_t, totals, phi_q, q_doc,
+            *quarters, *o_pieces, *earlier,
+        )
+
+    near = clock.wait(*go_part(0, (branch, beside), ()))
+    (mlp_beside,) = clock.wait(mlp_beside)
+    mlp_near = clock.tie(hidden + (mlp_near1.astype(f32) + mlp_beside.astype(f32)))
+    (across,) = clock.wait(across)
+    last = clock.tie(exchange(across, "tensor", 1))
+    mlp_across = exchange(clock.tie(mlp_far), "tensor", 2)
+    branch = [branch, beside, across, last]
+    numer, grad_totals, up_product, dstate = clock.wait(*go_part(2, branch[2:], near))
+
+    coming = [shifted(dstate, "seq", -by) for by in range(1, seq)]
 
     back_column = lambda r: pl.BlockSpec((r, CHUNK), lambda c, *_: (0, chunks - 1 - c))
     back_in = (
@@ -809,13 +1058,11 @@
         (doc_row, None),
         (q_doc, back_column(1)),
         (states, pl.BlockSpec((1, kv_heads, 2 * head, AUG), lambda c, *_: (chunks - 1 - c, 0, 0, 0))),
-        (later_in, None),
         (cos_q, back_column(head // 2)),
         (sin_q, back_column(head // 2)),
         (maps_q, None),
-        (maps_k, None),
     )
-    g_q, g_kt, g_vt, g_map_q, g_map_k = pl.pallas_call(
+    g_q, g_kt, g_vt, g_phi, g_map_q = pl.pallas_call(
         lambda *refs: backward_body((kv_heads, group, head, chunks), *refs),
         grid_spec=pltpu.PrefetchScalarGridSpec(
             num_scalar_prefetch=1,
@@ -825,115 +1072,163 @@
                 pl.BlockSpec((CHUNK, q_width), lambda c, *_: (chunks - 1 - c, 0)),
                 whole((kv_width, ext)),
                 whole((kv_width, ext)),
+                whole((2 * kv_width, ext)),
                 whole((kv_heads, group * head, group * head)),
-                whole((kv_width, kv_width)),
             ],
-            scratch_shapes=[pltpu.VMEM(dstate.shape, f32), pltpu.VMEM((2 * kv_width, ext), f32)],
+            scratch_shapes=[pltpu.VMEM(dstate.shape, f32)],
         ),
         out_shape=[
             jax.ShapeDtypeStruct((rows, q_width), bf16),
             jax.ShapeDtypeStruct((kv_width, ext), f32),
             jax.ShapeDtypeStruct((kv_width, ext), f32),
+            jax.ShapeDtypeStruct((2 * kv_width, ext), f32),
             jax.ShapeDtypeStruct((kv_heads, group * head, group * head), f32),
+        ],
+        compiler_params=params(52),
+        cost_estimate=SMALL,
+        name="attend_back",
+    )(clock.tie(last_docs), *[x for x, _ in back_in])
+
+    g_q, g_kt, g_vt, g_phi, g_map_q = clock.wait(g_q, g_kt, g_vt, g_phi, g_map_q)
+    (mlp_across,) = clock.wait(mlp_across)
+    out_rows = clock.tie((mlp_near + mlp_across.astype(f32)).astype(bf16))
+    out_across, out_beside = exchange(out_rows, "tensor", 2), exchange(out_rows, "tensor", 1)
+    coming = clock.wait(*coming)
+    factors = [jnp.ones((), f32)]
+    for by in range(1, seq - 1):
+        factors.append(factors[-1] * passes[jnp.minimum(here + by, seq - 1)])
+    g_own, g_halo, g_map_k = pl.pallas_call(
+        lambda *refs: keys_back_body((kv_heads, head, chunks, rows), *refs),
+        grid_spec=pltpu.PrefetchScalarGridSpec(
+            num_scalar_prefetch=2,
+            grid=(1,),
+            in_specs=[whole(x.shape) for x in (g_kt, g_vt, g_phi, v_a, phi_kt, k_t, doc_row, maps_k, *coming)],
+            out_specs=[whole((2 * kv_width, rows)), whole((2 * kv_width, CHUNK)), whole((kv_width, kv_width))],
+        ),
+        out_shape=[
+            jax.ShapeDtypeStruct((2 * kv_width, rows), f32),
+            jax.ShapeDtypeStruct((2 * kv_width, CHUNK), f32),
             jax.ShapeDtypeStruct((kv_width, kv_width), f32),
         ],
-        compiler_params=params(52),
-        cost_estimate=cost(6 * heads * rows * 256 * 256, 12 * MIB, rows * heads * 192),
-        name="attend_back",
-    )(last_docs, *[x for x, _ in back_in])
-
-    returned = shifted(jnp.concatenate([g_kt[:, :WIN], g_vt[:, :WIN]], axis=0), "seq", -1)
-    lead = ((0, 0), (rows - WIN, 0))
-    g_k = g_kt[:, WIN : WIN + rows] + jnp.pad(returned[:kv_width], lead)
-    g_v = g_vt[:, WIN : WIN + rows] + jnp.pad(returned[kv_width:], lead)
-    g_k = rope(g_k, cos_q, -sin_q)
-    g_kv = jnp.concatenate([g_k, g_v], axis=0).astype(bf16).T
+        compiler_params=params(BIG),
+        cost_estimate=SMALL,
+        name="keys_back",
+    )(clock.tie(last_docs), jnp.stack(factors), g_kt, g_vt, g_phi, v_a, phi_kt, k_t, doc_row, maps_k, *coming)
+
+    g_own, g_halo, g_map_k = clock.wait(g_own, g_halo, g_map_k)
+    g_halo = shifted(g_halo, "seq", -1)
+    (g_halo,) = clock.wait(g_halo)
 
     downs_t = jnp.concatenate([downs.T, downs.T], axis=0)
 
-    def gn_part(which):
-        by_rows = lambda w: pl.BlockSpec((quarter, w), lambda i, off, nat: (nat[i], 0))
+    adapters_in = (g_q, g_own, g_halo, cos_q, sin_q, ups, low[WIN : WIN + rows], normed, lowered, att, up_product, g_map_q, g_map_k, *branch)
+    sizes = [
+        ((rows, 2 * kv_width), bf16),
+        ((rows, 6 * rank), bf16),
+        ((heads + kv_heads, head, 2 * head), f32),
+        ((4 * rank, model), f32),
+    ]
+    g_kv, low_back, by_head, shared = pl.pallas_call(
+        lambda *refs: adapters_body((rows, WIN, head, rank), *refs),
+        grid_spec=pltpu.PrefetchScalarGridSpec(
+            num_scalar_prefetch=1,
+            grid=(1,),
+            in_specs=[whole(x.shape) for x in adapters_in],
+            out_specs=[whole(x) for x, _ in sizes],
+        ),
+        out_shape=[jax.ShapeDtypeStruct(x, d) for x, d in sizes],
+        compiler_params=params(BIG),
+        cost_estimate=SMALL,
+        name="adapters",
+    )(clock.tie(nat), *adapters_in)
+    g_kv, low_back, by_head, shared = clock.wait(g_kv, low_back, by_head, shared)
+    out_across, out_beside = clock.wait(out_across, out_beside)
+
+    def gn_part(first):
+        by_rows = lambda w: pl.BlockSpec((quarter, w), lambda i, off, nat: (nat[first - i], 0))
         return pl.pallas_call(
             lambda *refs: gn_body(n_pieces, *refs),
             grid_spec=pltpu.PrefetchScalarGridSpec(
                 num_scalar_prefetch=2,
                 grid=(2,),
-                in_specs=[
-                    by_rows(q_width),
-                    by_rows(2 * kv_width),
-                    whole((q_width, 3 * rank)),
-                    whole((2 * kv_width, 3 * rank)),
-                    whole(downs_t.shape),
-                ]
+                in_specs=[by_rows(q_width), by_rows(2 * kv_width), by_rows(6 * rank), whole(downs_t.shape)]
                 + [ANY] * n_pieces,
-                out_specs=[
-                    pl.BlockSpec((1, quarter, model), lambda i, *_: (i, 0, 0)),
-                    pl.BlockSpec((1, quarter, 3 * rank), lambda i, *_: (i, 0, 0)),
-                ],
+                out_specs=[whole((quarter, model))] * 2,
                 scratch_shapes=[held_qkv, sems],
             ),
-            out_shape=[
-                jax.ShapeDtypeStruct((2, quarter, model), bf16),
-                jax.ShapeDtypeStruct((2, quarter, 3 * rank), f32),
-            ],
-            compiler_params=params(32),
-            cost_estimate=cost(rows * model * qkv_width, 7 * MIB),
+            out_shape=[one_quarter, one_quarter],
+            compiler_params=params(BIG),
+            cost_estimate=SMALL,
             name="norm_back",
-        )(offsets, nat[which], g_q, g_kv, ups[:q_width], ups[q_width:], downs_t, *qkv_pieces)
-
-    gn_far, ups_far = gn_part(order_far)
-    gn_near, ups_near = gn_part(order_near)
-    grad_normed = reduce_quarters(gn_far, gn_near)
+        )(clock.tie(offsets), nat, g_q, g_kv, low_back, downs_t, *qkv_pieces)
+
+    gn_far0, gn_far1 = gn_part(3)
+    (gn_far0,) = clock.wait(gn_far0)
+    beside = exchange(gn_far0, "tensor", 1)
+
+    by_head = by_head.reshape(heads + kv_heads, ring, head // ring, 2 * head).transpose(1, 0, 2, 3)
+    shared = shared.reshape(4 * rank, ring, model // ring).transpose(1, 0, 2)
+    by_head, shared = clock.wait(by_head, shared)
+
+    def halved(x, axis, half, bit, over=0):
+        x = x.reshape(x.shape[:over] + (2, half) + x.shape[over + 1 :])
+        send = lax.dynamic_index_in_dim(x, 1 - bit, over, keepdims=False)
+        return lax.dynamic_index_in_dim(x, bit, over, keepdims=False), exchange(send, axis, half)
+
+    def summed_over(axis, size, xs):
+        while size > 1:
+            half = size // 2
+            both = [halved(x, axis, half, (lax.axis_index(axis) // half) % 2) for x in xs]
+            coming = clock.wait(*[coming for _, coming in both])
+            xs = [kept + x for (kept, _), x in zip(both, coming)]
+            size = half
+            yield xs
+
+    (beside,) = clock.wait(beside)
+    gn_far = clock.tie((gn_far1.astype(f32) + beside.astype(f32)).astype(bf16))
+    across = exchange(gn_far, "tensor", 2)
+    parts = [by_head, shared]
+    dp = ring // seq
+    parts = [x.reshape((dp, seq) + x.shape[1:]) for x in parts]
+    for parts in summed_over("dp", dp, parts):
+        pass
+    along_seq = summed_over("seq", seq, [x[0] for x in parts])
+    parts = next(along_seq)
+    gn_near0, gn_near1 = gn_part(1)
+    gn_near0, gn_near1 = clock.wait(gn_near0, gn_near1)
+    across, gn_near0 = clock.wait(across, gn_near0)
+    beside = exchange(gn_near0, "tensor", 1)
+    (beside,) = clock.wait(beside)
+    grad_normed = gn_near1.astype(f32) + beside.astype(f32) + across.astype(f32)
     grad_rows = grad_hidden + rms_back(own_rows(tokens).astype(f32), gain_attn, grad_normed)
-    grad_tokens = place(gather_quarters(grad_rows.astype(bf16)), nat, f32)
-    mlp = reduce_quarters(mlp_far, mlp_near)
-    block_out = place(gather_quarters((hidden + mlp).astype(bf16)), nat, bf16)
-
-    def joined(x):
-        return x[:, : x.shape[1] // 2] + x[:, x.shape[1] // 2 :]
-
-    low_own = halves_outside(low[WIN : WIN + rows], 1)
-    g_q_up = joined(tn(g_q, low_own))[:, :rank]
-    g_kv_up = joined(tn(g_kv, low_own))
-    g_k_up = g_kv_up[:kv_width, rank : 2 * rank]
-    g_v_up = g_kv_up[kv_width:, 2 * rank :]
-    ups_rel = jnp.stack([ups_near[1], ups_near[0], ups_far[1], ups_far[0]])
-    ups_nat = jnp.zeros_like(ups_rel).at[nat].set(ups_rel).reshape(rows, 3 * rank)
-    g_downs = joined(tn(normed[WIN : WIN + rows], halves_outside(ups_nat, 1)))
-    g_o_up = joined(tn(branch.reshape(rows, model), halves_outside(lowered, 1)))
-    g_o_down = joined(tn(att, halves_outside(up_product, 1)))
-    shared = jnp.concatenate([g_downs, g_o_up], axis=1).reshape(ring, 4, model // ring // 4, 4 * rank)
-    shared = reduce_to_own(shared.transpose(1, 0, 2, 3), "tensor")
-
-    def by_rows_of_head(x, count):
-        return x.reshape(count, ring, head // ring, -1).transpose(1, 0, 2, 3)
-
-    per_head = [
-        by_rows_of_head(g_q_up, heads),
-        by_rows_of_head(g_k_up, kv_heads),
-        by_rows_of_head(g_v_up, kv_heads),
-        by_rows_of_head(g_o_down, heads),
-        by_rows_of_head(jnp.concatenate([diagonal_blocks(g_map_q[k], group) for k in range(kv_heads)]), heads),
-        by_rows_of_head(diagonal_blocks(g_map_k, kv_heads), kv_heads),
-    ]
-    parts = [shared] + per_head
-    flat = jnp.concatenate([x.reshape(ring, -1) for x in parts], axis=1)
-    flat = reduce_to_own(flat.reshape(-1, seq, flat.shape[1]), "dp")
-    flat = reduce_to_own(flat, "seq")
-    out, at = [], 0
-    for x in parts:
-        size = x.size // ring
-        out.append(flat[at : at + size].reshape(x.shape[1:]))
-        at += size
-    shared_out = out[0]
+    grad_rows = clock.tie(grad_rows.astype(bf16))
+    across, beside = exchange(grad_rows, "tensor", 2), exchange(grad_rows, "tensor", 1)
+    out_last = clock.tie(exchange(out_across, "tensor", 1))
+    for parts in along_seq:
+        pass
+    by_head, shared = [x[0] for x in parts]
+    shared = shared.reshape(4 * rank, 2, 2, model // ring // 4)
+    kept, sent = halved(shared.reshape(4 * rank, 4, -1), "tensor", 2, far, 1)
+    shared = kept.reshape(4 * rank, 2, -1)
+    sent = sent.reshape(4 * rank, 2, -1)
+    block_out = clock.tie(place([out_rows, out_beside, out_across, out_last], nat, bf16))
+    beside, across, sent = clock.wait(beside, across, sent)
+    last = exchange(across, "tensor", 1)
+    kept, sent = halved(shared + sent, "tensor", 1, core, 1)
+    last, sent = clock.wait(last, sent)
+    shared = (kept + sent).reshape(4 * rank, -1).T
+    grad_tokens = clock.tie(place([grad_rows, beside, across, last], nat, f32))
+    of_q, of_kv = by_head[:heads], by_head[heads:]
+    first, second = slice(head, head + rank), slice(head + rank, head + 2 * rank)
+    out = [of_q[..., first], of_kv[..., first], of_kv[..., second], of_q[..., second], of_q[..., :head], of_kv[..., :head]]
     return (
         block_out,
         grad_tokens,
-        shared_out[:, :rank],
-        shared_out[:, rank : 2 * rank],
-        shared_out[:, 2 * rank : 3 * rank],
-        shared_out[:, 3 * rank :],
-        *out[1:],
+        shared[:, :rank] + clock.now.astype(f32),
+        shared[:, rank : 2 * rank],
+        shared[:, 2 * rank : 3 * rank],
+        shared[:, 3 * rank :],
+        *out,
     )
 
 

time: 790 us -> 681 us (0.86)
  local copies, waits for them, and re-layouts: 121 us -> 53.2 us
  Pallas kernels: 188 us -> 214 us
  waiting for transfers between devices: 272 us -> 246 us
  starting transfers between devices: 116 us -> 96.4 us
  other arithmetic: 62.3 us -> 50.8 us
  matrix products: 12.9 us -> 3.77 us
    ppermute x29 -> x32, waiting for transfers between devices: 135 us -> 55.6 us  [exchange(): return lax.ppermute(x, axis, [(i, i ^ bit) for i in range(count)])]
    unnamed x498 -> x280, local copies, waits for them, and re-layouts: 70.8 us -> 26.7 us
    ppermute x84 -> x56, waiting for transfers between devices: 127 us -> 171 us  [step(): lane.append(lax.ppermute(lane[-1], ('dp', 'seq'), way))]
    ppermute x84 -> x56, starting transfers between devices: 82.4 us -> 59.2 us  [step(): lane.append(lax.ppermute(lane[-1], ('dp', 'seq'), way))]
    pallas_call x6 -> x8, Pallas kernels: 109 us -> 133 us  [the longest x4 100 us: ffn(): pl.pallas_call(lambda *refs: ffn_body(sizes, units, bool(sums), last, *re...]
    another operation x13 -> x4, other arithmetic: 17.3 us -> 2.19 us  [the longest x1 1.26 us: per_device(): jnp.stack(factors)]
    ppermute x8, waiting for transfers between devices: 9.4 us -> 19.9 us  [shifted(): lax.ppermute(x, axis, [(i, i + by) for i in range(count) if 0 <= i + by <...]
    optimization_barrier x0 -> x8, local copies, waits for them, and re-layouts: none -> 8.92 us  [wait(): *out, self.now = lax.optimization_barrier((*arrays, self.now))]
  transfers between devices with their start and end apart: 121 -> 96, of which waited for: 47 -> 54; matrix products, arithmetic and copies ran while one was open for 17% -> 9% of each run, Pallas kernels for 22% -> 25%
where the time goes in v2:
time: 681 us; the launch traced here: 670 us
  waiting for transfers between devices  246 us (36%)
  Pallas kernels  214 us (31%)
  starting transfers between devices  96.4 us (14%)
  local copies, waits for them, and re-layouts  53.2 us (8%)
  other arithmetic  50.8 us (7%)
    ppermute x56, waiting for transfers between devices, step(): lane.append(lax.ppermute(lane[-1], ('dp', 'seq'), way))  171 us
    pallas_call x4, Pallas kernels, ffn(): pl.pallas_call(lambda *refs: ffn_body(sizes, units, bool(sums), last, *re...  100 us
    ppermute x56, starting transfers between devices, step(): lane.append(lax.ppermute(lane[-1], ('dp', 'seq'), way))  59.2 us
    ppermute x32, waiting for transfers between devices, exchange(): return lax.ppermute(x, axis, [(i, i ^ bit) for i in range(count)])  55.6 us
    unnamed x280, local copies, waits for them, and re-layouts  26.7 us
    ppermute x8, waiting for transfers between devices, shifted(): lax.ppermute(x, axis, [(i, i + by) for i in range(count) if 0 <= i + by <...  19.9 us
    ppermute x32, starting transfers between devices, exchange(): return lax.ppermute(x, axis, [(i, i ^ bit) for i in range(count)])  19.8 us
    pallas_call x2, Pallas kernels, go_part(): pl.pallas_call(lambda *refs: go_body((n_pieces, kv_heads, group, head, la...  18.2 us
  transfers between devices with their start and end apart: 96, of which 54 were waited for; matrix products, arithmetic and copies ran while one was open for 9% of the time, Pallas kernels for 25%

profile of v2, /device:TPU:0, one launch (start us, length us, event | category | flops | bytes accessed | tf_op | source)
XLA Modules:
  0.0 670.4 jit_solution(9004191373351053335)
XLA Ops:
  80.0 5.0 collective-permute-done.27.refs_18_.refs_13_
  90.5 15.4 %prep.1 = (bf16[512,1024]{1,0:T(8,128)(2,1)}, bf16[1024,1024]{1,0:T(8,128)(2,1)}, bf16[1152,128]{1,0:T(8,128)(2,1)}, bf16[128,1152]{1,0:T(8,128)(2,1)}, bf16[115...) custom-call(s32[16]{0:T(128)} %get-tuple-element.941.refs_0_, ...), custom_call_target="tpu_custom_call" | custom-call | flops 1 | bytes 1 | tf_op jit(solution)/shard_map/prep/pallas_call | solution.py:813
  135.5 9.1 %attend.1 = (bf16[1024,512]{1,0:T(8,128)(2,1)S(1)}, f32[512,1024]{1,0:T(8,128)}, f32[8,1024]{1,0:T(8,128)S(1)}, bf16[8,2,128,80]{3,2,1,0:T(8,128)(2,1)S(1)}) custom-call(s32[9]{0:T(128)S(1)} %copy-done.22, bf16[512,1024]{1,0:T(8,128)(2,1)S(1)} %copy-done.2, bf16[1024,1024]{1,0:T(8,128)(2,1)} %get-tuple-element.600.refs_2_.refs_7_, ...), custom_call_target="tpu_custom_call" | custom-call | flops 1 | bytes 1 | tf_op jit(solution)/shard_map/attend/pallas_call | solution.py:840
  148.3 7.3 %project.2 = (bf16[256,2048]{1,0:T(8,128)(2,1)}, bf16[256,2048]{1,0:T(8,128)(2,1)}, f32[1024,8]{1,0:T(8,128)}) custom-call(s32[16]{0:T(128)} %get-tuple-element.941.refs_0_, s32[4]{0:T(128)} %pad_add_fusion.refs_1_.refs_0_.nat, bf16[1024,512]{1,0:T(8,128)(2,1)} %copy-done, bf16[512,8]{1,0:T(8,128)(2,1)} %copy.133.refs_3_, ...), custom_call_target="tpu_custom_call" | custom-call | flops 1 | bytes 1 | tf_op jit(solution)/shard_map/project/pallas_call | solution.py:882
  155.7 7.5 %project.3 = (bf16[256,2048]{1,0:T(8,128)(2,1)}, bf16[256,2048]{1,0:T(8,128)(2,1)}, f32[1024,8]{1,0:T(8,128)}) custom-call(s32[16]{0:T(128)} %get-tuple-element.941.refs_0_, s32[4]{0:T(128)} %pad_add_fusion.refs_1_.refs_0_.nat, bf16[1024,512]{1,0:T(8,128)(2,1)} %copy-done, bf16[512,8]{1,0:T(8,128)(2,1)} %copy.133.refs_3_, ...), custom_call_target="tpu_custom_call", output_to_operand_aliasing={{2}: (21, {})} | custom-call | flops 1 | bytes 1 | tf_op jit(solution)/shard_map/project/pallas_call | solution.py:882
  169.9 13.1 %collective-permute-done.42.refs_9_ = bf16[256,1152]{1,0:T(8,128)(2,1)S(1)} collective-permute-done((bf16[256,1152]{1,0:T(8,128)(2,1)}, bf16[256,1152]{1,0:T(8,128)(2,1)S(1)}, u32[]{:S(2)}, u32[]{:S(2)}) %collective-permute-start.42) | collective-permute-done | bytes 589856 | tf_op jit(solution)/shard_map/ppermute | solution.py:113
  184.6 7.0 %collective-permute-done.40 = bf16[256,2048]{1,0:T(8,128)(2,1)} collective-permute-done((bf16[256,2048]{1,0:T(8,128)(2,1)S(1)}, bf16[256,2048]{1,0:T(8,128)(2,1)}, u32[]{:S(2)}, u32[]{:S(2)}) %collective-permute-start.40) | collective-permute-done | bytes 1048608 | tf_op jit(solution)/shard_map/ppermute | solution.py:47
  199.4 11.5 %collective-permute-done.44.refs_10_ = bf16[256,1152]{1,0:T(8,128)(2,1)S(1)} collective-permute-done((bf16[256,1152]{1,0:T(8,128)(2,1)S(1)}, bf16[256,1152]{1,0:T(8,128)(2,1)S(1)}, u32[]{:S(2)}, u32[]{:S(2)}) %collective-permute-start.44) | collective-permute-done | bytes 589856 | tf_op jit(solution)/shard_map/ppermute | solution.py:113
  214.3 12.2 %collective-permute-done.47.refs_11_ = bf16[256,1152]{1,0:T(8,128)(2,1)S(1)} collective-permute-done((bf16[256,1152]{1,0:T(8,128)(2,1)S(1)}, bf16[256,1152]{1,0:T(8,128)(2,1)S(1)}, u32[]{:S(2)}, u32[]{:S(2)}) %collective-permute-start.47) | collective-permute-done | bytes 589856 | tf_op jit(solution)/shard_map/ppermute | solution.py:113
  238.2 10.7 %collective-permute-done.49.refs_12_ = bf16[256,1152]{1,0:T(8,128)(2,1)S(1)} collective-permute-done((bf16[256,1152]{1,0:T(8,128)(2,1)}, bf16[256,1152]{1,0:T(8,128)(2,1)S(1)}, u32[]{:S(2)}, u32[]{:S(2)}) %collective-permute-start.49) | collective-permute-done | bytes 589856 | tf_op jit(solution)/shard_map/ppermute | solution.py:113
  252.9 20.2 %feed_forward.4 = (f32[2,256,2048]{2,1,0:T(8,128)}, f32[2,256,2048]{2,1,0:T(8,128)}) custom-call(s32[16]{0:T(128)} %get-tuple-element.807.refs_0_, s32[4]{0:T(128)} %pad_add_fusion.refs_1_.refs_0_.nat, bf16[1024,2048]{1,0:T(8,128)(2,1)} %refs_2_.7, bf16[256,2048]{1,0:T(8,128)(2,1)} %collective-permute-done.51.refs_3_, ...), custom_call_target="tpu_custom_call" | custom-call | flops 1 | bytes 1 | tf_op jit(solution)/shard_map/feed_forward/pallas_call | solution.py:937
  278.0 20.2 %feed_forward.5 = (f32[2,256,2048]{2,1,0:T(8,128)}, f32[2,256,2048]{2,1,0:T(8,128)}) custom-call(s32[16]{0:T(128)} %get-tuple-element.807.refs_0_, s32[4]{0:T(128)} %pad_add_fusion.refs_1_.refs_0_.nat, bf16[1024,2048]{1,0:T(8,128)(2,1)} %refs_2_.7, bf16[256,2048]{1,0:T(8,128)(2,1)} %copy-done.34, bf16[256,2048]{1,0:T(8,128)(2,1)} %copy-done.29, ...), custom_call_target="tpu_custom_call" | custom-call | flops 1 | bytes 1 | tf_op jit(solution)/shard_map/feed_forward/pallas_call | solution.py:937
  301.6 19.0 %collective-permute-done.57.refs_8_ = bf16[256,1920]{1,0:T(8,128)(2,1)S(1)} collective-permute-done((bf16[256,1920]{1,0:T(8,128)(2,1)S(1)}, bf16[256,1920]{1,0:T(8,128)(2,1)S(1)}, u32[]{:S(2)}, u32[]{:S(2)}) %collective-permute-start.57) | collective-permute-done | bytes 983072 | tf_op jit(solution)/shard_map/ppermute | solution.py:113
  323.6 18.9 %collective-permute-done.59.refs_9_ = bf16[256,1920]{1,0:T(8,128)(2,1)S(1)} collective-permute-done((bf16[256,1920]{1,0:T(8,128)(2,1)S(1)}, bf16[256,1920]{1,0:T(8,128)(2,1)S(1)}, u32[]{:S(2)}, u32[]{:S(2)}) %collective-permute-start.59) | collective-permute-done | bytes 983072 | tf_op jit(solution)/shard_map/ppermute | solution.py:113
  345.5 19.0 %collective-permute-done.61.refs_10_ = bf16[256,1920]{1,0:T(8,128)(2,1)S(1)} collective-permute-done((bf16[256,1920]{1,0:T(8,128)(2,1)S(1)}, bf16[256,1920]{1,0:T(8,128)(2,1)S(1)}, u32[]{:S(2)}, u32[]{:S(2)}) %collective-permute-start.61) | collective-permute-done | bytes 983072 | tf_op jit(solution)/shard_map/ppermute | solution.py:113
  367.4 18.9 %collective-permute-done.63.refs_11_ = bf16[256,1920]{1,0:T(8,128)(2,1)S(1)} collective-permute-done((bf16[256,1920]{1,0:T(8,128)(2,1)S(1)}, bf16[256,1920]{1,0:T(8,128)(2,1)S(1)}, u32[]{:S(2)}, u32[]{:S(2)}) %collective-permute-start.63) | collective-permute-done | bytes 983072 | tf_op jit(solution)/shard_map/ppermute | solution.py:113
  389.8 15.0 %collective-permute-done.65.refs_12_ = bf16[256,1920]{1,0:T(8,128)(2,1)S(1)} collective-permute-done((bf16[256,1920]{1,0:T(8,128)(2,1)S(1)}, bf16[256,1920]{1,0:T(8,128)(2,1)S(1)}, u32[]{:S(2)}, u32[]{:S(2)}) %collective-permute-start.65) | collective-permute-done | bytes 983072 | tf_op jit(solution)/shard_map/ppermute | solution.py:113
  405.8 29.8 %feed_forward.6 = (bf16[256,2048]{1,0:T(8,128)(2,1)}, bf16[256,2048]{1,0:T(8,128)(2,1)}, bf16[256,2048]{1,0:T(8,128)(2,1)}, bf16[256,2048]{1,0:T(8,128)(2,1)}) custom-call(s32[16]{0:T(128)} %get-tuple-element.807.refs_0_, s32[4]{0:T(128)} %pad_add_fusion.refs_1_.refs_0_.nat, bf16[1024,2048]{1,0:T(8,128)(2,1)} %refs_2_.7, ...), custom_call_target="tpu_custom_call" | custom-call | flops 1 | bytes 1 | tf_op jit(solution)/shard_map/feed_forward/pallas_call | solution.py:937
  443.4 30.1 %feed_forward.7 = (bf16[256,2048]{1,0:T(8,128)(2,1)}, bf16[256,2048]{1,0:T(8,128)(2,1)}, bf16[256,2048]{1,0:T(8,128)(2,1)}, bf16[256,2048]{1,0:T(8,128)(2,1)}) custom-call(s32[16]{0:T(128)} %get-tuple-element.807.refs_0_, s32[4]{0:T(128)} %pad_add_fusion.refs_1_.refs_0_.nat, bf16[1024,2048]{1,0:T(8,128)(2,1)} %refs_2_.7, bf16[256,2048]{1,0:T(8,128)(2,1)} %copy-done.34, ...), custom_call_target="tpu_custom_call" | custom-call | flops 1 | bytes 1 | tf_op jit(solution)/shard_map/feed_forward/pallas_call | solution.py:937
  486.7 9.2 %project_back.2 = (bf16[512,1024]{1,0:T(8,128)(2,1)}, f32[8,1024]{1,0:T(8,128)}, f32[1024,8]{1,0:T(8,128)}, f32[2,128,80]{2,1,0:T(8,128)}) custom-call(s32[16]{0:T(128)} %get-tuple-element.941.refs_0_, s32[4]{0:T(128)} %pad_add_fusion.refs_1_.refs_0_.nat, s32[1]{0:T(128)} %bitcast.82, bf16[2048,8]{1,0:T(8,128)(2,1)} %copy.137.refs_3_, ...), custom_call_target="tpu_custom_call" | custom-call | flops 1 | bytes 1 | tf_op jit(solution)/shard_map/project_back/pallas_call | solution.py:996
  499.4 10.3 %collective-permute-done.72.refs_9_.refs_16_ = bf16[256,2048]{1,0:T(8,128)(2,1)} collective-permute-done((bf16[256,2048]{1,0:T(8,128)(2,1)S(1)}, bf16[256,2048]{1,0:T(8,128)(2,1)}, u32[]{:S(2)}, u32[]{:S(2)}) %collective-permute-start.72) | collective-permute-done | bytes 1048608 | tf_op jit(solution)/shard_map/ppermute | solution.py:47
  513.5 9.0 %project_back.3 = (bf16[512,1024]{1,0:T(8,128)(2,1)}, f32[8,1024]{1,0:T(8,128)}, f32[1024,8]{1,0:T(8,128)}, f32[2,128,80]{2,1,0:T(8,128)}) custom-call(s32[16]{0:T(128)} %get-tuple-element.941.refs_0_, s32[4]{0:T(128)} %pad_add_fusion.refs_1_.refs_0_.nat, s32[1]{0:T(128)} %bitcast.83, ...), custom_call_target="tpu_custom_call", output_to_operand_aliasing={{0}: (27, {}), {1}: (28, {}), {2}: (29, {})} | custom-call | flops 1 | bytes 1 | tf_op jit(solution)/shard_map/project_back/pallas_call | solution.py:996
  523.4 17.0 %attend_back.1 = (bf16[1024,512]{1,0:T(8,128)(2,1)}, f32[128,1152]{1,0:T(8,128)}, f32[128,1152]{1,0:T(8,128)}, f32[256,1152]{1,0:T(8,128)}, f32[2,256,256]{2,1,0:T(8,128)}) custom-call(s32[9]{0:T(128)S(1)} %copy-done.23, bf16[512,1024]{1,0:T(8,128)(2,1)} %get-tuple-element.599.refs_1_, bf16[1024,1024]{1,0:T(8,128)(2,1)} %get-tuple-element.600.refs_2_.refs_7_, ...), custom_call_target="tpu_custom_call" | custom-call | flops 1 | bytes 1 | tf_op jit(solution)/shard_map/attend_back/pallas_call | solution.py:1065
  551.0 8.7 %collective-permute-done.78.refs_11_ = f32[2,128,80]{2,1,0:T(8,128)S(1)} collective-permute-done((f32[2,128,80]{2,1,0:T(8,128)S(1)}, f32[2,128,80]{2,1,0:T(8,128)S(1)}, u32[]{:S(2)}, u32[]{:S(2)}) %collective-permute-start.78) | collective-permute-done | bytes 81952 | tf_op jit(solution)/shard_map/ppermute | solution.py:52
  561.0 4.7 keys_back.1
  573.5 9.4 %adapters.1 = (bf16[1024,256]{1,0:T(8,128)(2,1)}, bf16[1024,48]{1,0:T(8,128)(2,1)}, f32[10,64,128]{2,1,0:T(8,128)}, f32[32,2048]{1,0:T(8,128)}) custom-call(s32[4]{0:T(128)} %pad_add_fusion.refs_1_.refs_0_.nat, bf16[1024,512]{1,0:T(8,128)(2,1)} %get-tuple-element.905.refs_1_.refs_2_, f32[256,1024]{1,0:T(8,128)} %get-tuple-element.906.refs_2_, ...), custom_call_target="tpu_custom_call" | custom-call | flops 1 | bytes 1 | tf_op jit(solution)/shard_map/adapters/pallas_call | solution.py:1131
  582.9 8.4 %norm_back.2 = (bf16[256,2048]{1,0:T(8,128)(2,1)}, bf16[256,2048]{1,0:T(8,128)(2,1)}) custom-call(s32[16]{0:T(128)} %get-tuple-element.941.refs_0_, s32[4]{0:T(128)} %pad_add_fusion.refs_1_.refs_0_.nat, bf16[1024,512]{1,0:T(8,128)(2,1)} %get-tuple-element.905.refs_1_.refs_2_, bf16[1024,256]{1,0:T(8,128)(2,1)} %get-tuple-element.924.refs_3_, ...), custom_call_target="tpu_custom_call" | custom-call | flops 1 | bytes 1 | tf_op jit(solution)/shard_map/norm_back/pallas_call | solution.py:1149
  602.0 5.6 collective-permute-done.83
  613.2 4.7 collective-permute-done.86
  617.9 8.0 %norm_back.3 = (bf16[256,2048]{1,0:T(8,128)(2,1)}, bf16[256,2048]{1,0:T(8,128)(2,1)}) custom-call(s32[16]{0:T(128)} %get-tuple-element.941.refs_0_, s32[4]{0:T(128)} %pad_add_fusion.refs_1_.refs_0_.nat, bf16[1024,512]{1,0:T(8,128)(2,1)} %get-tuple-element.905.refs_1_.refs_2_, bf16[1024,256]{1,0:T(8,128)(2,1)} %get-tuple-element.924.refs_3_, ...), custom_call_target="tpu_custom_call" | custom-call | flops 1 | bytes 1 | tf_op jit(solution)/shard_map/norm_back/pallas_call | solution.py:1149
  648.6 12.7 %collective-permute-done.93 = f32[32,2,64]{2,0,1:T(8,128)S(1)} collective-permute-done((f32[32,2,64]{2,0,1:T(8,128)S(1)}, f32[32,2,64]{2,0,1:T(8,128)S(1)}, u32[]{:S(2)}, u32[]{:S(2)}) %collective-permute-start.93) | collective-permute-done | bytes 16416 | tf_op jit(solution)/shard_map/ppermute | solution.py:47
  664.2 5.1 place.3
  (600 shorter events, 261.7 us)
Async XLA Ops:
  3.6 19.1 %collective-permute-start.2 = (bf16[128,768]{1,0:T(8,128)(2,1)S(1)}, bf16[128,768]{1,0:T(8,128)(2,1)S(1)}, u32[]{:S(2)}, u32[]{:S(2)}) collective-permute-start(bf16[128,768]{1,0:T(8,128)(2,1)S(1)} %get-tuple-element.520.refs_11_.refs_6_), channel_id=1, source_target_pairs={{0,4},{4,8},{8,12},{12,28},{28,24},{24,20},{20,16},{16,0},{1,5},{5... | collective-permute-start | bytes 589832 | tf_op jit(solution)/shard_map/ppermute | solution.py:113
  87.1 18.9 %collective-permute-start.33 = (bf16[256,1152]{1,0:T(8,128)(2,1)S(1)}, bf16[256,1152]{1,0:T(8,128)(2,1)S(1)}, u32[]{:S(2)}, u32[]{:S(2)}) collective-permute-start(bf16[256,1152]{1,0:T(8,128)(2,1)S(1)} %pad_maximum_fusion.3.refs_5_), channel_id=1, source_target_pairs={{0,4},{4,8},{8,12},{12,28},{28,24},{24,20},{20,16},{16,0},{1,5},{5... | collective-permute-start | bytes 1769480 | tf_op jit(solution)/shard_map/ppermute | solution.py:113
  106.0 19.3 %collective-permute-start.35 = (bf16[256,1152]{1,0:T(8,128)(2,1)S(1)}, bf16[256,1152]{1,0:T(8,128)(2,1)S(1)}, u32[]{:S(2)}, u32[]{:S(2)}) collective-permute-start(bf16[256,1152]{1,0:T(8,128)(2,1)S(1)} %collective-permute-done.33.refs_6_), channel_id=1, source_target_pairs={{0,4},{4,8},{8,12},{12,28},{28,24},{24,20},{20,16},{16,0},{1,5},{5... | collective-permute-start | bytes 1769480 | tf_op jit(solution)/shard_map/ppermute | solution.py:113
  106.9 18.3 %collective-permute-start.34 = (bf16[256,1152]{1,0:T(8,128)(2,1)S(1)}, bf16[256,1152]{1,0:T(8,128)(2,1)}, u32[]{:S(2)}, u32[]{:S(2)}) collective-permute-start(bf16[256,1152]{1,0:T(8,128)(2,1)S(1)} %collective-permute-done.32.refs_14_), channel_id=1, source_target_pairs={{4,0},{8,4},{12,8},{28,12},{24,28},{20,24},{16,20},{0,16},{5,1},{9... | collective-permute-start | bytes 1769480 | tf_op jit(solution)/shard_map/ppermute | solution.py:113
  125.3 30.3 %collective-permute-start.37 = (bf16[256,1152]{1,0:T(8,128)(2,1)S(1)}, bf16[256,1152]{1,0:T(8,128)(2,1)}, u32[]{:S(2)}, u32[]{:S(2)}) collective-permute-start(bf16[256,1152]{1,0:T(8,128)(2,1)S(1)} %collective-permute-done.35.refs_7_), channel_id=1, source_target_pairs={{0,4},{4,8},{8,12},{12,28},{28,24},{24,20},{20,16},{16,0},{1,5},{5... | collective-permute-start | bytes 1769480 | tf_op jit(solution)/shard_map/ppermute | solution.py:113
  125.7 30.0 %collective-permute-start.36 = (bf16[256,1152]{1,0:T(8,128)(2,1)}, bf16[256,1152]{1,0:T(8,128)(2,1)}, u32[]{:S(2)}, u32[]{:S(2)}) collective-permute-start(bf16[256,1152]{1,0:T(8,128)(2,1)} %collective-permute-done.34.refs_15_), channel_id=1, source_target_pairs={{4,0},{8,4},{12,8},{28,12},{24,28},{20,24},{16,20},{0,16},{5,1},{9... | collective-permute-start | bytes 1769480 | tf_op jit(solution)/shard_map/ppermute | solution.py:113
  127.6 19.4 %collective-permute-start.25 = (bf16[128,512]{1,0:T(8,128)(2,1)S(1)}, bf16[128,512]{1,0:T(8,128)(2,1)S(1)}, u32[]{:S(2)}, u32[]{:S(2)}) collective-permute-start(bf16[128,512]{1,0:T(8,128)(2,1)S(1)} %collective-permute-done.21.refs_11_.refs_17_), channel_id=1, source_target_pairs={{0,4},{4,8},{8,12},{12,28},{28,24},{24,20},{20,16},{16,0},{1,5},{5... | collective-permute-start | bytes 393224 | tf_op jit(solution)/shard_map/ppermute | solution.py:113
  128.6 18.4 %collective-permute-start.26 = (bf16[128,512]{1,0:T(8,128)(2,1)S(1)}, bf16[128,512]{1,0:T(8,128)(2,1)S(1)}, u32[]{:S(2)}, u32[]{:S(2)}) collective-permute-start(bf16[128,512]{1,0:T(8,128)(2,1)S(1)} %collective-permute-done.22.refs_19_.refs_25_), channel_id=1, source_target_pairs={{4,0},{8,4},{12,8},{28,12},{24,28},{20,24},{16,20},{0,16},{5,1},{9... | collective-permute-start | bytes 393224 | tf_op jit(solution)/shard_map/ppermute | solution.py:113
  166.2 25.4 %collective-permute-start.40 = (bf16[256,2048]{1,0:T(8,128)(2,1)S(1)}, bf16[256,2048]{1,0:T(8,128)(2,1)}, u32[]{:S(2)}, u32[]{:S(2)}) collective-permute-start(bf16[256,2048]{1,0:T(8,128)(2,1)S(1)} %add_convert_fusion.4), channel_id=1, source_target_pairs={{0,2},{1,3},{2,0},{3,1},{4,6},{5,7},{6,4},{7,5},{8,10},{9,11},{10,... | collective-permute-start | bytes 3145736 | tf_op jit(solution)/shard_map/ppermute | solution.py:47
  197.9 30.3 %collective-permute-start.50 = (bf16[256,2048]{1,0:T(8,128)(2,1)S(1)}, bf16[256,2048]{1,0:T(8,128)(2,1)}, u32[]{:S(2)}, u32[]{:S(2)}) collective-permute-start(bf16[256,2048]{1,0:T(8,128)(2,1)S(1)} %multiply_convert_fusion.refs_4_), channel_id=1, source_target_pairs={{0,2},{1,3},{2,0},{3,1},{4,6},{5,7},{6,4},{7,5},{8,10},{9,11},{10,... | collective-permute-start | bytes 3145736 | tf_op jit(solution)/shard_map/ppermute | solution.py:47
  250.9 23.2 %collective-permute-start.53 = (bf16[256,1920]{1,0:T(8,128)(2,1)S(1)}, bf16[256,1920]{1,0:T(8,128)(2,1)}, u32[]{:S(2)}, u32[]{:S(2)}) collective-permute-start(bf16[256,1920]{1,0:T(8,128)(2,1)S(1)} %pad_maximum_fusion.1.refs_5_), channel_id=1, source_target_pairs={{0,4},{4,8},{8,12},{12,28},{28,24},{24,20},{20,16},{16,0},{1,5},{5... | collective-permute-start | bytes 2949128 | tf_op jit(solution)/shard_map/ppermute | solution.py:113
  252.6 23.1 %collective-permute-start.52 = (bf16[256,1920]{1,0:T(8,128)(2,1)}, bf16[256,1920]{1,0:T(8,128)(2,1)}, u32[]{:S(2)}, u32[]{:S(2)}) collective-permute-start(bf16[256,1920]{1,0:T(8,128)(2,1)} %pad_maximum_fusion.refs_13_), channel_id=1, source_target_pairs={{4,0},{8,4},{12,8},{28,12},{24,28},{20,24},{16,20},{0,16},{5,1},{9... | collective-permute-start | bytes 2949128 | tf_op jit(solution)/shard_map/ppermute | solution.py:113
  275.7 22.5 %collective-permute-start.55 = (bf16[256,1920]{1,0:T(8,128)(2,1)}, bf16[256,1920]{1,0:T(8,128)(2,1)S(1)}, u32[]{:S(2)}, u32[]{:S(2)}) collective-permute-start(bf16[256,1920]{1,0:T(8,128)(2,1)} %collective-permute-done.53.refs_6_), channel_id=1, source_target_pairs={{0,4},{4,8},{8,12},{12,28},{28,24},{24,20},{20,16},{16,0},{1,5},{5... | collective-permute-start | bytes 2949128 | tf_op jit(solution)/shard_map/ppermute | solution.py:113
  277.2 22.4 %collective-permute-start.54 = (bf16[256,1920]{1,0:T(8,128)(2,1)}, bf16[256,1920]{1,0:T(8,128)(2,1)}, u32[]{:S(2)}, u32[]{:S(2)}) collective-permute-start(bf16[256,1920]{1,0:T(8,128)(2,1)} %collective-permute-done.52.refs_14_), channel_id=1, source_target_pairs={{4,0},{8,4},{12,8},{28,12},{24,28},{20,24},{16,20},{0,16},{5,1},{9... | collective-permute-start | bytes 2949128 | tf_op jit(solution)/shard_map/ppermute | solution.py:113
  299.6 21.0 %collective-permute-start.57 = (bf16[256,1920]{1,0:T(8,128)(2,1)S(1)}, bf16[256,1920]{1,0:T(8,128)(2,1)S(1)}, u32[]{:S(2)}, u32[]{:S(2)}) collective-permute-start(bf16[256,1920]{1,0:T(8,128)(2,1)S(1)} %collective-permute-done.55.refs_7_), channel_id=1, source_target_pairs={{0,4},{4,8},{8,12},{12,28},{28,24},{24,20},{20,16},{16,0},{1,5},{5... | collective-permute-start | bytes 2949128 | tf_op jit(solution)/shard_map/ppermute | solution.py:113
  300.3 21.1 %collective-permute-start.56 = (bf16[256,1920]{1,0:T(8,128)(2,1)}, bf16[256,1920]{1,0:T(8,128)(2,1)S(1)}, u32[]{:S(2)}, u32[]{:S(2)}) collective-permute-start(bf16[256,1920]{1,0:T(8,128)(2,1)} %collective-permute-done.54.refs_15_), channel_id=1, source_target_pairs={{4,0},{8,4},{12,8},{28,12},{24,28},{20,24},{16,20},{0,16},{5,1},{9... | collective-permute-start | bytes 2949128 | tf_op jit(solution)/shard_map/ppermute | solution.py:113
  321.6 20.9 %collective-permute-start.59 = (bf16[256,1920]{1,0:T(8,128)(2,1)S(1)}, bf16[256,1920]{1,0:T(8,128)(2,1)S(1)}, u32[]{:S(2)}, u32[]{:S(2)}) collective-permute-start(bf16[256,1920]{1,0:T(8,128)(2,1)S(1)} %collective-permute-done.57.refs_8_), channel_id=1, source_target_pairs={{0,4},{4,8},{8,12},{12,28},{28,24},{24,20},{20,16},{16,0},{1,5},{5... | collective-permute-start | bytes 2949128 | tf_op jit(solution)/shard_map/ppermute | solution.py:113
  322.4 20.9 %collective-permute-start.58 = (bf16[256,1920]{1,0:T(8,128)(2,1)S(1)}, bf16[256,1920]{1,0:T(8,128)(2,1)S(1)}, u32[]{:S(2)}, u32[]{:S(2)}) collective-permute-start(bf16[256,1920]{1,0:T(8,128)(2,1)S(1)} %collective-permute-done.56.refs_16_), channel_id=1, source_target_pairs={{4,0},{8,4},{12,8},{28,12},{24,28},{20,24},{16,20},{0,16},{5,1},{9... | collective-permute-start | bytes 2949128 | tf_op jit(solution)/shard_map/ppermute | solution.py:113
  343.5 21.0 %collective-permute-start.61 = (bf16[256,1920]{1,0:T(8,128)(2,1)S(1)}, bf16[256,1920]{1,0:T(8,128)(2,1)S(1)}, u32[]{:S(2)}, u32[]{:S(2)}) collective-permute-start(bf16[256,1920]{1,0:T(8,128)(2,1)S(1)} %collective-permute-done.59.refs_9_), channel_id=1, source_target_pairs={{0,4},{4,8},{8,12},{12,28},{28,24},{24,20},{20,16},{16,0},{1,5},{5... | collective-permute-start | bytes 2949128 | tf_op jit(solution)/shard_map/ppermute | solution.py:113
  344.3 20.9 %collective-permute-start.60 = (bf16[256,1920]{1,0:T(8,128)(2,1)S(1)}, bf16[256,1920]{1,0:T(8,128)(2,1)S(1)}, u32[]{:S(2)}, u32[]{:S(2)}) collective-permute-start(bf16[256,1920]{1,0:T(8,128)(2,1)S(1)} %collective-permute-done.58.refs_17_), channel_id=1, source_target_pairs={{4,0},{8,4},{12,8},{28,12},{24,28},{20,24},{16,20},{0,16},{5,1},{9... | collective-permute-start | bytes 2949128 | tf_op jit(solution)/shard_map/ppermute | solution.py:113
  365.4 20.9 %collective-permute-start.63 = (bf16[256,1920]{1,0:T(8,128)(2,1)S(1)}, bf16[256,1920]{1,0:T(8,128)(2,1)S(1)}, u32[]{:S(2)}, u32[]{:S(2)}) collective-permute-start(bf16[256,1920]{1,0:T(8,128)(2,1)S(1)} %collective-permute-done.61.refs_10_), channel_id=1, source_target_pairs={{0,4},{4,8},{8,12},{12,28},{28,24},{24,20},{20,16},{16,0},{1,5},{5... | collective-permute-start | bytes 2949128 | tf_op jit(solution)/shard_map/ppermute | solution.py:113
  366.2 20.4 %collective-permute-start.62 = (bf16[256,1920]{1,0:T(8,128)(2,1)S(1)}, bf16[256,1920]{1,0:T(8,128)(2,1)S(1)}, u32[]{:S(2)}, u32[]{:S(2)}) collective-permute-start(bf16[256,1920]{1,0:T(8,128)(2,1)S(1)} %collective-permute-done.60.refs_18_), channel_id=1, source_target_pairs={{4,0},{8,4},{12,8},{28,12},{24,28},{20,24},{16,20},{0,16},{5,1},{9... | collective-permute-start | bytes 2949128 | tf_op jit(solution)/shard_map/ppermute | solution.py:113
  435.7 37.7 %collective-permute-start.68 = (bf16[256,2048]{1,0:T(8,128)(2,1)}, bf16[256,2048]{1,0:T(8,128)(2,1)}, u32[]{:S(2)}, u32[]{:S(2)}) collective-permute-start(bf16[256,2048]{1,0:T(8,128)(2,1)} %get-tuple-element.821), channel_id=1, source_target_pairs={{0,1},{1,0},{2,3},{3,2},{4,5},{5,4},{6,7},{7,6},{8,9},{9,8},{10,11... | collective-permute-start | bytes 3145736 | tf_op jit(solution)/shard_map/ppermute | solution.py:47
  441.9 34.6 %collective-permute-start.67 = (bf16[256,2048]{1,0:T(8,128)(2,1)}, bf16[256,2048]{1,0:T(8,128)(2,1)S(1)}, u32[]{:S(2)}, u32[]{:S(2)}) collective-permute-start(bf16[256,2048]{1,0:T(8,128)(2,1)} %add_convert_fusion.3), channel_id=1, source_target_pairs={{0,2},{1,3},{2,0},{3,1},{4,6},{5,7},{6,4},{7,5},{8,10},{9,11},{10,... | collective-permute-start | bytes 3145736 | tf_op jit(solution)/shard_map/ppermute | solution.py:47
  484.3 25.3 %collective-permute-start.72 = (bf16[256,2048]{1,0:T(8,128)(2,1)S(1)}, bf16[256,2048]{1,0:T(8,128)(2,1)}, u32[]{:S(2)}, u32[]{:S(2)}) collective-permute-start(bf16[256,2048]{1,0:T(8,128)(2,1)S(1)} %convert_element_type.198.refs_9_.refs_14_), channel_id=1, source_target_pairs={{0,2},{1,3},{2,0},{3,1},{4,6},{5,7},{6,4},{7,5},{8,10},{9,11},{10,... | collective-permute-start | bytes 3145736 | tf_op jit(solution)/shard_map/ppermute | solution.py:47
  512.5 27.8 %collective-permute-start.74 = (bf16[256,2048]{1,0:T(8,128)(2,1)}, bf16[256,2048]{1,0:T(8,128)(2,1)S(1)}, u32[]{:S(2)}, u32[]{:S(2)}) collective-permute-start(bf16[256,2048]{1,0:T(8,128)(2,1)} %add_convert_fusion.2), channel_id=1, source_target_pairs={{0,2},{1,3},{2,0},{3,1},{4,6},{5,7},{6,4},{7,5},{8,10},{9,11},{10,... | collective-permute-start | bytes 3145736 | tf_op jit(solution)/shard_map/ppermute | solution.py:47
  540.7 42.2 %collective-permute-start.75 = (bf16[256,2048]{1,0:T(8,128)(2,1)S(1)}, bf16[256,2048]{1,0:T(8,128)(2,1)S(1)}, u32[]{:S(2)}, u32[]{:S(2)}) collective-permute-start(bf16[256,2048]{1,0:T(8,128)(2,1)S(1)} %add_convert_fusion.1.refs_0_), channel_id=1, source_target_pairs={{0,2},{1,3},{2,0},{3,1},{4,6},{5,7},{6,4},{7,5},{8,10},{9,11},{10,... | collective-permute-start | bytes 3145736 | tf_op jit(solution)/shard_map/ppermute | solution.py:47
  541.8 41.1 %collective-permute-start.76 = (bf16[256,2048]{1,0:T(8,128)(2,1)S(1)}, bf16[256,2048]{1,0:T(8,128)(2,1)S(1)}, u32[]{:S(2)}, u32[]{:S(2)}) collective-permute-start(bf16[256,2048]{1,0:T(8,128)(2,1)S(1)} %add_convert_fusion.1.refs_0_), channel_id=1, source_target_pairs={{0,1},{1,0},{2,3},{3,2},{4,5},{5,4},{6,7},{7,6},{8,9},{9,8},{10,11... | collective-permute-start | bytes 3145736 | tf_op jit(solution)/shard_map/ppermute | solution.py:47
  596.9 29.0 %collective-permute-start.87 = (bf16[256,2048]{1,0:T(8,128)(2,1)}, bf16[256,2048]{1,0:T(8,128)(2,1)S(1)}, u32[]{:S(2)}, u32[]{:S(2)}) collective-permute-start(bf16[256,2048]{1,0:T(8,128)(2,1)} %add_convert_fusion), channel_id=1, source_target_pairs={{0,2},{1,3},{2,0},{3,1},{4,6},{5,7},{6,4},{7,5},{8,10},{9,11},{10,... | collective-permute-start | bytes 3145736 | tf_op jit(solution)/shard_map/ppermute | solution.py:47
  635.0 26.3 %collective-permute-start.91 = (bf16[256,2048]{1,0:T(8,128)(2,1)S(1)}, bf16[256,2048]{1,0:T(8,128)(2,1)}, u32[]{:S(2)}, u32[]{:S(2)}) collective-permute-start(bf16[256,2048]{1,0:T(8,128)(2,1)S(1)} %fusion.9.refs_0_), channel_id=1, source_target_pairs={{0,1},{1,0},{2,3},{3,2},{4,5},{5,4},{6,7},{7,6},{8,9},{9,8},{10,11... | collective-permute-start | bytes 3145736 | tf_op jit(solution)/shard_map/ppermute | solution.py:47
  635.2 26.1 %collective-permute-start.92 = (bf16[256,2048]{1,0:T(8,128)(2,1)S(1)}, bf16[256,2048]{1,0:T(8,128)(2,1)}, u32[]{:S(2)}, u32[]{:S(2)}) collective-permute-start(bf16[256,2048]{1,0:T(8,128)(2,1)S(1)} %fusion.9.refs_0_), channel_id=1, source_target_pairs={{0,2},{1,3},{2,0},{3,1},{4,6},{5,7},{6,4},{7,5},{8,10},{9,11},{10,... | collective-permute-start | bytes 3145736 | tf_op jit(solution)/shard_map/ppermute | solution.py:47
  641.9 19.4 %collective-permute-start.93 = (f32[32,2,64]{2,0,1:T(8,128)S(1)}, f32[32,2,64]{2,0,1:T(8,128)S(1)}, u32[]{:S(2)}, u32[]{:S(2)}) collective-permute-start(f32[32,2,64]{2,0,1:T(8,128)S(1)} %bitcast.106), channel_id=1, source_target_pairs={{0,2},{1,3},{2,0},{3,1},{4,6},{5,7},{6,4},{7,5},{8,10},{9,11},{10,... | collective-permute-start | bytes 49160 | tf_op jit(solution)/shard_map/ppermute | solution.py:47
  (206 other events, 2365.4 us)

commit v3 on v2

--- a/solution.py
+++ b/solution.py
@@ -11,7 +11,7 @@
 CHUNK = 128
 AUG = 80
 RING = 8
-FFN_UNITS = ((384, 384), (640, 640))
+FFN_UNITS = ((512, 512), (512, 512))
 BIG = 60
 
 epsilon = 1e-05
@@ -35,11 +35,6 @@
 def halves(x, axis):
     high = x.astype(bf16)
     return jnp.concatenate([high, (x - high.astype(f32)).astype(bf16)], axis=axis)
-
-
-def halves_outside(x, axis):
-    high = lax.reduce_precision(x, 8, 7)
-    return jnp.concatenate([high, x - high], axis=axis).astype(bf16)
 
 
 def exchange(x, axis, bit):
@@ -117,10 +112,10 @@
         return [piece for lane in self.lanes for piece in lane]
 
 
-def load_pieces(pieces, offsets, held, sems):
+def load_pieces(pieces, offsets, held, sems, first=0):
     copies = [
         pltpu.make_async_copy(
-            piece,
+            piece.at[:, pl.ds(first, held.shape[1])],
             held.at[pl.ds(pl.multiple_of(offsets[i], 16), piece.shape[0])],
             sems.at[i],
         )
@@ -180,7 +175,59 @@
     return jnp.concatenate(out, axis=0).astype(bf16)
 
 
-def prep_body(dims, offsets, last_docs, nx, low_up, cos_q, sin_q, cos_k, sin_k, map_q, map_k, doc_row, *rest):
+def norm_body(tokens, halo, gain, downs, normed, low, held, sems):
+    rows, window = tokens.shape[0], halo.shape[0]
+    part = rows // 4
+
+    def copy(i):
+        return pltpu.make_async_copy(
+            tokens.at[pl.ds(i * part, part)], held.at[pl.ds(window + i * part, part)], sems.at[i]
+        )
+
+    for i in range(4):
+        copy(i).start()
+    held[:window, :] = halo[...]
+    held[window + rows :, :] = jnp.zeros((held.shape[0] - window - rows, held.shape[1]), bf16)
+    for i in range(4):
+        copy(i).wait()
+        first = window + i * part if i else 0
+        last = window + (i + 1) * part if i < 3 else held.shape[0]
+        x = held[first:last, :].astype(f32)
+        out = (x * rms_factor(x) * gain[...]).astype(bf16)
+        normed[first:last, :] = out
+        low[first:last, :] = nn(out, downs[...])
+
+
+def pack_body(units, gate, up, down, q_up, k_up, v_up, map_q, map_k, *outs):
+    packed, (ups, twice, maps_q, maps_k) = outs[:-4], outs[-4:]
+    at = 0
+    for size, out in zip(units, packed):
+        out[:, :size] = gate[:, at : at + size]
+        out[:, size : 2 * size] = up[:, at : at + size]
+        out[:, 2 * size :] = down[at : at + size, :].T
+        at += size
+    head, rank = q_up.shape[1:]
+    at = 0
+    for i, x in enumerate((q_up, k_up, v_up)):
+        for h in range(x.shape[0]):
+            row = jnp.concatenate(
+                [jnp.zeros((head, rank), bf16)] * i + [x[h]] + [jnp.zeros((head, rank), bf16)] * (2 - i), axis=1
+            )
+            ups[at : at + head, :] = row
+            twice[at : at + head, :] = jnp.concatenate([row, row], axis=1)
+            at += head
+    maps_q[...] = jnp.zeros(maps_q.shape, bf16)
+    maps_k[...] = jnp.zeros(maps_k.shape, bf16)
+    group = map_q.shape[0] // maps_q.shape[0]
+    for h in range(map_q.shape[0]):
+        mine = slice(h % group * head, (h % group + 1) * head)
+        maps_q[h // group, mine, mine] = map_q[h].astype(f32).T.astype(bf16)
+    for h in range(map_k.shape[0]):
+        mine = slice(h * head, (h + 1) * head)
+        maps_k[mine, mine] = map_k[h].astype(f32).T.astype(bf16)
+
+
+def prep_body(dims, offsets, last_docs, nx, low, ups, cos_q, sin_q, cos_k, sin_k, map_q, map_k, doc_row, *rest):
     tokens, ext, q_width, kv_width, head, n_pieces, chunks = dims
     pieces, rest = rest[:n_pieces], rest[n_pieces:]
     q_t, phi_q, k_n, k_t, v_n, v_a, phi_kn, phi_kt, contrib, held, sems = rest
@@ -190,7 +237,7 @@
     v_a[...] = jnp.zeros(v_a.shape, bf16)
     for at in range(0, ext, step):
         rows = pl.ds(at, step)
-        raw = nn(nx[rows, :], held[:, q_width:]) + low_up[rows, q_width:]
+        raw = nn(nx[rows, :], held[:, q_width:]) + nt(halves(low[rows, :], 1), ups[q_width:, :])
         v = raw[:, kv_width:].astype(bf16)
         v_n[rows, :] = v
         v_tr = raw[:, kv_width:].T.astype(bf16)
@@ -215,7 +262,7 @@
     for at in range(0, tokens, step):
         rows = pl.ds(at, step)
         raw = nn(nx[pl.ds(WIN + at, step), :], held[:, :q_width])
-        raw = raw + low_up[pl.ds(WIN + at, step), :q_width]
+        raw = raw + nt(halves(low[pl.ds(WIN + at, step), :], 1), ups[:q_width, :])
         q_bf = rope(raw.T, cos_q[:, rows], sin_q[:, rows]).astype(bf16)
         q_t[:, rows] = q_bf
         for k in range(kv_heads):
@@ -246,14 +293,18 @@
     return weights_win, jnp.concatenate([weights_win[:CHUNK] + linear, weights_win[CHUNK:]], axis=0)
 
 
-def forward_body(dims, last_docs, q_t, phi_q, k_n, v_a, phi_kn, doc_col, doc_row, q_doc, state_in, att, att_t, totals, states, state):
+def forward_body(dims, last_docs, factors, q_t, phi_q, k_n, v_a, phi_kn, doc_col, doc_row, q_doc, *rest):
     kv_heads, group, head = dims
+    earlier, (att, att_t, totals, states, state) = rest[:-5], rest[-5:]
     chunk = pl.program_id(0)
     start = pl.multiple_of(chunk * CHUNK, CHUNK)
 
     @pl.when(chunk == 0)
     def _():
-        state[...] = state_in[...]
+        total = jnp.zeros(state.shape, f32)
+        for i, x in enumerate(earlier):
+            total = total + factors[i] * x[...]
+        state[...] = total
 
     keys = CHUNK + WIN
     win, lin = masks(q_doc[...], doc_col[pl.ds(start, keys), :], group)
@@ -293,18 +344,17 @@
             out[...] = value.astype(out.dtype)
 
 
-def o_body(n_pieces, offsets, nat, att, down, up, *rest):
-    pieces = rest[:n_pieces]
-    part0, part1, lowered, held, sems = rest[-5:]
+def o_body(n_pieces, first, offsets, nat, att, down, up, *rest):
+    pieces, parts, (lowered, held, sems) = rest[:n_pieces], rest[n_pieces:-3], rest[-3:]
     step = pl.program_id(0)
 
     @pl.when(step == 0)
     def _():
-        load_pieces(pieces, offsets, held, sems)
+        load_pieces(pieces, offsets, held, sems, first)
 
     low = nn(att[...], down[...])
     lowered[...] = low
-    store_at(step, nt(att[...], held[...]) + nn(halves(low, 1), up[...]), (part0, part1))
+    store_at(step, nt(att[...], held[...]) + nn(halves(low, 1), up[...]), parts)
 
 
 def quarter_copies(quarters, held, sems, first=0):
@@ -414,7 +464,7 @@
 
 
 def go_body(dims, offsets, nat, before_doc, o_up, o_down, att_t, totals, phi_q, q_doc, *rest):
-    n_pieces, kv_heads, group, head, later = dims
+    n_pieces, first, kv_heads, group, head, later = dims
     quarters, pieces, rest = rest[:2], rest[2 : 2 + n_pieces], rest[2 + n_pieces :]
     earlier, rest = rest[: 4 * later], rest[4 * later :]
     numer, grad_totals, up_product, dstate, rows_held, rows_sems, held, sems = rest
@@ -424,7 +474,7 @@
     def _():
         for copy in quarter_copies(quarters, rows_held, rows_sems):
             copy.start()
-        load_pieces(pieces, offsets, held, sems)
+        load_pieces(pieces, offsets, held, sems, first)
         dstate[...] = earlier[3][...] if later else jnp.zeros(dstate.shape, f32)
 
     branch = quarter_of(step, quarters, rows_held, rows_sems)
@@ -554,17 +604,12 @@
     dims, nat, g_q, g_own, g_halo, cos, sin, ups, low, normed, lowered, att, up_product, g_map_q, g_map_k, *rest
 ):
     rows, window, head, rank = dims
-    branch, (g_kv, low_back, by_head, shared) = rest[:4], rest[4:]
+    branch, (by_head, shared) = rest[:4], rest[4:]
     half = g_own.shape[0] // 2
-    wide = rows - g_halo.shape[1]
-    k = jnp.concatenate([g_own[:half, :wide], g_own[:half, wide:] + g_halo[:half]], axis=1)
-    v = jnp.concatenate([g_own[half:, :wide], g_own[half:, wide:] + g_halo[half:]], axis=1)
-    kv = jnp.concatenate([rope(k, cos[...], -sin[...]), v], axis=0).T.astype(bf16)
-    g_kv[...] = kv
+    kv = keys_values(g_own[...], g_halo[...], cos[...], sin[...], 1.0)
     q_width = g_q.shape[1]
     up = nn(g_q[...], ups[:q_width]) + nn(kv, ups[q_width:])
     up_halves = halves(up, 1)
-    low_back[...] = up_halves
 
     def joined(x, axis):
         one, other = jnp.split(x, 2, axis=axis)
@@ -595,7 +640,13 @@
     shared[3 * rank :, :] = joined(o_up, 0)
 
 
-def gn_body(n_pieces, offsets, nat, g_q, g_kv, low_back, downs, *rest):
+def keys_values(own, halo, cos, sin, last):
+    half, wide = own.shape[0] // 2, own.shape[1] - halo.shape[1]
+    total = jnp.concatenate([own[:, :wide], own[:, wide:] + halo * last], axis=1)
+    return jnp.concatenate([rope(total[:half], cos, -sin), total[half:]], axis=0).T.astype(bf16)
+
+
+def gn_body(n_pieces, offsets, nat, g_q, g_own, g_halo, cos, sin, ups, downs, *rest):
     pieces = rest[:n_pieces]
     part0, part1, held, sems = rest[n_pieces:]
     step = pl.program_id(0)
@@ -605,38 +656,10 @@
         load_pieces(pieces, offsets, held, sems)
 
     q_width = g_q.shape[1]
-    total = nt(g_q[...], held[:, :q_width]) + nt(g_kv[...], held[:, q_width:])
-    store_at(step, total + nn(low_back[...], downs[...]), (part0, part1))
-
-
-def place_body(nat, *refs):
-    quarters, (out, held, sems) = refs[:4], refs[4:]
-    step = pl.program_id(0)
-
-    @pl.when(step == 0)
-    def _():
-        for copy in quarter_copies(quarters, held, sems):
-            copy.start()
-
-    out[...] = quarter_of(step, quarters, held, sems).astype(out.dtype)
-
-
-def place(quarters, nat, dtype):
-    rows, width = quarters[0].shape
-    return pl.pallas_call(
-        place_body,
-        grid_spec=pltpu.PrefetchScalarGridSpec(
-            num_scalar_prefetch=1,
-            grid=(4,),
-            in_specs=[ANY] * 4,
-            out_specs=pl.BlockSpec((rows, width), lambda i, nat: (nat[i], 0)),
-            scratch_shapes=[pltpu.VMEM((4, rows, width), bf16), pltpu.SemaphoreType.DMA((4,))],
-        ),
-        out_shape=jax.ShapeDtypeStruct((4 * rows, width), dtype),
-        compiler_params=params(32),
-        cost_estimate=SMALL,
-        name="place",
-    )(nat, *quarters)
+    kv = keys_values(g_own[...], g_halo[...], cos[...], sin[...], (nat[4 + step] == 3).astype(f32))
+    up = nn(g_q[...], ups[:q_width]) + nn(kv, ups[q_width:])
+    total = nt(g_q[...], held[:, :q_width]) + nt(kv, held[:, q_width:])
+    store_at(step, total + nn(halves(up, 1), downs[...]), (part0, part1))
 
 
 def rms_factor(x):
@@ -650,15 +673,74 @@
     return factor * (scaled - unit * jnp.mean(unit * scaled, axis=-1, keepdims=True))
 
 
-def block_diagonal(blocks):
-    count, rows, cols = blocks.shape
-    eye = jnp.eye(count, dtype=blocks.dtype)
-    return (blocks[:, :, None, :] * eye[:, None, :, None]).reshape(count * rows, count * cols)
-
-
-def diagonal_blocks(x, count):
-    size = x.shape[0] // count
-    return jnp.stack([x[i * size : (i + 1) * size, i * size : (i + 1) * size] for i in range(count)])
+def hidden_body(nat, near, beside, across, tokens, gain, hidden, normed):
+    total = near[...].astype(f32) + beside[...].astype(f32) + across[...].astype(f32)
+    hidden[...] = tokens[...].astype(f32) + total
+    normed[...] = (hidden[...] * rms_factor(hidden[...]) * gain[...]).astype(bf16)
+
+
+def grad_hidden_body(nat, near, beside, across, cotangent, hidden, gain, grad, rounded):
+    total = near[...].astype(f32) + beside[...].astype(f32) + across[...].astype(f32)
+    grad[...] = cotangent[...].astype(f32) + rms_back(hidden[...], gain[...], total)
+    rounded[...] = grad[...].astype(bf16)
+
+
+def grad_tokens_body(nat, near, beside, across, tokens, grad, gain, out):
+    total = near[...].astype(f32) + beside[...].astype(f32) + across[...].astype(f32)
+    out[...] = (grad[...] + rms_back(tokens[...].astype(f32), gain[...], total)).astype(bf16)
+
+
+def on_own_rows(body, nat, near, beside, across, placed, owned, gain, out_types):
+    rows, model = near.shape
+    steps = 2
+    block = pl.BlockSpec((rows // steps, model), lambda i, nat: (i, 0))
+    return pl.pallas_call(
+        body,
+        grid_spec=pltpu.PrefetchScalarGridSpec(
+            num_scalar_prefetch=1,
+            grid=(steps,),
+            in_specs=[block] * 3
+            + [pl.BlockSpec((rows // steps, model), lambda i, nat: (nat[0] * steps + i, 0))]
+            + [block] * len(owned)
+            + [whole((1, model))],
+            out_specs=[block] * len(out_types),
+        ),
+        out_shape=[jax.ShapeDtypeStruct((rows, model), x) for x in out_types],
+        compiler_params=params(BIG),
+        cost_estimate=SMALL,
+        name="own_rows",
+    )(nat, near, beside, across, placed, *owned, gain)
+
+
+def place_body(count, nat, *refs):
+    quarters, (out, held, sems) = refs[:count], refs[-3:]
+    step = pl.program_id(0)
+
+    @pl.when(step == 0)
+    def _():
+        for copy in quarter_copies(quarters, held, sems):
+            copy.start()
+
+    out[...] = quarter_of(step, quarters, held, sems).astype(out.dtype)
+
+
+def place(quarters, first, nat, dtype, earlier=()):
+    count, (rows, width) = len(quarters), quarters[0].shape
+    return pl.pallas_call(
+        lambda *refs: place_body(count, *refs),
+        grid_spec=pltpu.PrefetchScalarGridSpec(
+            num_scalar_prefetch=1,
+            grid=(count,),
+            in_specs=[ANY] * (count + len(earlier)),
+            out_specs=pl.BlockSpec((rows, width), lambda i, nat: (nat[first + i], 0)),
+            scratch_shapes=[pltpu.VMEM((count, rows, width), bf16), pltpu.SemaphoreType.DMA((count,))],
+        ),
+        out_shape=jax.ShapeDtypeStruct((4 * rows, width), dtype),
+        input_output_aliases={1 + count: 0} if earlier else {},
+        compiler_params=params(BIG),
+        cost_estimate=SMALL,
+        name="place",
+    )(nat, *quarters, *earlier)
 
 
 def per_device(
@@ -698,27 +780,16 @@
 
     core, far = lax.axis_index("tensor") % 2, lax.axis_index("tensor") // 2
     nat = jnp.stack([core * 2 + far, (1 - core) * 2 + far, core * 2 + 1 - far, (1 - core) * 2 + 1 - far]).astype(i32)
-    own_rows = lambda x: lax.dynamic_slice_in_dim(x, nat[0] * quarter, quarter, 0)
+    turned_far = jnp.concatenate([nat, nat[3:], nat[2:3]])
+    turned_near = jnp.concatenate([nat, nat[1:2], nat[:1]])
 
     clock = Clock()
-    beside_each_other = lambda *blocks: jnp.concatenate(blocks, axis=1)
-    qkv_chain = Chain(clock, 0, beside_each_other, query_weight, key_weight, value_weight)
-    qkv_chain.step()
-    o_chain = Chain(clock, 0, jnp.transpose, output_weight)
-    o_chain.step()
-    offsets = qkv_chain.offsets
+    pack = lambda q, k, v, o: jnp.concatenate([q, k, v, o.T], axis=1)
+    attn_chain = Chain(clock, 0, pack, query_weight, key_weight, value_weight, output_weight)
+    attn_chain.step()
+    offsets = attn_chain.offsets
     n_pieces = offsets.shape[0]
     assert sum(map(sum, FFN_UNITS)) == gate_weight.shape[1]
-
-    def ffn_chains(part):
-        made = []
-        at = sum(map(sum, FFN_UNITS[:part]))
-        for units, way in zip(FFN_UNITS[part], (1, -1)):
-            cols = slice(at, at + units)
-            pack = lambda gate, up, down, cols=cols: jnp.concatenate([gate[:, cols], up[:, cols], down[cols].T], axis=1)
-            made.append(Chain(clock, way, pack, gate_weight, up_weight, down_weight))
-            at += units
-        return made
 
     def turn(part):
         for chain in chains[part]:
@@ -726,9 +797,6 @@
         for chain in chains[part]:
             chain.step()
 
-    def round_qkv_o():
-        qkv_chain.step()
-        o_chain.step()
 
     lengths = sequence_lengths[0]
     ends = jnp.cumsum(lengths)
@@ -755,41 +823,70 @@
     last_docs = docs_of(first_row - WIN - 1 + CHUNK * jnp.arange(chunks + 1))
     block_docs = docs_of(rows * jnp.arange(seq + 1) - WIN - 1)
     passes = (block_docs[:-1] == block_docs[1:]).astype(f32)
+
+    halo = shifted(tokens[rows - WIN :], "seq", 1)
     cos_q, sin_q = angles_of(q_at)
     cos_k, sin_k = angles_of(k_at)
     cos_q, sin_q, cos_k, sin_k = clock.wait(cos_q, sin_q, cos_k, sin_k)
-
-    halo = shifted(tokens[rows - WIN :], "seq", 1)
-    round_qkv_o()
+    passed_before, passed_after = [jnp.ones((), f32)], [jnp.ones((), f32)]
+    for by in range(1, seq - 1):
+        passed_before.append(passed_before[-1] * passes[jnp.maximum(here - by, 0)])
+        passed_after.append(passed_after[-1] * passes[jnp.minimum(here + by, seq - 1)])
+    passed_before, passed_after = jnp.stack(passed_before), jnp.stack(passed_after)
+    q_doc, doc_col, doc_row, last_docs, passed_before, passed_after = clock.wait(
+        q_doc, doc_col, doc_row, last_docs, passed_before, passed_after
+    )
+    attn_chain.step()
     (halo,) = clock.wait(halo)
-    spare = jnp.zeros((ext - rows - WIN, model), bf16)
-    seen = jnp.concatenate([halo, tokens, spare], axis=0).astype(f32)
-    gain_attn = attention_norm_gain.astype(f32)
-    gain_mlp = feedforward_norm_gain.astype(f32)
-    factor = clock.tie(rms_factor(seen))
-    round_qkv_o()
-    normed = clock.tie((seen * factor * gain_attn).astype(bf16))
+    attn_chain.step()
+    gain_attn = attention_norm_gain.astype(f32)[None, :]
+    gain_mlp = feedforward_norm_gain.astype(f32)[None, :]
     downs = jnp.concatenate([query_adapter_down, key_adapter_down, value_adapter_down], axis=1)
-    low = clock.tie(nn(normed, downs))
-    round_qkv_o()
-    ups = jnp.zeros((q_width + 2 * kv_width, 3 * rank), bf16)
-    ups = ups.at[:q_width, :rank].set(query_adapter_up.reshape(q_width, rank))
-    ups = ups.at[q_width : q_width + kv_width, rank : 2 * rank].set(key_adapter_up.reshape(kv_width, rank))
-    ups = ups.at[q_width + kv_width :, 2 * rank :].set(value_adapter_up.reshape(kv_width, rank))
-    low_up = clock.tie(nt(halves_outside(low, 1), jnp.concatenate([ups, ups], axis=1)))
-    round_qkv_o()
-    maps_q = jnp.stack(
-        [block_diagonal(feature_map_query[k * group : (k + 1) * group].transpose(0, 2, 1)) for k in range(kv_heads)]
+    normed, low = pl.pallas_call(
+        norm_body,
+        grid_spec=pltpu.PrefetchScalarGridSpec(
+            num_scalar_prefetch=0,
+            grid=(1,),
+            in_specs=[ANY, whole((WIN, model)), whole((1, model)), whole((model, 3 * rank))],
+            out_specs=[whole((ext, model)), whole((ext, 3 * rank))],
+            scratch_shapes=[pltpu.VMEM((ext, model), bf16), pltpu.SemaphoreType.DMA((4,))],
+        ),
+        out_shape=[jax.ShapeDtypeStruct((ext, model), bf16), jax.ShapeDtypeStruct((ext, 3 * rank), f32)],
+        compiler_params=params(BIG),
+        cost_estimate=SMALL,
+        name="norm",
+    )(clock.tie(tokens), halo, gain_attn, downs)
+    normed, low = clock.wait(normed, low)
+    attn_chain.step()
+    all_units = [x for part in FFN_UNITS for x in part]
+    pack_in = (
+        gate_weight, up_weight, down_weight, query_adapter_up, key_adapter_up, value_adapter_up,
+        feature_map_query, feature_map_key,
     )
-    maps_k = block_diagonal(feature_map_key.transpose(0, 2, 1))
-    maps_q, maps_k = clock.wait(maps_q, maps_k)
-    round_qkv_o()
-    chains = [ffn_chains(0)]
-    for chain in chains[0]:
-        chain.settle()
-    for _ in range(ring - 7):
-        round_qkv_o()
-    qkv_pieces = qkv_chain.pieces()
+    pack_out = [(gate_weight.shape[0], 3 * x) for x in all_units] + [
+        (q_width + 2 * kv_width, 3 * rank),
+        (q_width + 2 * kv_width, 6 * rank),
+        (kv_heads, group * head, group * head),
+        (kv_width, kv_width),
+    ]
+    packed = pl.pallas_call(
+        lambda *refs: pack_body(all_units, *refs),
+        grid_spec=pltpu.PrefetchScalarGridSpec(
+            num_scalar_prefetch=0,
+            grid=(1,),
+            in_specs=[whole(x.shape) for x in pack_in],
+            out_specs=[whole(x) for x in pack_out],
+        ),
+        out_shape=[jax.ShapeDtypeStruct(x, bf16) for x in pack_out],
+        compiler_params=params(BIG),
+        cost_estimate=SMALL,
+        name="pack",
+    )(clock.tie(gate_weight), *pack_in[1:])
+    *packed, ups, ups_twice, maps_q, maps_k = clock.wait(*packed)
+    chains = [[Chain(clock, 1, lambda x: x, packed[2 * i]), Chain(clock, -1, lambda x: x, packed[2 * i + 1])] for i in range(2)]
+    for _ in range(ring - 5):
+        attn_chain.step()
+    attn_pieces = attn_chain.pieces()
     turn(0)
 
     sems = pltpu.SemaphoreType.DMA((n_pieces,))
@@ -809,7 +906,7 @@
         ((2 * kv_width, ext), bf16),
         ((kv_heads, AUG, 2 * head), f32),
     ]
-    prep_in = (normed, low_up, cos_q, sin_q, cos_k, sin_k, maps_q, maps_k, doc_row)
+    prep_in = (normed, low, ups_twice, cos_q, sin_q, cos_k, sin_k, maps_q, maps_k, doc_row)
     q_t, phi_q, k_n, k_t, v_n, v_a, phi_kn, phi_kt, contrib = pl.pallas_call(
         lambda *refs: prep_body(dims, *refs),
         grid_spec=pltpu.PrefetchScalarGridSpec(
@@ -823,24 +920,16 @@
         compiler_params=params(56),
         cost_estimate=SMALL,
         name="prep",
-    )(clock.tie(offsets), last_docs, *prep_in, *qkv_pieces)
+    )(clock.tie(offsets), last_docs, *prep_in, *attn_pieces)
     (contrib,) = clock.wait(contrib)
     turn(0)
 
     coming = clock.wait(*[shifted(contrib, "seq", by) for by in range(1, seq)])
-    state_in = jnp.zeros_like(contrib)
-    factor = jnp.ones((), f32)
-    for by in range(1, seq):
-        state_in = state_in + factor * coming[by - 1]
-        factor = factor * passes[jnp.maximum(here - by, 0)]
-    state_in = clock.tie(state_in)
-    turn(0)
-
     column = lambda r: pl.BlockSpec((r, CHUNK), lambda c, *_: (0, c))
     att, att_t, totals, states = pl.pallas_call(
         lambda *refs: forward_body((kv_heads, group, head), *refs),
         grid_spec=pltpu.PrefetchScalarGridSpec(
-            num_scalar_prefetch=1,
+            num_scalar_prefetch=2,
             grid=(chunks,),
             in_specs=[
                 column(q_width),
@@ -851,15 +940,15 @@
                 whole(doc_col.shape),
                 whole(doc_row.shape),
                 column(1),
-                whole(state_in.shape),
-            ],
+            ]
+            + [whole(contrib.shape)] * len(coming),
             out_specs=[
                 pl.BlockSpec((CHUNK, q_width), lambda c, *_: (c, 0)),
                 column(q_width),
                 column(heads),
                 pl.BlockSpec((1, kv_heads, 2 * head, AUG), lambda c, *_: (c, 0, 0, 0)),
             ],
-            scratch_shapes=[pltpu.VMEM(state_in.shape, f32)],
+            scratch_shapes=[pltpu.VMEM(contrib.shape, f32)],
         ),
         out_shape=[
             jax.ShapeDtypeStruct((rows, q_width), bf16),
@@ -867,71 +956,71 @@
             jax.ShapeDtypeStruct((heads, rows), f32),
             jax.ShapeDtypeStruct((chunks, kv_heads, 2 * head, AUG), bf16),
         ],
-        compiler_params=params(48),
+        compiler_params=params(BIG),
         cost_estimate=SMALL,
         name="attend",
-    )(last_docs, q_t, phi_q, k_n, v_a, phi_kn, doc_col, doc_row, q_doc, state_in)
+    )(clock.tie(last_docs), passed_before, q_t, phi_q, k_n, v_a, phi_kn, doc_col, doc_row, q_doc, *coming)
     att = clock.tie(att)
-
-    o_pieces = o_chain.pieces()
+    turn(0)
+
     o_down = output_adapter_down.reshape(q_width, rank)
     o_up_t = jnp.concatenate([output_adapter_up.T, output_adapter_up.T], axis=0)
     one_quarter = jax.ShapeDtypeStruct((quarter, model), bf16)
 
-    def o_part(first, earlier):
-        return pl.pallas_call(
-            lambda *refs: o_body(n_pieces, *refs),
-            grid_spec=pltpu.PrefetchScalarGridSpec(
-                num_scalar_prefetch=2,
-                grid=(2,),
-                in_specs=[
-                    pl.BlockSpec((quarter, q_width), lambda i, off, nat: (nat[first - i], 0)),
-                    whole(o_down.shape),
-                    whole(o_up_t.shape),
-                ]
-                + [ANY] * (n_pieces + len(earlier)),
-                out_specs=[whole((quarter, model))] * 2
-                + [pl.BlockSpec((quarter, rank), lambda i, off, nat: (nat[first - i], 0))],
-                scratch_shapes=[held_o, sems],
-            ),
-            out_shape=[one_quarter, one_quarter, jax.ShapeDtypeStruct((rows, rank), f32)],
-            input_output_aliases={5 + n_pieces: 2} if earlier else {},
-            compiler_params=params(BIG),
-            cost_estimate=SMALL,
-            name="project",
-        )(clock.tie(offsets), nat, att, o_down, o_up_t, *o_pieces, *earlier)
-
-    o_far0, o_far1, lowered = o_part(3, ())
-    (o_far0,) = clock.wait(o_far0)
+    *o_parts, lowered = pl.pallas_call(
+        lambda *refs: o_body(n_pieces, qkv_width, *refs),
+        grid_spec=pltpu.PrefetchScalarGridSpec(
+            num_scalar_prefetch=2,
+            grid=(4,),
+            in_specs=[
+                pl.BlockSpec((quarter, q_width), lambda i, off, nat: (nat[3 - i], 0)),
+                whole(o_down.shape),
+                whole(o_up_t.shape),
+            ]
+            + [ANY] * n_pieces,
+            out_specs=[whole((quarter, model))] * 4
+            + [pl.BlockSpec((quarter, rank), lambda i, off, nat: (nat[3 - i], 0))],
+            scratch_shapes=[held_o, sems],
+        ),
+        out_shape=[one_quarter] * 4 + [jax.ShapeDtypeStruct((rows, rank), f32)],
+        compiler_params=params(BIG),
+        cost_estimate=SMALL,
+        name="project",
+    )(clock.tie(offsets), nat, att, o_down, o_up_t, *attn_pieces)
+    o_far0, o_far1, o_near0, o_near1 = clock.wait(*o_parts)
     turn(0)
-    beside = exchange(clock.tie(o_far0), "tensor", 1)
-    o_near0, o_near1, lowered = o_part(1, (lowered,))
-    (beside,) = clock.wait(beside)
+    o_far0, o_near0 = clock.wait(o_far0, o_near0)
+    beside = exchange(o_far0, "tensor", 1)
+    beside_near = exchange(o_near0, "tensor", 1)
+    beside, beside_near = clock.wait(beside, beside_near)
     o_far = clock.tie((o_far1.astype(f32) + beside.astype(f32)).astype(bf16))
     across = exchange(o_far, "tensor", 2)
-    (o_near0,) = clock.wait(o_near0)
-    beside = exchange(o_near0, "tensor", 1)
-    (beside,) = clock.wait(beside)
-    chains.append(ffn_chains(1))
     turn(0)
     (across,) = clock.wait(across)
-    hidden = own_rows(tokens).astype(f32) + (o_near1.astype(f32) + beside.astype(f32) + across.astype(f32))
-    (hidden,) = clock.wait(hidden)
-    normed_mlp = clock.tie((hidden * rms_factor(hidden) * gain_mlp).astype(bf16))
+    beside = beside_near
+    hidden, normed_mlp = on_own_rows(
+        hidden_body, clock.tie(nat), o_near1, beside, across, tokens, (), gain_mlp, (f32, bf16)
+    )
+    hidden, normed_mlp = clock.wait(hidden, normed_mlp)
+    for _ in range(ring - 7):
+        turn(0)
+    normed_mlp = clock.tie(normed_mlp)
     across, beside = exchange(normed_mlp, "tensor", 2), exchange(normed_mlp, "tensor", 1)
     (beside,) = clock.wait(beside)
     turn(0)
-    turn(0)
     (across,) = clock.wait(across)
-    last = clock.tie(exchange(across, "tensor", 1))
+    for chain in chains[0]:
+        chain.settle()
+    turn(1)
+    last = clock.tie(exchange(clock.tie(across), "tensor", 1))
     normed_mlp = [normed_mlp, beside, across, last]
 
-    def ffn(part, quarters, sums):
-        units, last = FFN_UNITS[part], part == len(FFN_UNITS) - 1
-        lots = [chain.pieces() for chain in chains[part]]
+    def ffn(part, which, quarters, sums):
+        units, last = FFN_UNITS[part][which], part == len(FFN_UNITS) - 1
+        lots = [chain.pieces() for chain in chains[part][which]]
         sizes = tuple(map(len, lots))
         pieces = [piece for lot in lots for piece in lot]
-        ring_offsets = jnp.concatenate([chain.offsets for chain in chains[part]])
+        ring_offsets = jnp.concatenate([chain.offsets for chain in chains[part][which]])
         first = quarters[0]
         summed = jax.ShapeDtypeStruct((2, quarter, model), f32)
         return pl.pallas_call(
@@ -958,31 +1047,30 @@
             name="feed_forward",
         )(clock.tie(ring_offsets), nat, output_cotangent, *[normed_mlp[q] for q in quarters], *pieces, *sums)
 
-    for chain in chains[0]:
-        chain.settle()
-    turn(1)
-    sums_far = clock.wait(*ffn(0, (3, 2), ()))
-    turn(1)
-    sums_near = clock.wait(*ffn(0, (1, 0), ()))
-    for _ in range(ring - 3):
+    sums_far = sums_near = ()
+    up, down, both = slice(0, 1), slice(1, 2), slice(0, 2)
+    for way in (up, down):
+        sums_far = clock.wait(*ffn(0, way, (3, 2), sums_far))
         turn(1)
-    gn_far0, gn_far1, mlp_far0, mlp_far1 = ffn(1, (3, 2), sums_far)
+        sums_near = clock.wait(*ffn(0, way, (1, 0), sums_near))
+        turn(1)
+    for _ in range(ring - 6):
+        turn(1)
+    gn_far0, gn_far1, mlp_far0, mlp_far1 = ffn(1, both, (3, 2), sums_far)
     gn_far0, mlp_far0 = clock.wait(gn_far0, mlp_far0)
     beside = exchange(gn_far0, "tensor", 1)
     mlp_beside_far = exchange(mlp_far0, "tensor", 1)
     (beside,) = clock.wait(beside)
     across = exchange(clock.tie((gn_far1.astype(f32) + beside.astype(f32)).astype(bf16)), "tensor", 2)
-    gn_near0, gn_near1, mlp_near0, mlp_near1 = ffn(1, (1, 0), sums_near)
+    gn_near0, gn_near1, mlp_near0, mlp_near1 = ffn(1, both, (1, 0), sums_near)
     gn_near0, mlp_near0 = clock.wait(gn_near0, mlp_near0)
-    (mlp_beside_far,) = clock.wait(mlp_beside_far)
-    mlp_far = clock.tie((mlp_far1.astype(f32) + mlp_beside_far.astype(f32)).astype(bf16))
     across, gn_near0 = clock.wait(across, gn_near0)
     beside = exchange(gn_near0, "tensor", 1)
     (beside,) = clock.wait(beside)
-    grad_normed_mlp = gn_near1.astype(f32) + beside.astype(f32) + across.astype(f32)
-    grad_hidden = own_rows(output_cotangent).astype(f32) + rms_back(hidden, gain_mlp, grad_normed_mlp)
-    grad_hidden = clock.tie(grad_hidden)
-    branch = clock.tie(grad_hidden.astype(bf16))
+    grad_hidden, branch = on_own_rows(
+        grad_hidden_body, clock.tie(nat), gn_near1, beside, across, output_cotangent, (hidden,), gain_mlp, (f32, bf16)
+    )
+    grad_hidden, branch = clock.wait(grad_hidden, branch)
     across, beside = exchange(branch, "tensor", 2), exchange(branch, "tensor", 1)
     mlp_beside = exchange(clock.tie(mlp_near0), "tensor", 1)
     (beside,) = clock.wait(beside)
@@ -994,7 +1082,7 @@
         by_quarter = lambda r: pl.BlockSpec((r, quarter), lambda i, off, nat, before: (0, nat[first + i]))
         late = bool(earlier)
         return pl.pallas_call(
-            lambda *refs: go_body((n_pieces, kv_heads, group, head, late), *refs),
+            lambda *refs: go_body((n_pieces, qkv_width, kv_heads, group, head, late), *refs),
             grid_spec=pltpu.PrefetchScalarGridSpec(
                 num_scalar_prefetch=3,
                 grid=(2,),
@@ -1028,11 +1116,12 @@
             name="project_back",
         )(
             clock.tie(offsets), nat, last_docs[:1], output_adapter_up, o_down_t, att_t, totals, phi_q, q_doc,
-            *quarters, *o_pieces, *earlier,
+            *quarters, *attn_pieces, *earlier,
         )
 
     near = clock.wait(*go_part(0, (branch, beside), ()))
-    (mlp_beside,) = clock.wait(mlp_beside)
+    mlp_beside, mlp_beside_far = clock.wait(mlp_beside, mlp_beside_far)
+    mlp_far = clock.tie((mlp_far1.astype(f32) + mlp_beside_far.astype(f32)).astype(bf16))
     mlp_near = clock.tie(hidden + (mlp_near1.astype(f32) + mlp_beside.astype(f32)))
     (across,) = clock.wait(across)
     last = clock.tie(exchange(across, "tensor", 1))
@@ -1090,13 +1179,10 @@
     )(clock.tie(last_docs), *[x for x, _ in back_in])
 
     g_q, g_kt, g_vt, g_phi, g_map_q = clock.wait(g_q, g_kt, g_vt, g_phi, g_map_q)
+    coming = clock.wait(*coming)
     (mlp_across,) = clock.wait(mlp_across)
     out_rows = clock.tie((mlp_near + mlp_across.astype(f32)).astype(bf16))
     out_across, out_beside = exchange(out_rows, "tensor", 2), exchange(out_rows, "tensor", 1)
-    coming = clock.wait(*coming)
-    factors = [jnp.ones((), f32)]
-    for by in range(1, seq - 1):
-        factors.append(factors[-1] * passes[jnp.minimum(here + by, seq - 1)])
     g_own, g_halo, g_map_k = pl.pallas_call(
         lambda *refs: keys_back_body((kv_heads, head, chunks, rows), *refs),
         grid_spec=pltpu.PrefetchScalarGridSpec(
@@ -1113,7 +1199,7 @@
         compiler_params=params(BIG),
         cost_estimate=SMALL,
         name="keys_back",
-    )(clock.tie(last_docs), jnp.stack(factors), g_kt, g_vt, g_phi, v_a, phi_kt, k_t, doc_row, maps_k, *coming)
+    )(clock.tie(last_docs), passed_after, g_kt, g_vt, g_phi, v_a, phi_kt, k_t, doc_row, maps_k, *coming)
 
     g_own, g_halo, g_map_k = clock.wait(g_own, g_halo, g_map_k)
     g_halo = shifted(g_halo, "seq", -1)
@@ -1121,14 +1207,47 @@
 
     downs_t = jnp.concatenate([downs.T, downs.T], axis=0)
 
+    def gn_part(which):
+        by_rows = lambda w: pl.BlockSpec((quarter, w), lambda i, off, nat: (nat[4 + i], 0))
+        by_columns = lambda r: pl.BlockSpec((r, quarter), lambda i, off, nat: (0, nat[4 + i]))
+        return pl.pallas_call(
+            lambda *refs: gn_body(n_pieces, *refs),
+            grid_spec=pltpu.PrefetchScalarGridSpec(
+                num_scalar_prefetch=2,
+                grid=(2,),
+                in_specs=[
+                    by_rows(q_width),
+                    by_columns(2 * kv_width),
+                    whole(g_halo.shape),
+                    by_columns(head // 2),
+                    by_columns(head // 2),
+                    whole(ups.shape),
+                    whole(downs_t.shape),
+                ]
+                + [ANY] * n_pieces,
+                out_specs=[whole((quarter, model))] * 2,
+                scratch_shapes=[held_qkv, sems],
+            ),
+            out_shape=[one_quarter, one_quarter],
+            compiler_params=params(BIG),
+            cost_estimate=SMALL,
+            name="norm_back",
+        )(clock.tie(offsets), which, g_q, g_own, g_halo, cos_q, sin_q, ups, downs_t, *attn_pieces)
+
+    gn_far0, gn_far1 = gn_part(turned_far)
+    (gn_far0,) = clock.wait(gn_far0)
+    out_across, out_beside, gn_far0 = clock.wait(out_across, out_beside, gn_far0)
+    beside = exchange(gn_far0, "tensor", 1)
+    (beside,) = clock.wait(beside)
+    gn_far = clock.tie((gn_far1.astype(f32) + beside.astype(f32)).astype(bf16))
+    across = exchange(gn_far, "tensor", 2)
+
     adapters_in = (g_q, g_own, g_halo, cos_q, sin_q, ups, low[WIN : WIN + rows], normed, lowered, att, up_product, g_map_q, g_map_k, *branch)
     sizes = [
-        ((rows, 2 * kv_width), bf16),
-        ((rows, 6 * rank), bf16),
         ((heads + kv_heads, head, 2 * head), f32),
         ((4 * rank, model), f32),
     ]
-    g_kv, low_back, by_head, shared = pl.pallas_call(
+    by_head, shared = pl.pallas_call(
         lambda *refs: adapters_body((rows, WIN, head, rank), *refs),
         grid_spec=pltpu.PrefetchScalarGridSpec(
             num_scalar_prefetch=1,
@@ -1141,30 +1260,7 @@
         cost_estimate=SMALL,
         name="adapters",
     )(clock.tie(nat), *adapters_in)
-    g_kv, low_back, by_head, shared = clock.wait(g_kv, low_back, by_head, shared)
-    out_across, out_beside = clock.wait(out_across, out_beside)
-
-    def gn_part(first):
-        by_rows = lambda w: pl.BlockSpec((quarter, w), lambda i, off, nat: (nat[first - i], 0))
-        return pl.pallas_call(
-            lambda *refs: gn_body(n_pieces, *refs),
-            grid_spec=pltpu.PrefetchScalarGridSpec(
-                num_scalar_prefetch=2,
-                grid=(2,),
-                in_specs=[by_rows(q_width), by_rows(2 * kv_width), by_rows(6 * rank), whole(downs_t.shape)]
-                + [ANY] * n_pieces,
-                out_specs=[whole((quarter, model))] * 2,
-                scratch_shapes=[held_qkv, sems],
-            ),
-            out_shape=[one_quarter, one_quarter],
-            compiler_params=params(BIG),
-            cost_estimate=SMALL,
-            name="norm_back",
-        )(clock.tie(offsets), nat, g_q, g_kv, low_back, downs_t, *qkv_pieces)
-
-    gn_far0, gn_far1 = gn_part(3)
-    (gn_far0,) = clock.wait(gn_far0)
-    beside = exchange(gn_far0, "tensor", 1)
+    by_head, shared = clock.wait(by_head, shared)
 
     by_head = by_head.reshape(heads + kv_heads, ring, head // ring, 2 * head).transpose(1, 0, 2, 3)
     shared = shared.reshape(4 * rank, ring, model // ring).transpose(1, 0, 2)
@@ -1184,26 +1280,25 @@
             size = half
             yield xs
 
-    (beside,) = clock.wait(beside)
-    gn_far = clock.tie((gn_far1.astype(f32) + beside.astype(f32)).astype(bf16))
-    across = exchange(gn_far, "tensor", 2)
     parts = [by_head, shared]
     dp = ring // seq
     parts = [x.reshape((dp, seq) + x.shape[1:]) for x in parts]
     for parts in summed_over("dp", dp, parts):
         pass
-    along_seq = summed_over("seq", seq, [x[0] for x in parts])
-    parts = next(along_seq)
-    gn_near0, gn_near1 = gn_part(1)
+    gn_near0, gn_near1 = gn_part(turned_near)
     gn_near0, gn_near1 = clock.wait(gn_near0, gn_near1)
     across, gn_near0 = clock.wait(across, gn_near0)
     beside = exchange(gn_near0, "tensor", 1)
     (beside,) = clock.wait(beside)
-    grad_normed = gn_near1.astype(f32) + beside.astype(f32) + across.astype(f32)
-    grad_rows = grad_hidden + rms_back(own_rows(tokens).astype(f32), gain_attn, grad_normed)
-    grad_rows = clock.tie(grad_rows.astype(bf16))
+    (grad_rows,) = on_own_rows(
+        grad_tokens_body, clock.tie(nat), gn_near1, beside, across, tokens, (grad_hidden,), gain_attn, (bf16,)
+    )
+    (grad_rows,) = clock.wait(grad_rows)
     across, beside = exchange(grad_rows, "tensor", 2), exchange(grad_rows, "tensor", 1)
     out_last = clock.tie(exchange(out_across, "tensor", 1))
+    along_seq = summed_over("seq", seq, clock.wait(*[x[0] for x in parts]))
+    (beside,) = clock.wait(beside)
+    grad_tokens = clock.tie(place([grad_rows, beside], 0, nat, f32))
     for parts in along_seq:
         pass
     by_head, shared = [x[0] for x in parts]
@@ -1211,13 +1306,13 @@
     kept, sent = halved(shared.reshape(4 * rank, 4, -1), "tensor", 2, far, 1)
     shared = kept.reshape(4 * rank, 2, -1)
     sent = sent.reshape(4 * rank, 2, -1)
-    block_out = clock.tie(place([out_rows, out_beside, out_across, out_last], nat, bf16))
-    beside, across, sent = clock.wait(beside, across, sent)
+    block_out = clock.tie(place([out_rows, out_beside, out_across, out_last], 0, nat, bf16))
+    across, sent = clock.wait(across, sent)
     last = exchange(across, "tensor", 1)
     kept, sent = halved(shared + sent, "tensor", 1, core, 1)
     last, sent = clock.wait(last, sent)
     shared = (kept + sent).reshape(4 * rank, -1).T
-    grad_tokens = clock.tie(place([grad_rows, beside, across, last], nat, f32))
+    grad_tokens = clock.tie(place([across, last], 2, nat, f32, (grad_tokens,)))
     of_q, of_kv = by_head[:heads], by_head[heads:]
     first, second = slice(head, head + rank), slice(head + rank, head + 2 * rank)
     out = [of_q[..., first], of_kv[..., first], of_kv[..., second], of_q[..., second], of_q[..., :head], of_kv[..., :head]]

time: 681 us -> 607 us (0.89)
  waiting for transfers between devices: 246 us -> 200 us
  Pallas kernels: 214 us -> 255 us
  local copies, waits for them, and re-layouts: 53.2 us -> 25.8 us
  other arithmetic: 50.8 us -> 25.8 us
  starting transfers between devices: 96.4 us -> 86.3 us
    ppermute x56 -> x42, waiting for transfers between devices: 171 us -> 128 us  [step(): lane.append(lax.ppermute(lane[-1], ('dp', 'seq'), way))]
    pallas_call x6 -> x11, Pallas kernels: 41.8 us -> 69.4 us  [the longest x2 18.2 us: go_part(): pl.pallas_call(lambda *refs: go_body((n_pieces, qkv_width, kv_heads, grou...]
    ppermute x56 -> x42, starting transfers between devices: 59.2 us -> 46.1 us  [step(): lane.append(lax.ppermute(lane[-1], ('dp', 'seq'), way))]
    unnamed x280 -> x202, local copies, waits for them, and re-layouts: 26.7 us -> 16.4 us
    reduce_sum x5 -> x0, other arithmetic: 10.1 us -> none  [the longest x3 6.7 us: rms_factor(): return lax.rsqrt(jnp.mean(x * x, axis=-1, keepdims=True) + epsilon)]
    pallas_call x4 -> x6, Pallas kernels: 100 us -> 110 us  [ffn(): pl.pallas_call(lambda *refs: ffn_body(sizes, units, bool(sums), last, *re...]
    convert_element_type x8 -> x0, other arithmetic: 6.87 us -> none  [the longest x1 3.53 us: per_device(): normed = clock.tie((seen * factor * gain_attn).astype(bf16))]
  transfers between devices with their start and end apart: 96 -> 82, of which waited for: 54 -> 47; matrix products, arithmetic and copies ran while one was open for 9% -> 5% of each run, Pallas kernels for 25% -> 37%
where the time goes in v3:
time: 607 us; the launch traced here: 599 us
  Pallas kernels  255 us (42%)
  waiting for transfers between devices  200 us (33%)
  starting transfers between devices  86.3 us (14%)
  local copies, waits for them, and re-layouts  25.8 us (4%)
  other arithmetic  25.8 us (4%)
    ppermute x42, waiting for transfers between devices, step(): lane.append(lax.ppermute(lane[-1], ('dp', 'seq'), way))  128 us
    pallas_call x6, Pallas kernels, ffn(): pl.pallas_call(lambda *refs: ffn_body(sizes, units, bool(sums), last, *re...  110 us
    ppermute x32, waiting for transfers between devices, exchange(): return lax.ppermute(x, axis, [(i, i ^ bit) for i in range(count)])  56.7 us
    ppermute x42, starting transfers between devices, step(): lane.append(lax.ppermute(lane[-1], ('dp', 'seq'), way))  46.1 us
    ppermute x32, starting transfers between devices, exchange(): return lax.ppermute(x, axis, [(i, i ^ bit) for i in range(count)])  21.8 us
    ppermute x8, starting transfers between devices, shifted(): lax.ppermute(x, axis, [(i, i + by) for i in range(count) if 0 <= i + by <...  18.5 us
    pallas_call x2, Pallas kernels, go_part(): pl.pallas_call(lambda *refs: go_body((n_pieces, qkv_width, kv_heads, grou...  18.2 us
    pallas_call x1, Pallas kernels, per_device(): pl.pallas_call(lambda *refs: backward_body((kv_heads, group, head, chunks...  17.1 us
  transfers between devices with their start and end apart: 82, of which 47 were waited for; matrix products, arithmetic and copies ran while one was open for 5% of the time, Pallas kernels for 37%

profile of v3, /device:TPU:0, one launch (start us, length us, event | category | flops | bytes accessed | tf_op | source)
XLA Modules:
  0.0 598.5 jit_solution(13353755195242418474)
XLA Ops:
  24.4 7.1 %collective-permute-done.4.halo = bf16[64,2048]{1,0:T(8,128)(2,1)S(1)} collective-permute-done((bf16[64,2048]{1,0:T(8,128)(2,1)S(1)}, bf16[64,2048]{1,0:T(8,128)(2,1)S(1)}, u32[]{:S(2)}, u32[]{:S(2)}) %collective-permute-start.4) | collective-permute-done | bytes 262176 | tf_op jit(solution)/shard_map/ppermute | solution.py:47
  35.7 8.2 %norm.1 = (bf16[1152,2048]{1,0:T(8,128)(2,1)}, f32[1152,24]{1,0:T(8,128)}) custom-call(bf16[1024,2048]{1,0:T(8,128)(2,1)} %tokens.4, bf16[64,2048]{1,0:T(8,128)(2,1)} %copy-done.74, f32[1,2048]{1,0:T(1,128)} %bitcast.89, bf16[2048,24]{1,0:T(8,128)(2,1)} %copy.74.downs), custom_call_target="tpu_custom_call" | custom-call | flops 1 | bytes 1 | tf_op jit(solution)/shard_map/norm/pallas_call | solution.py:845
  65.3 7.4 %collective-permute-done.11.refs_18_.refs_11_.refs_17_.refs_15_ = bf16[128,1280]{1,0:T(8,128)(2,1)S(1)} collective-permute-done((bf16[128,1280]{1,0:T(8,128)(2,1)S(1)}, bf16[128,1280]{1,0:T(8,128)(2,1)S(1)}, u32[]{:S(2)}, u32[]{:S(2)}) %collective-permute-start.11) | collective-permute-done | bytes 327712 | tf_op jit(solution)/shard_map/ppermute | solution.py:108
  76.1 8.5 %collective-permute-done.13.refs_19_.refs_12_.refs_18_.refs_16_ = bf16[128,1280]{1,0:T(8,128)(2,1)S(1)} collective-permute-done((bf16[128,1280]{1,0:T(8,128)(2,1)S(1)}, bf16[128,1280]{1,0:T(8,128)(2,1)S(1)}, u32[]{:S(2)}, u32[]{:S(2)}) %collective-permute-start.13) | collective-permute-done | bytes 327712 | tf_op jit(solution)/shard_map/ppermute | solution.py:108
  89.3 17.0 %prep.1 = (bf16[512,1024]{1,0:T(8,128)(2,1)}, bf16[1024,1024]{1,0:T(8,128)(2,1)}, bf16[1152,128]{1,0:T(8,128)(2,1)}, bf16[128,1152]{1,0:T(8,128)(2,1)}, bf16[115...) custom-call(s32[16]{0:T(128)} %get-tuple-element.916.refs_0_, ...), custom_call_target="tpu_custom_call" | custom-call | flops 1 | bytes 1 | tf_op jit(solution)/shard_map/prep/pallas_call | solution.py:910
  121.1 10.5 %attend.1 = (bf16[1024,512]{1,0:T(8,128)(2,1)}, f32[512,1024]{1,0:T(8,128)}, f32[8,1024]{1,0:T(8,128)}, bf16[8,2,128,80]{3,2,1,0:T(8,128)(2,1)}) custom-call(s32[9]{0:T(128)} %compare_select_fusion.14.refs_1_.refs_0_, f32[3]{0:T(128)} %get-tuple-element.579.refs_1_, bf16[512,1024]{1,0:T(8,128)(2,1)} %get-tuple-element.580.refs_2_.refs_1_, ...), custom_call_target="tpu_custom_call" | custom-call | flops 1 | bytes 1 | tf_op jit(solution)/shard_map/attend/pallas_call | solution.py:929
  136.5 10.7 %project.1 = (bf16[256,2048]{1,0:T(8,128)(2,1)}, bf16[256,2048]{1,0:T(8,128)(2,1)}, bf16[256,2048]{1,0:T(8,128)(2,1)}, bf16[256,2048]{1,0:T(8,128)(2,1)}, f32[1024,8]{1,0:T(8,128)}) custom-call(s32[16]{0:T(128)} %get-tuple-element.916.refs_0_, s32[4]{0:T(128)} %pad_add_fusion.refs_1_.nat.refs_0_, bf16[1024,512]{1,0:T(8,128)(2,1)} %get-tuple-element.600.refs_2_.refs_10_, ...), custom_call_target="tpu_custom_call" | custom-call | flops 1 | bytes 1 | tf_op jit(solution)/shard_map/project/pallas_call | solution.py:970
  155.1 12.3 %collective-permute-done.28.refs_9_ = bf16[256,1536]{1,0:T(8,128)(2,1)S(1)} collective-permute-done((bf16[256,1536]{1,0:T(8,128)(2,1)S(1)}, bf16[256,1536]{1,0:T(8,128)(2,1)S(1)}, u32[]{:S(2)}, u32[]{:S(2)}) %collective-permute-start.28) | collective-permute-done | bytes 786464 | tf_op jit(solution)/shard_map/ppermute | solution.py:108
  172.0 6.8 %collective-permute-done.26.across = bf16[256,2048]{1,0:T(8,128)(2,1)S(1)} collective-permute-done((bf16[256,2048]{1,0:T(8,128)(2,1)S(1)}, bf16[256,2048]{1,0:T(8,128)(2,1)S(1)}, u32[]{:S(2)}, u32[]{:S(2)}) %collective-permute-start.26) | collective-permute-done | bytes 1048608 | tf_op jit(solution)/shard_map/ppermute | solution.py:42
  193.6 16.4 %collective-permute-done.32.refs_11_ = bf16[256,1536]{1,0:T(8,128)(2,1)S(1)} collective-permute-done((bf16[256,1536]{1,0:T(8,128)(2,1)S(1)}, bf16[256,1536]{1,0:T(8,128)(2,1)S(1)}, u32[]{:S(2)}, u32[]{:S(2)}) %collective-permute-start.32) | collective-permute-done | bytes 786464 | tf_op jit(solution)/shard_map/ppermute | solution.py:108
  217.3 12.9 %collective-permute-done.35.refs_12_ = bf16[256,1536]{1,0:T(8,128)(2,1)S(1)} collective-permute-done((bf16[256,1536]{1,0:T(8,128)(2,1)S(1)}, bf16[256,1536]{1,0:T(8,128)(2,1)S(1)}, u32[]{:S(2)}, u32[]{:S(2)}) %collective-permute-start.35) | collective-permute-done | bytes 786464 | tf_op jit(solution)/shard_map/ppermute | solution.py:108
  234.9 15.3 %feed_forward.6 = (f32[2,256,2048]{2,1,0:T(8,128)}, f32[2,256,2048]{2,1,0:T(8,128)}) custom-call(s32[8]{0:T(128)} %copy-done.91, s32[4]{0:T(128)} %pad_add_fusion.refs_1_.nat.refs_0_, bf16[1024,2048]{1,0:T(8,128)(2,1)} %cotangent.1, bf16[256,2048]{1,0:T(8,128)(2,1)} %copy-done.29, bf16[256,2048]{1,0:T(8,128)(2,1)} %copy-done.28, ...), custom_call_target="tpu_custom_call" | custom-call | flops 1 | bytes 1 | tf_op jit(solution)/shard_map/feed_forward/pallas_call | solution.py:1026
  254.3 15.3 %feed_forward.7 = (f32[2,256,2048]{2,1,0:T(8,128)}, f32[2,256,2048]{2,1,0:T(8,128)}) custom-call(s32[8]{0:T(128)} %copy-done.91, s32[4]{0:T(128)} %pad_add_fusion.refs_1_.nat.refs_0_, bf16[1024,2048]{1,0:T(8,128)(2,1)} %cotangent.1, bf16[256,2048]{1,0:T(8,128)(2,1)} %copy-done.27, bf16[256,2048]{1,0:T(8,128)(2,1)} %get-tuple-element.656.refs_4_, ...), custom_call_target="tpu_custom_call" | custom-call | flops 1 | bytes 1 | tf_op jit(solution)/shard_map/feed_forward/pallas_call | solution.py:1026
  273.7 16.2 %feed_forward.8 = (f32[2,256,2048]{2,1,0:T(8,128)}, f32[2,256,2048]{2,1,0:T(8,128)}) custom-call(s32[8]{0:T(128)} %copy-done.90, s32[4]{0:T(128)} %pad_add_fusion.refs_1_.nat.refs_0_, bf16[1024,2048]{1,0:T(8,128)(2,1)} %cotangent.1, bf16[256,2048]{1,0:T(8,128)(2,1)} %copy-done.29, bf16[256,2048]{1,0:T(8,128)(2,1)} %copy-done.28, ...), custom_call_target="tpu_custom_call" | custom-call | flops 1 | bytes 1 | tf_op jit(solution)/shard_map/feed_forward/pallas_call | solution.py:1026
  292.2 16.3 %feed_forward.9 = (f32[2,256,2048]{2,1,0:T(8,128)}, f32[2,256,2048]{2,1,0:T(8,128)}) custom-call(s32[8]{0:T(128)} %copy-done.90, s32[4]{0:T(128)} %pad_add_fusion.refs_1_.nat.refs_0_, bf16[1024,2048]{1,0:T(8,128)(2,1)} %cotangent.1, bf16[256,2048]{1,0:T(8,128)(2,1)} %copy-done.27, bf16[256,2048]{1,0:T(8,128)(2,1)} %get-tuple-element.656.refs_4_, ...), custom_call_target="tpu_custom_call" | custom-call | flops 1 | bytes 1 | tf_op jit(solution)/shard_map/feed_forward/pallas_call | solution.py:1026
  310.6 15.5 %collective-permute-done.47.refs_10_ = bf16[256,1536]{1,0:T(8,128)(2,1)S(1)} collective-permute-done((bf16[256,1536]{1,0:T(8,128)(2,1)S(1)}, bf16[256,1536]{1,0:T(8,128)(2,1)S(1)}, u32[]{:S(2)}, u32[]{:S(2)}) %collective-permute-start.47) | collective-permute-done | bytes 786464 | tf_op jit(solution)/shard_map/ppermute | solution.py:108
  328.5 15.6 %collective-permute-done.49.refs_11_ = bf16[256,1536]{1,0:T(8,128)(2,1)S(1)} collective-permute-done((bf16[256,1536]{1,0:T(8,128)(2,1)S(1)}, bf16[256,1536]{1,0:T(8,128)(2,1)S(1)}, u32[]{:S(2)}, u32[]{:S(2)}) %collective-permute-start.49) | collective-permute-done | bytes 786464 | tf_op jit(solution)/shard_map/ppermute | solution.py:108
  346.6 12.2 %collective-permute-done.51.refs_12_ = bf16[256,1536]{1,0:T(8,128)(2,1)S(1)} collective-permute-done((bf16[256,1536]{1,0:T(8,128)(2,1)S(1)}, bf16[256,1536]{1,0:T(8,128)(2,1)S(1)}, u32[]{:S(2)}, u32[]{:S(2)}) %collective-permute-start.51) | collective-permute-done | bytes 786464 | tf_op jit(solution)/shard_map/ppermute | solution.py:108
  360.7 23.5 %feed_forward.10 = (bf16[256,2048]{1,0:T(8,128)(2,1)}, bf16[256,2048]{1,0:T(8,128)(2,1)}, bf16[256,2048]{1,0:T(8,128)(2,1)}, bf16[256,2048]{1,0:T(8,128)(2,1)}) custom-call(s32[16]{0:T(128)} %get-tuple-element.784.refs_0_, s32[4]{0:T(128)} %pad_add_fusion.refs_1_.nat.refs_0_, bf16[1024,2048]{1,0:T(8,128)(2,1)} %cotangent.1, bf16[256,2048]{1,0:T(8,128)(2,1)} %copy-done.29, ...), custom_call_target="tpu_custom_call" | custom-call | flops 1 | bytes 1 | tf_op jit(solution)/shard_map/feed_forward/pallas_call | solution.py:1026
  390.3 23.7 %feed_forward.11 = (bf16[256,2048]{1,0:T(8,128)(2,1)}, bf16[256,2048]{1,0:T(8,128)(2,1)}, bf16[256,2048]{1,0:T(8,128)(2,1)}, bf16[256,2048]{1,0:T(8,128)(2,1)}) custom-call(s32[16]{0:T(128)} %get-tuple-element.784.refs_0_, s32[4]{0:T(128)} %pad_add_fusion.refs_1_.nat.refs_0_, bf16[1024,2048]{1,0:T(8,128)(2,1)} %cotangent.1, bf16[256,2048]{1,0:T(8,128)(2,1)} %copy-done.27, ...), custom_call_target="tpu_custom_call" | custom-call | flops 1 | bytes 1 | tf_op jit(solution)/shard_map/feed_forward/pallas_call | solution.py:1026
  418.0 5.6 own_rows.4
  428.3 9.1 %project_back.2 = (bf16[512,1024]{1,0:T(8,128)(2,1)}, f32[8,1024]{1,0:T(8,128)}, f32[1024,8]{1,0:T(8,128)}, f32[2,128,80]{2,1,0:T(8,128)}) custom-call(s32[16]{0:T(128)} %get-tuple-element.916.refs_0_, s32[4]{0:T(128)} %pad_add_fusion.refs_1_.nat.refs_0_, s32[1]{0:T(128)} %bitcast.72, bf16[2048,8]{1,0:T(8,128)(2,1)} %copy.80.refs_3_, ...), custom_call_target="tpu_custom_call" | custom-call | flops 1 | bytes 1 | tf_op jit(solution)/shard_map/project_back/pallas_call | solution.py:1084
  441.4 10.2 %collective-permute-done.58.refs_9_.refs_16_ = bf16[256,2048]{1,0:T(8,128)(2,1)} collective-permute-done((bf16[256,2048]{1,0:T(8,128)(2,1)}, bf16[256,2048]{1,0:T(8,128)(2,1)}, u32[]{:S(2)}, u32[]{:S(2)}) %collective-permute-start.58) | collective-permute-done | bytes 1048608 | tf_op jit(solution)/shard_map/ppermute | solution.py:42
  456.1 9.1 %project_back.3 = (bf16[512,1024]{1,0:T(8,128)(2,1)}, f32[8,1024]{1,0:T(8,128)}, f32[1024,8]{1,0:T(8,128)}, f32[2,128,80]{2,1,0:T(8,128)}) custom-call(s32[16]{0:T(128)} %get-tuple-element.916.refs_0_, s32[4]{0:T(128)} %pad_add_fusion.refs_1_.nat.refs_0_, s32[1]{0:T(128)} %bitcast.73, ...), custom_call_target="tpu_custom_call", output_to_operand_aliasing={{0}: (27, {}), {1}: (28, {}), {2}: (29, {})} | custom-call | flops 1 | bytes 1 | tf_op jit(solution)/shard_map/project_back/pallas_call | solution.py:1084
  469.9 17.1 %attend_back.1 = (bf16[1024,512]{1,0:T(8,128)(2,1)}, f32[128,1152]{1,0:T(8,128)}, f32[128,1152]{1,0:T(8,128)}, f32[256,1152]{1,0:T(8,128)}, f32[2,256,256]{2,1,0:T(8,128)}) custom-call(s32[9]{0:T(128)S(1)} %copy-done.10, bf16[512,1024]{1,0:T(8,128)(2,1)} %get-tuple-element.580.refs_2_.refs_1_, bf16[1024,1024]{1,0:T(8,128)(2,1)} %get-tuple-element.581.refs_3_.refs_7_.refs_2_, ...), custom_call_target="tpu_custom_call" | custom-call | flops 1 | bytes 1 | tf_op jit(solution)/shard_map/attend_back/pallas_call | solution.py:1154
  496.6 6.3 %collective-permute-done.66.refs_4_.refs_3_ = f32[256,128]{1,0:T(8,128)S(1)} collective-permute-done((f32[256,128]{1,0:T(8,128)}, f32[256,128]{1,0:T(8,128)S(1)}, u32[]{:S(2)}, u32[]{:S(2)}) %collective-permute-start.66) | collective-permute-done | bytes 131104 | tf_op jit(solution)/shard_map/ppermute | solution.py:47
  503.6 8.5 %norm_back.2 = (bf16[256,2048]{1,0:T(8,128)(2,1)}, bf16[256,2048]{1,0:T(8,128)(2,1)}) custom-call(s32[16]{0:T(128)} %get-tuple-element.916.refs_0_, s32[6]{0:T(128)} %concatenate.36.refs_1_, bf16[1024,512]{1,0:T(8,128)(2,1)} %get-tuple-element.884.refs_2_.refs_1_, f32[256,1024]{1,0:T(8,128)} %get-tuple-element.885.refs_3_.refs_2_, f32[256,128]{1,0:T(8,128)} %copy-done.56, ...), custom_call_target="tpu_custom_call" | custom-call | flops 1 | bytes 1 | tf_op jit(solution)/shard_map/norm_back/pallas_call | solution.py:1213
  519.8 9.4 %adapters.1 = (f32[10,64,128]{2,1,0:T(8,128)}, f32[32,2048]{1,0:T(8,128)}) custom-call(s32[4]{0:T(128)} %pad_add_fusion.refs_1_.nat.refs_0_, bf16[1024,512]{1,0:T(8,128)(2,1)} %get-tuple-element.884.refs_2_.refs_1_, f32[256,1024]{1,0:T(8,128)} %get-tuple-element.885.refs_3_.refs_2_, f32[256,128]{1,0:T(8,128)} %copy-done.56, ...), custom_call_target="tpu_custom_call" | custom-call | flops 1 | bytes 1 | tf_op jit(solution)/shard_map/adapters/pallas_call | solution.py:1250
  534.2 6.1 %collective-permute-done.71 = f32[1,4,32,256]{3,2,1,0:T(8,128)S(1)} collective-permute-done((f32[1,4,32,256]{3,2,1,0:T(8,128)S(1)}, f32[1,4,32,256]{3,2,1,0:T(8,128)S(1)}, u32[]{:S(2)}, u32[]{:S(2)}) %collective-permute-start.71) | collective-permute-done | bytes 131104 | tf_op jit(solution)/shard_map/ppermute | solution.py:42
  540.3 8.5 %norm_back.3 = (bf16[256,2048]{1,0:T(8,128)(2,1)}, bf16[256,2048]{1,0:T(8,128)(2,1)}) custom-call(s32[16]{0:T(128)} %get-tuple-element.916.refs_0_, s32[6]{0:T(128)} %concatenate.38.refs_1_, bf16[1024,512]{1,0:T(8,128)(2,1)} %get-tuple-element.884.refs_2_.refs_1_, f32[256,1024]{1,0:T(8,128)} %get-tuple-element.885.refs_3_.refs_2_, f32[256,128]{1,0:T(8,128)} %copy-done.56, ...), custom_call_target="tpu_custom_call" | custom-call | flops 1 | bytes 1 | tf_op jit(solution)/shard_map/norm_back/pallas_call | solution.py:1213
  552.7 5.2 own_rows.5.refs_1_
  579.9 9.5 %collective-permute-done.78.refs_1_ = bf16[256,2048]{1,0:T(8,128)(2,1)S(1)} collective-permute-done((bf16[256,2048]{1,0:T(8,128)(2,1)}, bf16[256,2048]{1,0:T(8,128)(2,1)S(1)}, u32[]{:S(2)}, u32[]{:S(2)}) %collective-permute-start.78) | collective-permute-done | bytes 1048608 | tf_op jit(solution)/shard_map/ppermute | solution.py:42
  (436 shorter events, 217.6 us)
Async XLA Ops:
  86.3 20.0 %collective-permute-start.16 = (bf16[256,1536]{1,0:T(8,128)(2,1)}, bf16[256,1536]{1,0:T(8,128)(2,1)}, u32[]{:S(2)}, u32[]{:S(2)}) collective-permute-start(bf16[256,1536]{1,0:T(8,128)(2,1)} %get-tuple-element.549.refs_5_), channel_id=1, source_target_pairs={{0,4},{4,8},{8,12},{12,28},{28,24},{24,20},{20,16},{16,0},{1,5},{5... | collective-permute-start | bytes 2359304 | tf_op jit(solution)/shard_map/ppermute | solution.py:108
  87.8 18.5 %collective-permute-start.15 = (bf16[256,1536]{1,0:T(8,128)(2,1)}, bf16[256,1536]{1,0:T(8,128)(2,1)}, u32[]{:S(2)}, u32[]{:S(2)}) collective-permute-start(bf16[256,1536]{1,0:T(8,128)(2,1)} %get-tuple-element.548.refs_5_), channel_id=1, source_target_pairs={{4,0},{8,4},{12,8},{28,12},{24,28},{20,24},{16,20},{0,16},{5,1},{9... | collective-permute-start | bytes 2359304 | tf_op jit(solution)/shard_map/ppermute | solution.py:108
  106.3 25.3 %collective-permute-start.18 = (bf16[256,1536]{1,0:T(8,128)(2,1)}, bf16[256,1536]{1,0:T(8,128)(2,1)S(1)}, u32[]{:S(2)}, u32[]{:S(2)}) collective-permute-start(bf16[256,1536]{1,0:T(8,128)(2,1)} %collective-permute-done.16.refs_6_), channel_id=1, source_target_pairs={{0,4},{4,8},{8,12},{12,28},{28,24},{24,20},{20,16},{16,0},{1,5},{5... | collective-permute-start | bytes 2359304 | tf_op jit(solution)/shard_map/ppermute | solution.py:108
  107.9 23.7 %collective-permute-start.17 = (bf16[256,1536]{1,0:T(8,128)(2,1)}, bf16[256,1536]{1,0:T(8,128)(2,1)S(1)}, u32[]{:S(2)}, u32[]{:S(2)}) collective-permute-start(bf16[256,1536]{1,0:T(8,128)(2,1)} %collective-permute-done.15.refs_6_), channel_id=1, source_target_pairs={{4,0},{8,4},{12,8},{28,12},{24,28},{20,24},{16,20},{0,16},{5,1},{9... | collective-permute-start | bytes 2359304 | tf_op jit(solution)/shard_map/ppermute | solution.py:108
  147.9 19.5 %collective-permute-start.28 = (bf16[256,1536]{1,0:T(8,128)(2,1)S(1)}, bf16[256,1536]{1,0:T(8,128)(2,1)S(1)}, u32[]{:S(2)}, u32[]{:S(2)}) collective-permute-start(bf16[256,1536]{1,0:T(8,128)(2,1)S(1)} %collective-permute-done.23.refs_8_), channel_id=1, source_target_pairs={{0,4},{4,8},{8,12},{12,28},{28,24},{24,20},{20,16},{16,0},{1,5},{5... | collective-permute-start | bytes 2359304 | tf_op jit(solution)/shard_map/ppermute | solution.py:108
  149.9 19.4 %collective-permute-start.27 = (bf16[256,1536]{1,0:T(8,128)(2,1)S(1)}, bf16[256,1536]{1,0:T(8,128)(2,1)}, u32[]{:S(2)}, u32[]{:S(2)}) collective-permute-start(bf16[256,1536]{1,0:T(8,128)(2,1)S(1)} %collective-permute-done.22.refs_8_), channel_id=1, source_target_pairs={{4,0},{8,4},{12,8},{28,12},{24,28},{20,24},{16,20},{0,16},{5,1},{9... | collective-permute-start | bytes 2359304 | tf_op jit(solution)/shard_map/ppermute | solution.py:108
  153.5 25.3 %collective-permute-start.26 = (bf16[256,2048]{1,0:T(8,128)(2,1)S(1)}, bf16[256,2048]{1,0:T(8,128)(2,1)S(1)}, u32[]{:S(2)}, u32[]{:S(2)}) collective-permute-start(bf16[256,2048]{1,0:T(8,128)(2,1)S(1)} %add_convert_fusion.4), channel_id=1, source_target_pairs={{0,2},{1,3},{2,0},{3,1},{4,6},{5,7},{6,4},{7,5},{8,10},{9,11},{10,... | collective-permute-start | bytes 3145736 | tf_op jit(solution)/shard_map/ppermute | solution.py:42
  169.4 18.4 %collective-permute-start.30 = (bf16[256,1536]{1,0:T(8,128)(2,1)S(1)}, bf16[256,1536]{1,0:T(8,128)(2,1)S(1)}, u32[]{:S(2)}, u32[]{:S(2)}) collective-permute-start(bf16[256,1536]{1,0:T(8,128)(2,1)S(1)} %collective-permute-done.28.refs_9_), channel_id=1, source_target_pairs={{0,4},{4,8},{8,12},{12,28},{28,24},{24,20},{20,16},{16,0},{1,5},{5... | collective-permute-start | bytes 2359304 | tf_op jit(solution)/shard_map/ppermute | solution.py:108
  171.4 18.7 %collective-permute-start.29 = (bf16[256,1536]{1,0:T(8,128)(2,1)}, bf16[256,1536]{1,0:T(8,128)(2,1)}, u32[]{:S(2)}, u32[]{:S(2)}) collective-permute-start(bf16[256,1536]{1,0:T(8,128)(2,1)} %collective-permute-done.27.refs_9_), channel_id=1, source_target_pairs={{4,0},{8,4},{12,8},{28,12},{24,28},{20,24},{16,20},{0,16},{5,1},{9... | collective-permute-start | bytes 2359304 | tf_op jit(solution)/shard_map/ppermute | solution.py:108
  190.1 20.0 %collective-permute-start.32 = (bf16[256,1536]{1,0:T(8,128)(2,1)S(1)}, bf16[256,1536]{1,0:T(8,128)(2,1)S(1)}, u32[]{:S(2)}, u32[]{:S(2)}) collective-permute-start(bf16[256,1536]{1,0:T(8,128)(2,1)S(1)} %collective-permute-done.30.refs_10_), channel_id=1, source_target_pairs={{0,4},{4,8},{8,12},{12,28},{28,24},{24,20},{20,16},{16,0},{1,5},{5... | collective-permute-start | bytes 2359304 | tf_op jit(solution)/shard_map/ppermute | solution.py:108
  191.5 19.9 %collective-permute-start.31 = (bf16[256,1536]{1,0:T(8,128)(2,1)}, bf16[256,1536]{1,0:T(8,128)(2,1)S(1)}, u32[]{:S(2)}, u32[]{:S(2)}) collective-permute-start(bf16[256,1536]{1,0:T(8,128)(2,1)} %collective-permute-done.29.refs_10_), channel_id=1, source_target_pairs={{4,0},{8,4},{12,8},{28,12},{24,28},{20,24},{16,20},{0,16},{5,1},{9... | collective-permute-start | bytes 2359304 | tf_op jit(solution)/shard_map/ppermute | solution.py:108
  192.1 25.2 %collective-permute-start.36 = (bf16[256,2048]{1,0:T(8,128)(2,1)}, bf16[256,2048]{1,0:T(8,128)(2,1)S(1)}, u32[]{:S(2)}, u32[]{:S(2)}) collective-permute-start(bf16[256,2048]{1,0:T(8,128)(2,1)} %get-tuple-element.656.refs_4_), channel_id=1, source_target_pairs={{0,2},{1,3},{2,0},{3,1},{4,6},{5,7},{6,4},{7,5},{8,10},{9,11},{10,... | collective-permute-start | bytes 3145736 | tf_op jit(solution)/shard_map/ppermute | solution.py:42
  211.4 18.9 %collective-permute-start.35 = (bf16[256,1536]{1,0:T(8,128)(2,1)S(1)}, bf16[256,1536]{1,0:T(8,128)(2,1)S(1)}, u32[]{:S(2)}, u32[]{:S(2)}) collective-permute-start(bf16[256,1536]{1,0:T(8,128)(2,1)S(1)} %collective-permute-done.32.refs_11_), channel_id=1, source_target_pairs={{0,4},{4,8},{8,12},{12,28},{28,24},{24,20},{20,16},{16,0},{1,5},{5... | collective-permute-start | bytes 2359304 | tf_op jit(solution)/shard_map/ppermute | solution.py:108
  212.7 18.6 %collective-permute-start.34 = (bf16[256,1536]{1,0:T(8,128)(2,1)S(1)}, bf16[256,1536]{1,0:T(8,128)(2,1)S(1)}, u32[]{:S(2)}, u32[]{:S(2)}) collective-permute-start(bf16[256,1536]{1,0:T(8,128)(2,1)S(1)} %collective-permute-done.31.refs_11_), channel_id=1, source_target_pairs={{4,0},{8,4},{12,8},{28,12},{24,28},{20,24},{16,20},{0,16},{5,1},{9... | collective-permute-start | bytes 2359304 | tf_op jit(solution)/shard_map/ppermute | solution.py:108
  231.3 20.7 %collective-permute-start.38 = (bf16[256,1536]{1,0:T(8,128)(2,1)}, bf16[256,1536]{1,0:T(8,128)(2,1)}, u32[]{:S(2)}, u32[]{:S(2)}) collective-permute-start(bf16[256,1536]{1,0:T(8,128)(2,1)} %get-tuple-element.676.refs_5_), channel_id=1, source_target_pairs={{0,4},{4,8},{8,12},{12,28},{28,24},{24,20},{20,16},{16,0},{1,5},{5... | collective-permute-start | bytes 2359304 | tf_op jit(solution)/shard_map/ppermute | solution.py:108
  232.3 20.0 %collective-permute-start.37 = (bf16[256,1536]{1,0:T(8,128)(2,1)}, bf16[256,1536]{1,0:T(8,128)(2,1)}, u32[]{:S(2)}, u32[]{:S(2)}) collective-permute-start(bf16[256,1536]{1,0:T(8,128)(2,1)} %get-tuple-element.675.refs_13_), channel_id=1, source_target_pairs={{4,0},{8,4},{12,8},{28,12},{24,28},{20,24},{16,20},{0,16},{5,1},{9... | collective-permute-start | bytes 2359304 | tf_op jit(solution)/shard_map/ppermute | solution.py:108
  252.3 19.1 %collective-permute-start.41 = (bf16[256,1536]{1,0:T(8,128)(2,1)}, bf16[256,1536]{1,0:T(8,128)(2,1)S(1)}, u32[]{:S(2)}, u32[]{:S(2)}) collective-permute-start(bf16[256,1536]{1,0:T(8,128)(2,1)} %collective-permute-done.38.refs_6_), channel_id=1, source_target_pairs={{0,4},{4,8},{8,12},{12,28},{28,24},{24,20},{20,16},{16,0},{1,5},{5... | collective-permute-start | bytes 2359304 | tf_op jit(solution)/shard_map/ppermute | solution.py:108
  252.8 18.8 %collective-permute-start.40 = (bf16[256,1536]{1,0:T(8,128)(2,1)}, bf16[256,1536]{1,0:T(8,128)(2,1)S(1)}, u32[]{:S(2)}, u32[]{:S(2)}) collective-permute-start(bf16[256,1536]{1,0:T(8,128)(2,1)} %collective-permute-done.37.refs_14_), channel_id=1, source_target_pairs={{4,0},{8,4},{12,8},{28,12},{24,28},{20,24},{16,20},{0,16},{5,1},{9... | collective-permute-start | bytes 2359304 | tf_op jit(solution)/shard_map/ppermute | solution.py:108
  271.7 18.2 %collective-permute-start.43 = (bf16[256,1536]{1,0:T(8,128)(2,1)S(1)}, bf16[256,1536]{1,0:T(8,128)(2,1)S(1)}, u32[]{:S(2)}, u32[]{:S(2)}) collective-permute-start(bf16[256,1536]{1,0:T(8,128)(2,1)S(1)} %collective-permute-done.41.refs_7_), channel_id=1, source_target_pairs={{0,4},{4,8},{8,12},{12,28},{28,24},{24,20},{20,16},{16,0},{1,5},{5... | collective-permute-start | bytes 2359304 | tf_op jit(solution)/shard_map/ppermute | solution.py:108
  272.2 17.7 %collective-permute-start.42 = (bf16[256,1536]{1,0:T(8,128)(2,1)S(1)}, bf16[256,1536]{1,0:T(8,128)(2,1)S(1)}, u32[]{:S(2)}, u32[]{:S(2)}) collective-permute-start(bf16[256,1536]{1,0:T(8,128)(2,1)S(1)} %collective-permute-done.40.refs_15_), channel_id=1, source_target_pairs={{4,0},{8,4},{12,8},{28,12},{24,28},{20,24},{16,20},{0,16},{5,1},{9... | collective-permute-start | bytes 2359304 | tf_op jit(solution)/shard_map/ppermute | solution.py:108
  290.0 18.5 %collective-permute-start.45 = (bf16[256,1536]{1,0:T(8,128)(2,1)S(1)}, bf16[256,1536]{1,0:T(8,128)(2,1)S(1)}, u32[]{:S(2)}, u32[]{:S(2)}) collective-permute-start(bf16[256,1536]{1,0:T(8,128)(2,1)S(1)} %collective-permute-done.43.refs_8_), channel_id=1, source_target_pairs={{0,4},{4,8},{8,12},{12,28},{28,24},{24,20},{20,16},{16,0},{1,5},{5... | collective-permute-start | bytes 2359304 | tf_op jit(solution)/shard_map/ppermute | solution.py:108
  290.5 17.9 %collective-permute-start.44 = (bf16[256,1536]{1,0:T(8,128)(2,1)S(1)}, bf16[256,1536]{1,0:T(8,128)(2,1)S(1)}, u32[]{:S(2)}, u32[]{:S(2)}) collective-permute-start(bf16[256,1536]{1,0:T(8,128)(2,1)S(1)} %collective-permute-done.42.refs_16_), channel_id=1, source_target_pairs={{4,0},{8,4},{12,8},{28,12},{24,28},{20,24},{16,20},{0,16},{5,1},{9... | collective-permute-start | bytes 2359304 | tf_op jit(solution)/shard_map/ppermute | solution.py:108
  388.7 25.3 %collective-permute-start.53 = (bf16[256,2048]{1,0:T(8,128)(2,1)S(1)}, bf16[256,2048]{1,0:T(8,128)(2,1)S(1)}, u32[]{:S(2)}, u32[]{:S(2)}) collective-permute-start(bf16[256,2048]{1,0:T(8,128)(2,1)S(1)} %add_convert_fusion.3), channel_id=1, source_target_pairs={{0,2},{1,3},{2,0},{3,1},{4,6},{5,7},{6,4},{7,5},{8,10},{9,11},{10,... | collective-permute-start | bytes 3145736 | tf_op jit(solution)/shard_map/ppermute | solution.py:42
  425.9 25.8 %collective-permute-start.58 = (bf16[256,2048]{1,0:T(8,128)(2,1)}, bf16[256,2048]{1,0:T(8,128)(2,1)}, u32[]{:S(2)}, u32[]{:S(2)}) collective-permute-start(bf16[256,2048]{1,0:T(8,128)(2,1)} %get-tuple-element.810.refs_9_.refs_14_), channel_id=1, source_target_pairs={{0,2},{1,3},{2,0},{3,1},{4,6},{5,7},{6,4},{7,5},{8,10},{9,11},{10,... | collective-permute-start | bytes 3145736 | tf_op jit(solution)/shard_map/ppermute | solution.py:42
  454.6 32.4 %collective-permute-start.60 = (bf16[256,2048]{1,0:T(8,128)(2,1)}, bf16[256,2048]{1,0:T(8,128)(2,1)}, u32[]{:S(2)}, u32[]{:S(2)}) collective-permute-start(bf16[256,2048]{1,0:T(8,128)(2,1)} %add_convert_fusion.2), channel_id=1, source_target_pairs={{0,2},{1,3},{2,0},{3,1},{4,6},{5,7},{6,4},{7,5},{8,10},{9,11},{10,... | collective-permute-start | bytes 3145736 | tf_op jit(solution)/shard_map/ppermute | solution.py:42
  465.1 21.9 %collective-permute-start.61 = (f32[2,128,80]{2,1,0:T(8,128)}, f32[2,128,80]{2,1,0:T(8,128)S(1)}, u32[]{:S(2)}, u32[]{:S(2)}) collective-permute-start(f32[2,128,80]{2,1,0:T(8,128)} %get-tuple-element.847), channel_id=1, source_target_pairs={{4,0},{8,4},{12,8},{5,1},{9,5},{13,9},{6,2},{10,6},{14,10},{7,3},{... | collective-permute-start | bytes 245768 | tf_op jit(solution)/shard_map/ppermute | solution.py:47
  466.4 20.6 %collective-permute-start.62 = (f32[2,128,80]{2,1,0:T(8,128)}, f32[2,128,80]{2,1,0:T(8,128)S(1)}, u32[]{:S(2)}, u32[]{:S(2)}) collective-permute-start(f32[2,128,80]{2,1,0:T(8,128)} %get-tuple-element.847), channel_id=1, source_target_pairs={{8,0},{12,4},{9,1},{13,5},{10,2},{14,6},{11,3},{15,7},{24,16},{28,... | collective-permute-start | bytes 245768 | tf_op jit(solution)/shard_map/ppermute | solution.py:47
  467.7 19.3 %collective-permute-start.63 = (f32[2,128,80]{2,1,0:T(8,128)}, f32[2,128,80]{2,1,0:T(8,128)S(1)}, u32[]{:S(2)}, u32[]{:S(2)}) collective-permute-start(f32[2,128,80]{2,1,0:T(8,128)} %get-tuple-element.847), channel_id=1, source_target_pairs={{12,0},{13,1},{14,2},{15,3},{28,16},{29,17},{30,18},{31,19}} | collective-permute-start | bytes 245768 | tf_op jit(solution)/shard_map/ppermute | solution.py:47
  488.7 25.1 %collective-permute-start.64 = (bf16[256,2048]{1,0:T(8,128)(2,1)S(1)}, bf16[256,2048]{1,0:T(8,128)(2,1)}, u32[]{:S(2)}, u32[]{:S(2)}) collective-permute-start(bf16[256,2048]{1,0:T(8,128)(2,1)S(1)} %add_convert_fusion.1.refs_1_), channel_id=1, source_target_pairs={{0,2},{1,3},{2,0},{3,1},{4,6},{5,7},{6,4},{7,5},{8,10},{9,11},{10,... | collective-permute-start | bytes 3145736 | tf_op jit(solution)/shard_map/ppermute | solution.py:42
  489.4 24.4 %collective-permute-start.65 = (bf16[256,2048]{1,0:T(8,128)(2,1)S(1)}, bf16[256,2048]{1,0:T(8,128)(2,1)}, u32[]{:S(2)}, u32[]{:S(2)}) collective-permute-start(bf16[256,2048]{1,0:T(8,128)(2,1)S(1)} %add_convert_fusion.1.refs_1_), channel_id=1, source_target_pairs={{0,1},{1,0},{2,3},{3,2},{4,5},{5,4},{6,7},{7,6},{8,9},{9,8},{10,11... | collective-permute-start | bytes 3145736 | tf_op jit(solution)/shard_map/ppermute | solution.py:42
  518.3 30.5 %collective-permute-start.69 = (bf16[256,2048]{1,0:T(8,128)(2,1)S(1)}, bf16[256,2048]{1,0:T(8,128)(2,1)S(1)}, u32[]{:S(2)}, u32[]{:S(2)}) collective-permute-start(bf16[256,2048]{1,0:T(8,128)(2,1)S(1)} %add_convert_fusion), channel_id=1, source_target_pairs={{0,2},{1,3},{2,0},{3,1},{4,6},{5,7},{6,4},{7,5},{8,10},{9,11},{10,... | collective-permute-start | bytes 3145736 | tf_op jit(solution)/shard_map/ppermute | solution.py:42
  563.8 25.6 %collective-permute-start.78 = (bf16[256,2048]{1,0:T(8,128)(2,1)}, bf16[256,2048]{1,0:T(8,128)(2,1)S(1)}, u32[]{:S(2)}, u32[]{:S(2)}) collective-permute-start(bf16[256,2048]{1,0:T(8,128)(2,1)} %own_rows.5.refs_1_), channel_id=1, source_target_pairs={{0,2},{1,3},{2,0},{3,1},{4,6},{5,7},{6,4},{7,5},{8,10},{9,11},{10,... | collective-permute-start | bytes 3145736 | tf_op jit(solution)/shard_map/ppermute | solution.py:42
  (147 other events, 2105.5 us)

commit v4 on v3

--- a/solution.py
+++ b/solution.py
@@ -103,8 +103,8 @@
 
     def step(self):
         if self.ringed:
-            self.settle()
             for lane, way in zip(self.lanes, self.ways):
+                (lane[-1],) = self.clock.wait(lane[-1])
                 lane.append(lax.ppermute(lane[-1], ("dp", "seq"), way))
 
     def pieces(self):
@@ -175,6 +175,47 @@
     return jnp.concatenate(out, axis=0).astype(bf16)
 
 
+def tables_body(seq, lengths, here, ladder, cos_q, sin_q, cos_k, sin_k, q_doc, doc_col, doc_row, last, before, after):
+    rows, ext = q_doc.shape[1], doc_row.shape[1]
+    ends = [lengths[0]]
+    for i in range(1, lengths.shape[0]):
+        ends.append(ends[-1] + lengths[i])
+
+    def document(at):
+        doc, start = 0, 0
+        for end in ends:
+            past = at >= end
+            doc = doc + past.astype(i32)
+            start = jnp.where(past, end, start)
+        return jnp.where(at >= 0, doc, -1), at - start
+
+    def angles(relative, cos, sin):
+        angle = ladder[...] * relative.astype(f32)
+        cos[...] = jnp.cos(angle)
+        sin[...] = jnp.sin(angle)
+
+    def passing(block):
+        ahead = rows * block - WIN - 1
+        return (document(ahead)[0] == document(ahead + rows)[0]).astype(f32)
+
+    first = here[0] * rows
+    q_doc[...], relative = document(first + lax.broadcasted_iota(i32, (1, rows), 1))
+    angles(relative, cos_q, sin_q)
+    index = lax.broadcasted_iota(i32, (1, ext), 1)
+    doc, relative = document(first - WIN + index)
+    doc_row[...] = jnp.where(index < rows + WIN, doc, -2)
+    angles(relative, cos_k, sin_k)
+    index = lax.broadcasted_iota(i32, (ext, 1), 0)
+    doc_col[...] = jnp.where(index < rows + WIN, document(first - WIN + index)[0], -2)
+    for i in range(last.shape[0]):
+        last[i] = document(first - WIN - 1 + CHUNK * i)[0]
+    earlier = later = jnp.float32(1.0)
+    for by in range(seq - 1):
+        before[by], after[by] = earlier, later
+        earlier = earlier * passing(jnp.maximum(here[0] - by - 1, 0))
+        later = later * passing(jnp.minimum(here[0] + by + 1, seq - 1))
+
+
 def norm_body(tokens, halo, gain, downs, normed, low, held, sems):
     rows, window = tokens.shape[0], halo.shape[0]
     part = rows // 4
@@ -198,8 +239,9 @@
         low[first:last, :] = nn(out, downs[...])
 
 
-def pack_body(units, gate, up, down, q_up, k_up, v_up, map_q, map_k, *outs):
-    packed, (ups, twice, maps_q, maps_k) = outs[:-4], outs[-4:]
+def pack_body(units, gate, up, down, q_up, k_up, v_up, map_q, map_k, o_up, *outs):
+    packed, (ups, twice, maps_q, maps_k, o_up_out) = outs[:-5], outs[-5:]
+    o_up_out[...] = o_up[...]
     at = 0
     for size, out in zip(units, packed):
         out[:, :size] = gate[:, at : at + size]
@@ -601,10 +643,9 @@
 
 
 def adapters_body(
-    dims, nat, g_q, g_own, g_halo, cos, sin, ups, low, normed, lowered, att, up_product, g_map_q, g_map_k, *rest
+    dims, g_q, g_own, g_halo, cos, sin, ups, low, normed, g_o_up, g_o_down, g_map_q, g_map_k, *outs
 ):
     rows, window, head, rank = dims
-    branch, (by_head, shared) = rest[:4], rest[4:]
     half = g_own.shape[0] // 2
     kv = keys_values(g_own[...], g_halo[...], cos[...], sin[...], 1.0)
     q_width = g_q.shape[1]
@@ -618,26 +659,62 @@
     low_halves = halves(low[...], 1)
     g_q_up = joined(tn(g_q[...], low_halves), 1)[:, :rank]
     g_kv_up = joined(tn(kv, low_halves), 1)
-    g_o_down = joined(tn(att[...], halves(up_product[...], 1)), 1)
-    by_head[...] = jnp.zeros(by_head.shape, f32)
+    if len(outs) == 1:
+        (slabs,) = outs
+        slabs[...] = jnp.zeros(slabs.shape, f32)
+        tall = slabs.shape[2]
+    else:
+        by_head, shared = outs
+        by_head[...] = jnp.zeros(by_head.shape, f32)
+
+    def put(h, first, x):
+        if len(outs) == 2:
+            by_head[h, :, first : first + x.shape[1]] = x
+            return
+        for r in range(slabs.shape[0]):
+            slabs[r, h, :, first : first + x.shape[1]] = x[r * tall : (r + 1) * tall]
+
+    def put_shared(first, x):
+        if len(outs) == 2:
+            shared[first : first + x.shape[0], :] = x
+            return
+        wide = x.shape[1] // slabs.shape[0] // 128
+        for i in range(x.shape[0] // tall):
+            for r in range(slabs.shape[0]):
+                for j in range(wide):
+                    at = (r * wide + j) * 128
+                    tile = x[i * tall : (i + 1) * tall, at : at + 128]
+                    slabs[r, q_heads + kv_heads + (first // tall + i) * wide + j] = tile
+
     q_heads, kv_heads = q_width // head, half // head
     group = q_heads // kv_heads
     for h in range(q_heads):
         mine, at = slice(h * head, (h + 1) * head), (h % group) * head
-        by_head[h, :, :head] = g_map_q[h // group, at : at + head, at : at + head]
-        by_head[h, :, head : head + rank] = g_q_up[mine]
-        by_head[h, :, head + rank : head + 2 * rank] = g_o_down[mine]
+        put(h, 0, g_map_q[h // group, at : at + head, at : at + head])
+        put(h, head, g_q_up[mine])
+        put(h, head + rank, g_o_down[mine, :])
     for h in range(kv_heads):
         mine = slice(h * head, (h + 1) * head)
-        by_head[q_heads + h, :, :head] = g_map_k[mine, mine]
-        by_head[q_heads + h, :, head : head + rank] = g_kv_up[mine, rank : 2 * rank]
-        by_head[q_heads + h, :, head + rank : head + 2 * rank] = g_kv_up[half + h * head : half + (h + 1) * head, 2 * rank :]
-    shared[: 3 * rank, :] = joined(tn(up_halves, normed[window : window + rows, :]), 0)
+        put(q_heads + h, 0, g_map_k[mine, mine])
+        put(q_heads + h, head, g_kv_up[mine, rank : 2 * rank])
+        put(q_heads + h, head + rank, g_kv_up[half + h * head : half + (h + 1) * head, 2 * rank :])
+    put_shared(0, joined(tn(up_halves, normed[window : window + rows, :]), 0))
+    put_shared(3 * rank, g_o_up[...])
+
+
+def adapter_o_body(nat, lowered, att, up_product, *rest):
+    branch, (g_o_up, g_o_down) = rest[:4], rest[4:]
+
+    def joined(x, axis):
+        one, other = jnp.split(x, 2, axis=axis)
+        return one + other
+
+    g_o_down[...] = joined(tn(att[...], halves(up_product[...], 1)), 1)
     o_up = 0.0
     for i, x in enumerate(branch):
         part = lowered[pl.ds(pl.multiple_of(nat[i] * x.shape[0], x.shape[0]), x.shape[0]), :]
         o_up = o_up + tn(halves(part, 1), x[...])
-    shared[3 * rank :, :] = joined(o_up, 0)
+    g_o_up[...] = joined(o_up, 0)
 
 
 def keys_values(own, halo, cos, sin, last):
@@ -648,7 +725,7 @@
 
 def gn_body(n_pieces, offsets, nat, g_q, g_own, g_halo, cos, sin, ups, downs, *rest):
     pieces = rest[:n_pieces]
-    part0, part1, held, sems = rest[n_pieces:]
+    parts, (held, sems) = rest[n_pieces:-2], rest[-2:]
     step = pl.program_id(0)
 
     @pl.when(step == 0)
@@ -656,10 +733,10 @@
         load_pieces(pieces, offsets, held, sems)
 
     q_width = g_q.shape[1]
-    kv = keys_values(g_own[...], g_halo[...], cos[...], sin[...], (nat[4 + step] == 3).astype(f32))
+    kv = keys_values(g_own[...], g_halo[...], cos[...], sin[...], (nat[3 - step] == 3).astype(f32))
     up = nn(g_q[...], ups[:q_width]) + nn(kv, ups[q_width:])
     total = nt(g_q[...], held[:, :q_width]) + nt(kv, held[:, q_width:])
-    store_at(step, total + nn(halves(up, 1), downs[...]), (part0, part1))
+    store_at(step, total + nn(halves(up, 1), downs[...]), parts)
 
 
 def rms_factor(x):
@@ -780,8 +857,6 @@
 
     core, far = lax.axis_index("tensor") % 2, lax.axis_index("tensor") // 2
     nat = jnp.stack([core * 2 + far, (1 - core) * 2 + far, core * 2 + 1 - far, (1 - core) * 2 + 1 - far]).astype(i32)
-    turned_far = jnp.concatenate([nat, nat[3:], nat[2:3]])
-    turned_near = jnp.concatenate([nat, nat[1:2], nat[:1]])
 
     clock = Clock()
     pack = lambda q, k, v, o: jnp.concatenate([q, k, v, o.T], axis=1)
@@ -793,52 +868,34 @@
 
     def turn(part):
         for chain in chains[part]:
-            chain.settle()
-        for chain in chains[part]:
             chain.step()
 
 
-    lengths = sequence_lengths[0]
-    ends = jnp.cumsum(lengths)
-    first_row = here * rows
-
-    def docs_of(at):
-        return jnp.where(at >= 0, jnp.sum((at[:, None] >= ends[None, :]).astype(i32), axis=1), -1)
-
-    def angles_of(at):
-        doc = docs_of(at)
-        starts = ends - lengths
-        start = jnp.sum(jnp.where(doc[:, None] == jnp.arange(lengths.shape[0])[None, :], starts[None, :], 0), axis=1)
-        ladder = jnp.arange(head // 2).astype(f32)
-        inverse = jnp.exp(ladder * (-2.0 * math.log(rope_base) / head))
-        angles = inverse[:, None] * (at - start).astype(f32)[None, :]
-        return jnp.cos(angles), jnp.sin(angles)
-
-    q_at = first_row + jnp.arange(rows)
-    k_index = jnp.arange(ext)
-    k_at = first_row - WIN + k_index
-    q_doc = docs_of(q_at)[None, :]
-    k_doc = jnp.where(k_index < rows + WIN, docs_of(k_at), -2)
-    doc_col, doc_row = k_doc[:, None], k_doc[None, :]
-    last_docs = docs_of(first_row - WIN - 1 + CHUNK * jnp.arange(chunks + 1))
-    block_docs = docs_of(rows * jnp.arange(seq + 1) - WIN - 1)
-    passes = (block_docs[:-1] == block_docs[1:]).astype(f32)
-
-    halo = shifted(tokens[rows - WIN :], "seq", 1)
-    cos_q, sin_q = angles_of(q_at)
-    cos_k, sin_k = angles_of(k_at)
-    cos_q, sin_q, cos_k, sin_k = clock.wait(cos_q, sin_q, cos_k, sin_k)
-    passed_before, passed_after = [jnp.ones((), f32)], [jnp.ones((), f32)]
-    for by in range(1, seq - 1):
-        passed_before.append(passed_before[-1] * passes[jnp.maximum(here - by, 0)])
-        passed_after.append(passed_after[-1] * passes[jnp.minimum(here + by, seq - 1)])
-    passed_before, passed_after = jnp.stack(passed_before), jnp.stack(passed_after)
+    ladder = jnp.exp(jnp.arange(head // 2).astype(f32) * (-2.0 * math.log(rope_base) / head))[:, None]
+    tables = [((head // 2, rows), f32)] * 2 + [((head // 2, ext), f32)] * 2
+    tables += [((1, rows), i32), ((ext, 1), i32), ((1, ext), i32)]
+    scalars = [((chunks + 1,), i32), ((seq - 1,), f32), ((seq - 1,), f32)]
+    cos_q, sin_q, cos_k, sin_k, q_doc, doc_col, doc_row, last_docs, passed_before, passed_after = pl.pallas_call(
+        lambda *refs: tables_body(seq, *refs),
+        grid_spec=pltpu.PrefetchScalarGridSpec(
+            num_scalar_prefetch=2,
+            grid=(1,),
+            in_specs=[whole(ladder.shape)],
+            out_specs=[whole(x) for x, _ in tables] + [pl.BlockSpec(memory_space=pltpu.SMEM)] * 3,
+        ),
+        out_shape=[jax.ShapeDtypeStruct(x, d) for x, d in tables + scalars],
+        compiler_params=params(32),
+        cost_estimate=SMALL,
+        name="tables",
+    )(sequence_lengths[0], here[None].astype(i32), ladder)
     q_doc, doc_col, doc_row, last_docs, passed_before, passed_after = clock.wait(
         q_doc, doc_col, doc_row, last_docs, passed_before, passed_after
     )
     attn_chain.step()
+
+    halo = shifted(clock.tie(tokens)[rows - WIN :], "seq", 1)
+    attn_chain.step()
     (halo,) = clock.wait(halo)
-    attn_chain.step()
     gain_attn = attention_norm_gain.astype(f32)[None, :]
     gain_mlp = feedforward_norm_gain.astype(f32)[None, :]
     downs = jnp.concatenate([query_adapter_down, key_adapter_down, value_adapter_down], axis=1)
@@ -861,13 +918,14 @@
     all_units = [x for part in FFN_UNITS for x in part]
     pack_in = (
         gate_weight, up_weight, down_weight, query_adapter_up, key_adapter_up, value_adapter_up,
-        feature_map_query, feature_map_key,
+        feature_map_query, feature_map_key, output_adapter_up,
     )
     pack_out = [(gate_weight.shape[0], 3 * x) for x in all_units] + [
         (q_width + 2 * kv_width, 3 * rank),
         (q_width + 2 * kv_width, 6 * rank),
         (kv_heads, group * head, group * head),
         (kv_width, kv_width),
+        (model, rank),
     ]
     packed = pl.pallas_call(
         lambda *refs: pack_body(all_units, *refs),
@@ -882,7 +940,7 @@
         cost_estimate=SMALL,
         name="pack",
     )(clock.tie(gate_weight), *pack_in[1:])
-    *packed, ups, ups_twice, maps_q, maps_k = clock.wait(*packed)
+    *packed, ups, ups_twice, maps_q, maps_k, o_up = clock.wait(*packed)
     chains = [[Chain(clock, 1, lambda x: x, packed[2 * i]), Chain(clock, -1, lambda x: x, packed[2 * i + 1])] for i in range(2)]
     for _ in range(ring - 5):
         attn_chain.step()
@@ -1115,7 +1173,7 @@
             cost_estimate=SMALL,
             name="project_back",
         )(
-            clock.tie(offsets), nat, last_docs[:1], output_adapter_up, o_down_t, att_t, totals, phi_q, q_doc,
+            clock.tie(offsets), nat, last_docs, o_up, o_down_t, att_t, totals, phi_q, q_doc,
             *quarters, *attn_pieces, *earlier,
         )
 
@@ -1203,54 +1261,68 @@
 
     g_own, g_halo, g_map_k = clock.wait(g_own, g_halo, g_map_k)
     g_halo = shifted(g_halo, "seq", -1)
-    (g_halo,) = clock.wait(g_halo)
+    o_in = (lowered, att, up_product, *branch)
+    g_o_up, g_o_down = pl.pallas_call(
+        adapter_o_body,
+        grid_spec=pltpu.PrefetchScalarGridSpec(
+            num_scalar_prefetch=1,
+            grid=(1,),
+            in_specs=[whole(x.shape) for x in o_in],
+            out_specs=[whole((rank, model)), whole((q_width, rank))],
+        ),
+        out_shape=[jax.ShapeDtypeStruct((rank, model), f32), jax.ShapeDtypeStruct((q_width, rank), f32)],
+        compiler_params=params(BIG),
+        cost_estimate=SMALL,
+        name="adapter_o",
+    )(clock.tie(nat), *o_in)
+    g_o_up, g_o_down, g_halo = clock.wait(g_o_up, g_o_down, g_halo)
 
     downs_t = jnp.concatenate([downs.T, downs.T], axis=0)
 
-    def gn_part(which):
-        by_rows = lambda w: pl.BlockSpec((quarter, w), lambda i, off, nat: (nat[4 + i], 0))
-        by_columns = lambda r: pl.BlockSpec((r, quarter), lambda i, off, nat: (0, nat[4 + i]))
-        return pl.pallas_call(
-            lambda *refs: gn_body(n_pieces, *refs),
-            grid_spec=pltpu.PrefetchScalarGridSpec(
-                num_scalar_prefetch=2,
-                grid=(2,),
-                in_specs=[
-                    by_rows(q_width),
-                    by_columns(2 * kv_width),
-                    whole(g_halo.shape),
-                    by_columns(head // 2),
-                    by_columns(head // 2),
-                    whole(ups.shape),
-                    whole(downs_t.shape),
-                ]
-                + [ANY] * n_pieces,
-                out_specs=[whole((quarter, model))] * 2,
-                scratch_shapes=[held_qkv, sems],
-            ),
-            out_shape=[one_quarter, one_quarter],
-            compiler_params=params(BIG),
-            cost_estimate=SMALL,
-            name="norm_back",
-        )(clock.tie(offsets), which, g_q, g_own, g_halo, cos_q, sin_q, ups, downs_t, *attn_pieces)
-
-    gn_far0, gn_far1 = gn_part(turned_far)
-    (gn_far0,) = clock.wait(gn_far0)
-    out_across, out_beside, gn_far0 = clock.wait(out_across, out_beside, gn_far0)
-    beside = exchange(gn_far0, "tensor", 1)
-    (beside,) = clock.wait(beside)
+    by_rows = lambda w: pl.BlockSpec((quarter, w), lambda i, off, nat: (nat[3 - i], 0))
+    by_columns = lambda r: pl.BlockSpec((r, quarter), lambda i, off, nat: (0, nat[3 - i]))
+    gn_parts = pl.pallas_call(
+        lambda *refs: gn_body(n_pieces, *refs),
+        grid_spec=pltpu.PrefetchScalarGridSpec(
+            num_scalar_prefetch=2,
+            grid=(4,),
+            in_specs=[
+                by_rows(q_width),
+                by_columns(2 * kv_width),
+                whole(g_halo.shape),
+                by_columns(head // 2),
+                by_columns(head // 2),
+                whole(ups.shape),
+                whole(downs_t.shape),
+            ]
+            + [ANY] * n_pieces,
+            out_specs=[whole((quarter, model))] * 4,
+            scratch_shapes=[held_qkv, sems],
+        ),
+        out_shape=[one_quarter] * 4,
+        compiler_params=params(BIG),
+        cost_estimate=SMALL,
+        name="norm_back",
+    )(clock.tie(offsets), nat, g_q, g_own, g_halo, cos_q, sin_q, ups, downs_t, *attn_pieces)
+    gn_far0, gn_far1, gn_near0, gn_near1 = clock.wait(*gn_parts)
+    out_across, out_beside, gn_far0, gn_near0 = clock.wait(out_across, out_beside, gn_far0, gn_near0)
+    beside, beside_near = exchange(gn_far0, "tensor", 1), exchange(gn_near0, "tensor", 1)
+    beside, beside_near = clock.wait(beside, beside_near)
     gn_far = clock.tie((gn_far1.astype(f32) + beside.astype(f32)).astype(bf16))
     across = exchange(gn_far, "tensor", 2)
 
-    adapters_in = (g_q, g_own, g_halo, cos_q, sin_q, ups, low[WIN : WIN + rows], normed, lowered, att, up_product, g_map_q, g_map_k, *branch)
-    sizes = [
-        ((heads + kv_heads, head, 2 * head), f32),
-        ((4 * rank, model), f32),
-    ]
-    by_head, shared = pl.pallas_call(
+    adapters_in = (g_q, g_own, g_halo, cos_q, sin_q, ups, low[WIN : WIN + rows], normed, g_o_up, g_o_down, g_map_q, g_map_k)
+    tall = head // ring
+    tiles = 4 * rank // 8 * (model // ring // 128)
+    in_tiles = tall == 8 and rank == 8 and model // ring % 128 == 0 and 2 * head == 128
+    if in_tiles:
+        sizes = [((ring, heads + kv_heads + tiles, tall, 2 * head), f32)]
+    else:
+        sizes = [((heads + kv_heads, head, 2 * head), f32), ((4 * rank, model), f32)]
+    parts = pl.pallas_call(
         lambda *refs: adapters_body((rows, WIN, head, rank), *refs),
         grid_spec=pltpu.PrefetchScalarGridSpec(
-            num_scalar_prefetch=1,
+            num_scalar_prefetch=0,
             grid=(1,),
             in_specs=[whole(x.shape) for x in adapters_in],
             out_specs=[whole(x) for x, _ in sizes],
@@ -1259,60 +1331,59 @@
         compiler_params=params(BIG),
         cost_estimate=SMALL,
         name="adapters",
-    )(clock.tie(nat), *adapters_in)
-    by_head, shared = clock.wait(by_head, shared)
-
-    by_head = by_head.reshape(heads + kv_heads, ring, head // ring, 2 * head).transpose(1, 0, 2, 3)
-    shared = shared.reshape(4 * rank, ring, model // ring).transpose(1, 0, 2)
-    by_head, shared = clock.wait(by_head, shared)
-
-    def halved(x, axis, half, bit, over=0):
+    )(clock.tie(adapters_in[0]), *adapters_in[1:])
+    if not in_tiles:
+        parts = [
+            parts[0].reshape(heads + kv_heads, ring, tall, 2 * head).transpose(1, 0, 2, 3),
+            parts[1].reshape(4 * rank, ring, model // ring).transpose(1, 0, 2),
+        ]
+    parts = clock.wait(*parts)
+
+    def halved(x, axis, half, bit, over=0, sent_as=f32):
         x = x.reshape(x.shape[:over] + (2, half) + x.shape[over + 1 :])
         send = lax.dynamic_index_in_dim(x, 1 - bit, over, keepdims=False)
-        return lax.dynamic_index_in_dim(x, bit, over, keepdims=False), exchange(send, axis, half)
+        return lax.dynamic_index_in_dim(x, bit, over, keepdims=False), exchange(send.astype(sent_as), axis, half)
 
     def summed_over(axis, size, xs):
         while size > 1:
             half = size // 2
-            both = [halved(x, axis, half, (lax.axis_index(axis) // half) % 2) for x in xs]
+            both = [halved(x, axis, half, (lax.axis_index(axis) // half) % 2, 0, bf16) for x in xs]
             coming = clock.wait(*[coming for _, coming in both])
-            xs = [kept + x for (kept, _), x in zip(both, coming)]
+            xs = [kept + x.astype(f32) for (kept, _), x in zip(both, coming)]
             size = half
             yield xs
 
-    parts = [by_head, shared]
     dp = ring // seq
     parts = [x.reshape((dp, seq) + x.shape[1:]) for x in parts]
     for parts in summed_over("dp", dp, parts):
         pass
-    gn_near0, gn_near1 = gn_part(turned_near)
-    gn_near0, gn_near1 = clock.wait(gn_near0, gn_near1)
-    across, gn_near0 = clock.wait(across, gn_near0)
-    beside = exchange(gn_near0, "tensor", 1)
-    (beside,) = clock.wait(beside)
+    along_seq = summed_over("seq", seq, clock.wait(*[x[0] for x in parts]))
+    parts = next(along_seq)
+    (across,) = clock.wait(across)
     (grad_rows,) = on_own_rows(
-        grad_tokens_body, clock.tie(nat), gn_near1, beside, across, tokens, (grad_hidden,), gain_attn, (bf16,)
+        grad_tokens_body, clock.tie(nat), gn_near1, beside_near, across, tokens, (grad_hidden,), gain_attn, (bf16,)
     )
     (grad_rows,) = clock.wait(grad_rows)
     across, beside = exchange(grad_rows, "tensor", 2), exchange(grad_rows, "tensor", 1)
     out_last = clock.tie(exchange(out_across, "tensor", 1))
-    along_seq = summed_over("seq", seq, clock.wait(*[x[0] for x in parts]))
     (beside,) = clock.wait(beside)
     grad_tokens = clock.tie(place([grad_rows, beside], 0, nat, f32))
     for parts in along_seq:
         pass
-    by_head, shared = [x[0] for x in parts]
-    shared = shared.reshape(4 * rank, 2, 2, model // ring // 4)
+    by_head, shared = parts[0][0], parts[-1][0]
+    if in_tiles:
+        by_head, shared = by_head[: heads + kv_heads], by_head[heads + kv_heads :]
+        shared = shared.reshape(4 * rank // 8, -1, 8, 128).transpose(0, 2, 1, 3)
     kept, sent = halved(shared.reshape(4 * rank, 4, -1), "tensor", 2, far, 1)
     shared = kept.reshape(4 * rank, 2, -1)
     sent = sent.reshape(4 * rank, 2, -1)
     block_out = clock.tie(place([out_rows, out_beside, out_across, out_last], 0, nat, bf16))
-    across, sent = clock.wait(across, sent)
+    (across,) = clock.wait(across)
     last = exchange(across, "tensor", 1)
-    kept, sent = halved(shared + sent, "tensor", 1, core, 1)
-    last, sent = clock.wait(last, sent)
-    shared = (kept + sent).reshape(4 * rank, -1).T
+    kept, sent = halved(shared + clock.tie(sent), "tensor", 1, core, 1)
+    (last,) = clock.wait(last)
     grad_tokens = clock.tie(place([across, last], 2, nat, f32, (grad_tokens,)))
+    shared = (kept + clock.tie(sent)).reshape(4 * rank, -1).T
     of_q, of_kv = by_head[:heads], by_head[heads:]
     first, second = slice(head, head + rank), slice(head + rank, head + 2 * rank)
     out = [of_q[..., first], of_kv[..., first], of_kv[..., second], of_q[..., second], of_q[..., :head], of_kv[..., :head]]

time: 607 us -> 595 us (0.980)
  other arithmetic: 25.8 us -> 18 us
    ppermute x8, waiting for transfers between devices: 16.1 us -> 4.96 us  [shifted(): lax.ppermute(x, axis, [(i, i + by) for i in range(count) if 0 <= i + by <...]
    unnamed x202 -> x211, local copies, waits for them, and re-layouts: 16.4 us -> 22.7 us
    ppermute x32 -> x29, waiting for transfers between devices: 56.7 us -> 61.6 us  [exchange(): return lax.ppermute(x, axis, [(i, i ^ bit) for i in range(count)])]
    pallas_call x2 -> x3, Pallas kernels: 16.9 us -> 19.9 us  [the longest x1 12.5 us: per_device(): pl.pallas_call(lambda *refs: gn_body(n_pieces, *refs), grid_spec=pltpu.Pr...]
    ppermute x32 -> x29, starting transfers between devices: 21.8 us -> 20.4 us  [exchange(): return lax.ppermute(x, axis, [(i, i ^ bit) for i in range(count)])]
  transfers between devices with their start and end apart: 82 -> 79, of which waited for: 47 -> 41; matrix products, arithmetic and copies ran while one was open for 5% -> 3% of each run, Pallas kernels for 37% -> 38%
where the time goes in v4:
time: 595 us; the launch traced here: 587 us
  Pallas kernels  254 us (43%)
  waiting for transfers between devices  195 us (33%)
  starting transfers between devices  86.8 us (15%)
  local copies, waits for them, and re-layouts  30.2 us (5%)
  other arithmetic  18 us (3%)
    ppermute x42, waiting for transfers between devices, step(): lane.append(lax.ppermute(lane[-1], ('dp', 'seq'), way))  128 us
    pallas_call x6, Pallas kernels, ffn(): pl.pallas_call(lambda *refs: ffn_body(sizes, units, bool(sums), last, *re...  110 us
    ppermute x29, waiting for transfers between devices, exchange(): return lax.ppermute(x, axis, [(i, i ^ bit) for i in range(count)])  61.6 us
    ppermute x42, starting transfers between devices, step(): lane.append(lax.ppermute(lane[-1], ('dp', 'seq'), way))  47.5 us
    unnamed x211, local copies, waits for them, and re-layouts  22.7 us
    ppermute x29, starting transfers between devices, exchange(): return lax.ppermute(x, axis, [(i, i ^ bit) for i in range(count)])  20.4 us
    ppermute x8, starting transfers between devices, shifted(): lax.ppermute(x, axis, [(i, i + by) for i in range(count) if 0 <= i + by <...  18.9 us
    pallas_call x1, Pallas kernels, per_device(): pl.pallas_call(lambda *refs: backward_body((kv_heads, group, head, chunks...  17.2 us
  transfers between devices with their start and end apart: 79, of which 41 were waited for; matrix products, arithmetic and copies ran while one was open for 3% of the time, Pallas kernels for 38%

profile of v4, /device:TPU:0, one launch (start us, length us, event | category | flops | bytes accessed | tf_op | source)
XLA Modules:
  0.0 586.6 jit_solution(2407114096120809973)
XLA Ops:
  31.1 8.3 %norm.1 = (bf16[1152,2048]{1,0:T(8,128)(2,1)}, f32[1152,24]{1,0:T(8,128)}) custom-call(bf16[1024,2048]{1,0:T(8,128)(2,1)} %tokens.4, bf16[64,2048]{1,0:T(8,128)(2,1)} %copy-done.82, f32[1,2048]{1,0:T(1,128)} %bitcast.62, bf16[2048,24]{1,0:T(8,128)(2,1)} %copy.56.downs), custom_call_target="tpu_custom_call" | custom-call | flops 1 | bytes 1 | tf_op jit(solution)/shard_map/norm/pallas_call | solution.py:902
  52.5 7.2 %collective-permute-done.8.refs_17_.refs_10_.refs_16_.refs_14_ = bf16[128,1280]{1,0:T(8,128)(2,1)S(1)} collective-permute-done((bf16[128,1280]{1,0:T(8,128)(2,1)S(1)}, bf16[128,1280]{1,0:T(8,128)(2,1)S(1)}, u32[]{:S(2)}, u32[]{:S(2)}) %collective-permute-start.8) | collective-permute-done | bytes 327712 | tf_op jit(solution)/shard_map/ppermute | solution.py:108
  62.4 6.9 %collective-permute-done.10.refs_18_.refs_11_.refs_17_.refs_15_ = bf16[128,1280]{1,0:T(8,128)(2,1)S(1)} collective-permute-done((bf16[128,1280]{1,0:T(8,128)(2,1)S(1)}, bf16[128,1280]{1,0:T(8,128)(2,1)S(1)}, u32[]{:S(2)}, u32[]{:S(2)}) %collective-permute-start.10) | collective-permute-done | bytes 327712 | tf_op jit(solution)/shard_map/ppermute | solution.py:108
  74.4 8.0 %collective-permute-done.14.refs_27_.refs_20_.refs_26_.refs_24_ = bf16[128,1280]{1,0:T(8,128)(2,1)S(1)} collective-permute-done((bf16[128,1280]{1,0:T(8,128)(2,1)S(1)}, bf16[128,1280]{1,0:T(8,128)(2,1)S(1)}, u32[]{:S(2)}, u32[]{:S(2)}) %collective-permute-start.14) | collective-permute-done | bytes 327712 | tf_op jit(solution)/shard_map/ppermute | solution.py:108
  86.3 16.9 %prep.1 = (bf16[512,1024]{1,0:T(8,128)(2,1)}, bf16[1024,1024]{1,0:T(8,128)(2,1)}, bf16[1152,128]{1,0:T(8,128)(2,1)}, bf16[128,1152]{1,0:T(8,128)(2,1)}, bf16[115...) custom-call(s32[16]{0:T(128)} %get-tuple-element.804.refs_0_, ...), custom_call_target="tpu_custom_call" | custom-call | flops 1 | bytes 1 | tf_op jit(solution)/shard_map/prep/pallas_call | solution.py:968
  118.3 10.5 %attend.1 = (bf16[1024,512]{1,0:T(8,128)(2,1)}, f32[512,1024]{1,0:T(8,128)}, f32[8,1024]{1,0:T(8,128)}, bf16[8,2,128,80]{3,2,1,0:T(8,128)(2,1)}) custom-call(s32[9]{0:T(128)} %copy-done.17, f32[3]{0:T(128)} %copy-done.20, bf16[512,1024]{1,0:T(8,128)(2,1)} %get-tuple-element.542.refs_2_.refs_1_, ...), custom_call_target="tpu_custom_call" | custom-call | flops 1 | bytes 1 | tf_op jit(solution)/shard_map/attend/pallas_call | solution.py:987
  133.7 10.7 %project.1 = (bf16[256,2048]{1,0:T(8,128)(2,1)}, bf16[256,2048]{1,0:T(8,128)(2,1)}, bf16[256,2048]{1,0:T(8,128)(2,1)}, bf16[256,2048]{1,0:T(8,128)(2,1)}, f32[1024,8]{1,0:T(8,128)}) custom-call(s32[16]{0:T(128)} %get-tuple-element.804.refs_0_, s32[4]{0:T(128)} %pad_add_fusion.refs_1_.nat.refs_0_, bf16[1024,512]{1,0:T(8,128)(2,1)} %get-tuple-element.558.refs_2_.att, ...), custom_call_target="tpu_custom_call" | custom-call | flops 1 | bytes 1 | tf_op jit(solution)/shard_map/project/pallas_call | solution.py:1028
  152.3 13.4 %collective-permute-done.28.refs_9_ = bf16[256,1536]{1,0:T(8,128)(2,1)S(1)} collective-permute-done((bf16[256,1536]{1,0:T(8,128)(2,1)S(1)}, bf16[256,1536]{1,0:T(8,128)(2,1)S(1)}, u32[]{:S(2)}, u32[]{:S(2)}) %collective-permute-start.28) | collective-permute-done | bytes 786464 | tf_op jit(solution)/shard_map/ppermute | solution.py:108
  168.4 7.6 %collective-permute-done.26.across = bf16[256,2048]{1,0:T(8,128)(2,1)S(1)} collective-permute-done((bf16[256,2048]{1,0:T(8,128)(2,1)S(1)}, bf16[256,2048]{1,0:T(8,128)(2,1)S(1)}, u32[]{:S(2)}, u32[]{:S(2)}) %collective-permute-start.26) | collective-permute-done | bytes 1048608 | tf_op jit(solution)/shard_map/ppermute | solution.py:42
  190.2 16.4 %collective-permute-done.32.refs_11_ = bf16[256,1536]{1,0:T(8,128)(2,1)S(1)} collective-permute-done((bf16[256,1536]{1,0:T(8,128)(2,1)S(1)}, bf16[256,1536]{1,0:T(8,128)(2,1)S(1)}, u32[]{:S(2)}, u32[]{:S(2)}) %collective-permute-start.32) | collective-permute-done | bytes 786464 | tf_op jit(solution)/shard_map/ppermute | solution.py:108
  208.7 5.3 collective-permute-done.36.refs_4_
  214.0 11.8 %collective-permute-done.35.refs_12_ = bf16[256,1536]{1,0:T(8,128)(2,1)S(1)} collective-permute-done((bf16[256,1536]{1,0:T(8,128)(2,1)S(1)}, bf16[256,1536]{1,0:T(8,128)(2,1)S(1)}, u32[]{:S(2)}, u32[]{:S(2)}) %collective-permute-start.35) | collective-permute-done | bytes 786464 | tf_op jit(solution)/shard_map/ppermute | solution.py:108
  231.1 15.3 %feed_forward.6 = (f32[2,256,2048]{2,1,0:T(8,128)}, f32[2,256,2048]{2,1,0:T(8,128)}) custom-call(s32[8]{0:T(128)} %copy-done.97, s32[4]{0:T(128)} %pad_add_fusion.refs_1_.nat.refs_0_, bf16[1024,2048]{1,0:T(8,128)(2,1)} %cotangent.1, bf16[256,2048]{1,0:T(8,128)(2,1)} %copy-done.26, bf16[256,2048]{1,0:T(8,128)(2,1)} %copy-done.25, ...), custom_call_target="tpu_custom_call" | custom-call | flops 1 | bytes 1 | tf_op jit(solution)/shard_map/feed_forward/pallas_call | solution.py:1084
  250.2 15.3 %feed_forward.7 = (f32[2,256,2048]{2,1,0:T(8,128)}, f32[2,256,2048]{2,1,0:T(8,128)}) custom-call(s32[8]{0:T(128)} %copy-done.97, s32[4]{0:T(128)} %pad_add_fusion.refs_1_.nat.refs_0_, bf16[1024,2048]{1,0:T(8,128)(2,1)} %cotangent.1, bf16[256,2048]{1,0:T(8,128)(2,1)} %copy-done.24, bf16[256,2048]{1,0:T(8,128)(2,1)} %get-tuple-element.602.refs_4_, ...), custom_call_target="tpu_custom_call" | custom-call | flops 1 | bytes 1 | tf_op jit(solution)/shard_map/feed_forward/pallas_call | solution.py:1084
  269.6 16.2 %feed_forward.8 = (f32[2,256,2048]{2,1,0:T(8,128)}, f32[2,256,2048]{2,1,0:T(8,128)}) custom-call(s32[8]{0:T(128)} %copy-done.96, s32[4]{0:T(128)} %pad_add_fusion.refs_1_.nat.refs_0_, bf16[1024,2048]{1,0:T(8,128)(2,1)} %cotangent.1, bf16[256,2048]{1,0:T(8,128)(2,1)} %copy-done.26, bf16[256,2048]{1,0:T(8,128)(2,1)} %copy-done.25, ...), custom_call_target="tpu_custom_call" | custom-call | flops 1 | bytes 1 | tf_op jit(solution)/shard_map/feed_forward/pallas_call | solution.py:1084
  288.1 16.2 %feed_forward.9 = (f32[2,256,2048]{2,1,0:T(8,128)}, f32[2,256,2048]{2,1,0:T(8,128)}) custom-call(s32[8]{0:T(128)} %copy-done.96, s32[4]{0:T(128)} %pad_add_fusion.refs_1_.nat.refs_0_, bf16[1024,2048]{1,0:T(8,128)(2,1)} %cotangent.1, bf16[256,2048]{1,0:T(8,128)(2,1)} %copy-done.24, bf16[256,2048]{1,0:T(8,128)(2,1)} %get-tuple-element.602.refs_4_, ...), custom_call_target="tpu_custom_call" | custom-call | flops 1 | bytes 1 | tf_op jit(solution)/shard_map/feed_forward/pallas_call | solution.py:1084
  306.4 15.7 %collective-permute-done.47.refs_10_ = bf16[256,1536]{1,0:T(8,128)(2,1)S(1)} collective-permute-done((bf16[256,1536]{1,0:T(8,128)(2,1)S(1)}, bf16[256,1536]{1,0:T(8,128)(2,1)S(1)}, u32[]{:S(2)}, u32[]{:S(2)}) %collective-permute-start.47) | collective-permute-done | bytes 786464 | tf_op jit(solution)/shard_map/ppermute | solution.py:108
  324.1 15.7 %collective-permute-done.49.refs_11_ = bf16[256,1536]{1,0:T(8,128)(2,1)S(1)} collective-permute-done((bf16[256,1536]{1,0:T(8,128)(2,1)S(1)}, bf16[256,1536]{1,0:T(8,128)(2,1)S(1)}, u32[]{:S(2)}, u32[]{:S(2)}) %collective-permute-start.49) | collective-permute-done | bytes 786464 | tf_op jit(solution)/shard_map/ppermute | solution.py:108
  341.9 13.5 %collective-permute-done.51.refs_12_ = bf16[256,1536]{1,0:T(8,128)(2,1)S(1)} collective-permute-done((bf16[256,1536]{1,0:T(8,128)(2,1)S(1)}, bf16[256,1536]{1,0:T(8,128)(2,1)S(1)}, u32[]{:S(2)}, u32[]{:S(2)}) %collective-permute-start.51) | collective-permute-done | bytes 786464 | tf_op jit(solution)/shard_map/ppermute | solution.py:108
  357.7 23.5 %feed_forward.10 = (bf16[256,2048]{1,0:T(8,128)(2,1)}, bf16[256,2048]{1,0:T(8,128)(2,1)}, bf16[256,2048]{1,0:T(8,128)(2,1)}, bf16[256,2048]{1,0:T(8,128)(2,1)}) custom-call(s32[16]{0:T(128)} %get-tuple-element.698.refs_0_, s32[4]{0:T(128)} %pad_add_fusion.refs_1_.nat.refs_0_, bf16[1024,2048]{1,0:T(8,128)(2,1)} %cotangent.1, bf16[256,2048]{1,0:T(8,128)(2,1)} %copy-done.26, ...), custom_call_target="tpu_custom_call" | custom-call | flops 1 | bytes 1 | tf_op jit(solution)/shard_map/feed_forward/pallas_call | solution.py:1084
  387.3 23.7 %feed_forward.11 = (bf16[256,2048]{1,0:T(8,128)(2,1)}, bf16[256,2048]{1,0:T(8,128)(2,1)}, bf16[256,2048]{1,0:T(8,128)(2,1)}, bf16[256,2048]{1,0:T(8,128)(2,1)}) custom-call(s32[16]{0:T(128)} %get-tuple-element.698.refs_0_, s32[4]{0:T(128)} %pad_add_fusion.refs_1_.nat.refs_0_, bf16[1024,2048]{1,0:T(8,128)(2,1)} %cotangent.1, bf16[256,2048]{1,0:T(8,128)(2,1)} %copy-done.24, ...), custom_call_target="tpu_custom_call" | custom-call | flops 1 | bytes 1 | tf_op jit(solution)/shard_map/feed_forward/pallas_call | solution.py:1084
  415.0 5.6 own_rows.4
  424.4 8.5 %project_back.2 = (bf16[512,1024]{1,0:T(8,128)(2,1)}, f32[8,1024]{1,0:T(8,128)}, f32[1024,8]{1,0:T(8,128)}, f32[2,128,80]{2,1,0:T(8,128)}) custom-call(s32[16]{0:T(128)} %get-tuple-element.804.refs_0_, s32[4]{0:T(128)} %pad_add_fusion.refs_1_.nat.refs_0_, s32[9]{0:T(128)} %copy-done.17, bf16[2048,8]{1,0:T(8,128)(2,1)} %get-tuple-element.728.refs_3_, ...), custom_call_target="tpu_custom_call" | custom-call | flops 1 | bytes 1 | tf_op jit(solution)/shard_map/project_back/pallas_call | solution.py:1142
  437.0 10.6 %collective-permute-done.58.refs_9_.rest_2_ = bf16[256,2048]{1,0:T(8,128)(2,1)} collective-permute-done((bf16[256,2048]{1,0:T(8,128)(2,1)}, bf16[256,2048]{1,0:T(8,128)(2,1)}, u32[]{:S(2)}, u32[]{:S(2)}) %collective-permute-start.58) | collective-permute-done | bytes 1048608 | tf_op jit(solution)/shard_map/ppermute | solution.py:42
  452.0 8.4 %project_back.3 = (bf16[512,1024]{1,0:T(8,128)(2,1)}, f32[8,1024]{1,0:T(8,128)}, f32[1024,8]{1,0:T(8,128)}, f32[2,128,80]{2,1,0:T(8,128)}) custom-call(s32[16]{0:T(128)} %get-tuple-element.804.refs_0_, s32[4]{0:T(128)} %pad_add_fusion.refs_1_.nat.refs_0_, s32[9]{0:T(128)} %copy-done.17, ...), custom_call_target="tpu_custom_call", output_to_operand_aliasing={{0}: (27, {}), {1}: (28, {}), {2}: (29, {})} | custom-call | flops 1 | bytes 1 | tf_op jit(solution)/shard_map/project_back/pallas_call | solution.py:1142
  465.2 17.2 %attend_back.1 = (bf16[1024,512]{1,0:T(8,128)(2,1)}, f32[128,1152]{1,0:T(8,128)}, f32[128,1152]{1,0:T(8,128)}, f32[256,1152]{1,0:T(8,128)}, f32[2,256,256]{2,1,0:T(8,128)}) custom-call(s32[9]{0:T(128)S(1)} %copy-done.18, bf16[512,1024]{1,0:T(8,128)(2,1)} %get-tuple-element.542.refs_2_.refs_1_, bf16[1024,1024]{1,0:T(8,128)(2,1)} %get-tuple-element.543.refs_3_.refs_7_.refs_2_, ...), custom_call_target="tpu_custom_call" | custom-call | flops 1 | bytes 1 | tf_op jit(solution)/shard_map/attend_back/pallas_call | solution.py:1212
  491.4 5.2 adapter_o.1
  498.4 12.5 %norm_back.1 = (bf16[256,2048]{1,0:T(8,128)(2,1)}, bf16[256,2048]{1,0:T(8,128)(2,1)}, bf16[256,2048]{1,0:T(8,128)(2,1)}, bf16[256,2048]{1,0:T(8,128)(2,1)}) custom-call(s32[16]{0:T(128)} %get-tuple-element.804.refs_0_, s32[4]{0:T(128)} %pad_add_fusion.refs_1_.nat.refs_0_, bf16[1024,512]{1,0:T(8,128)(2,1)} %get-tuple-element.827.refs_2_.refs_0_, ...), custom_call_target="tpu_custom_call" | custom-call | flops 1 | bytes 1 | tf_op jit(solution)/shard_map/norm_back/pallas_call | solution.py:1284
  520.6 6.2 %adapters.1 = f32[8,18,8,128]{3,2,1,0:T(8,128)} custom-call(bf16[1024,512]{1,0:T(8,128)(2,1)} %get-tuple-element.827.refs_2_.refs_0_, f32[256,1024]{1,0:T(8,128)} %get-tuple-element.806.refs_3_.refs_1_, f32[256,128]{1,0:T(8,128)} %copy-done.78, f32[32,1024]{1,0:T(8,128)} %copy-done.2, f32[32,1024]{1,0:T(8,128)} %copy-done.4, ...), custom_call_target="tpu_custom_call" | custom-call | flops 1 | bytes 1 | tf_op jit(solution)/shard_map/adapters/pallas_call | solution.py:1322
  528.1 5.3 collective-permute-done.71
  544.7 5.2 own_rows.5.refs_1_
  564.5 11.2 %collective-permute-done.75.refs_1_ = bf16[256,2048]{1,0:T(8,128)(2,1)S(1)} collective-permute-done((bf16[256,2048]{1,0:T(8,128)(2,1)}, bf16[256,2048]{1,0:T(8,128)(2,1)S(1)}, u32[]{:S(2)}, u32[]{:S(2)}) %collective-permute-start.75) | collective-permute-done | bytes 1048608 | tf_op jit(solution)/shard_map/ppermute | solution.py:42
  (405 shorter events, 210.2 us)
Async XLA Ops:
  83.3 20.0 %collective-permute-start.16 = (bf16[256,1536]{1,0:T(8,128)(2,1)}, bf16[256,1536]{1,0:T(8,128)(2,1)}, u32[]{:S(2)}, u32[]{:S(2)}) collective-permute-start(bf16[256,1536]{1,0:T(8,128)(2,1)} %get-tuple-element.515.refs_5_), channel_id=1, source_target_pairs={{0,4},{4,8},{8,12},{12,28},{28,24},{24,20},{20,16},{16,0},{1,5},{5... | collective-permute-start | bytes 2359304 | tf_op jit(solution)/shard_map/ppermute | solution.py:108
  85.1 20.1 %collective-permute-start.15 = (bf16[256,1536]{1,0:T(8,128)(2,1)}, bf16[256,1536]{1,0:T(8,128)(2,1)}, u32[]{:S(2)}, u32[]{:S(2)}) collective-permute-start(bf16[256,1536]{1,0:T(8,128)(2,1)} %get-tuple-element.514.refs_5_), channel_id=1, source_target_pairs={{4,0},{8,4},{12,8},{28,12},{24,28},{20,24},{16,20},{0,16},{5,1},{9... | collective-permute-start | bytes 2359304 | tf_op jit(solution)/shard_map/ppermute | solution.py:108
  103.3 25.5 %collective-permute-start.18 = (bf16[256,1536]{1,0:T(8,128)(2,1)}, bf16[256,1536]{1,0:T(8,128)(2,1)S(1)}, u32[]{:S(2)}, u32[]{:S(2)}) collective-permute-start(bf16[256,1536]{1,0:T(8,128)(2,1)} %collective-permute-done.16.refs_6_), channel_id=1, source_target_pairs={{0,4},{4,8},{8,12},{12,28},{28,24},{24,20},{20,16},{16,0},{1,5},{5... | collective-permute-start | bytes 2359304 | tf_op jit(solution)/shard_map/ppermute | solution.py:108
  105.1 26.4 %collective-permute-start.17 = (bf16[256,1536]{1,0:T(8,128)(2,1)}, bf16[256,1536]{1,0:T(8,128)(2,1)S(1)}, u32[]{:S(2)}, u32[]{:S(2)}) collective-permute-start(bf16[256,1536]{1,0:T(8,128)(2,1)} %collective-permute-done.15.refs_6_), channel_id=1, source_target_pairs={{4,0},{8,4},{12,8},{28,12},{24,28},{20,24},{16,20},{0,16},{5,1},{9... | collective-permute-start | bytes 2359304 | tf_op jit(solution)/shard_map/ppermute | solution.py:108
  145.1 20.6 %collective-permute-start.28 = (bf16[256,1536]{1,0:T(8,128)(2,1)S(1)}, bf16[256,1536]{1,0:T(8,128)(2,1)S(1)}, u32[]{:S(2)}, u32[]{:S(2)}) collective-permute-start(bf16[256,1536]{1,0:T(8,128)(2,1)S(1)} %collective-permute-done.23.refs_8_), channel_id=1, source_target_pairs={{0,4},{4,8},{8,12},{12,28},{28,24},{24,20},{20,16},{16,0},{1,5},{5... | collective-permute-start | bytes 2359304 | tf_op jit(solution)/shard_map/ppermute | solution.py:108
  147.1 19.5 %collective-permute-start.27 = (bf16[256,1536]{1,0:T(8,128)(2,1)S(1)}, bf16[256,1536]{1,0:T(8,128)(2,1)}, u32[]{:S(2)}, u32[]{:S(2)}) collective-permute-start(bf16[256,1536]{1,0:T(8,128)(2,1)S(1)} %collective-permute-done.22.refs_8_), channel_id=1, source_target_pairs={{4,0},{8,4},{12,8},{28,12},{24,28},{20,24},{16,20},{0,16},{5,1},{9... | collective-permute-start | bytes 2359304 | tf_op jit(solution)/shard_map/ppermute | solution.py:108
  150.7 25.3 %collective-permute-start.26 = (bf16[256,2048]{1,0:T(8,128)(2,1)S(1)}, bf16[256,2048]{1,0:T(8,128)(2,1)S(1)}, u32[]{:S(2)}, u32[]{:S(2)}) collective-permute-start(bf16[256,2048]{1,0:T(8,128)(2,1)S(1)} %add_convert_fusion.4), channel_id=1, source_target_pairs={{0,2},{1,3},{2,0},{3,1},{4,6},{5,7},{6,4},{7,5},{8,10},{9,11},{10,... | collective-permute-start | bytes 3145736 | tf_op jit(solution)/shard_map/ppermute | solution.py:42
  165.7 19.2 %collective-permute-start.30 = (bf16[256,1536]{1,0:T(8,128)(2,1)S(1)}, bf16[256,1536]{1,0:T(8,128)(2,1)S(1)}, u32[]{:S(2)}, u32[]{:S(2)}) collective-permute-start(bf16[256,1536]{1,0:T(8,128)(2,1)S(1)} %collective-permute-done.28.refs_9_), channel_id=1, source_target_pairs={{0,4},{4,8},{8,12},{12,28},{28,24},{24,20},{20,16},{16,0},{1,5},{5... | collective-permute-start | bytes 2359304 | tf_op jit(solution)/shard_map/ppermute | solution.py:108
  166.6 20.1 %collective-permute-start.29 = (bf16[256,1536]{1,0:T(8,128)(2,1)}, bf16[256,1536]{1,0:T(8,128)(2,1)}, u32[]{:S(2)}, u32[]{:S(2)}) collective-permute-start(bf16[256,1536]{1,0:T(8,128)(2,1)} %collective-permute-done.27.refs_9_), channel_id=1, source_target_pairs={{4,0},{8,4},{12,8},{28,12},{24,28},{20,24},{16,20},{0,16},{5,1},{9... | collective-permute-start | bytes 2359304 | tf_op jit(solution)/shard_map/ppermute | solution.py:108
  186.6 20.0 %collective-permute-start.32 = (bf16[256,1536]{1,0:T(8,128)(2,1)S(1)}, bf16[256,1536]{1,0:T(8,128)(2,1)S(1)}, u32[]{:S(2)}, u32[]{:S(2)}) collective-permute-start(bf16[256,1536]{1,0:T(8,128)(2,1)S(1)} %collective-permute-done.30.refs_10_), channel_id=1, source_target_pairs={{0,4},{4,8},{8,12},{12,28},{28,24},{24,20},{20,16},{16,0},{1,5},{5... | collective-permute-start | bytes 2359304 | tf_op jit(solution)/shard_map/ppermute | solution.py:108
  188.5 20.0 %collective-permute-start.31 = (bf16[256,1536]{1,0:T(8,128)(2,1)}, bf16[256,1536]{1,0:T(8,128)(2,1)S(1)}, u32[]{:S(2)}, u32[]{:S(2)}) collective-permute-start(bf16[256,1536]{1,0:T(8,128)(2,1)} %collective-permute-done.29.refs_10_), channel_id=1, source_target_pairs={{4,0},{8,4},{12,8},{28,12},{24,28},{20,24},{16,20},{0,16},{5,1},{9... | collective-permute-start | bytes 2359304 | tf_op jit(solution)/shard_map/ppermute | solution.py:108
  188.7 25.3 %collective-permute-start.36 = (bf16[256,2048]{1,0:T(8,128)(2,1)}, bf16[256,2048]{1,0:T(8,128)(2,1)S(1)}, u32[]{:S(2)}, u32[]{:S(2)}) collective-permute-start(bf16[256,2048]{1,0:T(8,128)(2,1)} %get-tuple-element.602.refs_4_), channel_id=1, source_target_pairs={{0,2},{1,3},{2,0},{3,1},{4,6},{5,7},{6,4},{7,5},{8,10},{9,11},{10,... | collective-permute-start | bytes 3145736 | tf_op jit(solution)/shard_map/ppermute | solution.py:42
  206.6 19.2 %collective-permute-start.35 = (bf16[256,1536]{1,0:T(8,128)(2,1)S(1)}, bf16[256,1536]{1,0:T(8,128)(2,1)S(1)}, u32[]{:S(2)}, u32[]{:S(2)}) collective-permute-start(bf16[256,1536]{1,0:T(8,128)(2,1)S(1)} %collective-permute-done.32.refs_11_), channel_id=1, source_target_pairs={{0,4},{4,8},{8,12},{12,28},{28,24},{24,20},{20,16},{16,0},{1,5},{5... | collective-permute-start | bytes 2359304 | tf_op jit(solution)/shard_map/ppermute | solution.py:108
  208.5 19.0 %collective-permute-start.34 = (bf16[256,1536]{1,0:T(8,128)(2,1)S(1)}, bf16[256,1536]{1,0:T(8,128)(2,1)S(1)}, u32[]{:S(2)}, u32[]{:S(2)}) collective-permute-start(bf16[256,1536]{1,0:T(8,128)(2,1)S(1)} %collective-permute-done.31.refs_11_), channel_id=1, source_target_pairs={{4,0},{8,4},{12,8},{28,12},{24,28},{20,24},{16,20},{0,16},{5,1},{9... | collective-permute-start | bytes 2359304 | tf_op jit(solution)/shard_map/ppermute | solution.py:108
  227.5 20.7 %collective-permute-start.38 = (bf16[256,1536]{1,0:T(8,128)(2,1)}, bf16[256,1536]{1,0:T(8,128)(2,1)}, u32[]{:S(2)}, u32[]{:S(2)}) collective-permute-start(bf16[256,1536]{1,0:T(8,128)(2,1)} %get-tuple-element.614.refs_5_), channel_id=1, source_target_pairs={{0,4},{4,8},{8,12},{12,28},{28,24},{24,20},{20,16},{16,0},{1,5},{5... | collective-permute-start | bytes 2359304 | tf_op jit(solution)/shard_map/ppermute | solution.py:108
  229.6 20.3 %collective-permute-start.37 = (bf16[256,1536]{1,0:T(8,128)(2,1)}, bf16[256,1536]{1,0:T(8,128)(2,1)}, u32[]{:S(2)}, u32[]{:S(2)}) collective-permute-start(bf16[256,1536]{1,0:T(8,128)(2,1)} %get-tuple-element.613.refs_13_), channel_id=1, source_target_pairs={{4,0},{8,4},{12,8},{28,12},{24,28},{20,24},{16,20},{0,16},{5,1},{9... | collective-permute-start | bytes 2359304 | tf_op jit(solution)/shard_map/ppermute | solution.py:108
  248.2 19.4 %collective-permute-start.41 = (bf16[256,1536]{1,0:T(8,128)(2,1)}, bf16[256,1536]{1,0:T(8,128)(2,1)S(1)}, u32[]{:S(2)}, u32[]{:S(2)}) collective-permute-start(bf16[256,1536]{1,0:T(8,128)(2,1)} %collective-permute-done.38.refs_6_), channel_id=1, source_target_pairs={{0,4},{4,8},{8,12},{12,28},{28,24},{24,20},{20,16},{16,0},{1,5},{5... | collective-permute-start | bytes 2359304 | tf_op jit(solution)/shard_map/ppermute | solution.py:108
  249.9 19.4 %collective-permute-start.40 = (bf16[256,1536]{1,0:T(8,128)(2,1)}, bf16[256,1536]{1,0:T(8,128)(2,1)S(1)}, u32[]{:S(2)}, u32[]{:S(2)}) collective-permute-start(bf16[256,1536]{1,0:T(8,128)(2,1)} %collective-permute-done.37.refs_14_), channel_id=1, source_target_pairs={{4,0},{8,4},{12,8},{28,12},{24,28},{20,24},{16,20},{0,16},{5,1},{9... | collective-permute-start | bytes 2359304 | tf_op jit(solution)/shard_map/ppermute | solution.py:108
  267.5 18.3 %collective-permute-start.43 = (bf16[256,1536]{1,0:T(8,128)(2,1)S(1)}, bf16[256,1536]{1,0:T(8,128)(2,1)S(1)}, u32[]{:S(2)}, u32[]{:S(2)}) collective-permute-start(bf16[256,1536]{1,0:T(8,128)(2,1)S(1)} %collective-permute-done.41.refs_7_), channel_id=1, source_target_pairs={{0,4},{4,8},{8,12},{12,28},{28,24},{24,20},{20,16},{16,0},{1,5},{5... | collective-permute-start | bytes 2359304 | tf_op jit(solution)/shard_map/ppermute | solution.py:108
  269.3 18.3 %collective-permute-start.42 = (bf16[256,1536]{1,0:T(8,128)(2,1)S(1)}, bf16[256,1536]{1,0:T(8,128)(2,1)S(1)}, u32[]{:S(2)}, u32[]{:S(2)}) collective-permute-start(bf16[256,1536]{1,0:T(8,128)(2,1)S(1)} %collective-permute-done.40.refs_15_), channel_id=1, source_target_pairs={{4,0},{8,4},{12,8},{28,12},{24,28},{20,24},{16,20},{0,16},{5,1},{9... | collective-permute-start | bytes 2359304 | tf_op jit(solution)/shard_map/ppermute | solution.py:108
  285.8 18.5 %collective-permute-start.45 = (bf16[256,1536]{1,0:T(8,128)(2,1)S(1)}, bf16[256,1536]{1,0:T(8,128)(2,1)S(1)}, u32[]{:S(2)}, u32[]{:S(2)}) collective-permute-start(bf16[256,1536]{1,0:T(8,128)(2,1)S(1)} %collective-permute-done.43.refs_8_), channel_id=1, source_target_pairs={{0,4},{4,8},{8,12},{12,28},{28,24},{24,20},{20,16},{16,0},{1,5},{5... | collective-permute-start | bytes 2359304 | tf_op jit(solution)/shard_map/ppermute | solution.py:108
  287.6 18.5 %collective-permute-start.44 = (bf16[256,1536]{1,0:T(8,128)(2,1)S(1)}, bf16[256,1536]{1,0:T(8,128)(2,1)S(1)}, u32[]{:S(2)}, u32[]{:S(2)}) collective-permute-start(bf16[256,1536]{1,0:T(8,128)(2,1)S(1)} %collective-permute-done.42.refs_16_), channel_id=1, source_target_pairs={{4,0},{8,4},{12,8},{28,12},{24,28},{20,24},{16,20},{0,16},{5,1},{9... | collective-permute-start | bytes 2359304 | tf_op jit(solution)/shard_map/ppermute | solution.py:108
  385.7 25.3 %collective-permute-start.53 = (bf16[256,2048]{1,0:T(8,128)(2,1)S(1)}, bf16[256,2048]{1,0:T(8,128)(2,1)S(1)}, u32[]{:S(2)}, u32[]{:S(2)}) collective-permute-start(bf16[256,2048]{1,0:T(8,128)(2,1)S(1)} %add_convert_fusion.3), channel_id=1, source_target_pairs={{0,2},{1,3},{2,0},{3,1},{4,6},{5,7},{6,4},{7,5},{8,10},{9,11},{10,... | collective-permute-start | bytes 3145736 | tf_op jit(solution)/shard_map/ppermute | solution.py:42
  421.8 25.8 %collective-permute-start.58 = (bf16[256,2048]{1,0:T(8,128)(2,1)}, bf16[256,2048]{1,0:T(8,128)(2,1)}, u32[]{:S(2)}, u32[]{:S(2)}) collective-permute-start(bf16[256,2048]{1,0:T(8,128)(2,1)} %get-tuple-element.724.refs_9_.rest_0_), channel_id=1, source_target_pairs={{0,2},{1,3},{2,0},{3,1},{4,6},{5,7},{6,4},{7,5},{8,10},{9,11},{10,... | collective-permute-start | bytes 3145736 | tf_op jit(solution)/shard_map/ppermute | solution.py:42
  450.6 31.9 %collective-permute-start.60 = (bf16[256,2048]{1,0:T(8,128)(2,1)}, bf16[256,2048]{1,0:T(8,128)(2,1)}, u32[]{:S(2)}, u32[]{:S(2)}) collective-permute-start(bf16[256,2048]{1,0:T(8,128)(2,1)} %add_convert_fusion.2), channel_id=1, source_target_pairs={{0,2},{1,3},{2,0},{3,1},{4,6},{5,7},{6,4},{7,5},{8,10},{9,11},{10,... | collective-permute-start | bytes 3145736 | tf_op jit(solution)/shard_map/ppermute | solution.py:42
  460.5 22.0 %collective-permute-start.61 = (f32[2,128,80]{2,1,0:T(8,128)}, f32[2,128,80]{2,1,0:T(8,128)S(1)}, u32[]{:S(2)}, u32[]{:S(2)}) collective-permute-start(f32[2,128,80]{2,1,0:T(8,128)} %get-tuple-element.762), channel_id=1, source_target_pairs={{4,0},{8,4},{12,8},{5,1},{9,5},{13,9},{6,2},{10,6},{14,10},{7,3},{... | collective-permute-start | bytes 245768 | tf_op jit(solution)/shard_map/ppermute | solution.py:47
  461.8 20.7 %collective-permute-start.62 = (f32[2,128,80]{2,1,0:T(8,128)}, f32[2,128,80]{2,1,0:T(8,128)S(1)}, u32[]{:S(2)}, u32[]{:S(2)}) collective-permute-start(f32[2,128,80]{2,1,0:T(8,128)} %get-tuple-element.762), channel_id=1, source_target_pairs={{8,0},{12,4},{9,1},{13,5},{10,2},{14,6},{11,3},{15,7},{24,16},{28,... | collective-permute-start | bytes 245768 | tf_op jit(solution)/shard_map/ppermute | solution.py:47
  463.1 19.4 %collective-permute-start.63 = (f32[2,128,80]{2,1,0:T(8,128)}, f32[2,128,80]{2,1,0:T(8,128)S(1)}, u32[]{:S(2)}, u32[]{:S(2)}) collective-permute-start(f32[2,128,80]{2,1,0:T(8,128)} %get-tuple-element.762), channel_id=1, source_target_pairs={{12,0},{13,1},{14,2},{15,3},{28,16},{29,17},{30,18},{31,19}} | collective-permute-start | bytes 245768 | tf_op jit(solution)/shard_map/ppermute | solution.py:47
  484.1 26.7 %collective-permute-start.64 = (bf16[256,2048]{1,0:T(8,128)(2,1)S(1)}, bf16[256,2048]{1,0:T(8,128)(2,1)}, u32[]{:S(2)}, u32[]{:S(2)}) collective-permute-start(bf16[256,2048]{1,0:T(8,128)(2,1)S(1)} %add_convert_fusion.1.refs_1_), channel_id=1, source_target_pairs={{0,2},{1,3},{2,0},{3,1},{4,6},{5,7},{6,4},{7,5},{8,10},{9,11},{10,... | collective-permute-start | bytes 3145736 | tf_op jit(solution)/shard_map/ppermute | solution.py:42
  484.8 26.1 %collective-permute-start.65 = (bf16[256,2048]{1,0:T(8,128)(2,1)S(1)}, bf16[256,2048]{1,0:T(8,128)(2,1)}, u32[]{:S(2)}, u32[]{:S(2)}) collective-permute-start(bf16[256,2048]{1,0:T(8,128)(2,1)S(1)} %add_convert_fusion.1.refs_1_), channel_id=1, source_target_pairs={{0,1},{1,0},{2,3},{3,2},{4,5},{5,4},{6,7},{7,6},{8,9},{9,8},{10,11... | collective-permute-start | bytes 3145736 | tf_op jit(solution)/shard_map/ppermute | solution.py:42
  518.3 25.4 %collective-permute-start.70 = (bf16[256,2048]{1,0:T(8,128)(2,1)}, bf16[256,2048]{1,0:T(8,128)(2,1)S(1)}, u32[]{:S(2)}, u32[]{:S(2)}) collective-permute-start(bf16[256,2048]{1,0:T(8,128)(2,1)} %add_convert_fusion), channel_id=1, source_target_pairs={{0,2},{1,3},{2,0},{3,1},{4,6},{5,7},{6,4},{7,5},{8,10},{9,11},{10,... | collective-permute-start | bytes 3145736 | tf_op jit(solution)/shard_map/ppermute | solution.py:42
  549.9 25.8 %collective-permute-start.75 = (bf16[256,2048]{1,0:T(8,128)(2,1)}, bf16[256,2048]{1,0:T(8,128)(2,1)S(1)}, u32[]{:S(2)}, u32[]{:S(2)}) collective-permute-start(bf16[256,2048]{1,0:T(8,128)(2,1)} %own_rows.5.refs_1_), channel_id=1, source_target_pairs={{0,2},{1,3},{2,0},{3,1},{4,6},{5,7},{6,4},{7,5},{8,10},{9,11},{10,... | collective-permute-start | bytes 3145736 | tf_op jit(solution)/shard_map/ppermute | solution.py:42
  (149 other events, 2026.1 us)

commit v5 on v4

--- a/solution.py
+++ b/solution.py
@@ -423,20 +423,20 @@
     def at_first(act):
         pl.when(step == 0)(act)
 
-    def copies(which):
-        made, at, i = [], 0, 0
-        for lot, size in zip(lots, units):
-            for _ in range(lot):
-                made.append(
-                    pltpu.make_async_copy(
-                        pieces[i].at[:, pl.ds(which * size, size)],
-                        held.at[which, pl.ds(pl.multiple_of(offsets[i], 16), pieces[i].shape[0]), pl.ds(at, size)],
-                        sems.at[which, i],
-                    )
-                )
-                i += 1
-            at += size
-        return made
+    starts = [sum(units[:i]) for i in range(len(units))]
+    blocks = [(which, lot) for which in range(3) for lot in range(len(lots))]
+
+    def copies(block):
+        which, lot = block
+        size = units[lot]
+        return [
+            pltpu.make_async_copy(
+                pieces[i].at[:, pl.ds(which * size, size)],
+                held.at[which, pl.ds(pl.multiple_of(offsets[i], 16), pieces[i].shape[0]), pl.ds(starts[lot], size)],
+                sems.at[which, i],
+            )
+            for i in range(sum(lots[:lot]), sum(lots[: lot + 1]))
+        ]
 
     def sum_copy(i, kind):
         return pltpu.make_async_copy(sums[kind].at[i], rest[0].at[i, kind], rest[1].at[i, kind])
@@ -447,42 +447,40 @@
 
     @at_first
     def _():
-        first = copies(0)
-        for copy in quarter_copies(quarters[:1], rows, rows_sems) + first:
+        for copy in quarter_copies(quarters[:1], rows, rows_sems) + copies(blocks[0]) + copies(blocks[1]):
             copy.start()
         for copy in quarter_copies(quarters[1:], rows, rows_sems, 1):
             copy.start()
-        for copy in first:
-            copy.wait()
-        for copy in copies(1):
-            copy.start()
+
+    def product(x, index):
+        @at_first
+        def _():
+            for copy in copies(blocks[index]):
+                copy.wait()
+            if index + 2 < len(blocks):
+                for copy in copies(blocks[index + 2]):
+                    copy.start()
+            elif index + 2 == len(blocks) and summed:
+                for i in range(2):
+                    for kind in (1, 0):
+                        sum_copy(i, kind).start()
+
+        which, lot = blocks[index]
+        return nn(x, held[which, :, starts[lot] : starts[lot] + units[lot]])
 
     n2 = quarter_of(step, quarters, rows, rows_sems)
-    gate = nn(n2, held[0])
-
-    @at_first
-    def _():
-        for copy in copies(1):
-            copy.wait()
-        for copy in copies(2):
-            copy.start()
-
-    up = nn(n2, held[1])
-
-    @at_first
-    def _():
-        for copy in copies(2):
-            copy.wait()
-        for i in range(2 if summed else 0):
-            for kind in (1, 0):
-                sum_copy(i, kind).start()
-
-    grad_act = nn(cot[...], held[2])
-    s = 1.0 / (1.0 + jnp.exp(-gate))
-    silu = gate * s
-    act = (silu * up).astype(bf16)
-    grad_gate = (grad_act * up * s * (1.0 + gate * (1.0 - s))).astype(bf16)
-    grad_up = (grad_act * silu).astype(bf16)
+    count = len(lots)
+    gates = [product(n2, i) for i in range(count)]
+    ups = [product(n2, count + i) for i in range(count)]
+    grads = [product(cot[...], 2 * count + i) for i in range(count)]
+    parts = [[], [], []]
+    for gate, up, grad_act in zip(gates, ups, grads):
+        s = 1.0 / (1.0 + jnp.exp(-gate))
+        silu = gate * s
+        parts[0].append((silu * up).astype(bf16))
+        parts[1].append((grad_act * up * s * (1.0 + gate * (1.0 - s))).astype(bf16))
+        parts[2].append((grad_act * silu).astype(bf16))
+    act, grad_gate, grad_up = [jnp.concatenate(x, axis=1) for x in parts]
 
     def finish(kind, total):
         if summed:
@@ -1374,16 +1372,17 @@
     if in_tiles:
         by_head, shared = by_head[: heads + kv_heads], by_head[heads + kv_heads :]
         shared = shared.reshape(4 * rank // 8, -1, 8, 128).transpose(0, 2, 1, 3)
-    kept, sent = halved(shared.reshape(4 * rank, 4, -1), "tensor", 2, far, 1)
-    shared = kept.reshape(4 * rank, 2, -1)
-    sent = sent.reshape(4 * rank, 2, -1)
+    shared = shared.reshape(4 * rank, 2, 2, -1).transpose(2, 1, 0, 3)
+    pick = lambda x, i: lax.dynamic_index_in_dim(x, i, 0, keepdims=False)
+    shared = pick(shared, core) + clock.tie(exchange(pick(shared, 1 - core), "tensor", 1))
+    shared = clock.tie(shared.reshape(2, 4 * rank, -1))
     block_out = clock.tie(place([out_rows, out_beside, out_across, out_last], 0, nat, bf16))
     (across,) = clock.wait(across)
-    last = exchange(across, "tensor", 1)
-    kept, sent = halved(shared + clock.tie(sent), "tensor", 1, core, 1)
-    (last,) = clock.wait(last)
+    (last,) = clock.wait(exchange(across, "tensor", 1))
+    shared = clock.tie(shared)
+    sent = exchange(pick(shared, 1 - far), "tensor", 2)
     grad_tokens = clock.tie(place([across, last], 2, nat, f32, (grad_tokens,)))
-    shared = (kept + clock.tie(sent)).reshape(4 * rank, -1).T
+    shared = (pick(shared, far) + clock.tie(sent)).T
     of_q, of_kv = by_head[:heads], by_head[heads:]
     first, second = slice(head, head + rank), slice(head + rank, head + 2 * rank)
     out = [of_q[..., first], of_kv[..., first], of_kv[..., second], of_q[..., second], of_q[..., :head], of_kv[..., :head]]

time: 595 us -> 592 us (level)
  transfers between devices with their start and end apart: 79 -> 79, of which waited for: 41 -> 42; matrix products, arithmetic and copies ran while one was open for 3% -> 3% of each run, Pallas kernels for 38% -> 38%
where the time goes in v5:
time: 592 us; the launch traced here: 585 us
  Pallas kernels  252 us (43%)
  waiting for transfers between devices  197 us (33%)
  starting transfers between devices  86.6 us (15%)
  local copies, waits for them, and re-layouts  28.4 us (5%)
  other arithmetic  18 us (3%)
    ppermute x42, waiting for transfers between devices, step(): lane.append(lax.ppermute(lane[-1], ('dp', 'seq'), way))  130 us
    pallas_call x6, Pallas kernels, ffn(): pl.pallas_call(lambda *refs: ffn_body(sizes, units, bool(sums), last, *re...  108 us
    ppermute x29, waiting for transfers between devices, exchange(): return lax.ppermute(x, axis, [(i, i ^ bit) for i in range(count)])  62.5 us
    ppermute x42, starting transfers between devices, step(): lane.append(lax.ppermute(lane[-1], ('dp', 'seq'), way))  47.4 us
    unnamed x211, local copies, waits for them, and re-layouts  20.7 us
    ppermute x29, starting transfers between devices, exchange(): return lax.ppermute(x, axis, [(i, i ^ bit) for i in range(count)])  20.3 us
    ppermute x8, starting transfers between devices, shifted(): lax.ppermute(x, axis, [(i, i + by) for i in range(count) if 0 <= i + by <...  18.9 us
    pallas_call x1, Pallas kernels, per_device(): pl.pallas_call(lambda *refs: backward_body((kv_heads, group, head, chunks...  17.2 us
  transfers between devices with their start and end apart: 79, of which 42 were waited for; matrix products, arithmetic and copies ran while one was open for 3% of the time, Pallas kernels for 38%

profile of v5, /device:TPU:0, one launch (start us, length us, event | category | flops | bytes accessed | tf_op | source)
XLA Modules:
  0.0 584.7 jit_solution(2777412204637465760)
XLA Ops:
  31.1 8.3 %norm.1 = (bf16[1152,2048]{1,0:T(8,128)(2,1)}, f32[1152,24]{1,0:T(8,128)}) custom-call(bf16[1024,2048]{1,0:T(8,128)(2,1)} %tokens.4, bf16[64,2048]{1,0:T(8,128)(2,1)} %copy-done.82, f32[1,2048]{1,0:T(1,128)} %bitcast.70, bf16[2048,24]{1,0:T(8,128)(2,1)} %copy.47.downs), custom_call_target="tpu_custom_call" | custom-call | flops 1 | bytes 1 | tf_op jit(solution)/shard_map/norm/pallas_call | solution.py:900
  52.5 7.2 %collective-permute-done.8.refs_17_.refs_10_.refs_16_.refs_14_ = bf16[128,1280]{1,0:T(8,128)(2,1)S(1)} collective-permute-done((bf16[128,1280]{1,0:T(8,128)(2,1)S(1)}, bf16[128,1280]{1,0:T(8,128)(2,1)S(1)}, u32[]{:S(2)}, u32[]{:S(2)}) %collective-permute-start.8) | collective-permute-done | bytes 327712 | tf_op jit(solution)/shard_map/ppermute | solution.py:108
  62.4 6.9 %collective-permute-done.10.refs_18_.refs_11_.refs_17_.refs_15_ = bf16[128,1280]{1,0:T(8,128)(2,1)S(1)} collective-permute-done((bf16[128,1280]{1,0:T(8,128)(2,1)S(1)}, bf16[128,1280]{1,0:T(8,128)(2,1)S(1)}, u32[]{:S(2)}, u32[]{:S(2)}) %collective-permute-start.10) | collective-permute-done | bytes 327712 | tf_op jit(solution)/shard_map/ppermute | solution.py:108
  74.4 8.0 %collective-permute-done.14.refs_27_.refs_20_.refs_26_.refs_24_ = bf16[128,1280]{1,0:T(8,128)(2,1)S(1)} collective-permute-done((bf16[128,1280]{1,0:T(8,128)(2,1)S(1)}, bf16[128,1280]{1,0:T(8,128)(2,1)S(1)}, u32[]{:S(2)}, u32[]{:S(2)}) %collective-permute-start.14) | collective-permute-done | bytes 327712 | tf_op jit(solution)/shard_map/ppermute | solution.py:108
  86.3 16.9 %prep.1 = (bf16[512,1024]{1,0:T(8,128)(2,1)}, bf16[1024,1024]{1,0:T(8,128)(2,1)}, bf16[1152,128]{1,0:T(8,128)(2,1)}, bf16[128,1152]{1,0:T(8,128)(2,1)}, bf16[115...) custom-call(s32[16]{0:T(128)} %get-tuple-element.808.refs_0_, ...), custom_call_target="tpu_custom_call" | custom-call | flops 1 | bytes 1 | tf_op jit(solution)/shard_map/prep/pallas_call | solution.py:966
  118.3 10.5 %attend.1 = (bf16[1024,512]{1,0:T(8,128)(2,1)}, f32[512,1024]{1,0:T(8,128)}, f32[8,1024]{1,0:T(8,128)}, bf16[8,2,128,80]{3,2,1,0:T(8,128)(2,1)}) custom-call(s32[9]{0:T(128)} %copy-done.17, f32[3]{0:T(128)} %copy-done.20, bf16[512,1024]{1,0:T(8,128)(2,1)} %get-tuple-element.546.refs_2_.refs_1_, ...), custom_call_target="tpu_custom_call" | custom-call | flops 1 | bytes 1 | tf_op jit(solution)/shard_map/attend/pallas_call | solution.py:985
  133.7 10.7 %project.1 = (bf16[256,2048]{1,0:T(8,128)(2,1)}, bf16[256,2048]{1,0:T(8,128)(2,1)}, bf16[256,2048]{1,0:T(8,128)(2,1)}, bf16[256,2048]{1,0:T(8,128)(2,1)}, f32[1024,8]{1,0:T(8,128)}) custom-call(s32[16]{0:T(128)} %get-tuple-element.808.refs_0_, s32[4]{0:T(128)} %pad_add_fusion.refs_1_.nat.refs_0_, bf16[1024,512]{1,0:T(8,128)(2,1)} %get-tuple-element.562.refs_2_.att, ...), custom_call_target="tpu_custom_call" | custom-call | flops 1 | bytes 1 | tf_op jit(solution)/shard_map/project/pallas_call | solution.py:1026
  152.3 13.4 %collective-permute-done.28.refs_9_ = bf16[256,1536]{1,0:T(8,128)(2,1)S(1)} collective-permute-done((bf16[256,1536]{1,0:T(8,128)(2,1)S(1)}, bf16[256,1536]{1,0:T(8,128)(2,1)S(1)}, u32[]{:S(2)}, u32[]{:S(2)}) %collective-permute-start.28) | collective-permute-done | bytes 786464 | tf_op jit(solution)/shard_map/ppermute | solution.py:108
  168.4 7.6 %collective-permute-done.26.across = bf16[256,2048]{1,0:T(8,128)(2,1)S(1)} collective-permute-done((bf16[256,2048]{1,0:T(8,128)(2,1)S(1)}, bf16[256,2048]{1,0:T(8,128)(2,1)S(1)}, u32[]{:S(2)}, u32[]{:S(2)}) %collective-permute-start.26) | collective-permute-done | bytes 1048608 | tf_op jit(solution)/shard_map/ppermute | solution.py:42
  190.2 16.4 %collective-permute-done.32.refs_11_ = bf16[256,1536]{1,0:T(8,128)(2,1)S(1)} collective-permute-done((bf16[256,1536]{1,0:T(8,128)(2,1)S(1)}, bf16[256,1536]{1,0:T(8,128)(2,1)S(1)}, u32[]{:S(2)}, u32[]{:S(2)}) %collective-permute-start.32) | collective-permute-done | bytes 786464 | tf_op jit(solution)/shard_map/ppermute | solution.py:108
  208.7 5.3 collective-permute-done.36.refs_4_
  214.0 11.8 %collective-permute-done.35.refs_12_ = bf16[256,1536]{1,0:T(8,128)(2,1)S(1)} collective-permute-done((bf16[256,1536]{1,0:T(8,128)(2,1)S(1)}, bf16[256,1536]{1,0:T(8,128)(2,1)S(1)}, u32[]{:S(2)}, u32[]{:S(2)}) %collective-permute-start.35) | collective-permute-done | bytes 786464 | tf_op jit(solution)/shard_map/ppermute | solution.py:108
  231.1 14.8 %feed_forward.6 = (f32[2,256,2048]{2,1,0:T(8,128)}, f32[2,256,2048]{2,1,0:T(8,128)}) custom-call(s32[8]{0:T(128)} %copy-done.97, s32[4]{0:T(128)} %pad_add_fusion.refs_1_.nat.refs_0_, bf16[1024,2048]{1,0:T(8,128)(2,1)} %cotangent.1, bf16[256,2048]{1,0:T(8,128)(2,1)} %copy-done.26, bf16[256,2048]{1,0:T(8,128)(2,1)} %copy-done.25, ...), custom_call_target="tpu_custom_call" | custom-call | flops 1 | bytes 1 | tf_op jit(solution)/shard_map/feed_forward/pallas_call | solution.py:1082
  250.2 14.7 %feed_forward.7 = (f32[2,256,2048]{2,1,0:T(8,128)}, f32[2,256,2048]{2,1,0:T(8,128)}) custom-call(s32[8]{0:T(128)} %copy-done.97, s32[4]{0:T(128)} %pad_add_fusion.refs_1_.nat.refs_0_, bf16[1024,2048]{1,0:T(8,128)(2,1)} %cotangent.1, bf16[256,2048]{1,0:T(8,128)(2,1)} %copy-done.24, bf16[256,2048]{1,0:T(8,128)(2,1)} %get-tuple-element.606.refs_4_, ...), custom_call_target="tpu_custom_call" | custom-call | flops 1 | bytes 1 | tf_op jit(solution)/shard_map/feed_forward/pallas_call | solution.py:1082
  269.6 15.6 %feed_forward.8 = (f32[2,256,2048]{2,1,0:T(8,128)}, f32[2,256,2048]{2,1,0:T(8,128)}) custom-call(s32[8]{0:T(128)} %copy-done.96, s32[4]{0:T(128)} %pad_add_fusion.refs_1_.nat.refs_0_, bf16[1024,2048]{1,0:T(8,128)(2,1)} %cotangent.1, bf16[256,2048]{1,0:T(8,128)(2,1)} %copy-done.26, bf16[256,2048]{1,0:T(8,128)(2,1)} %copy-done.25, ...), custom_call_target="tpu_custom_call" | custom-call | flops 1 | bytes 1 | tf_op jit(solution)/shard_map/feed_forward/pallas_call | solution.py:1082
  288.0 15.7 %feed_forward.9 = (f32[2,256,2048]{2,1,0:T(8,128)}, f32[2,256,2048]{2,1,0:T(8,128)}) custom-call(s32[8]{0:T(128)} %copy-done.96, s32[4]{0:T(128)} %pad_add_fusion.refs_1_.nat.refs_0_, bf16[1024,2048]{1,0:T(8,128)(2,1)} %cotangent.1, bf16[256,2048]{1,0:T(8,128)(2,1)} %copy-done.24, bf16[256,2048]{1,0:T(8,128)(2,1)} %get-tuple-element.606.refs_4_, ...), custom_call_target="tpu_custom_call" | custom-call | flops 1 | bytes 1 | tf_op jit(solution)/shard_map/feed_forward/pallas_call | solution.py:1082
  305.8 15.7 %collective-permute-done.47.refs_10_ = bf16[256,1536]{1,0:T(8,128)(2,1)S(1)} collective-permute-done((bf16[256,1536]{1,0:T(8,128)(2,1)S(1)}, bf16[256,1536]{1,0:T(8,128)(2,1)S(1)}, u32[]{:S(2)}, u32[]{:S(2)}) %collective-permute-start.47) | collective-permute-done | bytes 786464 | tf_op jit(solution)/shard_map/ppermute | solution.py:108
  323.5 15.7 %collective-permute-done.49.refs_11_ = bf16[256,1536]{1,0:T(8,128)(2,1)S(1)} collective-permute-done((bf16[256,1536]{1,0:T(8,128)(2,1)S(1)}, bf16[256,1536]{1,0:T(8,128)(2,1)S(1)}, u32[]{:S(2)}, u32[]{:S(2)}) %collective-permute-start.49) | collective-permute-done | bytes 786464 | tf_op jit(solution)/shard_map/ppermute | solution.py:108
  341.2 13.1 %collective-permute-done.51.refs_12_ = bf16[256,1536]{1,0:T(8,128)(2,1)S(1)} collective-permute-done((bf16[256,1536]{1,0:T(8,128)(2,1)S(1)}, bf16[256,1536]{1,0:T(8,128)(2,1)S(1)}, u32[]{:S(2)}, u32[]{:S(2)}) %collective-permute-start.51) | collective-permute-done | bytes 786464 | tf_op jit(solution)/shard_map/ppermute | solution.py:108
  356.7 23.5 %feed_forward.10 = (bf16[256,2048]{1,0:T(8,128)(2,1)}, bf16[256,2048]{1,0:T(8,128)(2,1)}, bf16[256,2048]{1,0:T(8,128)(2,1)}, bf16[256,2048]{1,0:T(8,128)(2,1)}) custom-call(s32[16]{0:T(128)} %get-tuple-element.702.refs_0_, s32[4]{0:T(128)} %pad_add_fusion.refs_1_.nat.refs_0_, bf16[1024,2048]{1,0:T(8,128)(2,1)} %cotangent.1, bf16[256,2048]{1,0:T(8,128)(2,1)} %copy-done.26, ...), custom_call_target="tpu_custom_call" | custom-call | flops 1 | bytes 1 | tf_op jit(solution)/shard_map/feed_forward/pallas_call | solution.py:1082
  386.3 23.7 %feed_forward.11 = (bf16[256,2048]{1,0:T(8,128)(2,1)}, bf16[256,2048]{1,0:T(8,128)(2,1)}, bf16[256,2048]{1,0:T(8,128)(2,1)}, bf16[256,2048]{1,0:T(8,128)(2,1)}) custom-call(s32[16]{0:T(128)} %get-tuple-element.702.refs_0_, s32[4]{0:T(128)} %pad_add_fusion.refs_1_.nat.refs_0_, bf16[1024,2048]{1,0:T(8,128)(2,1)} %cotangent.1, bf16[256,2048]{1,0:T(8,128)(2,1)} %copy-done.24, ...), custom_call_target="tpu_custom_call" | custom-call | flops 1 | bytes 1 | tf_op jit(solution)/shard_map/feed_forward/pallas_call | solution.py:1082
  414.0 5.6 own_rows.4
  423.5 8.5 %project_back.2 = (bf16[512,1024]{1,0:T(8,128)(2,1)}, f32[8,1024]{1,0:T(8,128)}, f32[1024,8]{1,0:T(8,128)}, f32[2,128,80]{2,1,0:T(8,128)}) custom-call(s32[16]{0:T(128)} %get-tuple-element.808.refs_0_, s32[4]{0:T(128)} %pad_add_fusion.refs_1_.nat.refs_0_, s32[9]{0:T(128)} %copy-done.17, bf16[2048,8]{1,0:T(8,128)(2,1)} %get-tuple-element.732.refs_3_, ...), custom_call_target="tpu_custom_call" | custom-call | flops 1 | bytes 1 | tf_op jit(solution)/shard_map/project_back/pallas_call | solution.py:1140
  436.0 10.6 %collective-permute-done.58.refs_9_.rest_2_ = bf16[256,2048]{1,0:T(8,128)(2,1)} collective-permute-done((bf16[256,2048]{1,0:T(8,128)(2,1)}, bf16[256,2048]{1,0:T(8,128)(2,1)}, u32[]{:S(2)}, u32[]{:S(2)}) %collective-permute-start.58) | collective-permute-done | bytes 1048608 | tf_op jit(solution)/shard_map/ppermute | solution.py:42
  451.1 8.4 %project_back.3 = (bf16[512,1024]{1,0:T(8,128)(2,1)}, f32[8,1024]{1,0:T(8,128)}, f32[1024,8]{1,0:T(8,128)}, f32[2,128,80]{2,1,0:T(8,128)}) custom-call(s32[16]{0:T(128)} %get-tuple-element.808.refs_0_, s32[4]{0:T(128)} %pad_add_fusion.refs_1_.nat.refs_0_, s32[9]{0:T(128)} %copy-done.17, ...), custom_call_target="tpu_custom_call", output_to_operand_aliasing={{0}: (27, {}), {1}: (28, {}), {2}: (29, {})} | custom-call | flops 1 | bytes 1 | tf_op jit(solution)/shard_map/project_back/pallas_call | solution.py:1140
  464.3 17.2 %attend_back.1 = (bf16[1024,512]{1,0:T(8,128)(2,1)}, f32[128,1152]{1,0:T(8,128)}, f32[128,1152]{1,0:T(8,128)}, f32[256,1152]{1,0:T(8,128)}, f32[2,256,256]{2,1,0:T(8,128)}) custom-call(s32[9]{0:T(128)S(1)} %copy-done.18, bf16[512,1024]{1,0:T(8,128)(2,1)} %get-tuple-element.546.refs_2_.refs_1_, bf16[1024,1024]{1,0:T(8,128)(2,1)} %get-tuple-element.547.refs_3_.refs_7_.refs_2_, ...), custom_call_target="tpu_custom_call" | custom-call | flops 1 | bytes 1 | tf_op jit(solution)/shard_map/attend_back/pallas_call | solution.py:1210
  490.5 5.2 adapter_o.1
  497.4 12.5 %norm_back.1 = (bf16[256,2048]{1,0:T(8,128)(2,1)}, bf16[256,2048]{1,0:T(8,128)(2,1)}, bf16[256,2048]{1,0:T(8,128)(2,1)}, bf16[256,2048]{1,0:T(8,128)(2,1)}) custom-call(s32[16]{0:T(128)} %get-tuple-element.808.refs_0_, s32[4]{0:T(128)} %pad_add_fusion.refs_1_.nat.refs_0_, bf16[1024,512]{1,0:T(8,128)(2,1)} %get-tuple-element.831.refs_2_.refs_0_, ...), custom_call_target="tpu_custom_call" | custom-call | flops 1 | bytes 1 | tf_op jit(solution)/shard_map/norm_back/pallas_call | solution.py:1282
  519.6 6.2 %adapters.1 = f32[8,18,8,128]{3,2,1,0:T(8,128)} custom-call(bf16[1024,512]{1,0:T(8,128)(2,1)} %get-tuple-element.831.refs_2_.refs_0_, f32[256,1024]{1,0:T(8,128)} %get-tuple-element.810.refs_3_.refs_1_, f32[256,128]{1,0:T(8,128)} %copy-done.78, f32[32,1024]{1,0:T(8,128)} %copy-done.2, f32[32,1024]{1,0:T(8,128)} %copy-done.4, ...), custom_call_target="tpu_custom_call" | custom-call | flops 1 | bytes 1 | tf_op jit(solution)/shard_map/adapters/pallas_call | solution.py:1320
  527.1 5.3 collective-permute-done.71
  543.7 5.2 own_rows.5.refs_1_
  562.7 12.0 %collective-permute-done.76.refs_1_ = bf16[256,2048]{1,0:T(8,128)(2,1)S(1)} collective-permute-done((bf16[256,2048]{1,0:T(8,128)(2,1)}, bf16[256,2048]{1,0:T(8,128)(2,1)S(1)}, u32[]{:S(2)}, u32[]{:S(2)}) %collective-permute-start.76) | collective-permute-done | bytes 1048608 | tf_op jit(solution)/shard_map/ppermute | solution.py:42
  (404 shorter events, 210.0 us)
Async XLA Ops:
  83.3 20.0 %collective-permute-start.16 = (bf16[256,1536]{1,0:T(8,128)(2,1)}, bf16[256,1536]{1,0:T(8,128)(2,1)}, u32[]{:S(2)}, u32[]{:S(2)}) collective-permute-start(bf16[256,1536]{1,0:T(8,128)(2,1)} %get-tuple-element.519.refs_5_), channel_id=1, source_target_pairs={{0,4},{4,8},{8,12},{12,28},{28,24},{24,20},{20,16},{16,0},{1,5},{5... | collective-permute-start | bytes 2359304 | tf_op jit(solution)/shard_map/ppermute | solution.py:108
  85.1 20.1 %collective-permute-start.15 = (bf16[256,1536]{1,0:T(8,128)(2,1)}, bf16[256,1536]{1,0:T(8,128)(2,1)}, u32[]{:S(2)}, u32[]{:S(2)}) collective-permute-start(bf16[256,1536]{1,0:T(8,128)(2,1)} %get-tuple-element.518.refs_5_), channel_id=1, source_target_pairs={{4,0},{8,4},{12,8},{28,12},{24,28},{20,24},{16,20},{0,16},{5,1},{9... | collective-permute-start | bytes 2359304 | tf_op jit(solution)/shard_map/ppermute | solution.py:108
  103.3 25.5 %collective-permute-start.18 = (bf16[256,1536]{1,0:T(8,128)(2,1)}, bf16[256,1536]{1,0:T(8,128)(2,1)S(1)}, u32[]{:S(2)}, u32[]{:S(2)}) collective-permute-start(bf16[256,1536]{1,0:T(8,128)(2,1)} %collective-permute-done.16.refs_6_), channel_id=1, source_target_pairs={{0,4},{4,8},{8,12},{12,28},{28,24},{24,20},{20,16},{16,0},{1,5},{5... | collective-permute-start | bytes 2359304 | tf_op jit(solution)/shard_map/ppermute | solution.py:108
  105.1 26.4 %collective-permute-start.17 = (bf16[256,1536]{1,0:T(8,128)(2,1)}, bf16[256,1536]{1,0:T(8,128)(2,1)S(1)}, u32[]{:S(2)}, u32[]{:S(2)}) collective-permute-start(bf16[256,1536]{1,0:T(8,128)(2,1)} %collective-permute-done.15.refs_6_), channel_id=1, source_target_pairs={{4,0},{8,4},{12,8},{28,12},{24,28},{20,24},{16,20},{0,16},{5,1},{9... | collective-permute-start | bytes 2359304 | tf_op jit(solution)/shard_map/ppermute | solution.py:108
  145.1 20.6 %collective-permute-start.28 = (bf16[256,1536]{1,0:T(8,128)(2,1)S(1)}, bf16[256,1536]{1,0:T(8,128)(2,1)S(1)}, u32[]{:S(2)}, u32[]{:S(2)}) collective-permute-start(bf16[256,1536]{1,0:T(8,128)(2,1)S(1)} %collective-permute-done.23.refs_8_), channel_id=1, source_target_pairs={{0,4},{4,8},{8,12},{12,28},{28,24},{24,20},{20,16},{16,0},{1,5},{5... | collective-permute-start | bytes 2359304 | tf_op jit(solution)/shard_map/ppermute | solution.py:108
  147.1 19.5 %collective-permute-start.27 = (bf16[256,1536]{1,0:T(8,128)(2,1)S(1)}, bf16[256,1536]{1,0:T(8,128)(2,1)}, u32[]{:S(2)}, u32[]{:S(2)}) collective-permute-start(bf16[256,1536]{1,0:T(8,128)(2,1)S(1)} %collective-permute-done.22.refs_8_), channel_id=1, source_target_pairs={{4,0},{8,4},{12,8},{28,12},{24,28},{20,24},{16,20},{0,16},{5,1},{9... | collective-permute-start | bytes 2359304 | tf_op jit(solution)/shard_map/ppermute | solution.py:108
  150.7 25.3 %collective-permute-start.26 = (bf16[256,2048]{1,0:T(8,128)(2,1)S(1)}, bf16[256,2048]{1,0:T(8,128)(2,1)S(1)}, u32[]{:S(2)}, u32[]{:S(2)}) collective-permute-start(bf16[256,2048]{1,0:T(8,128)(2,1)S(1)} %add_convert_fusion.4), channel_id=1, source_target_pairs={{0,2},{1,3},{2,0},{3,1},{4,6},{5,7},{6,4},{7,5},{8,10},{9,11},{10,... | collective-permute-start | bytes 3145736 | tf_op jit(solution)/shard_map/ppermute | solution.py:42
  165.7 19.2 %collective-permute-start.30 = (bf16[256,1536]{1,0:T(8,128)(2,1)S(1)}, bf16[256,1536]{1,0:T(8,128)(2,1)S(1)}, u32[]{:S(2)}, u32[]{:S(2)}) collective-permute-start(bf16[256,1536]{1,0:T(8,128)(2,1)S(1)} %collective-permute-done.28.refs_9_), channel_id=1, source_target_pairs={{0,4},{4,8},{8,12},{12,28},{28,24},{24,20},{20,16},{16,0},{1,5},{5... | collective-permute-start | bytes 2359304 | tf_op jit(solution)/shard_map/ppermute | solution.py:108
  166.6 20.1 %collective-permute-start.29 = (bf16[256,1536]{1,0:T(8,128)(2,1)}, bf16[256,1536]{1,0:T(8,128)(2,1)}, u32[]{:S(2)}, u32[]{:S(2)}) collective-permute-start(bf16[256,1536]{1,0:T(8,128)(2,1)} %collective-permute-done.27.refs_9_), channel_id=1, source_target_pairs={{4,0},{8,4},{12,8},{28,12},{24,28},{20,24},{16,20},{0,16},{5,1},{9... | collective-permute-start | bytes 2359304 | tf_op jit(solution)/shard_map/ppermute | solution.py:108
  186.6 20.0 %collective-permute-start.32 = (bf16[256,1536]{1,0:T(8,128)(2,1)S(1)}, bf16[256,1536]{1,0:T(8,128)(2,1)S(1)}, u32[]{:S(2)}, u32[]{:S(2)}) collective-permute-start(bf16[256,1536]{1,0:T(8,128)(2,1)S(1)} %collective-permute-done.30.refs_10_), channel_id=1, source_target_pairs={{0,4},{4,8},{8,12},{12,28},{28,24},{24,20},{20,16},{16,0},{1,5},{5... | collective-permute-start | bytes 2359304 | tf_op jit(solution)/shard_map/ppermute | solution.py:108
  188.5 20.0 %collective-permute-start.31 = (bf16[256,1536]{1,0:T(8,128)(2,1)}, bf16[256,1536]{1,0:T(8,128)(2,1)S(1)}, u32[]{:S(2)}, u32[]{:S(2)}) collective-permute-start(bf16[256,1536]{1,0:T(8,128)(2,1)} %collective-permute-done.29.refs_10_), channel_id=1, source_target_pairs={{4,0},{8,4},{12,8},{28,12},{24,28},{20,24},{16,20},{0,16},{5,1},{9... | collective-permute-start | bytes 2359304 | tf_op jit(solution)/shard_map/ppermute | solution.py:108
  188.7 25.3 %collective-permute-start.36 = (bf16[256,2048]{1,0:T(8,128)(2,1)}, bf16[256,2048]{1,0:T(8,128)(2,1)S(1)}, u32[]{:S(2)}, u32[]{:S(2)}) collective-permute-start(bf16[256,2048]{1,0:T(8,128)(2,1)} %get-tuple-element.606.refs_4_), channel_id=1, source_target_pairs={{0,2},{1,3},{2,0},{3,1},{4,6},{5,7},{6,4},{7,5},{8,10},{9,11},{10,... | collective-permute-start | bytes 3145736 | tf_op jit(solution)/shard_map/ppermute | solution.py:42
  206.6 19.2 %collective-permute-start.35 = (bf16[256,1536]{1,0:T(8,128)(2,1)S(1)}, bf16[256,1536]{1,0:T(8,128)(2,1)S(1)}, u32[]{:S(2)}, u32[]{:S(2)}) collective-permute-start(bf16[256,1536]{1,0:T(8,128)(2,1)S(1)} %collective-permute-done.32.refs_11_), channel_id=1, source_target_pairs={{0,4},{4,8},{8,12},{12,28},{28,24},{24,20},{20,16},{16,0},{1,5},{5... | collective-permute-start | bytes 2359304 | tf_op jit(solution)/shard_map/ppermute | solution.py:108
  208.5 19.0 %collective-permute-start.34 = (bf16[256,1536]{1,0:T(8,128)(2,1)S(1)}, bf16[256,1536]{1,0:T(8,128)(2,1)S(1)}, u32[]{:S(2)}, u32[]{:S(2)}) collective-permute-start(bf16[256,1536]{1,0:T(8,128)(2,1)S(1)} %collective-permute-done.31.refs_11_), channel_id=1, source_target_pairs={{4,0},{8,4},{12,8},{28,12},{24,28},{20,24},{16,20},{0,16},{5,1},{9... | collective-permute-start | bytes 2359304 | tf_op jit(solution)/shard_map/ppermute | solution.py:108
  227.5 20.7 %collective-permute-start.38 = (bf16[256,1536]{1,0:T(8,128)(2,1)}, bf16[256,1536]{1,0:T(8,128)(2,1)}, u32[]{:S(2)}, u32[]{:S(2)}) collective-permute-start(bf16[256,1536]{1,0:T(8,128)(2,1)} %get-tuple-element.618.refs_5_), channel_id=1, source_target_pairs={{0,4},{4,8},{8,12},{12,28},{28,24},{24,20},{20,16},{16,0},{1,5},{5... | collective-permute-start | bytes 2359304 | tf_op jit(solution)/shard_map/ppermute | solution.py:108
  229.6 20.3 %collective-permute-start.37 = (bf16[256,1536]{1,0:T(8,128)(2,1)}, bf16[256,1536]{1,0:T(8,128)(2,1)}, u32[]{:S(2)}, u32[]{:S(2)}) collective-permute-start(bf16[256,1536]{1,0:T(8,128)(2,1)} %get-tuple-element.617.refs_13_), channel_id=1, source_target_pairs={{4,0},{8,4},{12,8},{28,12},{24,28},{20,24},{16,20},{0,16},{5,1},{9... | collective-permute-start | bytes 2359304 | tf_op jit(solution)/shard_map/ppermute | solution.py:108
  248.2 19.4 %collective-permute-start.41 = (bf16[256,1536]{1,0:T(8,128)(2,1)}, bf16[256,1536]{1,0:T(8,128)(2,1)S(1)}, u32[]{:S(2)}, u32[]{:S(2)}) collective-permute-start(bf16[256,1536]{1,0:T(8,128)(2,1)} %collective-permute-done.38.refs_6_), channel_id=1, source_target_pairs={{0,4},{4,8},{8,12},{12,28},{28,24},{24,20},{20,16},{16,0},{1,5},{5... | collective-permute-start | bytes 2359304 | tf_op jit(solution)/shard_map/ppermute | solution.py:108
  249.9 19.4 %collective-permute-start.40 = (bf16[256,1536]{1,0:T(8,128)(2,1)}, bf16[256,1536]{1,0:T(8,128)(2,1)S(1)}, u32[]{:S(2)}, u32[]{:S(2)}) collective-permute-start(bf16[256,1536]{1,0:T(8,128)(2,1)} %collective-permute-done.37.refs_14_), channel_id=1, source_target_pairs={{4,0},{8,4},{12,8},{28,12},{24,28},{20,24},{16,20},{0,16},{5,1},{9... | collective-permute-start | bytes 2359304 | tf_op jit(solution)/shard_map/ppermute | solution.py:108
  267.5 18.3 %collective-permute-start.43 = (bf16[256,1536]{1,0:T(8,128)(2,1)S(1)}, bf16[256,1536]{1,0:T(8,128)(2,1)S(1)}, u32[]{:S(2)}, u32[]{:S(2)}) collective-permute-start(bf16[256,1536]{1,0:T(8,128)(2,1)S(1)} %collective-permute-done.41.refs_7_), channel_id=1, source_target_pairs={{0,4},{4,8},{8,12},{12,28},{28,24},{24,20},{20,16},{16,0},{1,5},{5... | collective-permute-start | bytes 2359304 | tf_op jit(solution)/shard_map/ppermute | solution.py:108
  269.3 18.3 %collective-permute-start.42 = (bf16[256,1536]{1,0:T(8,128)(2,1)S(1)}, bf16[256,1536]{1,0:T(8,128)(2,1)S(1)}, u32[]{:S(2)}, u32[]{:S(2)}) collective-permute-start(bf16[256,1536]{1,0:T(8,128)(2,1)S(1)} %collective-permute-done.40.refs_15_), channel_id=1, source_target_pairs={{4,0},{8,4},{12,8},{28,12},{24,28},{20,24},{16,20},{0,16},{5,1},{9... | collective-permute-start | bytes 2359304 | tf_op jit(solution)/shard_map/ppermute | solution.py:108
  285.8 17.9 %collective-permute-start.45 = (bf16[256,1536]{1,0:T(8,128)(2,1)S(1)}, bf16[256,1536]{1,0:T(8,128)(2,1)S(1)}, u32[]{:S(2)}, u32[]{:S(2)}) collective-permute-start(bf16[256,1536]{1,0:T(8,128)(2,1)S(1)} %collective-permute-done.43.refs_8_), channel_id=1, source_target_pairs={{0,4},{4,8},{8,12},{12,28},{28,24},{24,20},{20,16},{16,0},{1,5},{5... | collective-permute-start | bytes 2359304 | tf_op jit(solution)/shard_map/ppermute | solution.py:108
  287.6 18.0 %collective-permute-start.44 = (bf16[256,1536]{1,0:T(8,128)(2,1)S(1)}, bf16[256,1536]{1,0:T(8,128)(2,1)S(1)}, u32[]{:S(2)}, u32[]{:S(2)}) collective-permute-start(bf16[256,1536]{1,0:T(8,128)(2,1)S(1)} %collective-permute-done.42.refs_16_), channel_id=1, source_target_pairs={{4,0},{8,4},{12,8},{28,12},{24,28},{20,24},{16,20},{0,16},{5,1},{9... | collective-permute-start | bytes 2359304 | tf_op jit(solution)/shard_map/ppermute | solution.py:108
  384.8 25.3 %collective-permute-start.53 = (bf16[256,2048]{1,0:T(8,128)(2,1)S(1)}, bf16[256,2048]{1,0:T(8,128)(2,1)S(1)}, u32[]{:S(2)}, u32[]{:S(2)}) collective-permute-start(bf16[256,2048]{1,0:T(8,128)(2,1)S(1)} %add_convert_fusion.3), channel_id=1, source_target_pairs={{0,2},{1,3},{2,0},{3,1},{4,6},{5,7},{6,4},{7,5},{8,10},{9,11},{10,... | collective-permute-start | bytes 3145736 | tf_op jit(solution)/shard_map/ppermute | solution.py:42
  420.9 25.8 %collective-permute-start.58 = (bf16[256,2048]{1,0:T(8,128)(2,1)}, bf16[256,2048]{1,0:T(8,128)(2,1)}, u32[]{:S(2)}, u32[]{:S(2)}) collective-permute-start(bf16[256,2048]{1,0:T(8,128)(2,1)} %get-tuple-element.728.refs_9_.rest_0_), channel_id=1, source_target_pairs={{0,2},{1,3},{2,0},{3,1},{4,6},{5,7},{6,4},{7,5},{8,10},{9,11},{10,... | collective-permute-start | bytes 3145736 | tf_op jit(solution)/shard_map/ppermute | solution.py:42
  449.6 31.9 %collective-permute-start.60 = (bf16[256,2048]{1,0:T(8,128)(2,1)}, bf16[256,2048]{1,0:T(8,128)(2,1)}, u32[]{:S(2)}, u32[]{:S(2)}) collective-permute-start(bf16[256,2048]{1,0:T(8,128)(2,1)} %add_convert_fusion.2), channel_id=1, source_target_pairs={{0,2},{1,3},{2,0},{3,1},{4,6},{5,7},{6,4},{7,5},{8,10},{9,11},{10,... | collective-permute-start | bytes 3145736 | tf_op jit(solution)/shard_map/ppermute | solution.py:42
  459.5 21.9 %collective-permute-start.61 = (f32[2,128,80]{2,1,0:T(8,128)}, f32[2,128,80]{2,1,0:T(8,128)S(1)}, u32[]{:S(2)}, u32[]{:S(2)}) collective-permute-start(f32[2,128,80]{2,1,0:T(8,128)} %get-tuple-element.766), channel_id=1, source_target_pairs={{4,0},{8,4},{12,8},{5,1},{9,5},{13,9},{6,2},{10,6},{14,10},{7,3},{... | collective-permute-start | bytes 245768 | tf_op jit(solution)/shard_map/ppermute | solution.py:47
  460.8 20.7 %collective-permute-start.62 = (f32[2,128,80]{2,1,0:T(8,128)}, f32[2,128,80]{2,1,0:T(8,128)S(1)}, u32[]{:S(2)}, u32[]{:S(2)}) collective-permute-start(f32[2,128,80]{2,1,0:T(8,128)} %get-tuple-element.766), channel_id=1, source_target_pairs={{8,0},{12,4},{9,1},{13,5},{10,2},{14,6},{11,3},{15,7},{24,16},{28,... | collective-permute-start | bytes 245768 | tf_op jit(solution)/shard_map/ppermute | solution.py:47
  462.1 19.4 %collective-permute-start.63 = (f32[2,128,80]{2,1,0:T(8,128)}, f32[2,128,80]{2,1,0:T(8,128)S(1)}, u32[]{:S(2)}, u32[]{:S(2)}) collective-permute-start(f32[2,128,80]{2,1,0:T(8,128)} %get-tuple-element.766), channel_id=1, source_target_pairs={{12,0},{13,1},{14,2},{15,3},{28,16},{29,17},{30,18},{31,19}} | collective-permute-start | bytes 245768 | tf_op jit(solution)/shard_map/ppermute | solution.py:47
  483.2 26.8 %collective-permute-start.64 = (bf16[256,2048]{1,0:T(8,128)(2,1)S(1)}, bf16[256,2048]{1,0:T(8,128)(2,1)}, u32[]{:S(2)}, u32[]{:S(2)}) collective-permute-start(bf16[256,2048]{1,0:T(8,128)(2,1)S(1)} %add_convert_fusion.1.refs_1_), channel_id=1, source_target_pairs={{0,2},{1,3},{2,0},{3,1},{4,6},{5,7},{6,4},{7,5},{8,10},{9,11},{10,... | collective-permute-start | bytes 3145736 | tf_op jit(solution)/shard_map/ppermute | solution.py:42
  483.8 26.1 %collective-permute-start.65 = (bf16[256,2048]{1,0:T(8,128)(2,1)S(1)}, bf16[256,2048]{1,0:T(8,128)(2,1)}, u32[]{:S(2)}, u32[]{:S(2)}) collective-permute-start(bf16[256,2048]{1,0:T(8,128)(2,1)S(1)} %add_convert_fusion.1.refs_1_), channel_id=1, source_target_pairs={{0,1},{1,0},{2,3},{3,2},{4,5},{5,4},{6,7},{7,6},{8,9},{9,8},{10,11... | collective-permute-start | bytes 3145736 | tf_op jit(solution)/shard_map/ppermute | solution.py:42
  517.4 25.4 %collective-permute-start.70 = (bf16[256,2048]{1,0:T(8,128)(2,1)}, bf16[256,2048]{1,0:T(8,128)(2,1)S(1)}, u32[]{:S(2)}, u32[]{:S(2)}) collective-permute-start(bf16[256,2048]{1,0:T(8,128)(2,1)} %add_convert_fusion), channel_id=1, source_target_pairs={{0,2},{1,3},{2,0},{3,1},{4,6},{5,7},{6,4},{7,5},{8,10},{9,11},{10,... | collective-permute-start | bytes 3145736 | tf_op jit(solution)/shard_map/ppermute | solution.py:42
  548.9 25.8 %collective-permute-start.76 = (bf16[256,2048]{1,0:T(8,128)(2,1)}, bf16[256,2048]{1,0:T(8,128)(2,1)S(1)}, u32[]{:S(2)}, u32[]{:S(2)}) collective-permute-start(bf16[256,2048]{1,0:T(8,128)(2,1)} %own_rows.5.refs_1_), channel_id=1, source_target_pairs={{0,2},{1,3},{2,0},{3,1},{4,6},{5,7},{6,4},{7,5},{8,10},{9,11},{10,... | collective-permute-start | bytes 3145736 | tf_op jit(solution)/shard_map/ppermute | solution.py:42
  (149 other events, 2010.3 us)

commit v6 on v5

--- a/solution.py
+++ b/solution.py
@@ -216,27 +216,42 @@
         later = later * passing(jnp.minimum(here[0] + by + 1, seq - 1))
 
 
-def norm_body(tokens, halo, gain, downs, normed, low, held, sems):
-    rows, window = tokens.shape[0], halo.shape[0]
-    part = rows // 4
+def norm_body(half, tokens, halo, gain, downs, *rest):
+    normed, low, held, out_held, low_held, sems, out_sems = rest[-7:]
+    rows, window, size = tokens.shape[0] // 2, halo.shape[0], held.shape[0]
+    first = 0 if half else window
+    part = rows // 2
+    place = half * (window + rows)
 
     def copy(i):
-        return pltpu.make_async_copy(
-            tokens.at[pl.ds(i * part, part)], held.at[pl.ds(window + i * part, part)], sems.at[i]
-        )
-
-    for i in range(4):
+        source = tokens.at[pl.ds(half * rows + i * part, part)]
+        return pltpu.make_async_copy(source, held.at[pl.ds(first + i * part, part)], sems.at[i])
+
+    def out_copies(i):
+        at, count = spans[i][0], spans[i][1] - spans[i][0]
+        return [
+            pltpu.make_async_copy(x.at[pl.ds(at, count)], y.at[pl.ds(place + at, count)], out_sems.at[k, i])
+            for k, (x, y) in enumerate(((out_held, normed), (low_held, low)))
+        ]
+
+    spans = [(0, first + part), (first + part, size)]
+    for i in range(2):
         copy(i).start()
-    held[:window, :] = halo[...]
-    held[window + rows :, :] = jnp.zeros((held.shape[0] - window - rows, held.shape[1]), bf16)
-    for i in range(4):
+    if half:
+        held[2 * part :, :] = jnp.zeros((size - 2 * part, held.shape[1]), bf16)
+    else:
+        held[:window, :] = halo[...]
+    for i, (start, end) in enumerate(spans):
         copy(i).wait()
-        first = window + i * part if i else 0
-        last = window + (i + 1) * part if i < 3 else held.shape[0]
-        x = held[first:last, :].astype(f32)
+        x = held[start:end, :].astype(f32)
         out = (x * rms_factor(x) * gain[...]).astype(bf16)
-        normed[first:last, :] = out
-        low[first:last, :] = nn(out, downs[...])
+        out_held[start:end, :] = out
+        low_held[start:end, :] = nn(out, downs[...])
+        for one in out_copies(i):
+            one.start()
+    for i in range(2):
+        for one in out_copies(i):
+            one.wait()
 
 
 def pack_body(units, gate, up, down, q_up, k_up, v_up, map_q, map_k, o_up, *outs):
@@ -897,21 +912,35 @@
     gain_attn = attention_norm_gain.astype(f32)[None, :]
     gain_mlp = feedforward_norm_gain.astype(f32)[None, :]
     downs = jnp.concatenate([query_adapter_down, key_adapter_down, value_adapter_down], axis=1)
-    normed, low = pl.pallas_call(
-        norm_body,
-        grid_spec=pltpu.PrefetchScalarGridSpec(
-            num_scalar_prefetch=0,
-            grid=(1,),
-            in_specs=[ANY, whole((WIN, model)), whole((1, model)), whole((model, 3 * rank))],
-            out_specs=[whole((ext, model)), whole((ext, 3 * rank))],
-            scratch_shapes=[pltpu.VMEM((ext, model), bf16), pltpu.SemaphoreType.DMA((4,))],
-        ),
-        out_shape=[jax.ShapeDtypeStruct((ext, model), bf16), jax.ShapeDtypeStruct((ext, 3 * rank), f32)],
-        compiler_params=params(BIG),
-        cost_estimate=SMALL,
-        name="norm",
-    )(clock.tie(tokens), halo, gain_attn, downs)
-    normed, low = clock.wait(normed, low)
+    low_shape = (ext, 3 * rank)
+
+    def norm_half(half, earlier):
+        size = rows // 2 + (ext - rows - WIN if half else WIN)
+        return pl.pallas_call(
+            lambda *refs: norm_body(half, *refs),
+            grid_spec=pltpu.PrefetchScalarGridSpec(
+                num_scalar_prefetch=0,
+                grid=(1,),
+                in_specs=[ANY, whole((WIN, model)), whole((1, model)), whole((model, 3 * rank))] + [ANY] * len(earlier),
+                out_specs=[ANY, ANY],
+                scratch_shapes=[
+                    pltpu.VMEM((size, model), bf16),
+                    pltpu.VMEM((size, model), bf16),
+                    pltpu.VMEM((size, 3 * rank), f32),
+                    pltpu.SemaphoreType.DMA((2,)),
+                    pltpu.SemaphoreType.DMA((2, 2)),
+                ],
+            ),
+            out_shape=[jax.ShapeDtypeStruct((ext, model), bf16), jax.ShapeDtypeStruct(low_shape, f32)],
+            input_output_aliases={4: 0, 5: 1} if earlier else {},
+            compiler_params=params(BIG),
+            cost_estimate=SMALL,
+            name="norm",
+        )(clock.tie(tokens), halo, gain_attn, downs, *earlier)
+
+    normed_low = clock.wait(*norm_half(0, ()))
+    attn_chain.step()
+    normed, low = clock.wait(*norm_half(1, normed_low))
     attn_chain.step()
     all_units = [x for part in FFN_UNITS for x in part]
     pack_in = (
@@ -940,7 +969,7 @@
     )(clock.tie(gate_weight), *pack_in[1:])
     *packed, ups, ups_twice, maps_q, maps_k, o_up = clock.wait(*packed)
     chains = [[Chain(clock, 1, lambda x: x, packed[2 * i]), Chain(clock, -1, lambda x: x, packed[2 * i + 1])] for i in range(2)]
-    for _ in range(ring - 5):
+    for _ in range(ring - 6):
         attn_chain.step()
     attn_pieces = attn_chain.pieces()
     turn(0)

time: 592 us -> 588 us (level)
    ppermute x42, waiting for transfers between devices: 130 us -> 121 us  [step(): lane.append(lax.ppermute(lane[-1], ('dp', 'seq'), way))]
    unnamed x211 -> x209, local copies, waits for them, and re-layouts: 20.7 us -> 18.8 us
  transfers between devices with their start and end apart: 79 -> 79, of which waited for: 42 -> 41; matrix products, arithmetic and copies ran while one was open for 3% -> 3% of each run, Pallas kernels for 38% -> 39%
where the time goes in v6:
time: 588 us; the launch traced here: 580 us
  Pallas kernels  254 us (43%)
  waiting for transfers between devices  192 us (33%)
  starting transfers between devices  86.8 us (15%)
  local copies, waits for them, and re-layouts  26.3 us (4%)
  other arithmetic  18.8 us (3%)
    ppermute x42, waiting for transfers between devices, step(): lane.append(lax.ppermute(lane[-1], ('dp', 'seq'), way))  121 us
    pallas_call x6, Pallas kernels, ffn(): pl.pallas_call(lambda *refs: ffn_body(sizes, units, bool(sums), last, *re...  108 us
    ppermute x29, waiting for transfers between devices, exchange(): return lax.ppermute(x, axis, [(i, i ^ bit) for i in range(count)])  66.2 us
    ppermute x42, starting transfers between devices, step(): lane.append(lax.ppermute(lane[-1], ('dp', 'seq'), way))  46.9 us
    ppermute x29, starting transfers between devices, exchange(): return lax.ppermute(x, axis, [(i, i ^ bit) for i in range(count)])  20.4 us
    ppermute x8, starting transfers between devices, shifted(): lax.ppermute(x, axis, [(i, i + by) for i in range(count) if 0 <= i + by <...  19.4 us
    unnamed x209, local copies, waits for them, and re-layouts  18.8 us
    pallas_call x1, Pallas kernels, per_device(): pl.pallas_call(lambda *refs: backward_body((kv_heads, group, head, chunks...  17.2 us
  transfers between devices with their start and end apart: 79, of which 41 were waited for; matrix products, arithmetic and copies ran while one was open for 3% of the time, Pallas kernels for 39%

profile of v6, /device:TPU:0, one launch (start us, length us, event | category | flops | bytes accessed | tf_op | source)
XLA Modules:
  0.0 579.7 jit_solution(9441265084349974526)
XLA Ops:
  31.2 5.1 norm.2
  57.4 6.1 %collective-permute-done.10.refs_18_.refs_11_.refs_17_.refs_15_ = bf16[128,1280]{1,0:T(8,128)(2,1)S(1)} collective-permute-done((bf16[128,1280]{1,0:T(8,128)(2,1)S(1)}, bf16[128,1280]{1,0:T(8,128)(2,1)S(1)}, u32[]{:S(2)}, u32[]{:S(2)}) %collective-permute-start.10) | collective-permute-done | bytes 327712 | tf_op jit(solution)/shard_map/ppermute | solution.py:108
  69.6 7.5 %collective-permute-done.14.refs_27_.refs_20_.refs_26_.refs_24_ = bf16[128,1280]{1,0:T(8,128)(2,1)S(1)} collective-permute-done((bf16[128,1280]{1,0:T(8,128)(2,1)S(1)}, bf16[128,1280]{1,0:T(8,128)(2,1)S(1)}, u32[]{:S(2)}, u32[]{:S(2)}) %collective-permute-start.14) | collective-permute-done | bytes 327712 | tf_op jit(solution)/shard_map/ppermute | solution.py:108
  81.9 16.9 %prep.1 = (bf16[512,1024]{1,0:T(8,128)(2,1)}, bf16[1024,1024]{1,0:T(8,128)(2,1)}, bf16[1152,128]{1,0:T(8,128)(2,1)}, bf16[128,1152]{1,0:T(8,128)(2,1)}, bf16[115...) custom-call(s32[16]{0:T(128)} %get-tuple-element.822.refs_0_, ...), custom_call_target="tpu_custom_call" | custom-call | flops 1 | bytes 1 | tf_op jit(solution)/shard_map/prep/pallas_call | solution.py:995
  104.7 5.3 collective-permute-start.20
  114.4 10.5 %attend.1 = (bf16[1024,512]{1,0:T(8,128)(2,1)}, f32[512,1024]{1,0:T(8,128)}, f32[8,1024]{1,0:T(8,128)}, bf16[8,2,128,80]{3,2,1,0:T(8,128)(2,1)}) custom-call(s32[9]{0:T(128)} %copy-done.17, f32[3]{0:T(128)} %copy-done.20, bf16[512,1024]{1,0:T(8,128)(2,1)} %get-tuple-element.560.refs_2_.refs_1_, ...), custom_call_target="tpu_custom_call" | custom-call | flops 1 | bytes 1 | tf_op jit(solution)/shard_map/attend/pallas_call | solution.py:1014
  129.4 10.7 %project.1 = (bf16[256,2048]{1,0:T(8,128)(2,1)}, bf16[256,2048]{1,0:T(8,128)(2,1)}, bf16[256,2048]{1,0:T(8,128)(2,1)}, bf16[256,2048]{1,0:T(8,128)(2,1)}, f32[1024,8]{1,0:T(8,128)}) custom-call(s32[16]{0:T(128)} %get-tuple-element.822.refs_0_, s32[4]{0:T(128)} %pad_add_fusion.refs_1_.nat.refs_0_, bf16[1024,512]{1,0:T(8,128)(2,1)} %get-tuple-element.576.refs_2_.att, ...), custom_call_target="tpu_custom_call" | custom-call | flops 1 | bytes 1 | tf_op jit(solution)/shard_map/project/pallas_call | solution.py:1055
  147.9 12.7 %collective-permute-done.28.refs_9_ = bf16[256,1536]{1,0:T(8,128)(2,1)S(1)} collective-permute-done((bf16[256,1536]{1,0:T(8,128)(2,1)S(1)}, bf16[256,1536]{1,0:T(8,128)(2,1)S(1)}, u32[]{:S(2)}, u32[]{:S(2)}) %collective-permute-start.28) | collective-permute-done | bytes 786464 | tf_op jit(solution)/shard_map/ppermute | solution.py:108
  163.3 8.4 %collective-permute-done.26.across = bf16[256,2048]{1,0:T(8,128)(2,1)S(1)} collective-permute-done((bf16[256,2048]{1,0:T(8,128)(2,1)S(1)}, bf16[256,2048]{1,0:T(8,128)(2,1)S(1)}, u32[]{:S(2)}, u32[]{:S(2)}) %collective-permute-start.26) | collective-permute-done | bytes 1048608 | tf_op jit(solution)/shard_map/ppermute | solution.py:42
  185.0 16.4 %collective-permute-done.32.refs_11_ = bf16[256,1536]{1,0:T(8,128)(2,1)S(1)} collective-permute-done((bf16[256,1536]{1,0:T(8,128)(2,1)S(1)}, bf16[256,1536]{1,0:T(8,128)(2,1)S(1)}, u32[]{:S(2)}, u32[]{:S(2)}) %collective-permute-start.32) | collective-permute-done | bytes 786464 | tf_op jit(solution)/shard_map/ppermute | solution.py:108
  203.6 5.3 collective-permute-done.36.refs_4_
  209.0 11.6 %collective-permute-done.35.refs_12_ = bf16[256,1536]{1,0:T(8,128)(2,1)S(1)} collective-permute-done((bf16[256,1536]{1,0:T(8,128)(2,1)S(1)}, bf16[256,1536]{1,0:T(8,128)(2,1)S(1)}, u32[]{:S(2)}, u32[]{:S(2)}) %collective-permute-start.35) | collective-permute-done | bytes 786464 | tf_op jit(solution)/shard_map/ppermute | solution.py:108
  226.0 14.7 %feed_forward.6 = (f32[2,256,2048]{2,1,0:T(8,128)}, f32[2,256,2048]{2,1,0:T(8,128)}) custom-call(s32[8]{0:T(128)} %copy-done.96, s32[4]{0:T(128)} %pad_add_fusion.refs_1_.nat.refs_0_, bf16[1024,2048]{1,0:T(8,128)(2,1)} %cotangent.1, bf16[256,2048]{1,0:T(8,128)(2,1)} %copy-done.26, bf16[256,2048]{1,0:T(8,128)(2,1)} %copy-done.25, ...), custom_call_target="tpu_custom_call" | custom-call | flops 1 | bytes 1 | tf_op jit(solution)/shard_map/feed_forward/pallas_call | solution.py:1111
  245.1 14.7 %feed_forward.7 = (f32[2,256,2048]{2,1,0:T(8,128)}, f32[2,256,2048]{2,1,0:T(8,128)}) custom-call(s32[8]{0:T(128)} %copy-done.96, s32[4]{0:T(128)} %pad_add_fusion.refs_1_.nat.refs_0_, bf16[1024,2048]{1,0:T(8,128)(2,1)} %cotangent.1, bf16[256,2048]{1,0:T(8,128)(2,1)} %copy-done.24, bf16[256,2048]{1,0:T(8,128)(2,1)} %get-tuple-element.620.refs_4_, ...), custom_call_target="tpu_custom_call" | custom-call | flops 1 | bytes 1 | tf_op jit(solution)/shard_map/feed_forward/pallas_call | solution.py:1111
  264.5 15.6 %feed_forward.8 = (f32[2,256,2048]{2,1,0:T(8,128)}, f32[2,256,2048]{2,1,0:T(8,128)}) custom-call(s32[8]{0:T(128)} %copy-done.95, s32[4]{0:T(128)} %pad_add_fusion.refs_1_.nat.refs_0_, bf16[1024,2048]{1,0:T(8,128)(2,1)} %cotangent.1, bf16[256,2048]{1,0:T(8,128)(2,1)} %copy-done.26, bf16[256,2048]{1,0:T(8,128)(2,1)} %copy-done.25, ...), custom_call_target="tpu_custom_call" | custom-call | flops 1 | bytes 1 | tf_op jit(solution)/shard_map/feed_forward/pallas_call | solution.py:1111
  282.9 15.7 %feed_forward.9 = (f32[2,256,2048]{2,1,0:T(8,128)}, f32[2,256,2048]{2,1,0:T(8,128)}) custom-call(s32[8]{0:T(128)} %copy-done.95, s32[4]{0:T(128)} %pad_add_fusion.refs_1_.nat.refs_0_, bf16[1024,2048]{1,0:T(8,128)(2,1)} %cotangent.1, bf16[256,2048]{1,0:T(8,128)(2,1)} %copy-done.24, bf16[256,2048]{1,0:T(8,128)(2,1)} %get-tuple-element.620.refs_4_, ...), custom_call_target="tpu_custom_call" | custom-call | flops 1 | bytes 1 | tf_op jit(solution)/shard_map/feed_forward/pallas_call | solution.py:1111
  300.7 15.7 %collective-permute-done.47.refs_10_ = bf16[256,1536]{1,0:T(8,128)(2,1)S(1)} collective-permute-done((bf16[256,1536]{1,0:T(8,128)(2,1)S(1)}, bf16[256,1536]{1,0:T(8,128)(2,1)S(1)}, u32[]{:S(2)}, u32[]{:S(2)}) %collective-permute-start.47) | collective-permute-done | bytes 786464 | tf_op jit(solution)/shard_map/ppermute | solution.py:108
  318.4 15.7 %collective-permute-done.49.refs_11_ = bf16[256,1536]{1,0:T(8,128)(2,1)S(1)} collective-permute-done((bf16[256,1536]{1,0:T(8,128)(2,1)S(1)}, bf16[256,1536]{1,0:T(8,128)(2,1)S(1)}, u32[]{:S(2)}, u32[]{:S(2)}) %collective-permute-start.49) | collective-permute-done | bytes 786464 | tf_op jit(solution)/shard_map/ppermute | solution.py:108
  336.2 13.1 %collective-permute-done.51.refs_12_ = bf16[256,1536]{1,0:T(8,128)(2,1)S(1)} collective-permute-done((bf16[256,1536]{1,0:T(8,128)(2,1)S(1)}, bf16[256,1536]{1,0:T(8,128)(2,1)S(1)}, u32[]{:S(2)}, u32[]{:S(2)}) %collective-permute-start.51) | collective-permute-done | bytes 786464 | tf_op jit(solution)/shard_map/ppermute | solution.py:108
  351.6 23.5 %feed_forward.10 = (bf16[256,2048]{1,0:T(8,128)(2,1)}, bf16[256,2048]{1,0:T(8,128)(2,1)}, bf16[256,2048]{1,0:T(8,128)(2,1)}, bf16[256,2048]{1,0:T(8,128)(2,1)}) custom-call(s32[16]{0:T(128)} %get-tuple-element.716.refs_0_, s32[4]{0:T(128)} %pad_add_fusion.refs_1_.nat.refs_0_, bf16[1024,2048]{1,0:T(8,128)(2,1)} %cotangent.1, bf16[256,2048]{1,0:T(8,128)(2,1)} %copy-done.26, ...), custom_call_target="tpu_custom_call" | custom-call | flops 1 | bytes 1 | tf_op jit(solution)/shard_map/feed_forward/pallas_call | solution.py:1111
  381.2 23.7 %feed_forward.11 = (bf16[256,2048]{1,0:T(8,128)(2,1)}, bf16[256,2048]{1,0:T(8,128)(2,1)}, bf16[256,2048]{1,0:T(8,128)(2,1)}, bf16[256,2048]{1,0:T(8,128)(2,1)}) custom-call(s32[16]{0:T(128)} %get-tuple-element.716.refs_0_, s32[4]{0:T(128)} %pad_add_fusion.refs_1_.nat.refs_0_, bf16[1024,2048]{1,0:T(8,128)(2,1)} %cotangent.1, bf16[256,2048]{1,0:T(8,128)(2,1)} %copy-done.24, ...), custom_call_target="tpu_custom_call" | custom-call | flops 1 | bytes 1 | tf_op jit(solution)/shard_map/feed_forward/pallas_call | solution.py:1111
  408.9 5.6 own_rows.4
  418.4 8.5 %project_back.2 = (bf16[512,1024]{1,0:T(8,128)(2,1)}, f32[8,1024]{1,0:T(8,128)}, f32[1024,8]{1,0:T(8,128)}, f32[2,128,80]{2,1,0:T(8,128)}) custom-call(s32[16]{0:T(128)} %get-tuple-element.822.refs_0_, s32[4]{0:T(128)} %pad_add_fusion.refs_1_.nat.refs_0_, s32[9]{0:T(128)} %copy-done.17, bf16[2048,8]{1,0:T(8,128)(2,1)} %get-tuple-element.746.refs_3_, ...), custom_call_target="tpu_custom_call" | custom-call | flops 1 | bytes 1 | tf_op jit(solution)/shard_map/project_back/pallas_call | solution.py:1169
  430.9 10.6 %collective-permute-done.58.refs_9_.rest_2_ = bf16[256,2048]{1,0:T(8,128)(2,1)} collective-permute-done((bf16[256,2048]{1,0:T(8,128)(2,1)}, bf16[256,2048]{1,0:T(8,128)(2,1)}, u32[]{:S(2)}, u32[]{:S(2)}) %collective-permute-start.58) | collective-permute-done | bytes 1048608 | tf_op jit(solution)/shard_map/ppermute | solution.py:42
  445.9 8.4 %project_back.3 = (bf16[512,1024]{1,0:T(8,128)(2,1)}, f32[8,1024]{1,0:T(8,128)}, f32[1024,8]{1,0:T(8,128)}, f32[2,128,80]{2,1,0:T(8,128)}) custom-call(s32[16]{0:T(128)} %get-tuple-element.822.refs_0_, s32[4]{0:T(128)} %pad_add_fusion.refs_1_.nat.refs_0_, s32[9]{0:T(128)} %copy-done.17, ...), custom_call_target="tpu_custom_call", output_to_operand_aliasing={{0}: (27, {}), {1}: (28, {}), {2}: (29, {})} | custom-call | flops 1 | bytes 1 | tf_op jit(solution)/shard_map/project_back/pallas_call | solution.py:1169
  459.1 17.2 %attend_back.1 = (bf16[1024,512]{1,0:T(8,128)(2,1)}, f32[128,1152]{1,0:T(8,128)}, f32[128,1152]{1,0:T(8,128)}, f32[256,1152]{1,0:T(8,128)}, f32[2,256,256]{2,1,0:T(8,128)}) custom-call(s32[9]{0:T(128)S(1)} %copy-done.18, bf16[512,1024]{1,0:T(8,128)(2,1)} %get-tuple-element.560.refs_2_.refs_1_, bf16[1024,1024]{1,0:T(8,128)(2,1)} %get-tuple-element.561.refs_3_.refs_7_.refs_2_, ...), custom_call_target="tpu_custom_call" | custom-call | flops 1 | bytes 1 | tf_op jit(solution)/shard_map/attend_back/pallas_call | solution.py:1239
  486.3 5.2 adapter_o.1
  493.3 12.4 %norm_back.1 = (bf16[256,2048]{1,0:T(8,128)(2,1)}, bf16[256,2048]{1,0:T(8,128)(2,1)}, bf16[256,2048]{1,0:T(8,128)(2,1)}, bf16[256,2048]{1,0:T(8,128)(2,1)}) custom-call(s32[16]{0:T(128)} %get-tuple-element.822.refs_0_, s32[4]{0:T(128)} %pad_add_fusion.refs_1_.nat.refs_0_, bf16[1024,512]{1,0:T(8,128)(2,1)} %get-tuple-element.845.refs_2_.refs_0_, ...), custom_call_target="tpu_custom_call" | custom-call | flops 1 | bytes 1 | tf_op jit(solution)/shard_map/norm_back/pallas_call | solution.py:1311
  515.3 6.2 %adapters.1 = f32[8,18,8,128]{3,2,1,0:T(8,128)} custom-call(bf16[1024,512]{1,0:T(8,128)(2,1)} %get-tuple-element.845.refs_2_.refs_0_, f32[256,1024]{1,0:T(8,128)} %get-tuple-element.824.refs_3_.refs_1_, f32[256,128]{1,0:T(8,128)} %copy-done.79, f32[32,1024]{1,0:T(8,128)} %copy-done.2, f32[32,1024]{1,0:T(8,128)} %copy-done.4, ...), custom_call_target="tpu_custom_call" | custom-call | flops 1 | bytes 1 | tf_op jit(solution)/shard_map/adapters/pallas_call | solution.py:1349
  522.8 5.3 collective-permute-done.71
  538.5 5.2 own_rows.5.refs_1_
  555.9 13.7 %collective-permute-done.76.refs_1_ = bf16[256,2048]{1,0:T(8,128)(2,1)} collective-permute-done((bf16[256,2048]{1,0:T(8,128)(2,1)}, bf16[256,2048]{1,0:T(8,128)(2,1)}, u32[]{:S(2)}, u32[]{:S(2)}) %collective-permute-start.76) | collective-permute-done | bytes 1048608 | tf_op jit(solution)/shard_map/ppermute | solution.py:42
  (403 shorter events, 210.2 us)
Async XLA Ops:
  78.3 20.5 %collective-permute-start.16 = (bf16[256,1536]{1,0:T(8,128)(2,1)}, bf16[256,1536]{1,0:T(8,128)(2,1)S(1)}, u32[]{:S(2)}, u32[]{:S(2)}) collective-permute-start(bf16[256,1536]{1,0:T(8,128)(2,1)} %get-tuple-element.533.refs_5_), channel_id=1, source_target_pairs={{0,4},{4,8},{8,12},{12,28},{28,24},{24,20},{20,16},{16,0},{1,5},{5... | collective-permute-start | bytes 2359304 | tf_op jit(solution)/shard_map/ppermute | solution.py:108
  80.2 20.5 %collective-permute-start.15 = (bf16[256,1536]{1,0:T(8,128)(2,1)}, bf16[256,1536]{1,0:T(8,128)(2,1)S(1)}, u32[]{:S(2)}, u32[]{:S(2)}) collective-permute-start(bf16[256,1536]{1,0:T(8,128)(2,1)} %get-tuple-element.532.refs_5_), channel_id=1, source_target_pairs={{4,0},{8,4},{12,8},{28,12},{24,28},{20,24},{16,20},{0,16},{5,1},{9... | collective-permute-start | bytes 2359304 | tf_op jit(solution)/shard_map/ppermute | solution.py:108
  98.8 26.1 %collective-permute-start.18 = (bf16[256,1536]{1,0:T(8,128)(2,1)S(1)}, bf16[256,1536]{1,0:T(8,128)(2,1)S(1)}, u32[]{:S(2)}, u32[]{:S(2)}) collective-permute-start(bf16[256,1536]{1,0:T(8,128)(2,1)S(1)} %collective-permute-done.16.refs_6_), channel_id=1, source_target_pairs={{0,4},{4,8},{8,12},{12,28},{28,24},{24,20},{20,16},{16,0},{1,5},{5... | collective-permute-start | bytes 2359304 | tf_op jit(solution)/shard_map/ppermute | solution.py:108
  100.8 26.4 %collective-permute-start.17 = (bf16[256,1536]{1,0:T(8,128)(2,1)S(1)}, bf16[256,1536]{1,0:T(8,128)(2,1)}, u32[]{:S(2)}, u32[]{:S(2)}) collective-permute-start(bf16[256,1536]{1,0:T(8,128)(2,1)S(1)} %collective-permute-done.15.refs_6_), channel_id=1, source_target_pairs={{4,0},{8,4},{12,8},{28,12},{24,28},{20,24},{16,20},{0,16},{5,1},{9... | collective-permute-start | bytes 2359304 | tf_op jit(solution)/shard_map/ppermute | solution.py:108
  140.8 19.8 %collective-permute-start.28 = (bf16[256,1536]{1,0:T(8,128)(2,1)S(1)}, bf16[256,1536]{1,0:T(8,128)(2,1)S(1)}, u32[]{:S(2)}, u32[]{:S(2)}) collective-permute-start(bf16[256,1536]{1,0:T(8,128)(2,1)S(1)} %collective-permute-done.23.refs_8_), channel_id=1, source_target_pairs={{0,4},{4,8},{8,12},{12,28},{28,24},{24,20},{20,16},{16,0},{1,5},{5... | collective-permute-start | bytes 2359304 | tf_op jit(solution)/shard_map/ppermute | solution.py:108
  142.8 19.5 %collective-permute-start.27 = (bf16[256,1536]{1,0:T(8,128)(2,1)S(1)}, bf16[256,1536]{1,0:T(8,128)(2,1)}, u32[]{:S(2)}, u32[]{:S(2)}) collective-permute-start(bf16[256,1536]{1,0:T(8,128)(2,1)S(1)} %collective-permute-done.22.refs_8_), channel_id=1, source_target_pairs={{4,0},{8,4},{12,8},{28,12},{24,28},{20,24},{16,20},{0,16},{5,1},{9... | collective-permute-start | bytes 2359304 | tf_op jit(solution)/shard_map/ppermute | solution.py:108
  146.4 25.3 %collective-permute-start.26 = (bf16[256,2048]{1,0:T(8,128)(2,1)S(1)}, bf16[256,2048]{1,0:T(8,128)(2,1)S(1)}, u32[]{:S(2)}, u32[]{:S(2)}) collective-permute-start(bf16[256,2048]{1,0:T(8,128)(2,1)S(1)} %add_convert_fusion.4), channel_id=1, source_target_pairs={{0,2},{1,3},{2,0},{3,1},{4,6},{5,7},{6,4},{7,5},{8,10},{9,11},{10,... | collective-permute-start | bytes 3145736 | tf_op jit(solution)/shard_map/ppermute | solution.py:42
  160.6 19.2 %collective-permute-start.30 = (bf16[256,1536]{1,0:T(8,128)(2,1)S(1)}, bf16[256,1536]{1,0:T(8,128)(2,1)S(1)}, u32[]{:S(2)}, u32[]{:S(2)}) collective-permute-start(bf16[256,1536]{1,0:T(8,128)(2,1)S(1)} %collective-permute-done.28.refs_9_), channel_id=1, source_target_pairs={{0,4},{4,8},{8,12},{12,28},{28,24},{24,20},{20,16},{16,0},{1,5},{5... | collective-permute-start | bytes 2359304 | tf_op jit(solution)/shard_map/ppermute | solution.py:108
  162.3 19.2 %collective-permute-start.29 = (bf16[256,1536]{1,0:T(8,128)(2,1)}, bf16[256,1536]{1,0:T(8,128)(2,1)}, u32[]{:S(2)}, u32[]{:S(2)}) collective-permute-start(bf16[256,1536]{1,0:T(8,128)(2,1)} %collective-permute-done.27.refs_9_), channel_id=1, source_target_pairs={{4,0},{8,4},{12,8},{28,12},{24,28},{20,24},{16,20},{0,16},{5,1},{9... | collective-permute-start | bytes 2359304 | tf_op jit(solution)/shard_map/ppermute | solution.py:108
  181.5 20.0 %collective-permute-start.32 = (bf16[256,1536]{1,0:T(8,128)(2,1)S(1)}, bf16[256,1536]{1,0:T(8,128)(2,1)S(1)}, u32[]{:S(2)}, u32[]{:S(2)}) collective-permute-start(bf16[256,1536]{1,0:T(8,128)(2,1)S(1)} %collective-permute-done.30.refs_10_), channel_id=1, source_target_pairs={{0,4},{4,8},{8,12},{12,28},{28,24},{24,20},{20,16},{16,0},{1,5},{5... | collective-permute-start | bytes 2359304 | tf_op jit(solution)/shard_map/ppermute | solution.py:108
  183.5 20.0 %collective-permute-start.31 = (bf16[256,1536]{1,0:T(8,128)(2,1)}, bf16[256,1536]{1,0:T(8,128)(2,1)S(1)}, u32[]{:S(2)}, u32[]{:S(2)}) collective-permute-start(bf16[256,1536]{1,0:T(8,128)(2,1)} %collective-permute-done.29.refs_10_), channel_id=1, source_target_pairs={{4,0},{8,4},{12,8},{28,12},{24,28},{20,24},{16,20},{0,16},{5,1},{9... | collective-permute-start | bytes 2359304 | tf_op jit(solution)/shard_map/ppermute | solution.py:108
  183.5 25.5 %collective-permute-start.36 = (bf16[256,2048]{1,0:T(8,128)(2,1)}, bf16[256,2048]{1,0:T(8,128)(2,1)S(1)}, u32[]{:S(2)}, u32[]{:S(2)}) collective-permute-start(bf16[256,2048]{1,0:T(8,128)(2,1)} %get-tuple-element.620.refs_4_), channel_id=1, source_target_pairs={{0,2},{1,3},{2,0},{3,1},{4,6},{5,7},{6,4},{7,5},{8,10},{9,11},{10,... | collective-permute-start | bytes 3145736 | tf_op jit(solution)/shard_map/ppermute | solution.py:42
  201.4 19.2 %collective-permute-start.35 = (bf16[256,1536]{1,0:T(8,128)(2,1)S(1)}, bf16[256,1536]{1,0:T(8,128)(2,1)S(1)}, u32[]{:S(2)}, u32[]{:S(2)}) collective-permute-start(bf16[256,1536]{1,0:T(8,128)(2,1)S(1)} %collective-permute-done.32.refs_11_), channel_id=1, source_target_pairs={{0,4},{4,8},{8,12},{12,28},{28,24},{24,20},{20,16},{16,0},{1,5},{5... | collective-permute-start | bytes 2359304 | tf_op jit(solution)/shard_map/ppermute | solution.py:108
  203.4 18.9 %collective-permute-start.34 = (bf16[256,1536]{1,0:T(8,128)(2,1)S(1)}, bf16[256,1536]{1,0:T(8,128)(2,1)S(1)}, u32[]{:S(2)}, u32[]{:S(2)}) collective-permute-start(bf16[256,1536]{1,0:T(8,128)(2,1)S(1)} %collective-permute-done.31.refs_11_), channel_id=1, source_target_pairs={{4,0},{8,4},{12,8},{28,12},{24,28},{20,24},{16,20},{0,16},{5,1},{9... | collective-permute-start | bytes 2359304 | tf_op jit(solution)/shard_map/ppermute | solution.py:108
  222.4 20.7 %collective-permute-start.38 = (bf16[256,1536]{1,0:T(8,128)(2,1)}, bf16[256,1536]{1,0:T(8,128)(2,1)}, u32[]{:S(2)}, u32[]{:S(2)}) collective-permute-start(bf16[256,1536]{1,0:T(8,128)(2,1)} %get-tuple-element.632.refs_5_), channel_id=1, source_target_pairs={{0,4},{4,8},{8,12},{12,28},{28,24},{24,20},{20,16},{16,0},{1,5},{5... | collective-permute-start | bytes 2359304 | tf_op jit(solution)/shard_map/ppermute | solution.py:108
  224.5 20.3 %collective-permute-start.37 = (bf16[256,1536]{1,0:T(8,128)(2,1)}, bf16[256,1536]{1,0:T(8,128)(2,1)}, u32[]{:S(2)}, u32[]{:S(2)}) collective-permute-start(bf16[256,1536]{1,0:T(8,128)(2,1)} %get-tuple-element.631.refs_13_), channel_id=1, source_target_pairs={{4,0},{8,4},{12,8},{28,12},{24,28},{20,24},{16,20},{0,16},{5,1},{9... | collective-permute-start | bytes 2359304 | tf_op jit(solution)/shard_map/ppermute | solution.py:108
  243.1 19.4 %collective-permute-start.41 = (bf16[256,1536]{1,0:T(8,128)(2,1)}, bf16[256,1536]{1,0:T(8,128)(2,1)S(1)}, u32[]{:S(2)}, u32[]{:S(2)}) collective-permute-start(bf16[256,1536]{1,0:T(8,128)(2,1)} %collective-permute-done.38.refs_6_), channel_id=1, source_target_pairs={{0,4},{4,8},{8,12},{12,28},{28,24},{24,20},{20,16},{16,0},{1,5},{5... | collective-permute-start | bytes 2359304 | tf_op jit(solution)/shard_map/ppermute | solution.py:108
  244.8 19.4 %collective-permute-start.40 = (bf16[256,1536]{1,0:T(8,128)(2,1)}, bf16[256,1536]{1,0:T(8,128)(2,1)S(1)}, u32[]{:S(2)}, u32[]{:S(2)}) collective-permute-start(bf16[256,1536]{1,0:T(8,128)(2,1)} %collective-permute-done.37.refs_14_), channel_id=1, source_target_pairs={{4,0},{8,4},{12,8},{28,12},{24,28},{20,24},{16,20},{0,16},{5,1},{9... | collective-permute-start | bytes 2359304 | tf_op jit(solution)/shard_map/ppermute | solution.py:108
  262.4 18.3 %collective-permute-start.43 = (bf16[256,1536]{1,0:T(8,128)(2,1)S(1)}, bf16[256,1536]{1,0:T(8,128)(2,1)S(1)}, u32[]{:S(2)}, u32[]{:S(2)}) collective-permute-start(bf16[256,1536]{1,0:T(8,128)(2,1)S(1)} %collective-permute-done.41.refs_7_), channel_id=1, source_target_pairs={{0,4},{4,8},{8,12},{12,28},{28,24},{24,20},{20,16},{16,0},{1,5},{5... | collective-permute-start | bytes 2359304 | tf_op jit(solution)/shard_map/ppermute | solution.py:108
  264.2 18.3 %collective-permute-start.42 = (bf16[256,1536]{1,0:T(8,128)(2,1)S(1)}, bf16[256,1536]{1,0:T(8,128)(2,1)S(1)}, u32[]{:S(2)}, u32[]{:S(2)}) collective-permute-start(bf16[256,1536]{1,0:T(8,128)(2,1)S(1)} %collective-permute-done.40.refs_15_), channel_id=1, source_target_pairs={{4,0},{8,4},{12,8},{28,12},{24,28},{20,24},{16,20},{0,16},{5,1},{9... | collective-permute-start | bytes 2359304 | tf_op jit(solution)/shard_map/ppermute | solution.py:108
  280.7 17.9 %collective-permute-start.45 = (bf16[256,1536]{1,0:T(8,128)(2,1)S(1)}, bf16[256,1536]{1,0:T(8,128)(2,1)S(1)}, u32[]{:S(2)}, u32[]{:S(2)}) collective-permute-start(bf16[256,1536]{1,0:T(8,128)(2,1)S(1)} %collective-permute-done.43.refs_8_), channel_id=1, source_target_pairs={{0,4},{4,8},{8,12},{12,28},{28,24},{24,20},{20,16},{16,0},{1,5},{5... | collective-permute-start | bytes 2359304 | tf_op jit(solution)/shard_map/ppermute | solution.py:108
  282.5 18.0 %collective-permute-start.44 = (bf16[256,1536]{1,0:T(8,128)(2,1)S(1)}, bf16[256,1536]{1,0:T(8,128)(2,1)S(1)}, u32[]{:S(2)}, u32[]{:S(2)}) collective-permute-start(bf16[256,1536]{1,0:T(8,128)(2,1)S(1)} %collective-permute-done.42.refs_16_), channel_id=1, source_target_pairs={{4,0},{8,4},{12,8},{28,12},{24,28},{20,24},{16,20},{0,16},{5,1},{9... | collective-permute-start | bytes 2359304 | tf_op jit(solution)/shard_map/ppermute | solution.py:108
  379.7 25.3 %collective-permute-start.53 = (bf16[256,2048]{1,0:T(8,128)(2,1)S(1)}, bf16[256,2048]{1,0:T(8,128)(2,1)S(1)}, u32[]{:S(2)}, u32[]{:S(2)}) collective-permute-start(bf16[256,2048]{1,0:T(8,128)(2,1)S(1)} %add_convert_fusion.3), channel_id=1, source_target_pairs={{0,2},{1,3},{2,0},{3,1},{4,6},{5,7},{6,4},{7,5},{8,10},{9,11},{10,... | collective-permute-start | bytes 3145736 | tf_op jit(solution)/shard_map/ppermute | solution.py:42
  415.7 25.8 %collective-permute-start.58 = (bf16[256,2048]{1,0:T(8,128)(2,1)}, bf16[256,2048]{1,0:T(8,128)(2,1)}, u32[]{:S(2)}, u32[]{:S(2)}) collective-permute-start(bf16[256,2048]{1,0:T(8,128)(2,1)} %get-tuple-element.742.refs_9_.rest_0_), channel_id=1, source_target_pairs={{0,2},{1,3},{2,0},{3,1},{4,6},{5,7},{6,4},{7,5},{8,10},{9,11},{10,... | collective-permute-start | bytes 3145736 | tf_op jit(solution)/shard_map/ppermute | solution.py:42
  444.5 31.8 %collective-permute-start.60 = (bf16[256,2048]{1,0:T(8,128)(2,1)}, bf16[256,2048]{1,0:T(8,128)(2,1)}, u32[]{:S(2)}, u32[]{:S(2)}) collective-permute-start(bf16[256,2048]{1,0:T(8,128)(2,1)} %add_convert_fusion.2), channel_id=1, source_target_pairs={{0,2},{1,3},{2,0},{3,1},{4,6},{5,7},{6,4},{7,5},{8,10},{9,11},{10,... | collective-permute-start | bytes 3145736 | tf_op jit(solution)/shard_map/ppermute | solution.py:42
  454.4 21.9 %collective-permute-start.61 = (f32[2,128,80]{2,1,0:T(8,128)}, f32[2,128,80]{2,1,0:T(8,128)S(1)}, u32[]{:S(2)}, u32[]{:S(2)}) collective-permute-start(f32[2,128,80]{2,1,0:T(8,128)} %get-tuple-element.780), channel_id=1, source_target_pairs={{4,0},{8,4},{12,8},{5,1},{9,5},{13,9},{6,2},{10,6},{14,10},{7,3},{... | collective-permute-start | bytes 245768 | tf_op jit(solution)/shard_map/ppermute | solution.py:47
  455.7 20.6 %collective-permute-start.62 = (f32[2,128,80]{2,1,0:T(8,128)}, f32[2,128,80]{2,1,0:T(8,128)S(1)}, u32[]{:S(2)}, u32[]{:S(2)}) collective-permute-start(f32[2,128,80]{2,1,0:T(8,128)} %get-tuple-element.780), channel_id=1, source_target_pairs={{8,0},{12,4},{9,1},{13,5},{10,2},{14,6},{11,3},{15,7},{24,16},{28,... | collective-permute-start | bytes 245768 | tf_op jit(solution)/shard_map/ppermute | solution.py:47
  457.0 19.4 %collective-permute-start.63 = (f32[2,128,80]{2,1,0:T(8,128)}, f32[2,128,80]{2,1,0:T(8,128)S(1)}, u32[]{:S(2)}, u32[]{:S(2)}) collective-permute-start(f32[2,128,80]{2,1,0:T(8,128)} %get-tuple-element.780), channel_id=1, source_target_pairs={{12,0},{13,1},{14,2},{15,3},{28,16},{29,17},{30,18},{31,19}} | collective-permute-start | bytes 245768 | tf_op jit(solution)/shard_map/ppermute | solution.py:47
  479.0 26.7 %collective-permute-start.64 = (bf16[256,2048]{1,0:T(8,128)(2,1)}, bf16[256,2048]{1,0:T(8,128)(2,1)S(1)}, u32[]{:S(2)}, u32[]{:S(2)}) collective-permute-start(bf16[256,2048]{1,0:T(8,128)(2,1)} %add_convert_fusion.1.refs_1_), channel_id=1, source_target_pairs={{0,2},{1,3},{2,0},{3,1},{4,6},{5,7},{6,4},{7,5},{8,10},{9,11},{10,... | collective-permute-start | bytes 3145736 | tf_op jit(solution)/shard_map/ppermute | solution.py:42
  479.6 26.1 %collective-permute-start.65 = (bf16[256,2048]{1,0:T(8,128)(2,1)}, bf16[256,2048]{1,0:T(8,128)(2,1)S(1)}, u32[]{:S(2)}, u32[]{:S(2)}) collective-permute-start(bf16[256,2048]{1,0:T(8,128)(2,1)} %add_convert_fusion.1.refs_1_), channel_id=1, source_target_pairs={{0,1},{1,0},{2,3},{3,2},{4,5},{5,4},{6,7},{7,6},{8,9},{9,8},{10,11... | collective-permute-start | bytes 3145736 | tf_op jit(solution)/shard_map/ppermute | solution.py:42
  513.0 25.5 %collective-permute-start.70 = (bf16[256,2048]{1,0:T(8,128)(2,1)}, bf16[256,2048]{1,0:T(8,128)(2,1)}, u32[]{:S(2)}, u32[]{:S(2)}) collective-permute-start(bf16[256,2048]{1,0:T(8,128)(2,1)} %add_convert_fusion), channel_id=1, source_target_pairs={{0,2},{1,3},{2,0},{3,1},{4,6},{5,7},{6,4},{7,5},{8,10},{9,11},{10,... | collective-permute-start | bytes 3145736 | tf_op jit(solution)/shard_map/ppermute | solution.py:42
  543.7 25.9 %collective-permute-start.76 = (bf16[256,2048]{1,0:T(8,128)(2,1)}, bf16[256,2048]{1,0:T(8,128)(2,1)}, u32[]{:S(2)}, u32[]{:S(2)}) collective-permute-start(bf16[256,2048]{1,0:T(8,128)(2,1)} %own_rows.5.refs_1_), channel_id=1, source_target_pairs={{0,2},{1,3},{2,0},{3,1},{4,6},{5,7},{6,4},{7,5},{8,10},{9,11},{10,... | collective-permute-start | bytes 3145736 | tf_op jit(solution)/shard_map/ppermute | solution.py:42
  (148 other events, 1900.5 us)

commit v7 on v6

--- a/solution.py
+++ b/solution.py
@@ -908,13 +908,12 @@
 
     halo = shifted(clock.tie(tokens)[rows - WIN :], "seq", 1)
     attn_chain.step()
-    (halo,) = clock.wait(halo)
     gain_attn = attention_norm_gain.astype(f32)[None, :]
     gain_mlp = feedforward_norm_gain.astype(f32)[None, :]
     downs = jnp.concatenate([query_adapter_down, key_adapter_down, value_adapter_down], axis=1)
     low_shape = (ext, 3 * rank)
 
-    def norm_half(half, earlier):
+    def norm_half(half, halo, earlier):
         size = rows // 2 + (ext - rows - WIN if half else WIN)
         return pl.pallas_call(
             lambda *refs: norm_body(half, *refs),
@@ -938,9 +937,10 @@
             name="norm",
         )(clock.tie(tokens), halo, gain_attn, downs, *earlier)
 
-    normed_low = clock.wait(*norm_half(0, ()))
+    normed_low = clock.wait(*norm_half(1, jnp.zeros((WIN, model), bf16), ()))
     attn_chain.step()
-    normed, low = clock.wait(*norm_half(1, normed_low))
+    (halo,) = clock.wait(halo)
+    normed, low = clock.wait(*norm_half(0, halo, normed_low))
     attn_chain.step()
     all_units = [x for part in FFN_UNITS for x in part]
     pack_in = (

time: 588 us -> 594 us (1.010)
  waiting for transfers between devices: 192 us -> 198 us
  transfers between devices with their start and end apart: 79 -> 79, of which waited for: 41 -> 41; matrix products, arithmetic and copies ran while one was open for 3% -> 3% of each run, Pallas kernels for 39% -> 38%
where the time goes in v7:
time: 594 us; the launch traced here: 586 us
  Pallas kernels  253 us (43%)
  waiting for transfers between devices  198 us (33%)
  starting transfers between devices  86.4 us (15%)
  local copies, waits for them, and re-layouts  26.9 us (5%)
  other arithmetic  18.8 us (3%)
    ppermute x42, waiting for transfers between devices, step(): lane.append(lax.ppermute(lane[-1], ('dp', 'seq'), way))  122 us
    pallas_call x6, Pallas kernels, ffn(): pl.pallas_call(lambda *refs: ffn_body(sizes, units, bool(sums), last, *re...  108 us
    ppermute x29, waiting for transfers between devices, exchange(): return lax.ppermute(x, axis, [(i, i ^ bit) for i in range(count)])  66.4 us
    ppermute x42, starting transfers between devices, step(): lane.append(lax.ppermute(lane[-1], ('dp', 'seq'), way))  46.9 us
    ppermute x29, starting transfers between devices, exchange(): return lax.ppermute(x, axis, [(i, i ^ bit) for i in range(count)])  20.4 us
    ppermute x8, starting transfers between devices, shifted(): lax.ppermute(x, axis, [(i, i + by) for i in range(count) if 0 <= i + by <...  19.1 us
    unnamed x209, local copies, waits for them, and re-layouts  18.8 us
    pallas_call x1, Pallas kernels, per_device(): pl.pallas_call(lambda *refs: backward_body((kv_heads, group, head, chunks...  17.2 us
  transfers between devices with their start and end apart: 79, of which 41 were waited for; matrix products, arithmetic and copies ran while one was open for 3% of the time, Pallas kernels for 38%

profile of v7, /device:TPU:0, one launch (start us, length us, event | category | flops | bytes accessed | tf_op | source)
XLA Modules:
  0.0 586.2 jit_solution(11013625030518617831)
XLA Ops:
  16.7 7.1 %collective-permute-done.3.refs_14_.refs_7_.refs_13_.refs_11_ = bf16[128,1280]{1,0:T(8,128)(2,1)S(1)} collective-permute-done((bf16[128,1280]{1,0:T(8,128)(2,1)S(1)}, bf16[128,1280]{1,0:T(8,128)(2,1)S(1)}, u32[]{:S(2)}, u32[]{:S(2)}) %collective-permute-start.3) | collective-permute-done | bytes 327712 | tf_op jit(solution)/shard_map/ppermute | solution.py:108
  41.4 5.2 collective-permute-done.8.refs_1_
  75.7 5.8 collective-permute-done.14.refs_27_.refs_20_.refs_26_.refs_24_
  87.1 16.9 %prep.1 = (bf16[512,1024]{1,0:T(8,128)(2,1)}, bf16[1024,1024]{1,0:T(8,128)(2,1)}, bf16[1152,128]{1,0:T(8,128)(2,1)}, bf16[128,1152]{1,0:T(8,128)(2,1)}, bf16[115...) custom-call(s32[16]{0:T(128)} %get-tuple-element.822.refs_0_, ...), custom_call_target="tpu_custom_call" | custom-call | flops 1 | bytes 1 | tf_op jit(solution)/shard_map/prep/pallas_call | solution.py:995
  110.0 5.1 collective-permute-start.20
  120.2 10.5 %attend.1 = (bf16[1024,512]{1,0:T(8,128)(2,1)}, f32[512,1024]{1,0:T(8,128)}, f32[8,1024]{1,0:T(8,128)}, bf16[8,2,128,80]{3,2,1,0:T(8,128)(2,1)}) custom-call(s32[9]{0:T(128)} %copy-done.17, f32[3]{0:T(128)} %copy-done.20, bf16[512,1024]{1,0:T(8,128)(2,1)} %get-tuple-element.560.refs_2_.refs_1_, ...), custom_call_target="tpu_custom_call" | custom-call | flops 1 | bytes 1 | tf_op jit(solution)/shard_map/attend/pallas_call | solution.py:1014
  136.2 10.7 %project.1 = (bf16[256,2048]{1,0:T(8,128)(2,1)}, bf16[256,2048]{1,0:T(8,128)(2,1)}, bf16[256,2048]{1,0:T(8,128)(2,1)}, bf16[256,2048]{1,0:T(8,128)(2,1)}, f32[1024,8]{1,0:T(8,128)}) custom-call(s32[16]{0:T(128)} %get-tuple-element.822.refs_0_, s32[4]{0:T(128)} %pad_add_fusion.refs_1_.nat.refs_0_, bf16[1024,512]{1,0:T(8,128)(2,1)} %get-tuple-element.576.refs_2_.att, ...), custom_call_target="tpu_custom_call" | custom-call | flops 1 | bytes 1 | tf_op jit(solution)/shard_map/project/pallas_call | solution.py:1055
  154.7 12.4 %collective-permute-done.28.refs_9_ = bf16[256,1536]{1,0:T(8,128)(2,1)S(1)} collective-permute-done((bf16[256,1536]{1,0:T(8,128)(2,1)S(1)}, bf16[256,1536]{1,0:T(8,128)(2,1)S(1)}, u32[]{:S(2)}, u32[]{:S(2)}) %collective-permute-start.28) | collective-permute-done | bytes 786464 | tf_op jit(solution)/shard_map/ppermute | solution.py:108
  169.8 8.6 %collective-permute-done.26.across = bf16[256,2048]{1,0:T(8,128)(2,1)S(1)} collective-permute-done((bf16[256,2048]{1,0:T(8,128)(2,1)S(1)}, bf16[256,2048]{1,0:T(8,128)(2,1)S(1)}, u32[]{:S(2)}, u32[]{:S(2)}) %collective-permute-start.26) | collective-permute-done | bytes 1048608 | tf_op jit(solution)/shard_map/ppermute | solution.py:42
  191.8 16.4 %collective-permute-done.32.refs_11_ = bf16[256,1536]{1,0:T(8,128)(2,1)S(1)} collective-permute-done((bf16[256,1536]{1,0:T(8,128)(2,1)S(1)}, bf16[256,1536]{1,0:T(8,128)(2,1)S(1)}, u32[]{:S(2)}, u32[]{:S(2)}) %collective-permute-start.32) | collective-permute-done | bytes 786464 | tf_op jit(solution)/shard_map/ppermute | solution.py:108
  210.3 5.3 collective-permute-done.36.refs_4_
  215.6 11.9 %collective-permute-done.35.refs_12_ = bf16[256,1536]{1,0:T(8,128)(2,1)S(1)} collective-permute-done((bf16[256,1536]{1,0:T(8,128)(2,1)S(1)}, bf16[256,1536]{1,0:T(8,128)(2,1)S(1)}, u32[]{:S(2)}, u32[]{:S(2)}) %collective-permute-start.35) | collective-permute-done | bytes 786464 | tf_op jit(solution)/shard_map/ppermute | solution.py:108
  232.6 14.8 %feed_forward.6 = (f32[2,256,2048]{2,1,0:T(8,128)}, f32[2,256,2048]{2,1,0:T(8,128)}) custom-call(s32[8]{0:T(128)} %copy-done.96, s32[4]{0:T(128)} %pad_add_fusion.refs_1_.nat.refs_0_, bf16[1024,2048]{1,0:T(8,128)(2,1)} %cotangent.1, bf16[256,2048]{1,0:T(8,128)(2,1)} %copy-done.26, bf16[256,2048]{1,0:T(8,128)(2,1)} %copy-done.25, ...), custom_call_target="tpu_custom_call" | custom-call | flops 1 | bytes 1 | tf_op jit(solution)/shard_map/feed_forward/pallas_call | solution.py:1111
  251.6 14.7 %feed_forward.7 = (f32[2,256,2048]{2,1,0:T(8,128)}, f32[2,256,2048]{2,1,0:T(8,128)}) custom-call(s32[8]{0:T(128)} %copy-done.96, s32[4]{0:T(128)} %pad_add_fusion.refs_1_.nat.refs_0_, bf16[1024,2048]{1,0:T(8,128)(2,1)} %cotangent.1, bf16[256,2048]{1,0:T(8,128)(2,1)} %copy-done.24, bf16[256,2048]{1,0:T(8,128)(2,1)} %get-tuple-element.620.refs_4_, ...), custom_call_target="tpu_custom_call" | custom-call | flops 1 | bytes 1 | tf_op jit(solution)/shard_map/feed_forward/pallas_call | solution.py:1111
  271.0 15.6 %feed_forward.8 = (f32[2,256,2048]{2,1,0:T(8,128)}, f32[2,256,2048]{2,1,0:T(8,128)}) custom-call(s32[8]{0:T(128)} %copy-done.95, s32[4]{0:T(128)} %pad_add_fusion.refs_1_.nat.refs_0_, bf16[1024,2048]{1,0:T(8,128)(2,1)} %cotangent.1, bf16[256,2048]{1,0:T(8,128)(2,1)} %copy-done.26, bf16[256,2048]{1,0:T(8,128)(2,1)} %copy-done.25, ...), custom_call_target="tpu_custom_call" | custom-call | flops 1 | bytes 1 | tf_op jit(solution)/shard_map/feed_forward/pallas_call | solution.py:1111
  289.5 15.7 %feed_forward.9 = (f32[2,256,2048]{2,1,0:T(8,128)}, f32[2,256,2048]{2,1,0:T(8,128)}) custom-call(s32[8]{0:T(128)} %copy-done.95, s32[4]{0:T(128)} %pad_add_fusion.refs_1_.nat.refs_0_, bf16[1024,2048]{1,0:T(8,128)(2,1)} %cotangent.1, bf16[256,2048]{1,0:T(8,128)(2,1)} %copy-done.24, bf16[256,2048]{1,0:T(8,128)(2,1)} %get-tuple-element.620.refs_4_, ...), custom_call_target="tpu_custom_call" | custom-call | flops 1 | bytes 1 | tf_op jit(solution)/shard_map/feed_forward/pallas_call | solution.py:1111
  307.3 15.7 %collective-permute-done.47.refs_10_ = bf16[256,1536]{1,0:T(8,128)(2,1)S(1)} collective-permute-done((bf16[256,1536]{1,0:T(8,128)(2,1)S(1)}, bf16[256,1536]{1,0:T(8,128)(2,1)S(1)}, u32[]{:S(2)}, u32[]{:S(2)}) %collective-permute-start.47) | collective-permute-done | bytes 786464 | tf_op jit(solution)/shard_map/ppermute | solution.py:108
  325.0 15.7 %collective-permute-done.49.refs_11_ = bf16[256,1536]{1,0:T(8,128)(2,1)S(1)} collective-permute-done((bf16[256,1536]{1,0:T(8,128)(2,1)S(1)}, bf16[256,1536]{1,0:T(8,128)(2,1)S(1)}, u32[]{:S(2)}, u32[]{:S(2)}) %collective-permute-start.49) | collective-permute-done | bytes 786464 | tf_op jit(solution)/shard_map/ppermute | solution.py:108
  342.7 13.1 %collective-permute-done.51.refs_12_ = bf16[256,1536]{1,0:T(8,128)(2,1)S(1)} collective-permute-done((bf16[256,1536]{1,0:T(8,128)(2,1)S(1)}, bf16[256,1536]{1,0:T(8,128)(2,1)S(1)}, u32[]{:S(2)}, u32[]{:S(2)}) %collective-permute-start.51) | collective-permute-done | bytes 786464 | tf_op jit(solution)/shard_map/ppermute | solution.py:108
  358.2 23.5 %feed_forward.10 = (bf16[256,2048]{1,0:T(8,128)(2,1)}, bf16[256,2048]{1,0:T(8,128)(2,1)}, bf16[256,2048]{1,0:T(8,128)(2,1)}, bf16[256,2048]{1,0:T(8,128)(2,1)}) custom-call(s32[16]{0:T(128)} %get-tuple-element.716.refs_0_, s32[4]{0:T(128)} %pad_add_fusion.refs_1_.nat.refs_0_, bf16[1024,2048]{1,0:T(8,128)(2,1)} %cotangent.1, bf16[256,2048]{1,0:T(8,128)(2,1)} %copy-done.26, ...), custom_call_target="tpu_custom_call" | custom-call | flops 1 | bytes 1 | tf_op jit(solution)/shard_map/feed_forward/pallas_call | solution.py:1111
  387.8 23.7 %feed_forward.11 = (bf16[256,2048]{1,0:T(8,128)(2,1)}, bf16[256,2048]{1,0:T(8,128)(2,1)}, bf16[256,2048]{1,0:T(8,128)(2,1)}, bf16[256,2048]{1,0:T(8,128)(2,1)}) custom-call(s32[16]{0:T(128)} %get-tuple-element.716.refs_0_, s32[4]{0:T(128)} %pad_add_fusion.refs_1_.nat.refs_0_, bf16[1024,2048]{1,0:T(8,128)(2,1)} %cotangent.1, bf16[256,2048]{1,0:T(8,128)(2,1)} %copy-done.24, ...), custom_call_target="tpu_custom_call" | custom-call | flops 1 | bytes 1 | tf_op jit(solution)/shard_map/feed_forward/pallas_call | solution.py:1111
  415.4 5.6 own_rows.4
  424.9 8.5 %project_back.2 = (bf16[512,1024]{1,0:T(8,128)(2,1)}, f32[8,1024]{1,0:T(8,128)}, f32[1024,8]{1,0:T(8,128)}, f32[2,128,80]{2,1,0:T(8,128)}) custom-call(s32[16]{0:T(128)} %get-tuple-element.822.refs_0_, s32[4]{0:T(128)} %pad_add_fusion.refs_1_.nat.refs_0_, s32[9]{0:T(128)} %copy-done.17, bf16[2048,8]{1,0:T(8,128)(2,1)} %get-tuple-element.746.refs_3_, ...), custom_call_target="tpu_custom_call" | custom-call | flops 1 | bytes 1 | tf_op jit(solution)/shard_map/project_back/pallas_call | solution.py:1169
  437.4 10.6 %collective-permute-done.58.refs_9_.rest_2_ = bf16[256,2048]{1,0:T(8,128)(2,1)} collective-permute-done((bf16[256,2048]{1,0:T(8,128)(2,1)}, bf16[256,2048]{1,0:T(8,128)(2,1)}, u32[]{:S(2)}, u32[]{:S(2)}) %collective-permute-start.58) | collective-permute-done | bytes 1048608 | tf_op jit(solution)/shard_map/ppermute | solution.py:42
  452.5 8.4 %project_back.3 = (bf16[512,1024]{1,0:T(8,128)(2,1)}, f32[8,1024]{1,0:T(8,128)}, f32[1024,8]{1,0:T(8,128)}, f32[2,128,80]{2,1,0:T(8,128)}) custom-call(s32[16]{0:T(128)} %get-tuple-element.822.refs_0_, s32[4]{0:T(128)} %pad_add_fusion.refs_1_.nat.refs_0_, s32[9]{0:T(128)} %copy-done.17, ...), custom_call_target="tpu_custom_call", output_to_operand_aliasing={{0}: (27, {}), {1}: (28, {}), {2}: (29, {})} | custom-call | flops 1 | bytes 1 | tf_op jit(solution)/shard_map/project_back/pallas_call | solution.py:1169
  465.6 17.2 %attend_back.1 = (bf16[1024,512]{1,0:T(8,128)(2,1)}, f32[128,1152]{1,0:T(8,128)}, f32[128,1152]{1,0:T(8,128)}, f32[256,1152]{1,0:T(8,128)}, f32[2,256,256]{2,1,0:T(8,128)}) custom-call(s32[9]{0:T(128)S(1)} %copy-done.18, bf16[512,1024]{1,0:T(8,128)(2,1)} %get-tuple-element.560.refs_2_.refs_1_, bf16[1024,1024]{1,0:T(8,128)(2,1)} %get-tuple-element.561.refs_3_.refs_7_.refs_2_, ...), custom_call_target="tpu_custom_call" | custom-call | flops 1 | bytes 1 | tf_op jit(solution)/shard_map/attend_back/pallas_call | solution.py:1239
  492.8 5.2 adapter_o.1
  499.8 12.4 %norm_back.1 = (bf16[256,2048]{1,0:T(8,128)(2,1)}, bf16[256,2048]{1,0:T(8,128)(2,1)}, bf16[256,2048]{1,0:T(8,128)(2,1)}, bf16[256,2048]{1,0:T(8,128)(2,1)}) custom-call(s32[16]{0:T(128)} %get-tuple-element.822.refs_0_, s32[4]{0:T(128)} %pad_add_fusion.refs_1_.nat.refs_0_, bf16[1024,512]{1,0:T(8,128)(2,1)} %get-tuple-element.845.refs_2_.refs_0_, ...), custom_call_target="tpu_custom_call" | custom-call | flops 1 | bytes 1 | tf_op jit(solution)/shard_map/norm_back/pallas_call | solution.py:1311
  521.8 6.2 %adapters.1 = f32[8,18,8,128]{3,2,1,0:T(8,128)} custom-call(bf16[1024,512]{1,0:T(8,128)(2,1)} %get-tuple-element.845.refs_2_.refs_0_, f32[256,1024]{1,0:T(8,128)} %get-tuple-element.824.refs_3_.refs_1_, f32[256,128]{1,0:T(8,128)} %copy-done.78, f32[32,1024]{1,0:T(8,128)} %copy-done.2, f32[32,1024]{1,0:T(8,128)} %copy-done.4, ...), custom_call_target="tpu_custom_call" | custom-call | flops 1 | bytes 1 | tf_op jit(solution)/shard_map/adapters/pallas_call | solution.py:1349
  529.3 5.3 collective-permute-done.71
  545.0 5.2 own_rows.5.refs_1_
  562.4 13.7 %collective-permute-done.76.refs_1_ = bf16[256,2048]{1,0:T(8,128)(2,1)} collective-permute-done((bf16[256,2048]{1,0:T(8,128)(2,1)}, bf16[256,2048]{1,0:T(8,128)(2,1)}, u32[]{:S(2)}, u32[]{:S(2)}) %collective-permute-start.76) | collective-permute-done | bytes 1048608 | tf_op jit(solution)/shard_map/ppermute | solution.py:42
  (404 shorter events, 217.4 us)
Async XLA Ops:
  36.3 18.6 %collective-permute-start.6 = (bf16[128,1280]{1,0:T(8,128)(2,1)S(1)}, bf16[128,1280]{1,0:T(8,128)(2,1)S(1)}, u32[]{:S(2)}, u32[]{:S(2)}) collective-permute-start(bf16[128,1280]{1,0:T(8,128)(2,1)S(1)} %collective-permute-done.4.refs_23_.refs_16_.refs_22_.refs_20_), channel_id=1, source_target_pairs={{4,0},{8,4},{12,8},{28,12},{24,28},{20,24},{16,20},{0,16},{5,1},{9... | collective-permute-start | bytes 983048 | tf_op jit(solution)/shard_map/ppermute | solution.py:108
  83.1 20.9 %collective-permute-start.16 = (bf16[256,1536]{1,0:T(8,128)(2,1)}, bf16[256,1536]{1,0:T(8,128)(2,1)S(1)}, u32[]{:S(2)}, u32[]{:S(2)}) collective-permute-start(bf16[256,1536]{1,0:T(8,128)(2,1)} %get-tuple-element.533.refs_5_), channel_id=1, source_target_pairs={{0,4},{4,8},{8,12},{12,28},{28,24},{24,20},{20,16},{16,0},{1,5},{5... | collective-permute-start | bytes 2359304 | tf_op jit(solution)/shard_map/ppermute | solution.py:108
  85.6 20.5 %collective-permute-start.15 = (bf16[256,1536]{1,0:T(8,128)(2,1)}, bf16[256,1536]{1,0:T(8,128)(2,1)S(1)}, u32[]{:S(2)}, u32[]{:S(2)}) collective-permute-start(bf16[256,1536]{1,0:T(8,128)(2,1)} %get-tuple-element.532.refs_5_), channel_id=1, source_target_pairs={{4,0},{8,4},{12,8},{28,12},{24,28},{20,24},{16,20},{0,16},{5,1},{9... | collective-permute-start | bytes 2359304 | tf_op jit(solution)/shard_map/ppermute | solution.py:108
  104.0 26.6 %collective-permute-start.18 = (bf16[256,1536]{1,0:T(8,128)(2,1)S(1)}, bf16[256,1536]{1,0:T(8,128)(2,1)S(1)}, u32[]{:S(2)}, u32[]{:S(2)}) collective-permute-start(bf16[256,1536]{1,0:T(8,128)(2,1)S(1)} %collective-permute-done.16.refs_6_), channel_id=1, source_target_pairs={{0,4},{4,8},{8,12},{12,28},{28,24},{24,20},{20,16},{16,0},{1,5},{5... | collective-permute-start | bytes 2359304 | tf_op jit(solution)/shard_map/ppermute | solution.py:108
  106.1 28.0 %collective-permute-start.17 = (bf16[256,1536]{1,0:T(8,128)(2,1)S(1)}, bf16[256,1536]{1,0:T(8,128)(2,1)}, u32[]{:S(2)}, u32[]{:S(2)}) collective-permute-start(bf16[256,1536]{1,0:T(8,128)(2,1)S(1)} %collective-permute-done.15.refs_6_), channel_id=1, source_target_pairs={{4,0},{8,4},{12,8},{28,12},{24,28},{20,24},{16,20},{0,16},{5,1},{9... | collective-permute-start | bytes 2359304 | tf_op jit(solution)/shard_map/ppermute | solution.py:108
  147.6 19.5 %collective-permute-start.28 = (bf16[256,1536]{1,0:T(8,128)(2,1)S(1)}, bf16[256,1536]{1,0:T(8,128)(2,1)S(1)}, u32[]{:S(2)}, u32[]{:S(2)}) collective-permute-start(bf16[256,1536]{1,0:T(8,128)(2,1)S(1)} %collective-permute-done.23.refs_8_), channel_id=1, source_target_pairs={{0,4},{4,8},{8,12},{12,28},{28,24},{24,20},{20,16},{16,0},{1,5},{5... | collective-permute-start | bytes 2359304 | tf_op jit(solution)/shard_map/ppermute | solution.py:108
  149.6 19.5 %collective-permute-start.27 = (bf16[256,1536]{1,0:T(8,128)(2,1)S(1)}, bf16[256,1536]{1,0:T(8,128)(2,1)}, u32[]{:S(2)}, u32[]{:S(2)}) collective-permute-start(bf16[256,1536]{1,0:T(8,128)(2,1)S(1)} %collective-permute-done.22.refs_8_), channel_id=1, source_target_pairs={{4,0},{8,4},{12,8},{28,12},{24,28},{20,24},{16,20},{0,16},{5,1},{9... | collective-permute-start | bytes 2359304 | tf_op jit(solution)/shard_map/ppermute | solution.py:108
  153.2 25.3 %collective-permute-start.26 = (bf16[256,2048]{1,0:T(8,128)(2,1)S(1)}, bf16[256,2048]{1,0:T(8,128)(2,1)S(1)}, u32[]{:S(2)}, u32[]{:S(2)}) collective-permute-start(bf16[256,2048]{1,0:T(8,128)(2,1)S(1)} %add_convert_fusion.4), channel_id=1, source_target_pairs={{0,2},{1,3},{2,0},{3,1},{4,6},{5,7},{6,4},{7,5},{8,10},{9,11},{10,... | collective-permute-start | bytes 3145736 | tf_op jit(solution)/shard_map/ppermute | solution.py:42
  167.1 18.8 %collective-permute-start.30 = (bf16[256,1536]{1,0:T(8,128)(2,1)S(1)}, bf16[256,1536]{1,0:T(8,128)(2,1)S(1)}, u32[]{:S(2)}, u32[]{:S(2)}) collective-permute-start(bf16[256,1536]{1,0:T(8,128)(2,1)S(1)} %collective-permute-done.28.refs_9_), channel_id=1, source_target_pairs={{0,4},{4,8},{8,12},{12,28},{28,24},{24,20},{20,16},{16,0},{1,5},{5... | collective-permute-start | bytes 2359304 | tf_op jit(solution)/shard_map/ppermute | solution.py:108
  169.1 19.2 %collective-permute-start.29 = (bf16[256,1536]{1,0:T(8,128)(2,1)}, bf16[256,1536]{1,0:T(8,128)(2,1)}, u32[]{:S(2)}, u32[]{:S(2)}) collective-permute-start(bf16[256,1536]{1,0:T(8,128)(2,1)} %collective-permute-done.27.refs_9_), channel_id=1, source_target_pairs={{4,0},{8,4},{12,8},{28,12},{24,28},{20,24},{16,20},{0,16},{5,1},{9... | collective-permute-start | bytes 2359304 | tf_op jit(solution)/shard_map/ppermute | solution.py:108
  188.3 20.0 %collective-permute-start.32 = (bf16[256,1536]{1,0:T(8,128)(2,1)S(1)}, bf16[256,1536]{1,0:T(8,128)(2,1)S(1)}, u32[]{:S(2)}, u32[]{:S(2)}) collective-permute-start(bf16[256,1536]{1,0:T(8,128)(2,1)S(1)} %collective-permute-done.30.refs_10_), channel_id=1, source_target_pairs={{0,4},{4,8},{8,12},{12,28},{28,24},{24,20},{20,16},{16,0},{1,5},{5... | collective-permute-start | bytes 2359304 | tf_op jit(solution)/shard_map/ppermute | solution.py:108
  190.1 20.0 %collective-permute-start.31 = (bf16[256,1536]{1,0:T(8,128)(2,1)}, bf16[256,1536]{1,0:T(8,128)(2,1)S(1)}, u32[]{:S(2)}, u32[]{:S(2)}) collective-permute-start(bf16[256,1536]{1,0:T(8,128)(2,1)} %collective-permute-done.29.refs_10_), channel_id=1, source_target_pairs={{4,0},{8,4},{12,8},{28,12},{24,28},{20,24},{16,20},{0,16},{5,1},{9... | collective-permute-start | bytes 2359304 | tf_op jit(solution)/shard_map/ppermute | solution.py:108
  190.3 25.2 %collective-permute-start.36 = (bf16[256,2048]{1,0:T(8,128)(2,1)}, bf16[256,2048]{1,0:T(8,128)(2,1)S(1)}, u32[]{:S(2)}, u32[]{:S(2)}) collective-permute-start(bf16[256,2048]{1,0:T(8,128)(2,1)} %get-tuple-element.620.refs_4_), channel_id=1, source_target_pairs={{0,2},{1,3},{2,0},{3,1},{4,6},{5,7},{6,4},{7,5},{8,10},{9,11},{10,... | collective-permute-start | bytes 3145736 | tf_op jit(solution)/shard_map/ppermute | solution.py:42
  208.3 19.2 %collective-permute-start.35 = (bf16[256,1536]{1,0:T(8,128)(2,1)S(1)}, bf16[256,1536]{1,0:T(8,128)(2,1)S(1)}, u32[]{:S(2)}, u32[]{:S(2)}) collective-permute-start(bf16[256,1536]{1,0:T(8,128)(2,1)S(1)} %collective-permute-done.32.refs_11_), channel_id=1, source_target_pairs={{0,4},{4,8},{8,12},{12,28},{28,24},{24,20},{20,16},{16,0},{1,5},{5... | collective-permute-start | bytes 2359304 | tf_op jit(solution)/shard_map/ppermute | solution.py:108
  210.0 18.9 %collective-permute-start.34 = (bf16[256,1536]{1,0:T(8,128)(2,1)S(1)}, bf16[256,1536]{1,0:T(8,128)(2,1)S(1)}, u32[]{:S(2)}, u32[]{:S(2)}) collective-permute-start(bf16[256,1536]{1,0:T(8,128)(2,1)S(1)} %collective-permute-done.31.refs_11_), channel_id=1, source_target_pairs={{4,0},{8,4},{12,8},{28,12},{24,28},{20,24},{16,20},{0,16},{5,1},{9... | collective-permute-start | bytes 2359304 | tf_op jit(solution)/shard_map/ppermute | solution.py:108
  228.9 20.7 %collective-permute-start.38 = (bf16[256,1536]{1,0:T(8,128)(2,1)}, bf16[256,1536]{1,0:T(8,128)(2,1)}, u32[]{:S(2)}, u32[]{:S(2)}) collective-permute-start(bf16[256,1536]{1,0:T(8,128)(2,1)} %get-tuple-element.632.refs_5_), channel_id=1, source_target_pairs={{0,4},{4,8},{8,12},{12,28},{28,24},{24,20},{20,16},{16,0},{1,5},{5... | collective-permute-start | bytes 2359304 | tf_op jit(solution)/shard_map/ppermute | solution.py:108
  231.1 20.3 %collective-permute-start.37 = (bf16[256,1536]{1,0:T(8,128)(2,1)}, bf16[256,1536]{1,0:T(8,128)(2,1)}, u32[]{:S(2)}, u32[]{:S(2)}) collective-permute-start(bf16[256,1536]{1,0:T(8,128)(2,1)} %get-tuple-element.631.refs_13_), channel_id=1, source_target_pairs={{4,0},{8,4},{12,8},{28,12},{24,28},{20,24},{16,20},{0,16},{5,1},{9... | collective-permute-start | bytes 2359304 | tf_op jit(solution)/shard_map/ppermute | solution.py:108
  249.6 19.4 %collective-permute-start.41 = (bf16[256,1536]{1,0:T(8,128)(2,1)}, bf16[256,1536]{1,0:T(8,128)(2,1)S(1)}, u32[]{:S(2)}, u32[]{:S(2)}) collective-permute-start(bf16[256,1536]{1,0:T(8,128)(2,1)} %collective-permute-done.38.refs_6_), channel_id=1, source_target_pairs={{0,4},{4,8},{8,12},{12,28},{28,24},{24,20},{20,16},{16,0},{1,5},{5... | collective-permute-start | bytes 2359304 | tf_op jit(solution)/shard_map/ppermute | solution.py:108
  251.4 19.4 %collective-permute-start.40 = (bf16[256,1536]{1,0:T(8,128)(2,1)}, bf16[256,1536]{1,0:T(8,128)(2,1)S(1)}, u32[]{:S(2)}, u32[]{:S(2)}) collective-permute-start(bf16[256,1536]{1,0:T(8,128)(2,1)} %collective-permute-done.37.refs_14_), channel_id=1, source_target_pairs={{4,0},{8,4},{12,8},{28,12},{24,28},{20,24},{16,20},{0,16},{5,1},{9... | collective-permute-start | bytes 2359304 | tf_op jit(solution)/shard_map/ppermute | solution.py:108
  269.0 18.3 %collective-permute-start.43 = (bf16[256,1536]{1,0:T(8,128)(2,1)S(1)}, bf16[256,1536]{1,0:T(8,128)(2,1)S(1)}, u32[]{:S(2)}, u32[]{:S(2)}) collective-permute-start(bf16[256,1536]{1,0:T(8,128)(2,1)S(1)} %collective-permute-done.41.refs_7_), channel_id=1, source_target_pairs={{0,4},{4,8},{8,12},{12,28},{28,24},{24,20},{20,16},{16,0},{1,5},{5... | collective-permute-start | bytes 2359304 | tf_op jit(solution)/shard_map/ppermute | solution.py:108
  270.7 18.3 %collective-permute-start.42 = (bf16[256,1536]{1,0:T(8,128)(2,1)S(1)}, bf16[256,1536]{1,0:T(8,128)(2,1)S(1)}, u32[]{:S(2)}, u32[]{:S(2)}) collective-permute-start(bf16[256,1536]{1,0:T(8,128)(2,1)S(1)} %collective-permute-done.40.refs_15_), channel_id=1, source_target_pairs={{4,0},{8,4},{12,8},{28,12},{24,28},{20,24},{16,20},{0,16},{5,1},{9... | collective-permute-start | bytes 2359304 | tf_op jit(solution)/shard_map/ppermute | solution.py:108
  289.0 18.0 %collective-permute-start.44 = (bf16[256,1536]{1,0:T(8,128)(2,1)S(1)}, bf16[256,1536]{1,0:T(8,128)(2,1)S(1)}, u32[]{:S(2)}, u32[]{:S(2)}) collective-permute-start(bf16[256,1536]{1,0:T(8,128)(2,1)S(1)} %collective-permute-done.42.refs_16_), channel_id=1, source_target_pairs={{4,0},{8,4},{12,8},{28,12},{24,28},{20,24},{16,20},{0,16},{5,1},{9... | collective-permute-start | bytes 2359304 | tf_op jit(solution)/shard_map/ppermute | solution.py:108
  386.2 25.3 %collective-permute-start.53 = (bf16[256,2048]{1,0:T(8,128)(2,1)S(1)}, bf16[256,2048]{1,0:T(8,128)(2,1)S(1)}, u32[]{:S(2)}, u32[]{:S(2)}) collective-permute-start(bf16[256,2048]{1,0:T(8,128)(2,1)S(1)} %add_convert_fusion.3), channel_id=1, source_target_pairs={{0,2},{1,3},{2,0},{3,1},{4,6},{5,7},{6,4},{7,5},{8,10},{9,11},{10,... | collective-permute-start | bytes 3145736 | tf_op jit(solution)/shard_map/ppermute | solution.py:42
  422.3 25.8 %collective-permute-start.58 = (bf16[256,2048]{1,0:T(8,128)(2,1)}, bf16[256,2048]{1,0:T(8,128)(2,1)}, u32[]{:S(2)}, u32[]{:S(2)}) collective-permute-start(bf16[256,2048]{1,0:T(8,128)(2,1)} %get-tuple-element.742.refs_9_.rest_0_), channel_id=1, source_target_pairs={{0,2},{1,3},{2,0},{3,1},{4,6},{5,7},{6,4},{7,5},{8,10},{9,11},{10,... | collective-permute-start | bytes 3145736 | tf_op jit(solution)/shard_map/ppermute | solution.py:42
  451.0 31.8 %collective-permute-start.60 = (bf16[256,2048]{1,0:T(8,128)(2,1)}, bf16[256,2048]{1,0:T(8,128)(2,1)}, u32[]{:S(2)}, u32[]{:S(2)}) collective-permute-start(bf16[256,2048]{1,0:T(8,128)(2,1)} %add_convert_fusion.2), channel_id=1, source_target_pairs={{0,2},{1,3},{2,0},{3,1},{4,6},{5,7},{6,4},{7,5},{8,10},{9,11},{10,... | collective-permute-start | bytes 3145736 | tf_op jit(solution)/shard_map/ppermute | solution.py:42
  460.9 21.9 %collective-permute-start.61 = (f32[2,128,80]{2,1,0:T(8,128)}, f32[2,128,80]{2,1,0:T(8,128)S(1)}, u32[]{:S(2)}, u32[]{:S(2)}) collective-permute-start(f32[2,128,80]{2,1,0:T(8,128)} %get-tuple-element.780), channel_id=1, source_target_pairs={{4,0},{8,4},{12,8},{5,1},{9,5},{13,9},{6,2},{10,6},{14,10},{7,3},{... | collective-permute-start | bytes 245768 | tf_op jit(solution)/shard_map/ppermute | solution.py:47
  462.2 20.6 %collective-permute-start.62 = (f32[2,128,80]{2,1,0:T(8,128)}, f32[2,128,80]{2,1,0:T(8,128)S(1)}, u32[]{:S(2)}, u32[]{:S(2)}) collective-permute-start(f32[2,128,80]{2,1,0:T(8,128)} %get-tuple-element.780), channel_id=1, source_target_pairs={{8,0},{12,4},{9,1},{13,5},{10,2},{14,6},{11,3},{15,7},{24,16},{28,... | collective-permute-start | bytes 245768 | tf_op jit(solution)/shard_map/ppermute | solution.py:47
  463.5 19.4 %collective-permute-start.63 = (f32[2,128,80]{2,1,0:T(8,128)}, f32[2,128,80]{2,1,0:T(8,128)S(1)}, u32[]{:S(2)}, u32[]{:S(2)}) collective-permute-start(f32[2,128,80]{2,1,0:T(8,128)} %get-tuple-element.780), channel_id=1, source_target_pairs={{12,0},{13,1},{14,2},{15,3},{28,16},{29,17},{30,18},{31,19}} | collective-permute-start | bytes 245768 | tf_op jit(solution)/shard_map/ppermute | solution.py:47
  485.5 26.7 %collective-permute-start.64 = (bf16[256,2048]{1,0:T(8,128)(2,1)}, bf16[256,2048]{1,0:T(8,128)(2,1)S(1)}, u32[]{:S(2)}, u32[]{:S(2)}) collective-permute-start(bf16[256,2048]{1,0:T(8,128)(2,1)} %add_convert_fusion.1.refs_1_), channel_id=1, source_target_pairs={{0,2},{1,3},{2,0},{3,1},{4,6},{5,7},{6,4},{7,5},{8,10},{9,11},{10,... | collective-permute-start | bytes 3145736 | tf_op jit(solution)/shard_map/ppermute | solution.py:42
  486.2 26.1 %collective-permute-start.65 = (bf16[256,2048]{1,0:T(8,128)(2,1)}, bf16[256,2048]{1,0:T(8,128)(2,1)S(1)}, u32[]{:S(2)}, u32[]{:S(2)}) collective-permute-start(bf16[256,2048]{1,0:T(8,128)(2,1)} %add_convert_fusion.1.refs_1_), channel_id=1, source_target_pairs={{0,1},{1,0},{2,3},{3,2},{4,5},{5,4},{6,7},{7,6},{8,9},{9,8},{10,11... | collective-permute-start | bytes 3145736 | tf_op jit(solution)/shard_map/ppermute | solution.py:42
  519.5 25.5 %collective-permute-start.70 = (bf16[256,2048]{1,0:T(8,128)(2,1)}, bf16[256,2048]{1,0:T(8,128)(2,1)}, u32[]{:S(2)}, u32[]{:S(2)}) collective-permute-start(bf16[256,2048]{1,0:T(8,128)(2,1)} %add_convert_fusion), channel_id=1, source_target_pairs={{0,2},{1,3},{2,0},{3,1},{4,6},{5,7},{6,4},{7,5},{8,10},{9,11},{10,... | collective-permute-start | bytes 3145736 | tf_op jit(solution)/shard_map/ppermute | solution.py:42
  550.2 25.9 %collective-permute-start.76 = (bf16[256,2048]{1,0:T(8,128)(2,1)}, bf16[256,2048]{1,0:T(8,128)(2,1)}, u32[]{:S(2)}, u32[]{:S(2)}) collective-permute-start(bf16[256,2048]{1,0:T(8,128)(2,1)} %own_rows.5.refs_1_), channel_id=1, source_target_pairs={{0,2},{1,3},{2,0},{3,1},{4,6},{5,7},{6,4},{7,5},{8,10},{9,11},{10,... | collective-permute-start | bytes 3145736 | tf_op jit(solution)/shard_map/ppermute | solution.py:42
  (148 other events, 1956.1 us)
